TPU v7x, 32 devices: a whole 2x2x4 slice. The times are simulated.
32 devices in a mesh: grp: 4 (over y, core), dev: 8 (over z, x).
Axes of the slice: x: 2, y: 2, z: 4, core: 2. Of those that a mesh axis runs over, the one named last changes fastest.
Arguments:
- suffix_queries: bfloat16 [4096, 2048], P(('grp', 'dev')), may hold values from -12 to 12
- suffix_keys: bfloat16 [4096, 2048], P(('grp', 'dev')), may hold values from -12 to 12
- suffix_values: bfloat16 [4096, 2048], P(('grp', 'dev')), may hold values from -6 to 6
- layer_input: bfloat16 [4096, 2048], P(('grp', 'dev')), may hold values from -6 to 6
- suffix_lengths: int32 [32, 4], P(('grp', 'dev')), may hold values from 1 to 64, as said below
- request_group: int32 [32, 4], P(('grp', 'dev')), may hold values from 0 to 3, as said below
- prefix_keys: bfloat16 [4, 4096, 2048], P('grp', None, 'dev'), may hold values from -12 to 12
- prefix_values: bfloat16 [4, 4096, 2048], P('grp', None, 'dev'), may hold values from -6 to 6
- up_weight: bfloat16 [2048, 8192], P(None, ('grp', 'dev')), may hold values from -0.125 to 0.125
- up_bias: bfloat16 [8192], P(('grp', 'dev')), may hold values from -3 to 3
- down_weight: bfloat16 [8192, 2048], P(('grp', 'dev')), may hold values from -0.0625 to 0.0625
- down_bias: float32 [2048], replicated, may hold values from -3 to 3
- attn_gain: float32 [2048], replicated, may hold values from 0.5 to 1.5
- attn_shift: float32 [2048], replicated, may hold values from -2 to 2
- out_gain: float32 [2048], replicated, may hold values from 0.5 to 1.5
- out_shift: float32 [2048], replicated, may hold values from -2 to 2
Outputs:
- layer_output: bfloat16 [4096, 2048], P(('grp', 'dev'))
Inputs may be any that keep to these rules, and one draw needn't show every extreme that they name: `suffix_lengths`: each row lists one device's 4 requests in slot order; they fill its 128 slots exactly, and at least one of them has 64 tokens. `request_group`: the 4 requests of one row name every prefix exactly once.
All inputs are finite; a program needn't handle non-finite values.
Results may differ from a plain program's by a relative error of at most 0.014.
Values may be sent and summed in bfloat16 or wider, within the bound.
No kernel may reach another device: no remote copies, remote signals or barrier semaphores. Data moves between devices by JAX's collectives and lax.ppermute only.
A program may use at most 128 MiB of HBM per device.

v0:
```python
import math

import jax
import jax.numpy as jnp
from jax import lax
from jax.sharding import PartitionSpec as P

HD = 128


norm_eps = 1e-12


def layer_norm(summed, norm_gain, norm_shift):
    row_mean = jnp.mean(summed, axis=-1, keepdims=True)
    centred = summed - row_mean
    spread = jnp.mean(centred * centred, axis=-1, keepdims=True)
    return centred * lax.rsqrt(spread + norm_eps) * norm_gain + norm_shift


def request_layout(lengths, slot_count):
    end_points = jnp.cumsum(lengths)
    starts = end_points - lengths
    positions = lax.iota(jnp.int32, slot_count)
    member = (positions[:, None] >= starts[None, :]) & (positions[:, None] < end_points[None, :])
    slot_ids = lax.iota(jnp.int32, lengths.shape[0])
    segment = jnp.sum(jnp.where(member, slot_ids[None, :], 0), axis=1)
    return (starts, segment)


def expand_rows(piece_rows, up_matrix, up_offset):
    product = jnp.dot(piece_rows, up_matrix, preferred_element_type=jnp.float32)
    return jax.nn.gelu(product + up_offset.astype(jnp.float32), approximate=True).astype(
        jnp.bfloat16
    )


def attend_prefix(arrived, cache_keys, cache_values):
    sources, row_count, part_width = arrived.shape
    local_heads = part_width // HD
    per_block = math.gcd(sources, max(1, 512 // row_count))
    query_blocks = arrived.reshape(sources // per_block, per_block * row_count, local_heads, HD)
    key_heads = cache_keys.reshape(-1, local_heads, HD)
    value_heads = cache_values.reshape(-1, local_heads, HD)

    def one_block(query_block):
        scores = jnp.einsum(
            "qhd,khd->hqk", query_block, key_heads, preferred_element_type=jnp.float32
        ) * HD ** (-0.5)
        row_top = jnp.max(scores, axis=2).astype(jnp.bfloat16)
        weights = jnp.exp(
            scores - lax.optimization_barrier(row_top).astype(jnp.float32)[:, :, None]
        )
        row_sum = jnp.sum(weights, axis=2)
        mixed_sum = jnp.einsum(
            "hqk,khd->qhd",
            weights.astype(jnp.bfloat16),
            value_heads,
            preferred_element_type=jnp.float32,
        )
        answer = (mixed_sum / row_sum.T[:, :, None]).astype(jnp.bfloat16)
        return (answer.reshape(-1, part_width), row_top.T, row_sum.T.astype(jnp.bfloat16))

    answer, row_top, row_sum = lax.map(one_block, query_blocks)
    return (
        answer.reshape(sources, row_count, part_width),
        row_top.reshape(sources, row_count, local_heads),
        row_sum.reshape(sources, row_count, local_heads),
    )


def attend_suffix(query_rows, key_rows, value_rows, segment, head_count):
    slot_count = query_rows.shape[0]
    query_heads = query_rows.reshape(slot_count, head_count, HD)
    key_heads = key_rows.reshape(slot_count, head_count, HD)
    value_heads = value_rows.reshape(slot_count, head_count, HD)
    scores = jnp.einsum(
        "qhd,khd->hqk", query_heads, key_heads, preferred_element_type=jnp.float32
    ) * HD ** (-0.5)
    positions = lax.iota(jnp.int32, slot_count)
    visible = ((segment[:, None] == segment[None, :]) & (positions[None, :] <= positions[:, None]))[
        None
    ]
    row_top = jnp.max(jnp.where(visible, scores, -jnp.inf), axis=2)
    weights = jnp.where(visible, jnp.exp(scores - row_top[:, :, None]), 0.0)
    row_sum = jnp.sum(weights, axis=2)
    mixed_sum = jnp.einsum(
        "hqk,khd->qhd",
        weights.astype(jnp.bfloat16),
        value_heads,
        preferred_element_type=jnp.float32,
    )
    return (row_top.T, row_sum.T, mixed_sum)


def merge_parts(far_answer, far_top, far_sum, own_top, own_sum, own_mixed):
    far_top = far_top.astype(jnp.float32)
    far_sum = far_sum.astype(jnp.float32)
    joint_top = jnp.maximum(far_top, own_top)
    far_weight = jnp.exp(far_top - joint_top) * far_sum
    own_weight = jnp.exp(own_top - joint_top)
    numerator = (
        far_weight[:, :, None] * far_answer.astype(jnp.float32) + own_weight[:, :, None] * own_mixed
    )
    return numerator / (far_weight + own_weight * own_sum)[:, :, None]


def on_device(
    suffix_queries,
    suffix_keys,
    suffix_values,
    layer_input,
    suffix_lengths,
    request_group,
    prefix_keys,
    prefix_values,
    up_weight,
    up_bias,
    down_weight,
    down_bias,
    attn_gain,
    attn_shift,
    out_gain,
    out_shift,
):
    slot_count, model_width = suffix_queries.shape
    head_count = model_width // HD
    group_count = lax.axis_size("grp")
    column_count = lax.axis_size("dev")
    part_width = model_width // column_count
    local_heads = part_width // HD
    capacity = 2 * slot_count // group_count
    lengths = suffix_lengths[0]
    groups = request_group[0]
    request_total = lengths.shape[0]
    starts, segment = request_layout(lengths, slot_count)
    anchor = jnp.zeros((), jnp.int32)
    padded = jnp.concatenate(
        [suffix_queries, jnp.zeros((capacity, model_width), jnp.bfloat16)], axis=0
    )
    slot_rank = lax.iota(jnp.int32, capacity)
    outgoing = jnp.zeros((group_count, column_count, capacity, part_width), jnp.bfloat16)
    for request in range(request_total):
        taken = lax.dynamic_slice_in_dim(padded, starts[request], capacity, 0)
        taken = jnp.where((slot_rank < lengths[request])[:, None], taken, jnp.zeros_like(taken))
        split_rows = taken.reshape(capacity, column_count, part_width).transpose(1, 0, 2)
        outgoing = lax.dynamic_update_slice(
            outgoing, split_rows[None], (groups[request], anchor, anchor, anchor)
        )
    cache_keys = prefix_keys[0]
    cache_values = prefix_values[0]
    answer_part, top_part, sum_part = attend_prefix(
        lax.all_to_all(
            outgoing.reshape(group_count * column_count, capacity, part_width),
            ("grp", "dev"),
            split_axis=0,
            concat_axis=0,
            tiled=True,
        ),
        cache_keys,
        cache_values,
    )
    answer = lax.all_to_all(answer_part, ("grp", "dev"), split_axis=0, concat_axis=0, tiled=True)
    far_top = lax.all_to_all(top_part, ("grp", "dev"), split_axis=0, concat_axis=0, tiled=True)
    far_sum = lax.all_to_all(sum_part, ("grp", "dev"), split_axis=0, concat_axis=0, tiled=True)
    answer = answer.reshape(group_count, column_count, capacity, part_width)
    far_top = far_top.reshape(group_count, column_count, capacity, local_heads)
    far_sum = far_sum.reshape(group_count, column_count, capacity, local_heads)
    placed_answer = jnp.zeros((slot_count + capacity, model_width), jnp.bfloat16)
    placed_top = jnp.zeros((slot_count + capacity, head_count), jnp.bfloat16)
    placed_sum = jnp.zeros((slot_count + capacity, head_count), jnp.bfloat16)
    for request in range(request_total):
        own_answer = (
            lax.dynamic_index_in_dim(answer, groups[request], 0, keepdims=False)
            .transpose(1, 0, 2)
            .reshape(capacity, model_width)
        )
        own_top_rows = (
            lax.dynamic_index_in_dim(far_top, groups[request], 0, keepdims=False)
            .transpose(1, 0, 2)
            .reshape(capacity, head_count)
        )
        own_sum_rows = (
            lax.dynamic_index_in_dim(far_sum, groups[request], 0, keepdims=False)
            .transpose(1, 0, 2)
            .reshape(capacity, head_count)
        )
        placed_answer = lax.dynamic_update_slice(
            placed_answer, own_answer, (starts[request], anchor)
        )
        placed_top = lax.dynamic_update_slice(placed_top, own_top_rows, (starts[request], anchor))
        placed_sum = lax.dynamic_update_slice(placed_sum, own_sum_rows, (starts[request], anchor))
    own_top, own_sum, own_mixed = attend_suffix(
        suffix_queries, suffix_keys, suffix_values, segment, head_count
    )
    far_rows = placed_answer[:slot_count].reshape(slot_count, head_count, HD)
    context = merge_parts(
        far_rows, placed_top[:slot_count], placed_sum[:slot_count], own_top, own_sum, own_mixed
    )
    hidden_state = layer_norm(
        layer_input.astype(jnp.float32) + context.reshape(slot_count, model_width),
        attn_gain,
        attn_shift,
    ).astype(jnp.bfloat16)
    up_slice, bias_slice, down_slice = (
        lax.all_gather(up_weight, "grp", axis=1, tiled=True),
        lax.all_gather(up_bias, "grp", axis=0, tiled=True),
        lax.all_gather(down_weight, "grp", axis=0, tiled=True),
    )
    activation = expand_rows(
        lax.all_gather(hidden_state, "dev", axis=0, tiled=True), up_slice, bias_slice
    )
    mlp_sum = lax.psum_scatter(
        jnp.dot(activation, down_slice, preferred_element_type=jnp.float32).astype(jnp.bfloat16),
        "dev",
        scatter_dimension=0,
        tiled=True,
    ).astype(jnp.float32)
    return layer_norm(
        hidden_state.astype(jnp.float32) + mlp_sum + down_bias, out_gain, out_shift
    ).astype(jnp.bfloat16)


def solution(mesh):
    placed = (
        P(("grp", "dev"), None),
        P(("grp", "dev"), None),
        P(("grp", "dev"), None),
        P(("grp", "dev"), None),
        P(("grp", "dev"), None),
        P(("grp", "dev"), None),
        P("grp", None, "dev"),
        P("grp", None, "dev"),
        P(None, ("grp", "dev")),
        P(("grp", "dev")),
        P(("grp", "dev"), None),
        P(),
        P(),
        P(),
        P(),
        P(),
    )
    return jax.shard_map(
        on_device, mesh=mesh, in_specs=placed, out_specs=P(("grp", "dev"), None), check_vma=False
    )
```

profile of v0, /device:TPU:0, one launch (start us, length us, event | category | flops | bytes accessed | tf_op | source)
XLA Modules:
  0.0 444.8 jit_solution(7886990404582159969)
XLA Ops:
  37.5 7.5 %all-to-all-start = ((bf16[32,64,256]{2,1,0:T(8,128)(2,1)}), bf16[32,64,256]{2,1,0:T(8,128)(2,1)}, u32[]{:S(2)}, u32[]{:S(2)}) async-start(bf16[32,64,256]{2,1,0:T(8,128)(2,1)} %bitcast.30), calls=%async_computation | async-start | bytes 2097152 | tf_op jit(solution)/shard_map/all_to_all | solution.py:153
  52.0 4.1 copy.174
  56.1 16.5 %all-to-all-done = bf16[32,64,256]{2,1,0:T(8,128)(2,1)} async-done(((bf16[32,64,256]{2,1,0:T(8,128)(2,1)}), bf16[32,64,256]{2,1,0:T(8,128)(2,1)}, u32[]{:S(2)}, u32[]{:S(2)}) %all-to-all-start) | async-done | bytes 1048608 | tf_op jit(solution)/shard_map/all_to_all | solution.py:153
  74.8 113.5 %while.14 = (s32[]{:T(128)}, bf16[4,512,256]{2,1,0:T(8,128)(2,1)}, bf16[4,512,2]{1,2,0:T(2,128)(2,1)S(1)}, bf16[4,512,2]{1,2,0:T(2,128)(2,1)S(1)}, bf16[4,512,2,...) while((s32[]{:T(128)}, bf16[4,512,256]{2,1,0:T(8,128)(2,1)}, ...), condition=%wide.region_4.5_spmd, body=%wide.region_1.4_spmd.sunk | while | flops 2181300224 | bytes 56658524 | solution.py:64
  75.9 8.1 %multiply_reduce_fusion.4 = (bf16[2,512]{1,0:T(2,128)(2,1)S(1)}, f32[2,512,4096]{2,1,0:T(8,128)}) fusion(bf16[4096,2,128]{2,0,1:T(8,128)(2,1)S(1)} %get-tuple-element.216, bf16[1,512,2,128]{3,2,1,0:T(2,128)(2,1)S(1)} %constant_dynamic-slice_fusion.10), kind=kOutput, calls=%fused_computation.1.clone.1 | convolution fusion | flops 1082129408 | bytes 19138560 | tf_op jit(solution)/shard_map/while/body/eval_jaxpr/qhd,khd->hqk/dot_general | solution.py:47
  84.0 8.7 %fusion.91 = f32[2,512]{1,0:T(2,128)S(1)} fusion(f32[2,512,4096]{2,1,0:T(8,128)} %get-tuple-element.191, f32[2,512]{1,0:T(2,128)S(1)} %convert_element_type.128), kind=kLoop, calls=%fused_computation.2.clone.1 | loop fusion | flops 12581888 | bytes 16785408 | tf_op jit(solution)/shard_map/while/body/eval_jaxpr/reduce_sum | solution.py:54
  92.7 9.6 %fusion.92 = bf16[512,2,128]{0,2,1:T(8,128)(2,1)S(1)} fusion(bf16[4096,2,128]{0,2,1:T(8,128)(2,1)} %get-tuple-element.217, f32[2,512,4096]{2,1,0:T(8,128)} %get-tuple-element.191, f32[2,512]{1,0:T(2,128)S(1)} %convert_element_type.128, f32[512,2]{0,1:T(2,128)S(1)} %bitcast.222), kind=kOutput, calls=%fused_computation.7.clone.1 | convolution fusion | flops 1086586880 | bytes 19144704 | tf_op jit(solution)/shard_map/while/body/eval_jaxpr/hqk,khd->qhd/dot_general | solution.py:55
  104.3 8.1 %multiply_reduce_fusion.4 = (bf16[2,512]{1,0:T(2,128)(2,1)S(1)}, f32[2,512,4096]{2,1,0:T(8,128)}) fusion(bf16[4096,2,128]{2,0,1:T(8,128)(2,1)S(1)} %get-tuple-element.216, bf16[1,512,2,128]{3,2,1,0:T(2,128)(2,1)S(1)} %constant_dynamic-slice_fusion.10), kind=kOutput, calls=%fused_computation.1.clone.1 | convolution fusion | flops 1082129408 | bytes 19138560 | tf_op jit(solution)/shard_map/while/body/eval_jaxpr/qhd,khd->hqk/dot_general | solution.py:47
  112.4 8.6 %fusion.91 = f32[2,512]{1,0:T(2,128)S(1)} fusion(f32[2,512,4096]{2,1,0:T(8,128)} %get-tuple-element.191, f32[2,512]{1,0:T(2,128)S(1)} %convert_element_type.128), kind=kLoop, calls=%fused_computation.2.clone.1 | loop fusion | flops 12581888 | bytes 16785408 | tf_op jit(solution)/shard_map/while/body/eval_jaxpr/reduce_sum | solution.py:54
  121.0 9.6 %fusion.92 = bf16[512,2,128]{0,2,1:T(8,128)(2,1)S(1)} fusion(bf16[4096,2,128]{0,2,1:T(8,128)(2,1)} %get-tuple-element.217, f32[2,512,4096]{2,1,0:T(8,128)} %get-tuple-element.191, f32[2,512]{1,0:T(2,128)S(1)} %convert_element_type.128, f32[512,2]{0,1:T(2,128)S(1)} %bitcast.222), kind=kOutput, calls=%fused_computation.7.clone.1 | convolution fusion | flops 1086586880 | bytes 19144704 | tf_op jit(solution)/shard_map/while/body/eval_jaxpr/hqk,khd->qhd/dot_general | solution.py:55
  132.7 8.1 %multiply_reduce_fusion.4 = (bf16[2,512]{1,0:T(2,128)(2,1)S(1)}, f32[2,512,4096]{2,1,0:T(8,128)}) fusion(bf16[4096,2,128]{2,0,1:T(8,128)(2,1)S(1)} %get-tuple-element.216, bf16[1,512,2,128]{3,2,1,0:T(2,128)(2,1)S(1)} %constant_dynamic-slice_fusion.10), kind=kOutput, calls=%fused_computation.1.clone.1 | convolution fusion | flops 1082129408 | bytes 19138560 | tf_op jit(solution)/shard_map/while/body/eval_jaxpr/qhd,khd->hqk/dot_general | solution.py:47
  140.8 8.6 %fusion.91 = f32[2,512]{1,0:T(2,128)S(1)} fusion(f32[2,512,4096]{2,1,0:T(8,128)} %get-tuple-element.191, f32[2,512]{1,0:T(2,128)S(1)} %convert_element_type.128), kind=kLoop, calls=%fused_computation.2.clone.1 | loop fusion | flops 12581888 | bytes 16785408 | tf_op jit(solution)/shard_map/while/body/eval_jaxpr/reduce_sum | solution.py:54
  149.4 9.6 %fusion.92 = bf16[512,2,128]{0,2,1:T(8,128)(2,1)S(1)} fusion(bf16[4096,2,128]{0,2,1:T(8,128)(2,1)} %get-tuple-element.217, f32[2,512,4096]{2,1,0:T(8,128)} %get-tuple-element.191, f32[2,512]{1,0:T(2,128)S(1)} %convert_element_type.128, f32[512,2]{0,1:T(2,128)S(1)} %bitcast.222), kind=kOutput, calls=%fused_computation.7.clone.1 | convolution fusion | flops 1086586880 | bytes 19144704 | tf_op jit(solution)/shard_map/while/body/eval_jaxpr/hqk,khd->qhd/dot_general | solution.py:55
  161.0 8.1 %multiply_reduce_fusion.4 = (bf16[2,512]{1,0:T(2,128)(2,1)S(1)}, f32[2,512,4096]{2,1,0:T(8,128)}) fusion(bf16[4096,2,128]{2,0,1:T(8,128)(2,1)S(1)} %get-tuple-element.216, bf16[1,512,2,128]{3,2,1,0:T(2,128)(2,1)S(1)} %constant_dynamic-slice_fusion.10), kind=kOutput, calls=%fused_computation.1.clone.1 | convolution fusion | flops 1082129408 | bytes 19138560 | tf_op jit(solution)/shard_map/while/body/eval_jaxpr/qhd,khd->hqk/dot_general | solution.py:47
  169.1 8.6 %fusion.91 = f32[2,512]{1,0:T(2,128)S(1)} fusion(f32[2,512,4096]{2,1,0:T(8,128)} %get-tuple-element.191, f32[2,512]{1,0:T(2,128)S(1)} %convert_element_type.128), kind=kLoop, calls=%fused_computation.2.clone.1 | loop fusion | flops 12581888 | bytes 16785408 | tf_op jit(solution)/shard_map/while/body/eval_jaxpr/reduce_sum | solution.py:54
  177.7 9.6 %fusion.92 = bf16[512,2,128]{0,2,1:T(8,128)(2,1)S(1)} fusion(bf16[4096,2,128]{0,2,1:T(8,128)(2,1)} %get-tuple-element.217, f32[2,512,4096]{2,1,0:T(8,128)} %get-tuple-element.191, f32[2,512]{1,0:T(2,128)S(1)} %convert_element_type.128, f32[512,2]{0,1:T(2,128)S(1)} %bitcast.222), kind=kOutput, calls=%fused_computation.7.clone.1 | convolution fusion | flops 1086586880 | bytes 19144704 | tf_op jit(solution)/shard_map/while/body/eval_jaxpr/hqk,khd->qhd/dot_general | solution.py:55
  191.7 6.9 %all-to-all-done.2 = bf16[32,64,2]{1,2,0:T(2,128)(2,1)S(1)} async-done(((bf16[32,64,2]{1,2,0:T(2,128)(2,1)}), bf16[32,64,2]{1,2,0:T(2,128)(2,1)S(1)}, u32[]{:S(2)}, u32[]{:S(2)}) %all-to-all-start.2) | async-done | bytes 8224 | tf_op jit(solution)/shard_map/all_to_all | solution.py:165
  198.6 8.8 %all_to_all.20 = bf16[32,64,2]{1,2,0:T(2,128)(2,1)S(1)} all-to-all(bf16[32,64,2]{1,2,0:T(2,128)(2,1)S(1)} %copy.178), channel_id=1, replica_groups=mesh['grp'=4,'dev'=8] {'grp','dev'}, dimensions={0} | all-to-all | bytes 16384 | tf_op jit(solution)/shard_map/all_to_all | solution.py:164
  217.5 20.3 %all-to-all-done.3 = bf16[32,64,256]{2,1,0:T(8,128)(2,1)S(1)} async-done(((bf16[32,64,256]{2,1,0:T(8,128)(2,1)}), bf16[32,64,256]{2,1,0:T(8,128)(2,1)S(1)}, u32[]{:S(2)}, u32[]{:S(2)}) %all-to-all-start.3) | async-done | bytes 1048608 | tf_op jit(solution)/shard_map/all_to_all | solution.py:163
  239.8 4.9 %dynamic_update_slice.71 = bf16[192,2048]{0,1:T(8,128)(2,1)S(1)} dynamic-update-slice(bf16[192,2048]{0,1:T(8,128)(2,1)S(1)} %broadcast_in_dim.129, bf16[64,2048]{0,1:T(8,128)(2,1)} %bitcast.208, s32[]{:T(128)S(6)} %select_n.74, s32[]{:T(128)} %constant.72.clone.1) | dynamic-update-slice | bytes 524292 | tf_op jit(solution)/shard_map/dynamic_update_slice | solution.py:188
  260.7 5.3 %all-gather = bf16[4,1,256]{2,1,0:T(2,128)(2,1)S(1)} all-gather(bf16[1,1,256]{2,1,0:T(2,128)(2,1)S(1)} %reshape.241), channel_id=1, replica_groups=mesh['grp'=4,'dev'=8] {'grp'}, dimensions={0}, use_global_device_ids=true | all-gather | bytes 2560 | tf_op jit(solution)/shard_map/all_gather | solution.py:207
  266.0 65.8 %all-gather.5.cloned.1.call-done = bf16[1024,2048]{1,0:T(8,128)(2,1)} async-done(((bf16[128,2048]{1,0:T(8,128)(2,1)}), bf16[1024,2048]{1,0:T(8,128)(2,1)}) %all-gather.5.cloned.1.call-update) | async-done | bytes 4194320 | tf_op jit(solution)/shard_map/all_gather | solution.py:211
  331.8 15.2 %convolution_convert_fusion = bf16[1024,2048]{1,0:T(8,128)(2,1)} fusion(bf16[1024,2048]{1,0:T(8,128)(2,1)} %all-gather.9.cloned.1.call-done, f32[1024]{0:T(1024)S(1)} %bitcast.234, bf16[1024,2048]{1,0:T(8,128)(2,1)} %all-gather.5.cloned.1.call-done, bf16[2048,1024]{1,0:T(8,128)(2,1)} %all-gather.7.cloned.1.call-done), kind=kOutput, calls=%fused_computation.24 | convolution fusion | flops 8602517504 | bytes 16781312 | tf_op jit(solution)/shard_map/dot_general | solution.py:214
  347.1 86.3 %reduce-scatter.2.cloned.1.call-done = bf16[128,2048]{1,0:T(8,128)(2,1)} async-done(((bf16[1024,2048]{1,0:T(8,128)(2,1)}), bf16[128,2048]{1,0:T(8,128)(2,1)}) %reduce-scatter.2.cloned.1.call-update) | async-done | bytes 524304 | tf_op jit(solution)/shard_map/reduce_scatter | solution.py:213
  (139 shorter events, 68.9 us)
Async XLA Ops:
  6.5 206.0 %copy-start = (bf16[128,2048]{1,0:T(8,128)(2,1)S(1)}, bf16[128,2048]{1,0:T(8,128)(2,1)}, u32[]{:S(2)}) copy-start(bf16[128,2048]{1,0:T(8,128)(2,1)} %param.19) | copy-start | bytes 1572868
  6.5 259.5 %all-gather.7.cloned.1.call-start = ((), (), s32[]{:S(2)}) async-start(), calls=%async_computation.6 | async-start | bytes 5242880 | tf_op jit(solution)/shard_map/all_gather | solution.py:206
  29.0 16.9 %copy-start.3 = (bf16[1,4096,256]{2,1,0:T(8,128)(2,1)S(1)}, bf16[1,4096,256]{2,1,0:T(8,128)(2,1)}, u32[]{:S(2)}) copy-start(bf16[1,4096,256]{2,1,0:T(8,128)(2,1)} %param.24) | copy-start | bytes 6291460
  37.5 35.1 %all-to-all-start = ((bf16[32,64,256]{2,1,0:T(8,128)(2,1)}), bf16[32,64,256]{2,1,0:T(8,128)(2,1)}, u32[]{:S(2)}, u32[]{:S(2)}) async-start(bf16[32,64,256]{2,1,0:T(8,128)(2,1)} %bitcast.30), calls=%async_computation | async-start | bytes 2097152 | tf_op jit(solution)/shard_map/all_to_all | solution.py:153
  45.1 221.0 %all-gather.9.cloned.1.call-start = ((), (), s32[]{:S(2)}) async-start(), calls=%async_computation.7 | async-start | bytes 5242880 | tf_op jit(solution)/shard_map/all_gather | solution.py:208
  74.8 137.5 %copy-start.10 = (s32[1,4]{1,0:T(1,128)S(1)}, s32[1,4]{1,0:T(1,128)}, u32[]{:S(2)}) copy-start(s32[1,4]{1,0:T(1,128)} %param.22) | copy-start | bytes 52
  189.0 9.6 %all-to-all-start.2 = ((bf16[32,64,2]{1,2,0:T(2,128)(2,1)}), bf16[32,64,2]{1,2,0:T(2,128)(2,1)S(1)}, u32[]{:S(2)}, u32[]{:S(2)}) async-start(bf16[32,64,2]{1,2,0:T(2,128)(2,1)} %copy.187), calls=%async_computation.2 | async-start | bytes 32768 | tf_op jit(solution)/shard_map/all_to_all | solution.py:165
  207.4 30.4 %all-to-all-start.3 = ((bf16[32,64,256]{2,1,0:T(8,128)(2,1)}), bf16[32,64,256]{2,1,0:T(8,128)(2,1)S(1)}, u32[]{:S(2)}, u32[]{:S(2)}) async-start(bf16[32,64,256]{2,1,0:T(8,128)(2,1)} %bitcast.214), calls=%async_computation.3 | async-start | bytes 2097152 | tf_op jit(solution)/shard_map/all_to_all | solution.py:163
  210.2 121.6 %all-gather.5.cloned.1.call-start = ((), (), s32[]{:S(2)}) async-start(), calls=%async_computation.5 | async-start | bytes 4718592 | tf_op jit(solution)/shard_map/all_gather | solution.py:211
  214.0 1.1 copy-start.4
  256.8 2.2 copy-start.2
  256.9 2.7 copy-start.6
  256.9 2.7 copy-start.7
  258.7 2.0 copy-start.11
  260.6 172.8 %reduce-scatter.2.cloned.1.call-start = ((), (), s32[]{:S(2)}) async-start(), calls=%async_computation.8 | async-start | bytes 4718592 | tf_op jit(solution)/shard_map/reduce_scatter | solution.py:213
  347.1 86.3 %copy-start.1 = (bf16[128,2048]{1,0:T(8,128)(2,1)S(1)}, bf16[128,2048]{1,0:T(8,128)(2,1)}, u32[]{:S(2)}) copy-start(bf16[128,2048]{1,0:T(8,128)(2,1)} %add_convert_fusion.1) | copy-start | bytes 1572868
  347.1 86.3 %copy-start.5 = (f32[2048]{0:T(1024)S(1)}, f32[2048]{0:T(1024)}, u32[]{:S(2)}) copy-start(f32[2048]{0:T(1024)} %param.29) | copy-start | bytes 24580
  347.1 89.0 %copy-start.8 = (f32[2048]{0:T(1024)S(1)}, f32[2048]{0:T(1024)}, u32[]{:S(2)}) copy-start(f32[2048]{0:T(1024)} %param.33) | copy-start | bytes 24580
  347.1 89.0 %copy-start.9 = (f32[2048]{0:T(1024)S(1)}, f32[2048]{0:T(1024)}, u32[]{:S(2)}) copy-start(f32[2048]{0:T(1024)} %param.32) | copy-start | bytes 24580
Sparse Core Ops, SparseCore 0:
  8.9 37.7 all-gather.6
  48.3 37.3 all-gather.8
  260.8 71.0 all-gather.4
  347.2 86.1 reduce-scatter.1
where the time goes:
time: 446 us; the launch traced here: 445 us
  waiting for transfers between devices  197 us (44%)
  matrix products  89.5 us (20%)
  local copies, waits for them, and re-layouts  55.1 us (12%)
  other arithmetic  47 us (11%)
  between operations  28.7 us (6%)
  blocking collectives  14.1 us (3%)
  starting transfers between devices  13 us (3%)
    reduce_scatter x1, waiting for transfers between devices, on_device(): lax.psum_scatter(jnp.dot(activation, down_slice, preferred_element_type=j...  86.3 us
    all_gather x1, waiting for transfers between devices, on_device(): lax.all_gather(hidden_state, 'dev', axis=0, tiled=True)  65.8 us
    dot_general x4, matrix products, one_block(): jnp.einsum('hqk,khd->qhd', weights.astype(jnp.bfloat16), value_heads, pre...  38.5 us
    reduce_sum x4, other arithmetic, one_block(): row_sum = jnp.sum(weights, axis=2)  34.5 us
    dot_general x4, matrix products, one_block(): jnp.einsum('qhd,khd->hqk', query_block, key_heads, preferred_element_type...  32.4 us
    all_to_all x1, waiting for transfers between devices, on_device(): lax.all_to_all(answer_part, ('grp', 'dev'), split_axis=0, concat_axis=0,...  20.3 us
    dynamic_update_slice x4, local copies, waits for them, and re-layouts, on_device(): lax.dynamic_update_slice(placed_answer, own_answer, (starts[request], anc...  16.9 us
    all_to_all x1, waiting for transfers between devices, on_device(): lax.all_to_all(outgoing.reshape(group_count * column_count, capacity, par...  16.5 us
  transfers between devices with their start and end apart: 7, of which 5 were waited for; matrix products, arithmetic and copies ran while one was open for 38% of the time, Pallas kernels for 0%

commit v1 on v0

v1 whole, which is shorter than its diff:
```python
import functools
import math

import jax
import jax.numpy as jnp
from jax import lax
from jax.experimental import pallas as pl
from jax.experimental.pallas import tpu as pltpu
from jax.sharding import PartitionSpec as P

HD = 128
LANES = 128
STAT_ROWS = 8
ROW_BLOCK = 256
KEY_CHUNK = 1024

norm_eps = 1e-12
score_scale = HD ** (-0.5)
log2_e = math.log2(math.e)
kernel_vmem = 56 * 1024 * 1024


def layer_norm(summed, norm_gain, norm_shift):
    row_mean = jnp.mean(summed, axis=-1, keepdims=True)
    centred = summed - row_mean
    spread = jnp.mean(centred * centred, axis=-1, keepdims=True)
    return centred * lax.rsqrt(spread + norm_eps) * norm_gain + norm_shift


def vmem_spec():
    return pl.BlockSpec(memory_space=pltpu.VMEM)


def smem_spec():
    return pl.BlockSpec(memory_space=pltpu.SMEM)


def pack_kernel(lengths_ref, groups_ref, query_ref, out_ref, wide_ref):
    request_total = lengths_ref.shape[1]
    _, column_count, capacity, part_width = out_ref.shape
    slot_count = query_ref.shape[0]
    tiles = part_width // LANES
    for tile in range(wide_ref.shape[0]):
        wide_ref[tile, 0:slot_count, :] = query_ref[
            :, tile * LANES : (tile + 1) * LANES
        ].astype(jnp.float32)
        wide_ref[tile, slot_count : slot_count + capacity, :] = jnp.zeros(
            (capacity, LANES), jnp.float32
        )
    start = 0
    for request in range(request_total):
        group = groups_ref[0, request]
        for column in range(column_count):
            for tile in range(tiles):
                rows = wide_ref[column * tiles + tile, pl.ds(start, capacity), :]
                out_ref[group, column, :, tile * LANES : (tile + 1) * LANES] = rows.astype(
                    jnp.bfloat16
                )
        start = start + lengths_ref[0, request]


def pack_queries(lengths, groups, queries, group_count, column_count, capacity):
    slot_count, model_width = queries.shape
    part_width = model_width // column_count
    return pl.pallas_call(
        pack_kernel,
        out_shape=jax.ShapeDtypeStruct(
            (group_count, column_count, capacity, part_width), jnp.bfloat16
        ),
        in_specs=[smem_spec(), smem_spec(), vmem_spec()],
        out_specs=vmem_spec(),
        scratch_shapes=[
            pltpu.VMEM((model_width // LANES, slot_count + capacity, LANES), jnp.float32)
        ],
        compiler_params=pltpu.CompilerParams(vmem_limit_bytes=kernel_vmem),
        name="pack_queries",
    )(lengths, groups, queries)


def far_kernel(
    counts_ref,
    arrived_ref,
    keys_ref,
    values_ref,
    out_ref,
    query_ref,
    answer_ref,
    stat_ref,
    score_ref,
    top_ref,
):
    sources, capacity, part_width = arrived_ref.shape
    local_heads = part_width // HD
    key_total = keys_ref.shape[1]
    chunks = key_total // KEY_CHUNK

    def take(source, offset):
        for head in range(local_heads):
            query_ref[head, pl.ds(offset, capacity), :] = arrived_ref[
                source, :, head * HD : (head + 1) * HD
            ].astype(jnp.float32)
        return offset + counts_ref[source]

    total = lax.fori_loop(0, sources, take, jnp.int32(0))
    blocks = (total + ROW_BLOCK - 1) // ROW_BLOCK
    lane = lax.broadcasted_iota(jnp.int32, (ROW_BLOCK, LANES), 1)

    def block_rows(block):
        return pl.ds(pl.multiple_of(block * ROW_BLOCK, ROW_BLOCK), ROW_BLOCK)

    def load_queries(block, head):
        return query_ref[head, block_rows(block), :].astype(jnp.bfloat16)

    def score_chunk(rows, head, slot, chunk, part_top):
        columns = slice(chunk * KEY_CHUNK, (chunk + 1) * KEY_CHUNK)
        scores = jnp.dot(
            rows,
            keys_ref[head * HD : (head + 1) * HD, columns],
            preferred_element_type=jnp.float32,
        )
        score_ref[slot, :, columns] = scores
        for piece in range(KEY_CHUNK // LANES):
            part = scores[:, piece * LANES : (piece + 1) * LANES]
            part_top = part if part_top is None else jnp.maximum(part_top, part)
        return part_top

    def finish_top(part_top, slot):
        row_top = jnp.max(part_top, axis=1, keepdims=True) * score_scale
        row_top = row_top.astype(jnp.bfloat16).astype(jnp.float32)
        top_ref[slot] = jnp.broadcast_to(row_top, (ROW_BLOCK, LANES))

    def weigh_chunk(head, slot, chunk, shift):
        columns = slice(chunk * KEY_CHUNK, (chunk + 1) * KEY_CHUNK)
        weights = jnp.exp2(score_ref[slot, :, columns] * (score_scale * log2_e) - shift)
        return jnp.dot(
            weights.astype(jnp.bfloat16),
            values_ref[head, columns, :],
            preferred_element_type=jnp.float32,
        )

    def finish_answer(block, head, slot, mixed):
        rows = block_rows(block)
        row_sum = mixed[:, HD:]
        answer_ref[head, rows, :] = mixed[:, :HD] / row_sum
        top = top_ref[slot]
        if head == 0:
            stat_ref[rows, :] = jnp.where(lane == 0, top, row_sum)
        else:
            before = stat_ref[rows, :]
            with_top = jnp.where(lane == head, top, before)
            stat_ref[rows, :] = jnp.where(lane == local_heads + head, row_sum, with_top)

    def slot_of(block, head):
        return (block * local_heads + head) % 2 if local_heads % 2 else head % 2

    first_rows = load_queries(0, 0)
    part_top = None
    for chunk in range(chunks):
        part_top = score_chunk(first_rows, 0, 0, chunk, part_top)
    finish_top(part_top, 0)

    def one_block(block, carry):
        for head in range(local_heads):
            slot = slot_of(block, head)
            if head + 1 < local_heads:
                next_block, next_head = block, head + 1
            else:
                next_block, next_head = jnp.minimum(block + 1, blocks - 1), 0
            next_slot = 1 - slot
            next_rows = load_queries(next_block, next_head)
            shift = top_ref[slot][:, 0:1] * log2_e
            part_top = None
            mixed = None
            for chunk in range(chunks):
                part_top = score_chunk(next_rows, next_head, next_slot, chunk, part_top)
                part = weigh_chunk(head, slot, chunk, shift)
                mixed = part if mixed is None else mixed + part
            finish_answer(block, head, slot, mixed)
            finish_top(part_top, next_slot)
        return carry

    lax.fori_loop(0, blocks, one_block, 0)

    def give(source, offset):
        rows = [answer_ref[head, pl.ds(offset, capacity), :] for head in range(local_heads)]
        turned = jnp.transpose(stat_ref[pl.ds(offset, LANES), :])[:STAT_ROWS, :]
        if part_width > LANES:
            turned = jnp.concatenate(
                [turned, jnp.zeros((STAT_ROWS, part_width - LANES), jnp.float32)], axis=1
            )
        rows = jnp.concatenate(rows, axis=1)
        out_ref[source] = jnp.concatenate([rows, turned], axis=0).astype(jnp.bfloat16)
        return offset + counts_ref[source]

    lax.fori_loop(0, sources, give, jnp.int32(0))


def attend_prefix(counts, arrived, turned_keys, wide_values):
    sources, capacity, part_width = arrived.shape
    local_heads = part_width // HD
    key_total = turned_keys.shape[1]
    row_total = -(-sources * capacity // ROW_BLOCK) * ROW_BLOCK + LANES
    return pl.pallas_call(
        far_kernel,
        out_shape=jax.ShapeDtypeStruct((sources, capacity + STAT_ROWS, part_width), jnp.bfloat16),
        in_specs=[smem_spec(), vmem_spec(), vmem_spec(), vmem_spec()],
        out_specs=vmem_spec(),
        scratch_shapes=[
            pltpu.VMEM((local_heads, row_total, HD), jnp.float32),
            pltpu.VMEM((local_heads, row_total, HD), jnp.float32),
            pltpu.VMEM((row_total, LANES), jnp.float32),
            pltpu.VMEM((2, ROW_BLOCK, key_total), jnp.float32),
            pltpu.VMEM((2, ROW_BLOCK, LANES), jnp.float32),
        ],
        compiler_params=pltpu.CompilerParams(vmem_limit_bytes=kernel_vmem),
        cost_estimate=pl.CostEstimate(
            flops=4 * sources * capacity * key_total * part_width,
            bytes_accessed=8 * key_total * part_width,
            transcendentals=sources * capacity * key_total * local_heads,
        ),
        name="attend_prefix",
    )(counts, arrived, turned_keys, wide_values)


def stat_lane(head, local_heads):
    return (head // local_heads) * STAT_ROWS + head % local_heads


def own_kernel(local_heads, lengths_ref, query_ref, key_ref, value_ref, mixed_ref, top_ref, sum_ref):
    slot_count, model_width = query_ref.shape
    head_count = model_width // HD
    row = lax.broadcasted_iota(jnp.int32, (slot_count, slot_count), 0)
    column = lax.broadcasted_iota(jnp.int32, (slot_count, slot_count), 1)
    row_segment = jnp.zeros((slot_count, slot_count), jnp.int32)
    column_segment = jnp.zeros((slot_count, slot_count), jnp.int32)
    start = 0
    for request in range(lengths_ref.shape[1]):
        start = start + lengths_ref[0, request]
        row_segment = row_segment + (row >= start).astype(jnp.int32)
        column_segment = column_segment + (column >= start).astype(jnp.int32)
    visible = (row_segment == column_segment) & (column <= row)
    lane = lax.broadcasted_iota(jnp.int32, (slot_count, LANES), 1)
    tops = jnp.zeros((slot_count, LANES), jnp.float32)
    sums = jnp.ones((slot_count, LANES), jnp.float32)
    for head in range(head_count):
        columns = slice(head * HD, (head + 1) * HD)
        scores = (
            lax.dot_general(
                query_ref[:, columns],
                key_ref[:, columns],
                (((1,), (1,)), ((), ())),
                preferred_element_type=jnp.float32,
            )
            * score_scale
        )
        top = jnp.max(jnp.where(visible, scores, -jnp.inf), axis=1, keepdims=True)
        weights = jnp.where(visible, jnp.exp(scores - top), 0.0)
        mixed_ref[:, columns] = jnp.dot(
            weights.astype(jnp.bfloat16),
            value_ref[:, columns],
            preferred_element_type=jnp.float32,
        )
        at = stat_lane(head, local_heads)
        tops = jnp.where(lane == at, top, tops)
        sums = jnp.where(lane == at, jnp.sum(weights, axis=1, keepdims=True), sums)
    top_ref[...] = tops
    sum_ref[...] = sums


def attend_suffix(lengths, queries, keys, values, local_heads):
    slot_count, model_width = queries.shape
    stats = jax.ShapeDtypeStruct((slot_count, LANES), jnp.float32)
    return pl.pallas_call(
        functools.partial(own_kernel, local_heads),
        out_shape=(jax.ShapeDtypeStruct((slot_count, model_width), jnp.float32), stats, stats),
        in_specs=[smem_spec()] + [vmem_spec()] * 3,
        out_specs=(vmem_spec(), vmem_spec(), vmem_spec()),
        compiler_params=pltpu.CompilerParams(vmem_limit_bytes=kernel_vmem),
        cost_estimate=pl.CostEstimate(
            flops=40 * slot_count * slot_count * model_width,
            bytes_accessed=8 * slot_count * model_width,
            transcendentals=slot_count * model_width,
        ),
        name="attend_suffix",
    )(lengths, queries, keys, values)


def merge_kernel(
    lengths_ref,
    groups_ref,
    arrived_ref,
    own_mixed_ref,
    own_top_ref,
    own_sum_ref,
    input_ref,
    gain_ref,
    shift_ref,
    hidden_ref,
    far_ref,
    stat_ref,
):
    _, column_count, chunk_rows, part_width = arrived_ref.shape
    slot_count, model_width = input_ref.shape
    capacity = chunk_rows - STAT_ROWS
    local_heads = part_width // HD
    head_count = model_width // HD
    start = 0
    for request in range(lengths_ref.shape[1]):
        group = groups_ref[0, request]
        pieces = []
        for column in range(column_count):
            block = arrived_ref[group, column].astype(jnp.float32)
            for head in range(local_heads):
                far_ref[column * local_heads + head, pl.ds(start, capacity), :] = block[
                    :capacity, head * HD : (head + 1) * HD
                ]
            pieces.append(block[capacity:, :LANES])
        if column_count * STAT_ROWS < LANES:
            pieces.append(jnp.zeros((LANES - column_count * STAT_ROWS, LANES), jnp.float32))
        turned = jnp.transpose(jnp.concatenate(pieces, axis=0))
        stat_ref[pl.ds(start, capacity), :] = turned[:capacity]
        start = start + lengths_ref[0, request]
    far_top = stat_ref[:slot_count, :]
    far_sum = pltpu.roll(far_top, LANES - local_heads, 1)
    own_top = own_top_ref[...]
    joint_top = jnp.maximum(far_top, own_top)
    far_weight = jnp.exp(far_top - joint_top) * far_sum
    own_weight = jnp.exp(own_top - joint_top)
    bottom = far_weight + own_weight * own_sum_ref[...]
    far_weight = far_weight / bottom
    own_weight = own_weight / bottom
    total = jnp.zeros((slot_count, LANES), jnp.float32)
    for head in range(head_count):
        columns = slice(head * HD, (head + 1) * HD)
        at = stat_lane(head, local_heads)
        summed = (
            input_ref[:, columns].astype(jnp.float32)
            + far_weight[:, at : at + 1] * far_ref[head, :slot_count, :]
            + own_weight[:, at : at + 1] * own_mixed_ref[:, columns]
        )
        far_ref[head, :slot_count, :] = summed
        total = total + summed
    row_mean = jnp.sum(total, axis=1, keepdims=True) * (1.0 / model_width)
    total = jnp.zeros((slot_count, LANES), jnp.float32)
    for head in range(head_count):
        centred = far_ref[head, :slot_count, :] - row_mean
        total = total + centred * centred
    spread = jnp.sum(total, axis=1, keepdims=True) * (1.0 / model_width)
    factor = lax.rsqrt(spread + norm_eps)
    for head in range(head_count):
        columns = slice(head * HD, (head + 1) * HD)
        centred = far_ref[head, :slot_count, :] - row_mean
        hidden_ref[:, columns] = (
            centred * factor * gain_ref[:, columns] + shift_ref[:, columns]
        ).astype(jnp.bfloat16)


def merge_parts(lengths, groups, arrived, own_mixed, own_top, own_sum, layer_input, gain, shift):
    slot_count, model_width = layer_input.shape
    capacity = arrived.shape[2] - STAT_ROWS
    return pl.pallas_call(
        merge_kernel,
        out_shape=jax.ShapeDtypeStruct((slot_count, model_width), jnp.bfloat16),
        in_specs=[smem_spec(), smem_spec()] + [vmem_spec()] * 7,
        out_specs=vmem_spec(),
        scratch_shapes=[
            pltpu.VMEM((model_width // HD, slot_count + capacity, HD), jnp.float32),
            pltpu.VMEM((slot_count + capacity, LANES), jnp.float32),
        ],
        compiler_params=pltpu.CompilerParams(vmem_limit_bytes=kernel_vmem),
        name="merge_parts",
    )(
        lengths,
        groups,
        arrived,
        own_mixed,
        own_top,
        own_sum,
        layer_input,
        gain.reshape(1, model_width),
        shift.reshape(1, model_width),
    )


def expand_rows(piece_rows, up_matrix, up_offset):
    product = jnp.dot(piece_rows, up_matrix, preferred_element_type=jnp.float32)
    return jax.nn.gelu(product + up_offset.astype(jnp.float32), approximate=True).astype(
        jnp.bfloat16
    )


def on_device(
    suffix_queries,
    suffix_keys,
    suffix_values,
    layer_input,
    suffix_lengths,
    request_group,
    prefix_keys,
    prefix_values,
    up_weight,
    up_bias,
    down_weight,
    down_bias,
    attn_gain,
    attn_shift,
    out_gain,
    out_shift,
):
    slot_count, model_width = suffix_queries.shape
    group_count = lax.axis_size("grp")
    column_count = lax.axis_size("dev")
    part_width = model_width // column_count
    local_heads = part_width // HD
    capacity = 2 * slot_count // group_count
    sources = group_count * column_count
    request_total = suffix_lengths.shape[1]

    table = lax.all_gather(
        jnp.concatenate([suffix_lengths, request_group], axis=1),
        ("grp", "dev"),
        axis=0,
        tiled=True,
    )
    counts = jnp.sum(
        jnp.where(table[:, request_total:] == lax.axis_index("grp"), table[:, :request_total], 0),
        axis=1,
    )

    outgoing = pack_queries(
        suffix_lengths, request_group, suffix_queries, group_count, column_count, capacity
    )
    arrived = lax.all_to_all(
        outgoing.reshape(sources, capacity, part_width),
        ("grp", "dev"),
        split_axis=0,
        concat_axis=0,
        tiled=True,
    )
    turned_keys = prefix_keys[0].T
    value_heads = prefix_values[0].reshape(-1, local_heads, HD).transpose(1, 0, 2)
    wide_values = jnp.concatenate([value_heads, jnp.ones_like(value_heads)], axis=2)
    answer_part = attend_prefix(counts, arrived, turned_keys, wide_values)
    answer = lax.all_to_all(
        answer_part, ("grp", "dev"), split_axis=0, concat_axis=0, tiled=True
    ).reshape(group_count, column_count, capacity + STAT_ROWS, part_width)
    own_mixed, own_top, own_sum = attend_suffix(
        suffix_lengths, suffix_queries, suffix_keys, suffix_values, local_heads
    )
    hidden_state = merge_parts(
        suffix_lengths,
        request_group,
        answer,
        own_mixed,
        own_top,
        own_sum,
        layer_input,
        attn_gain,
        attn_shift,
    )
    up_slice, bias_slice, down_slice = (
        lax.all_gather(up_weight, "grp", axis=1, tiled=True),
        lax.all_gather(up_bias, "grp", axis=0, tiled=True),
        lax.all_gather(down_weight, "grp", axis=0, tiled=True),
    )
    activation = expand_rows(
        lax.all_gather(hidden_state, "dev", axis=0, tiled=True), up_slice, bias_slice
    )
    mlp_sum = lax.psum_scatter(
        jnp.dot(activation, down_slice, preferred_element_type=jnp.float32).astype(jnp.bfloat16),
        "dev",
        scatter_dimension=0,
        tiled=True,
    ).astype(jnp.float32)
    return layer_norm(
        hidden_state.astype(jnp.float32) + mlp_sum + down_bias, out_gain, out_shift
    ).astype(jnp.bfloat16)


def solution(mesh):
    placed = (
        P(("grp", "dev"), None),
        P(("grp", "dev"), None),
        P(("grp", "dev"), None),
        P(("grp", "dev"), None),
        P(("grp", "dev"), None),
        P(("grp", "dev"), None),
        P("grp", None, "dev"),
        P("grp", None, "dev"),
        P(None, ("grp", "dev")),
        P(("grp", "dev")),
        P(("grp", "dev"), None),
        P(),
        P(),
        P(),
        P(),
        P(),
    )
    return jax.shard_map(
        on_device, mesh=mesh, in_specs=placed, out_specs=P(("grp", "dev"), None), check_vma=False
    )
```

time: 446 us -> 342 us (0.77)
  matrix products: 89.5 us -> 15.3 us
  blocking collectives: 14.1 us -> 73.6 us
  other arithmetic: 47 us -> 5.66 us
  local copies, waits for them, and re-layouts: 55.1 us -> 14.6 us
  Pallas kernels: 0 us -> 30.4 us
  waiting for transfers between devices: 197 us -> 178 us
  between operations: 28.7 us -> 13.2 us
    dot_general x10 -> x0, matrix products: 74.2 us -> none  [the longest x4 38.5 us: one_block(): jnp.einsum('hqk,khd->qhd', weights.astype(jnp.bfloat16), value_heads, pre...]
    all_gather x0 -> x1, blocking collectives: none -> 68.3 us  [on_device(): lax.all_gather(jnp.concatenate([suffix_lengths, request_group], axis=1),...]
    reduce_sum x6 -> x1, other arithmetic: 34.8 us -> 0.69 us  [on_device(): jnp.sum(jnp.where(table[:, request_total:] == lax.axis_index('grp'), tabl...]
    pallas_call x0 -> x4, Pallas kernels: none -> 30.4 us  [the longest x1 17.9 us: attend_prefix(): pl.pallas_call(far_kernel, out_shape=jax.ShapeDtypeStruct((sources, capac...]
    dynamic_update_slice x24 -> x0, local copies, waits for them, and re-layouts: 26.3 us -> none  [the longest x4 16.9 us: on_device(): lax.dynamic_update_slice(placed_answer, own_answer, (starts[request], anc...]
    all_to_all x2 -> x1, waiting for transfers between devices: 23.5 us -> 0.01 us  [on_device(): lax.all_to_all(outgoing.reshape(sources, capacity, part_width), ('grp', '...]
    all_to_all x1 -> x0, blocking collectives: 8.79 us -> none  [on_device(): lax.all_to_all(top_part, ('grp', 'dev'), split_axis=0, concat_axis=0, til...]
    reshape x11 -> x0, local copies, waits for them, and re-layouts: 7.19 us -> none  [the longest x1 2.15 us: attend_prefix(): arrived.reshape(sources // per_block, per_block * row_count, local_heads,...]
  transfers between devices with their start and end apart: 7 -> 6, of which waited for: 5 -> 3; matrix products, arithmetic and copies ran while one was open for 38% -> 4% of each run, Pallas kernels for 0% -> 9%
where the time goes in v1:
time: 342 us; the launch traced here: 340 us
  waiting for transfers between devices  178 us (52%)
  blocking collectives  73.6 us (22%)
  Pallas kernels  30.4 us (9%)
  matrix products  15.3 us (4%)
  local copies, waits for them, and re-layouts  14.6 us (4%)
  between operations  13.2 us (4%)
  starting transfers between devices  10.1 us (3%)
  other arithmetic  5.66 us (2%)
    reduce_scatter x1, waiting for transfers between devices, on_device(): lax.psum_scatter(jnp.dot(activation, down_slice, preferred_element_type=j...  86.3 us
    all_gather x1, blocking collectives, on_device(): lax.all_gather(jnp.concatenate([suffix_lengths, request_group], axis=1),...  68.3 us
    all_gather x1, waiting for transfers between devices, on_device(): lax.all_gather(hidden_state, 'dev', axis=0, tiled=True)  65.9 us
    all_to_all x1, waiting for transfers between devices, on_device(): lax.all_to_all(answer_part, ('grp', 'dev'), split_axis=0, concat_axis=0,...  24 us
    pallas_call x1, Pallas kernels, attend_prefix(): pl.pallas_call(far_kernel, out_shape=jax.ShapeDtypeStruct((sources, capac...  17.9 us
    dot_general x1, matrix products, on_device(): jnp.dot(activation, down_slice, preferred_element_type=jnp.float32)  15.3 us
    unnamed x23, local copies, waits for them, and re-layouts  9.05 us
    all_to_all x1, starting transfers between devices, on_device(): lax.all_to_all(outgoing.reshape(sources, capacity, part_width), ('grp', '...  7.3 us
  transfers between devices with their start and end apart: 6, of which 3 were waited for; matrix products, arithmetic and copies ran while one was open for 4% of the time, Pallas kernels for 9%

profile of v1, /device:TPU:0, one launch (start us, length us, event | category | flops | bytes accessed | tf_op | source)
XLA Modules:
  0.0 340.5 jit_solution(4999619157344613173)
XLA Ops:
  6.5 0.7 all-gather.10.cloned.1.call-update
  7.3 0.7 all-gather.8.cloned.1.call-update
  8.0 2.3 pack_queries.1
  10.3 7.3 %all-to-all-start = ((bf16[32,64,256]{2,1,0:T(8,128)(2,1)}), bf16[32,64,256]{2,1,0:T(8,128)(2,1)S(1)}, u32[]{:S(2)}, u32[]{:S(2)}) async-start(bf16[32,64,256]{2,1,0:T(8,128)(2,1)} %bitcast.19), calls=%async_computation | async-start | bytes 2097152 | tf_op jit(solution)/shard_map/all_to_all | solution.py:433
  17.6 2.9 copy.22
  20.5 3.2 copy.23
  23.7 4.1 %copy.21 = bf16[1,4096,256]{1,2,0:T(8,128)(2,1)} copy(bf16[1,4096,256]{2,1,0:T(8,128)(2,1)} %param.22) | data formatting | bytes 4194304 | tf_op args[6]
  27.8 2.4 concatenate.7.values_ref
  30.2 68.3 %all-gather = s32[32,1,8]{2,1,0:T(1,128)S(1)} all-gather(s32[1,1,8]{2,1,0:T(1,128)S(1)} %add_bitcast_fusion), channel_id=1, replica_groups=mesh['grp'=4,'dev'=8] {'grp','dev'}, dimensions={0}, use_global_device_ids=true | all-gather | bytes 1056 | tf_op jit(solution)/shard_map/all_gather | solution.py:419
  98.6 0.7 fusion.17.counts_ref
  99.3 1.0 copy-done.3
  100.2 17.9 %attend_prefix.1 = bf16[32,72,256]{2,1,0:T(8,128)(2,1)} custom-call(s32[32]{0:T(128)} %fusion.17.counts_ref, bf16[32,64,256]{2,1,0:T(8,128)(2,1)} %copy-done.3, bf16[256,4096]{1,0:T(8,128)(2,1)} %bitcast.20, bf16[2,4096,256]{2,1,0:T(8,128)(2,1)} %concatenate.7.values_ref), custom_call_target="tpu_custom_call" | custom-call | flops 8589934592 | bytes 8388608 | tf_op jit(solution)/shard_map/attend_prefix/pallas_call | solution.py:203
  118.1 2.7 all-to-all-start.1
  120.8 6.3 %attend_suffix.1 = (f32[128,2048]{1,0:T(8,128)}, f32[128,128]{1,0:T(8,128)}, f32[128,128]{1,0:T(8,128)}) custom-call(s32[1,4]{1,0:T(1,128)} %lengths_ref.5, bf16[128,2048]{1,0:T(8,128)(2,1)} %query_ref.3, bf16[128,2048]{1,0:T(8,128)(2,1)} %key_ref.1, bf16[128,2048]{1,0:T(8,128)(2,1)} %value_ref.1), custom_call_target="tpu_custom_call" | custom-call | flops 1342177280 | bytes 2097152 | tf_op jit(solution)/shard_map/attend_suffix/pallas_call | solution.py:273
  127.2 24.0 %all-to-all-done.1 = bf16[32,72,256]{2,1,0:T(8,128)(2,1)S(1)} async-done(((bf16[32,72,256]{2,1,0:T(8,128)(2,1)}), bf16[32,72,256]{2,1,0:T(8,128)(2,1)S(1)}, u32[]{:S(2)}, u32[]{:S(2)}) %all-to-all-start.1) | async-done | bytes 1179680 | tf_op jit(solution)/shard_map/all_to_all | solution.py:444
  151.2 1.1 copy-done.1
  152.3 3.8 %merge_parts.1 = bf16[128,2048]{1,0:T(8,128)(2,1)} custom-call(s32[1,4]{1,0:T(1,128)} %lengths_ref.5, s32[1,4]{1,0:T(1,128)} %groups_ref.3, bf16[4,8,72,256]{3,2,1,0:T(8,128)(2,1)} %bitcast.18, f32[128,2048]{1,0:T(8,128)} %get-tuple-element.8.own_mixed_ref, f32[128,128]{1,0:T(8,128)} %get-tuple-element.9.own_top_ref, ...), custom_call_target="tpu_custom_call" | custom-call | tf_op jit(solution)/shard_map/merge_parts/pallas_call | solution.py:361
  156.2 5.3 %all-gather.1 = bf16[4,1,256]{2,1,0:T(2,128)(2,1)S(1)} all-gather(bf16[1,1,256]{2,1,0:T(2,128)(2,1)S(1)} %reshape.34), channel_id=1, replica_groups=mesh['grp'=4,'dev'=8] {'grp'}, dimensions={0}, use_global_device_ids=true | all-gather | bytes 2560 | tf_op jit(solution)/shard_map/all_gather | solution.py:463
  161.5 65.9 %all-gather.6.cloned.1.call-done = bf16[1024,2048]{1,0:T(8,128)(2,1)} async-done(((bf16[128,2048]{1,0:T(8,128)(2,1)}), bf16[1024,2048]{1,0:T(8,128)(2,1)}) %all-gather.6.cloned.1.call-update) | async-done | bytes 4194320 | tf_op jit(solution)/shard_map/all_gather | solution.py:467
  227.4 15.3 %convolution_convert_fusion = bf16[1024,2048]{1,0:T(8,128)(2,1)} fusion(bf16[1024,2048]{1,0:T(8,128)(2,1)} %all-gather.10.cloned.1.call-done, f32[1024]{0:T(1024)S(1)} %bitcast.24, bf16[1024,2048]{1,0:T(8,128)(2,1)} %all-gather.6.cloned.1.call-done, bf16[2048,1024]{1,0:T(8,128)(2,1)} %all-gather.8.cloned.1.call-done), kind=kOutput, calls=%fused_computation.9 | convolution fusion | flops 8602517504 | bytes 16781312 | tf_op jit(solution)/shard_map/dot_general | solution.py:470
  242.7 86.3 %reduce-scatter.2.cloned.1.call-done = bf16[128,2048]{1,0:T(8,128)(2,1)} async-done(((bf16[1024,2048]{1,0:T(8,128)(2,1)}), bf16[128,2048]{1,0:T(8,128)(2,1)}) %reduce-scatter.2.cloned.1.call-update) | async-done | bytes 524304 | tf_op jit(solution)/shard_map/reduce_scatter | solution.py:469
  329.0 1.3 fusion.16
  330.3 1.4 multiply_reduce_fusion
  331.7 2.2 add_convert_fusion
  (32 shorter events, 0.3 us)
Async XLA Ops:
  6.5 11.1 %copy-start.2 = (bf16[1,4096,256]{2,1,0:T(8,128)(2,1)S(1)}, bf16[1,4096,256]{2,1,0:T(8,128)(2,1)}, u32[]{:S(2)}) copy-start(bf16[1,4096,256]{2,1,0:T(8,128)(2,1)} %param.23) | copy-start | bytes 6291460
  6.5 154.9 %all-gather.10.cloned.1.call-start = ((), (), s32[]{:S(2)}) async-start(), calls=%async_computation.5 | async-start | bytes 5242880 | tf_op jit(solution)/shard_map/all_gather | solution.py:464
  7.3 154.2 %all-gather.8.cloned.1.call-start = ((), (), s32[]{:S(2)}) async-start(), calls=%async_computation.4 | async-start | bytes 5242880 | tf_op jit(solution)/shard_map/all_gather | solution.py:462
  10.3 89.0 %all-to-all-start = ((bf16[32,64,256]{2,1,0:T(8,128)(2,1)}), bf16[32,64,256]{2,1,0:T(8,128)(2,1)S(1)}, u32[]{:S(2)}, u32[]{:S(2)}) async-start(bf16[32,64,256]{2,1,0:T(8,128)(2,1)} %bitcast.19), calls=%async_computation | async-start | bytes 2097152 | tf_op jit(solution)/shard_map/all_to_all | solution.py:433
  27.8 2.4 copy-start.7
  27.8 2.4 copy-start.8
  99.3 1.0 copy-start.3
  118.1 33.1 %all-to-all-start.1 = ((bf16[32,72,256]{2,1,0:T(8,128)(2,1)}), bf16[32,72,256]{2,1,0:T(8,128)(2,1)S(1)}, u32[]{:S(2)}, u32[]{:S(2)}) async-start(bf16[32,72,256]{2,1,0:T(8,128)(2,1)} %attend_prefix.1), calls=%async_computation.1 | async-start | bytes 2359296 | tf_op jit(solution)/shard_map/all_to_all | solution.py:444
  120.8 35.4 %copy-start.9 = (bf16[256]{0:T(256)(128)(2,1)S(1)}, bf16[256]{0:T(256)(128)(2,1)}, u32[]{:S(2)}) copy-start(bf16[256]{0:T(256)(128)(2,1)} %param.25) | copy-start | bytes 1540
  120.8 106.6 %all-gather.6.cloned.1.call-start = ((), (), s32[]{:S(2)}) async-start(), calls=%async_computation.3 | async-start | bytes 4718592 | tf_op jit(solution)/shard_map/all_gather | solution.py:467
  151.2 1.1 copy-start.1
  156.1 172.9 %reduce-scatter.2.cloned.1.call-start = ((), (), s32[]{:S(2)}) async-start(), calls=%async_computation.6 | async-start | bytes 4718592 | tf_op jit(solution)/shard_map/reduce_scatter | solution.py:469
  242.6 86.4 %copy-start = (bf16[128,2048]{1,0:T(8,128)(2,1)S(1)}, bf16[128,2048]{1,0:T(8,128)(2,1)}, u32[]{:S(2)}) copy-start(bf16[128,2048]{1,0:T(8,128)(2,1)} %merge_parts.1) | copy-start | bytes 1572868
  242.6 86.4 %copy-start.4 = (f32[2048]{0:T(1024)S(1)}, f32[2048]{0:T(1024)}, u32[]{:S(2)}) copy-start(f32[2048]{0:T(1024)} %param.27) | copy-start | bytes 24580
  242.7 89.1 %copy-start.5 = (f32[2048]{0:T(1024)S(1)}, f32[2048]{0:T(1024)}, u32[]{:S(2)}) copy-start(f32[2048]{0:T(1024)} %param.31) | copy-start | bytes 24580
  242.7 89.1 %copy-start.6 = (f32[2048]{0:T(1024)S(1)}, f32[2048]{0:T(1024)}, u32[]{:S(2)}) copy-start(f32[2048]{0:T(1024)} %param.30) | copy-start | bytes 24580
Sparse Core Ops, SparseCore 0:
  8.9 46.9 all-gather.9
  57.4 34.9 all-gather.7
  156.3 71.0 all-gather.5
  242.8 86.1 reduce-scatter.1

commit v2 on v1

--- a/solution.py
+++ b/solution.py
@@ -37,7 +37,8 @@
 
 def pack_kernel(lengths_ref, groups_ref, query_ref, out_ref, wide_ref):
     request_total = lengths_ref.shape[1]
-    _, column_count, capacity, part_width = out_ref.shape
+    _, column_count, chunk_rows, part_width = out_ref.shape
+    capacity = chunk_rows - STAT_ROWS
     slot_count = query_ref.shape[0]
     tiles = part_width // LANES
     for tile in range(wide_ref.shape[0]):
@@ -50,9 +51,11 @@
     start = 0
     for request in range(request_total):
         group = groups_ref[0, request]
+        count = jnp.full((STAT_ROWS, LANES), lengths_ref[0, request], jnp.int32).astype(jnp.float32)
         for column in range(column_count):
             for tile in range(tiles):
                 rows = wide_ref[column * tiles + tile, pl.ds(start, capacity), :]
+                rows = jnp.concatenate([rows, count], axis=0)
                 out_ref[group, column, :, tile * LANES : (tile + 1) * LANES] = rows.astype(
                     jnp.bfloat16
                 )
@@ -65,7 +68,7 @@
     return pl.pallas_call(
         pack_kernel,
         out_shape=jax.ShapeDtypeStruct(
-            (group_count, column_count, capacity, part_width), jnp.bfloat16
+            (group_count, column_count, capacity + STAT_ROWS, part_width), jnp.bfloat16
         ),
         in_specs=[smem_spec(), smem_spec(), vmem_spec()],
         out_specs=vmem_spec(),
@@ -89,16 +92,16 @@
     score_ref,
     top_ref,
 ):
-    sources, capacity, part_width = arrived_ref.shape
+    sources, chunk_rows, part_width = arrived_ref.shape
+    capacity = chunk_rows - STAT_ROWS
     local_heads = part_width // HD
     key_total = keys_ref.shape[1]
     chunks = key_total // KEY_CHUNK
 
     def take(source, offset):
         for head in range(local_heads):
-            query_ref[head, pl.ds(offset, capacity), :] = arrived_ref[
-                source, :, head * HD : (head + 1) * HD
-            ].astype(jnp.float32)
+            rows = arrived_ref[source, :, head * HD : (head + 1) * HD].astype(jnp.float32)
+            query_ref[head, pl.ds(offset, capacity), :] = rows[:capacity]
         return offset + counts_ref[source]
 
     total = lax.fori_loop(0, sources, take, jnp.int32(0))
@@ -196,7 +199,8 @@
 
 
 def attend_prefix(counts, arrived, turned_keys, wide_values):
-    sources, capacity, part_width = arrived.shape
+    sources, chunk_rows, part_width = arrived.shape
+    capacity = chunk_rows - STAT_ROWS
     local_heads = part_width // HD
     key_total = turned_keys.shape[1]
     row_total = -(-sources * capacity // ROW_BLOCK) * ROW_BLOCK + LANES
@@ -382,10 +386,112 @@
     )
 
 
-def expand_rows(piece_rows, up_matrix, up_offset):
-    product = jnp.dot(piece_rows, up_matrix, preferred_element_type=jnp.float32)
-    return jax.nn.gelu(product + up_offset.astype(jnp.float32), approximate=True).astype(
-        jnp.bfloat16
+def swap(value, mask):
+    total = lax.axis_size("grp") * lax.axis_size("dev")
+    return lax.ppermute(value, ("grp", "dev"), [(here, here ^ mask) for here in range(total)])
+
+
+def spread(block, masks):
+    held = {0: block}
+    for mask in masks:
+        held.update({mask ^ at: swap(held[at], mask) for at in list(held)})
+    return held
+
+
+def mlp_kernel(parts, *refs):
+    rows_ref, refs = refs[0], refs[1:]
+    ups, downs = refs[:parts], refs[parts : 2 * parts]
+    out_ref, up_ref, down_ref, sems = refs[2 * parts :]
+    model_width = rows_ref.shape[1]
+    copies = []
+    for part in range(parts):
+        up_copy = pltpu.make_async_copy(ups[part], up_ref.at[part], sems.at[part, 0])
+        down_copy = pltpu.make_async_copy(downs[part], down_ref.at[part], sems.at[part, 1])
+        up_copy.start()
+        down_copy.start()
+        copies.append((up_copy, down_copy))
+    rows = rows_ref[...]
+    total = None
+    for part in range(parts):
+        copies[part][0].wait()
+        product = jnp.dot(
+            rows, up_ref[part, :model_width, :], preferred_element_type=jnp.float32
+        )
+        offset = up_ref[part, model_width:, :].astype(jnp.float32)[0:1]
+        activation = jax.nn.gelu(product + offset, approximate=True).astype(jnp.bfloat16)
+        copies[part][1].wait()
+        term = jnp.dot(activation, down_ref[part], preferred_element_type=jnp.float32)
+        total = term if total is None else total + term
+    out_ref[...] = total.astype(jnp.bfloat16)
+
+
+def feed_forward(rows, ups, downs):
+    parts = len(ups)
+    row_count, model_width = rows.shape
+    up_rows, units = ups[0].shape
+    return pl.pallas_call(
+        functools.partial(mlp_kernel, parts),
+        out_shape=jax.ShapeDtypeStruct((row_count, model_width), jnp.bfloat16),
+        in_specs=[vmem_spec()] + [pl.BlockSpec(memory_space=pl.ANY)] * (2 * parts),
+        out_specs=vmem_spec(),
+        scratch_shapes=[
+            pltpu.VMEM((parts, up_rows, units), jnp.bfloat16),
+            pltpu.VMEM((parts, units, model_width), jnp.bfloat16),
+            pltpu.SemaphoreType.DMA((parts, 2)),
+        ],
+        compiler_params=pltpu.CompilerParams(vmem_limit_bytes=kernel_vmem),
+        cost_estimate=pl.CostEstimate(
+            flops=4 * row_count * model_width * parts * units,
+            bytes_accessed=4 * parts * model_width * units,
+            transcendentals=row_count * parts * units,
+        ),
+        name="feed_forward",
+    )(rows, *ups, *downs)
+
+
+def add_kernel(here_ref, there_ref, out_ref):
+    out_ref[...] = (
+        here_ref[...].astype(jnp.float32) + there_ref[...].astype(jnp.float32)
+    ).astype(jnp.bfloat16)
+
+
+def add_rows(here, there):
+    return pl.pallas_call(
+        add_kernel,
+        out_shape=jax.ShapeDtypeStruct(here.shape, jnp.bfloat16),
+        in_specs=[vmem_spec(), vmem_spec()],
+        out_specs=vmem_spec(),
+        name="add_rows",
+    )(here, there)
+
+
+def finish_kernel(hidden_ref, own_ref, near_ref, far_ref, bias_ref, gain_ref, shift_ref, out_ref):
+    summed = hidden_ref[...].astype(jnp.float32) + (
+        own_ref[...].astype(jnp.float32)
+        + near_ref[...].astype(jnp.float32)
+        + far_ref[...].astype(jnp.float32)
+    )
+    summed = summed + bias_ref[...]
+    out_ref[...] = layer_norm(summed, gain_ref[...], shift_ref[...]).astype(jnp.bfloat16)
+
+
+def finish_rows(hidden, own, near, far, bias, gain, shift):
+    model_width = hidden.shape[1]
+    return pl.pallas_call(
+        finish_kernel,
+        out_shape=jax.ShapeDtypeStruct(hidden.shape, jnp.bfloat16),
+        in_specs=[vmem_spec()] * 7,
+        out_specs=vmem_spec(),
+        compiler_params=pltpu.CompilerParams(vmem_limit_bytes=kernel_vmem),
+        name="finish_rows",
+    )(
+        hidden,
+        own,
+        near,
+        far,
+        bias.reshape(1, model_width),
+        gain.reshape(1, model_width),
+        shift.reshape(1, model_width),
     )
 
 
@@ -414,29 +520,18 @@
     local_heads = part_width // HD
     capacity = 2 * slot_count // group_count
     sources = group_count * column_count
-    request_total = suffix_lengths.shape[1]
-
-    table = lax.all_gather(
-        jnp.concatenate([suffix_lengths, request_group], axis=1),
-        ("grp", "dev"),
-        axis=0,
-        tiled=True,
-    )
-    counts = jnp.sum(
-        jnp.where(table[:, request_total:] == lax.axis_index("grp"), table[:, :request_total], 0),
-        axis=1,
-    )
 
     outgoing = pack_queries(
         suffix_lengths, request_group, suffix_queries, group_count, column_count, capacity
     )
     arrived = lax.all_to_all(
-        outgoing.reshape(sources, capacity, part_width),
+        outgoing.reshape(sources, capacity + STAT_ROWS, part_width),
         ("grp", "dev"),
         split_axis=0,
         concat_axis=0,
         tiled=True,
     )
+    counts = arrived[:, capacity, 0].astype(jnp.int32)
     turned_keys = prefix_keys[0].T
     value_heads = prefix_values[0].reshape(-1, local_heads, HD).transpose(1, 0, 2)
     wide_values = jnp.concatenate([value_heads, jnp.ones_like(value_heads)], axis=2)
@@ -458,23 +553,30 @@
         attn_gain,
         attn_shift,
     )
-    up_slice, bias_slice, down_slice = (
-        lax.all_gather(up_weight, "grp", axis=1, tiled=True),
-        lax.all_gather(up_bias, "grp", axis=0, tiled=True),
-        lax.all_gather(down_weight, "grp", axis=0, tiled=True),
-    )
-    activation = expand_rows(
-        lax.all_gather(hidden_state, "dev", axis=0, tiled=True), up_slice, bias_slice
-    )
-    mlp_sum = lax.psum_scatter(
-        jnp.dot(activation, down_slice, preferred_element_type=jnp.float32).astype(jnp.bfloat16),
-        "dev",
-        scatter_dimension=0,
-        tiled=True,
-    ).astype(jnp.float32)
-    return layer_norm(
-        hidden_state.astype(jnp.float32) + mlp_sum + down_bias, out_gain, out_shift
-    ).astype(jnp.bfloat16)
+    near_mask = group_count // 2 * column_count
+    far_mask = column_count // 2
+    column_masks = [1 << bit for bit in range(far_mask.bit_length() - 1)]
+    group_masks = [column_count << bit for bit in range((group_count // 2).bit_length() - 1)]
+    bias_rows = jnp.broadcast_to(up_bias[None, :], (16, up_bias.shape[0]))
+    ups = spread(jnp.concatenate([up_weight, bias_rows], axis=0), column_masks[::-1] + group_masks)
+    downs = spread(down_weight, column_masks + group_masks)
+    order = sorted(ups)
+    ups = [ups[mask] for mask in order]
+    downs = [downs[mask] for mask in order]
+
+    far_hidden = swap(hidden_state, far_mask)
+    near_hidden = swap(hidden_state, near_mask)
+    cross_hidden = swap(far_hidden, near_mask)
+    own_part = feed_forward(hidden_state, ups, downs)
+    near_part = feed_forward(near_hidden, ups, downs)
+    far_part = feed_forward(far_hidden, ups, downs)
+    cross_part = feed_forward(cross_hidden, ups, downs)
+    near_sum = swap(near_part, near_mask)
+    cross_sum = swap(cross_part, near_mask)
+    far_sum = swap(add_rows(far_part, cross_sum), far_mask)
+    return finish_rows(
+        hidden_state, own_part, near_sum, far_sum, down_bias, out_gain, out_shift
+    )
 
 
 def solution(mesh):

time: 342 us -> 270 us (0.79)
  blocking collectives: 73.6 us -> 0 us
  Pallas kernels: 30.4 us -> 70.3 us
  waiting for transfers between devices: 178 us -> 152 us
  starting transfers between devices: 10.1 us -> 28.6 us
  matrix products: 15.3 us -> 0 us
  between operations: 13.2 us -> 0.25 us
  other arithmetic: 5.66 us -> 1.25 us
    ppermute x0 -> x20, waiting for transfers between devices: none -> 136 us  [swap(): lax.ppermute(value, ('grp', 'dev'), [(here, here ^ mask) for here in rang...]
    reduce_scatter x1 -> x0, waiting for transfers between devices: 86.3 us -> none  [on_device(): lax.psum_scatter(jnp.dot(activation, down_slice, preferred_element_type=j...]
    all_gather x2 -> x0, blocking collectives: 73.6 us -> none  [the longest x1 68.3 us: on_device(): lax.all_gather(jnp.concatenate([suffix_lengths, request_group], axis=1),...]
    all_gather x3 -> x0, waiting for transfers between devices: 65.9 us -> none  [the longest x1 65.9 us: on_device(): lax.all_gather(hidden_state, 'dev', axis=0, tiled=True)]
    pallas_call x0 -> x6, Pallas kernels: none -> 39.8 us  [the longest x4 34.7 us: feed_forward(): pl.pallas_call(functools.partial(mlp_kernel, parts), out_shape=jax.ShapeD...]
    all_to_all x1, waiting for transfers between devices: 24 us -> 0.01 us  [on_device(): lax.all_to_all(answer_part, ('grp', 'dev'), split_axis=0, concat_axis=0,...]
    ppermute x0 -> x20, starting transfers between devices: none -> 16 us  [swap(): lax.ppermute(value, ('grp', 'dev'), [(here, here ^ mask) for here in rang...]
    all_to_all x1, waiting for transfers between devices: 0.01 us -> 15.8 us  [on_device(): lax.all_to_all(outgoing.reshape(sources, capacity + STAT_ROWS, part_width...]
  transfers between devices with their start and end apart: 6 -> 22, of which waited for: 3 -> 7; matrix products, arithmetic and copies ran while one was open for 4% -> 5% of each run, Pallas kernels for 9% -> 24%
where the time goes in v2:
time: 270 us; the launch traced here: 269 us
  waiting for transfers between devices  152 us (56%)
  Pallas kernels  70.3 us (26%)
  starting transfers between devices  28.6 us (11%)
  local copies, waits for them, and re-layouts  17 us (6%)
    ppermute x20, waiting for transfers between devices, swap(): lax.ppermute(value, ('grp', 'dev'), [(here, here ^ mask) for here in rang...  136 us
    pallas_call x4, Pallas kernels, feed_forward(): pl.pallas_call(functools.partial(mlp_kernel, parts), out_shape=jax.ShapeD...  34.7 us
    pallas_call x1, Pallas kernels, attend_prefix(): pl.pallas_call(far_kernel, out_shape=jax.ShapeDtypeStruct((sources, capac...  17.9 us
    ppermute x20, starting transfers between devices, swap(): lax.ppermute(value, ('grp', 'dev'), [(here, here ^ mask) for here in rang...  16 us
    all_to_all x1, waiting for transfers between devices, on_device(): lax.all_to_all(outgoing.reshape(sources, capacity + STAT_ROWS, part_width...  15.8 us
    unnamed x38, local copies, waits for them, and re-layouts  11.4 us
    all_to_all x1, starting transfers between devices, on_device(): lax.all_to_all(outgoing.reshape(sources, capacity + STAT_ROWS, part_width...  7.3 us
    pallas_call x1, Pallas kernels, attend_suffix(): pl.pallas_call(functools.partial(own_kernel, local_heads), out_shape=(jax...  6.28 us
  transfers between devices with their start and end apart: 22, of which 7 were waited for; matrix products, arithmetic and copies ran while one was open for 5% of the time, Pallas kernels for 24%

profile of v2, /device:TPU:0, one launch (start us, length us, event | category | flops | bytes accessed | tf_op | source)
XLA Modules:
  0.0 269.2 jit_solution(463835372111656119)
XLA Ops:
  0.0 2.4 pack_queries.1
  2.4 7.3 %all-to-all-start = ((bf16[32,72,256]{2,1,0:T(8,128)(2,1)}), bf16[32,72,256]{2,1,0:T(8,128)(2,1)S(1)}, u32[]{:S(2)}, u32[]{:S(2)}) async-start(bf16[32,72,256]{2,1,0:T(8,128)(2,1)} %bitcast.14), calls=%async_computation | async-start | bytes 2359296 | tf_op jit(solution)/shard_map/all_to_all | solution.py:527
  11.5 3.0 %copy.19 = bf16[1,4096,256]{1,2,0:T(8,128)(2,1)} copy(bf16[1,4096,256]{2,1,0:T(8,128)(2,1)S(1)} %copy-done.8) | data formatting | bytes 4194304 | tf_op args[7]
  14.5 3.1 %copy.20 = bf16[4096,2,128]{2,0,1:T(8,128)(2,1)S(1)} copy(bf16[4096,2,128]{0,2,1:T(8,128)(2,1)} %bitcast.13) | data formatting | bytes 4194304 | tf_op jit(solution)/shard_map/reshape;squeeze | solution.py:536
  17.6 4.2 %copy.18 = bf16[1,4096,256]{1,2,0:T(8,128)(2,1)} copy(bf16[1,4096,256]{2,1,0:T(8,128)(2,1)} %param.22) | data formatting | bytes 4194304 | tf_op args[6]
  21.8 2.5 concatenate.6.values_ref
  24.3 15.8 %all-to-all-done.arrived_ref = bf16[32,72,256]{2,1,0:T(8,128)(2,1)S(1)} async-done(((bf16[32,72,256]{2,1,0:T(8,128)(2,1)}), bf16[32,72,256]{2,1,0:T(8,128)(2,1)S(1)}, u32[]{:S(2)}, u32[]{:S(2)}) %all-to-all-start) | async-done | bytes 1179680 | tf_op jit(solution)/shard_map/all_to_all | solution.py:527
  41.3 17.9 %attend_prefix.1 = bf16[32,72,256]{2,1,0:T(8,128)(2,1)} custom-call(s32[32]{0:T(128)} %fusion.counts_ref, bf16[32,72,256]{2,1,0:T(8,128)(2,1)} %copy-done.9, bf16[256,4096]{1,0:T(8,128)(2,1)} %bitcast.15, bf16[2,4096,256]{2,1,0:T(8,128)(2,1)} %concatenate.6.values_ref), custom_call_target="tpu_custom_call" | custom-call | flops 8589934592 | bytes 8388608 | tf_op jit(solution)/shard_map/attend_prefix/pallas_call | solution.py:207
  59.2 5.3 %all-to-all-start.1 = ((bf16[32,72,256]{2,1,0:T(8,128)(2,1)}), bf16[32,72,256]{2,1,0:T(8,128)(2,1)}, u32[]{:S(2)}, u32[]{:S(2)}) async-start(bf16[32,72,256]{2,1,0:T(8,128)(2,1)} %attend_prefix.1), calls=%async_computation.1 | async-start | bytes 2359296 | tf_op jit(solution)/shard_map/all_to_all | solution.py:539
  69.0 40.2 %collective-permute-done.1.refs_3_ = bf16[2064,256]{1,0:T(8,128)(2,1)S(1)} collective-permute-done((bf16[2064,256]{1,0:T(8,128)(2,1)S(1)}, bf16[2064,256]{1,0:T(8,128)(2,1)S(1)}, u32[]{:S(2)}, u32[]{:S(2)}) %collective-permute-start.1) | collective-permute-done | bytes 1056800 | tf_op jit(solution)/shard_map/ppermute | solution.py:391
  110.7 20.6 %collective-permute-done.8.refs_11_ = bf16[256,2048]{1,0:T(8,128)(2,1)} collective-permute-done((bf16[256,2048]{1,0:T(8,128)(2,1)}, bf16[256,2048]{1,0:T(8,128)(2,1)}, u32[]{:S(2)}, u32[]{:S(2)}) %collective-permute-start.8) | collective-permute-done | bytes 1048608 | tf_op jit(solution)/shard_map/ppermute | solution.py:391
  132.3 23.9 %collective-permute-done.9.refs_12_ = bf16[256,2048]{1,0:T(8,128)(2,1)S(1)} collective-permute-done((bf16[256,2048]{1,0:T(8,128)(2,1)}, bf16[256,2048]{1,0:T(8,128)(2,1)S(1)}, u32[]{:S(2)}, u32[]{:S(2)}) %collective-permute-start.9) | collective-permute-done | bytes 1048608 | tf_op jit(solution)/shard_map/ppermute | solution.py:391
  157.2 6.3 %attend_suffix.1 = (f32[128,2048]{1,0:T(8,128)}, f32[128,128]{1,0:T(8,128)}, f32[128,128]{1,0:T(8,128)}) custom-call(s32[1,4]{1,0:T(1,128)} %lengths_ref.5, bf16[128,2048]{1,0:T(8,128)(2,1)} %query_ref.3, bf16[128,2048]{1,0:T(8,128)(2,1)} %key_ref.1, bf16[128,2048]{1,0:T(8,128)(2,1)} %value_ref.1), custom_call_target="tpu_custom_call" | custom-call | flops 1342177280 | bytes 2097152 | tf_op jit(solution)/shard_map/attend_suffix/pallas_call | solution.py:277
  163.5 3.9 %merge_parts.1.refs_0_.hidden_ref = bf16[128,2048]{1,0:T(8,128)(2,1)} custom-call(s32[1,4]{1,0:T(1,128)} %lengths_ref.5, s32[1,4]{1,0:T(1,128)} %groups_ref.3, bf16[4,8,72,256]{3,2,1,0:T(8,128)(2,1)} %bitcast.5.arrived_ref, f32[128,2048]{1,0:T(8,128)} %get-tuple-element.8.own_mixed_ref, f32[128,128]{1,0:T(8,128)} %get-tuple-element.9.own_top_ref, ...), custom_call_target="tpu_custom_call" | custom-call | tf_op jit(solution)/shard_map/merge_parts/pallas_call | solution.py:365
  168.1 2.5 collective-permute-start.16
  170.5 23.8 %collective-permute-done.16.refs_0_ = bf16[128,2048]{1,0:T(8,128)(2,1)S(1)} collective-permute-done((bf16[128,2048]{1,0:T(8,128)(2,1)}, bf16[128,2048]{1,0:T(8,128)(2,1)S(1)}, u32[]{:S(2)}, u32[]{:S(2)}) %collective-permute-start.16) | collective-permute-done | bytes 524320 | tf_op jit(solution)/shard_map/ppermute | solution.py:391
  196.3 12.7 %collective-permute-done.17.refs_0_ = bf16[128,2048]{1,0:T(8,128)(2,1)S(1)} collective-permute-done((bf16[128,2048]{1,0:T(8,128)(2,1)S(1)}, bf16[128,2048]{1,0:T(8,128)(2,1)S(1)}, u32[]{:S(2)}, u32[]{:S(2)}) %collective-permute-start.17) | collective-permute-done | bytes 524320 | tf_op jit(solution)/shard_map/ppermute | solution.py:391
  209.9 8.6 %feed_forward.7 = bf16[128,2048]{1,0:T(8,128)(2,1)} custom-call(bf16[128,2048]{1,0:T(8,128)(2,1)} %copy-done.15, bf16[2064,256]{1,0:T(8,128)(2,1)} %copy-done, bf16[2064,256]{1,0:T(8,128)(2,1)} %copy-done.2, bf16[2064,256]{1,0:T(8,128)(2,1)} %copy-done.1, bf16[2064,256]{1,0:T(8,128)(2,1)} %collective-permute-done.2.refs_4_, bf16[2064,256]{1,0:T(8,128)(2,1)} %copy-done.3, ...), custom_call_target="tpu_custom_call" | custom-call | flops 2147483648 | bytes 16777216 | tf_op jit(solution)/shard_map/feed_forward/pallas_call | solution.py:432
  220.9 8.6 %feed_forward.5 = bf16[128,2048]{1,0:T(8,128)(2,1)} custom-call(bf16[128,2048]{1,0:T(8,128)(2,1)} %copy-done.14, bf16[2064,256]{1,0:T(8,128)(2,1)} %copy-done, bf16[2064,256]{1,0:T(8,128)(2,1)} %copy-done.2, bf16[2064,256]{1,0:T(8,128)(2,1)} %copy-done.1, bf16[2064,256]{1,0:T(8,128)(2,1)} %collective-permute-done.2.refs_4_, bf16[2064,256]{1,0:T(8,128)(2,1)} %copy-done.3, ...), custom_call_target="tpu_custom_call" | custom-call | flops 2147483648 | bytes 16777216 | tf_op jit(solution)/shard_map/feed_forward/pallas_call | solution.py:432
  230.4 8.8 %feed_forward.6.here_ref = bf16[128,2048]{1,0:T(8,128)(2,1)} custom-call(bf16[128,2048]{1,0:T(8,128)(2,1)} %copy-done.11, bf16[2064,256]{1,0:T(8,128)(2,1)} %copy-done, bf16[2064,256]{1,0:T(8,128)(2,1)} %copy-done.2, bf16[2064,256]{1,0:T(8,128)(2,1)} %copy-done.1, bf16[2064,256]{1,0:T(8,128)(2,1)} %collective-permute-done.2.refs_4_, ...), custom_call_target="tpu_custom_call" | custom-call | flops 2147483648 | bytes 16777216 | tf_op jit(solution)/shard_map/feed_forward/pallas_call | solution.py:432
  240.0 2.1 add_rows.1
  242.2 8.6 %feed_forward.4.own_ref = bf16[128,2048]{1,0:T(8,128)(2,1)} custom-call(bf16[128,2048]{1,0:T(8,128)(2,1)} %merge_parts.1.refs_0_.hidden_ref, bf16[2064,256]{1,0:T(8,128)(2,1)} %copy-done, bf16[2064,256]{1,0:T(8,128)(2,1)} %copy-done.2, bf16[2064,256]{1,0:T(8,128)(2,1)} %copy-done.1, bf16[2064,256]{1,0:T(8,128)(2,1)} %collective-permute-done.2.refs_4_, ...), custom_call_target="tpu_custom_call" | custom-call | flops 2147483648 | bytes 16777216 | tf_op jit(solution)/shard_map/feed_forward/pallas_call | solution.py:432
  250.8 14.6 %collective-permute-done.19.far_ref = bf16[128,2048]{1,0:T(8,128)(2,1)S(1)} collective-permute-done((bf16[128,2048]{1,0:T(8,128)(2,1)}, bf16[128,2048]{1,0:T(8,128)(2,1)S(1)}, u32[]{:S(2)}, u32[]{:S(2)}) %collective-permute-start.19) | collective-permute-done | bytes 524320 | tf_op jit(solution)/shard_map/ppermute | solution.py:391
  266.2 3.0 %finish_rows.1 = bf16[128,2048]{1,0:T(8,128)(2,1)} custom-call(bf16[128,2048]{1,0:T(8,128)(2,1)} %merge_parts.1.refs_0_.hidden_ref, bf16[128,2048]{1,0:T(8,128)(2,1)} %feed_forward.4.own_ref, bf16[128,2048]{1,0:T(8,128)(2,1)} %copy-done.12, bf16[128,2048]{1,0:T(8,128)(2,1)} %copy-done.13, f32[1,2048]{1,0:T(1,128)} %bitcast.18, f32[1,2048]{1,0:T(1,128)} %bitcast.19, ...), custom_call_target="tpu_custom_call" | custom-call | tf_op jit(solution)/shard_map/finish_rows/pallas_call | solution.py:480
  (73 shorter events, 19.0 us)
Async XLA Ops:
  2.4 37.8 %all-to-all-start = ((bf16[32,72,256]{2,1,0:T(8,128)(2,1)}), bf16[32,72,256]{2,1,0:T(8,128)(2,1)S(1)}, u32[]{:S(2)}, u32[]{:S(2)}) async-start(bf16[32,72,256]{2,1,0:T(8,128)(2,1)} %bitcast.14), calls=%async_computation | async-start | bytes 2359296 | tf_op jit(solution)/shard_map/all_to_all | solution.py:527
  9.7 58.8 %collective-permute-start.7 = (bf16[256,2048]{1,0:T(8,128)(2,1)}, bf16[256,2048]{1,0:T(8,128)(2,1)}, u32[]{:S(2)}, u32[]{:S(2)}) collective-permute-start(bf16[256,2048]{1,0:T(8,128)(2,1)} %refs_9_.7), channel_id=1, source_target_pairs={{0,1},{1,0},{2,3},{3,2},{4,5},{5,4},{6,7},{7,6},{8,9},{9,8},{10,11... | collective-permute-start | bytes 3145736 | tf_op jit(solution)/shard_map/ppermute | solution.py:391
  59.2 104.3 %all-to-all-start.1 = ((bf16[32,72,256]{2,1,0:T(8,128)(2,1)}), bf16[32,72,256]{2,1,0:T(8,128)(2,1)}, u32[]{:S(2)}, u32[]{:S(2)}) async-start(bf16[32,72,256]{2,1,0:T(8,128)(2,1)} %attend_prefix.1), calls=%async_computation.1 | async-start | bytes 2359296 | tf_op jit(solution)/shard_map/all_to_all | solution.py:539
  64.7 98.9 %copy-start = (bf16[2064,256]{1,0:T(8,128)(2,1)}, bf16[2064,256]{1,0:T(8,128)(2,1)S(1)}, u32[]{:S(2)}) copy-start(bf16[2064,256]{1,0:T(8,128)(2,1)S(1)} %pad_maximum_fusion.refs_1_) | copy-start | bytes 3170308
  64.7 44.5 %collective-permute-start.1 = (bf16[2064,256]{1,0:T(8,128)(2,1)S(1)}, bf16[2064,256]{1,0:T(8,128)(2,1)S(1)}, u32[]{:S(2)}, u32[]{:S(2)}) collective-permute-start(bf16[2064,256]{1,0:T(8,128)(2,1)S(1)} %pad_maximum_fusion.refs_1_), channel_id=1, source_target_pairs={{0,2},{1,3},{2,0},{3,1},{4,6},{5,7},{6,4},{7,5},{8,10},{9,11},{10,... | collective-permute-start | bytes 3170312 | tf_op jit(solution)/shard_map/ppermute | solution.py:391
  66.4 64.9 %collective-permute-start.8 = (bf16[256,2048]{1,0:T(8,128)(2,1)}, bf16[256,2048]{1,0:T(8,128)(2,1)}, u32[]{:S(2)}, u32[]{:S(2)}) collective-permute-start(bf16[256,2048]{1,0:T(8,128)(2,1)} %refs_9_.7), channel_id=1, source_target_pairs={{0,2},{1,3},{2,0},{3,1},{4,6},{5,7},{6,4},{7,5},{8,10},{9,11},{10,... | collective-permute-start | bytes 3145736 | tf_op jit(solution)/shard_map/ppermute | solution.py:391
  66.8 64.9 %collective-permute-start = (bf16[2064,256]{1,0:T(8,128)(2,1)S(1)}, bf16[2064,256]{1,0:T(8,128)(2,1)S(1)}, u32[]{:S(2)}, u32[]{:S(2)}) collective-permute-start(bf16[2064,256]{1,0:T(8,128)(2,1)S(1)} %pad_maximum_fusion.refs_1_), channel_id=1, source_target_pairs={{0,1},{1,0},{2,3},{3,2},{4,5},{5,4},{6,7},{7,6},{8,9},{9,8},{10,11... | collective-permute-start | bytes 3170312 | tf_op jit(solution)/shard_map/ppermute | solution.py:391
  68.5 63.2 %collective-permute-start.10 = (bf16[256,2048]{1,0:T(8,128)(2,1)}, bf16[256,2048]{1,0:T(8,128)(2,1)S(1)}, u32[]{:S(2)}, u32[]{:S(2)}) collective-permute-start(bf16[256,2048]{1,0:T(8,128)(2,1)} %refs_9_.7), channel_id=1, source_target_pairs={{0,8},{1,9},{2,10},{3,11},{4,12},{5,13},{6,14},{7,15},{8,0},{9,1},... | collective-permute-start | bytes 3145736 | tf_op jit(solution)/shard_map/ppermute | solution.py:391
  68.5 63.7 %collective-permute-start.3 = (bf16[2064,256]{1,0:T(8,128)(2,1)S(1)}, bf16[2064,256]{1,0:T(8,128)(2,1)S(1)}, u32[]{:S(2)}, u32[]{:S(2)}) collective-permute-start(bf16[2064,256]{1,0:T(8,128)(2,1)S(1)} %pad_maximum_fusion.refs_1_), channel_id=1, source_target_pairs={{0,8},{1,9},{2,10},{3,11},{4,12},{5,13},{6,14},{7,15},{8,0},{9,1},... | collective-permute-start | bytes 3170312 | tf_op jit(solution)/shard_map/ppermute | solution.py:391
  109.2 54.3 %copy-start.1 = (bf16[2064,256]{1,0:T(8,128)(2,1)}, bf16[2064,256]{1,0:T(8,128)(2,1)S(1)}, u32[]{:S(2)}) copy-start(bf16[2064,256]{1,0:T(8,128)(2,1)S(1)} %collective-permute-done.1.refs_3_) | copy-start | bytes 3170308
  109.2 47.0 %collective-permute-start.2 = (bf16[2064,256]{1,0:T(8,128)(2,1)S(1)}, bf16[2064,256]{1,0:T(8,128)(2,1)}, u32[]{:S(2)}, u32[]{:S(2)}) collective-permute-start(bf16[2064,256]{1,0:T(8,128)(2,1)S(1)} %collective-permute-done.1.refs_3_), channel_id=1, source_target_pairs={{0,1},{1,0},{2,3},{3,2},{4,5},{5,4},{6,7},{7,6},{8,9},{9,8},{10,11... | collective-permute-start | bytes 3170312 | tf_op jit(solution)/shard_map/ppermute | solution.py:391
  131.3 24.9 %collective-permute-start.9 = (bf16[256,2048]{1,0:T(8,128)(2,1)}, bf16[256,2048]{1,0:T(8,128)(2,1)S(1)}, u32[]{:S(2)}, u32[]{:S(2)}) collective-permute-start(bf16[256,2048]{1,0:T(8,128)(2,1)} %collective-permute-done.7.refs_10_), channel_id=1, source_target_pairs={{0,2},{1,3},{2,0},{3,1},{4,6},{5,7},{6,4},{7,5},{8,10},{9,11},{10,... | collective-permute-start | bytes 3145736 | tf_op jit(solution)/shard_map/ppermute | solution.py:391
  131.7 35.8 %collective-permute-start.11 = (bf16[256,2048]{1,0:T(8,128)(2,1)}, bf16[256,2048]{1,0:T(8,128)(2,1)}, u32[]{:S(2)}, u32[]{:S(2)}) collective-permute-start(bf16[256,2048]{1,0:T(8,128)(2,1)} %collective-permute-done.7.refs_10_), channel_id=1, source_target_pairs={{0,8},{1,9},{2,10},{3,11},{4,12},{5,13},{6,14},{7,15},{8,0},{9,1},... | collective-permute-start | bytes 3145736 | tf_op jit(solution)/shard_map/ppermute | solution.py:391
  131.7 36.4 %collective-permute-start.12 = (bf16[256,2048]{1,0:T(8,128)(2,1)}, bf16[256,2048]{1,0:T(8,128)(2,1)}, u32[]{:S(2)}, u32[]{:S(2)}) collective-permute-start(bf16[256,2048]{1,0:T(8,128)(2,1)} %collective-permute-done.8.refs_11_), channel_id=1, source_target_pairs={{0,8},{1,9},{2,10},{3,11},{4,12},{5,13},{6,14},{7,15},{8,0},{9,1},... | collective-permute-start | bytes 3145736 | tf_op jit(solution)/shard_map/ppermute | solution.py:391
  132.2 63.6 %collective-permute-start.5 = (bf16[2064,256]{1,0:T(8,128)(2,1)S(1)}, bf16[2064,256]{1,0:T(8,128)(2,1)}, u32[]{:S(2)}, u32[]{:S(2)}) collective-permute-start(bf16[2064,256]{1,0:T(8,128)(2,1)S(1)} %collective-permute-done.1.refs_3_), channel_id=1, source_target_pairs={{0,8},{1,9},{2,10},{3,11},{4,12},{5,13},{6,14},{7,15},{8,0},{9,1},... | collective-permute-start | bytes 3170312 | tf_op jit(solution)/shard_map/ppermute | solution.py:391
  156.2 40.1 %collective-permute-start.4 = (bf16[2064,256]{1,0:T(8,128)(2,1)S(1)}, bf16[2064,256]{1,0:T(8,128)(2,1)}, u32[]{:S(2)}, u32[]{:S(2)}) collective-permute-start(bf16[2064,256]{1,0:T(8,128)(2,1)S(1)} %collective-permute-done.refs_2_), channel_id=1, source_target_pairs={{0,8},{1,9},{2,10},{3,11},{4,12},{5,13},{6,14},{7,15},{8,0},{9,1},... | collective-permute-start | bytes 3170312 | tf_op jit(solution)/shard_map/ppermute | solution.py:391
  157.2 39.1 %collective-permute-start.6 = (bf16[2064,256]{1,0:T(8,128)(2,1)}, bf16[2064,256]{1,0:T(8,128)(2,1)}, u32[]{:S(2)}, u32[]{:S(2)}) collective-permute-start(bf16[2064,256]{1,0:T(8,128)(2,1)} %collective-permute-done.2.refs_4_), channel_id=1, source_target_pairs={{0,8},{1,9},{2,10},{3,11},{4,12},{5,13},{6,14},{7,15},{8,0},{9,1},... | collective-permute-start | bytes 3170312 | tf_op jit(solution)/shard_map/ppermute | solution.py:391
  167.5 28.8 %collective-permute-start.13 = (bf16[256,2048]{1,0:T(8,128)(2,1)S(1)}, bf16[256,2048]{1,0:T(8,128)(2,1)S(1)}, u32[]{:S(2)}, u32[]{:S(2)}) collective-permute-start(bf16[256,2048]{1,0:T(8,128)(2,1)S(1)} %copy-done.6), channel_id=1, source_target_pairs={{0,8},{1,9},{2,10},{3,11},{4,12},{5,13},{6,14},{7,15},{8,0},{9,1},... | collective-permute-start | bytes 3145736 | tf_op jit(solution)/shard_map/ppermute | solution.py:391
  168.1 26.2 %collective-permute-start.16 = (bf16[128,2048]{1,0:T(8,128)(2,1)}, bf16[128,2048]{1,0:T(8,128)(2,1)S(1)}, u32[]{:S(2)}, u32[]{:S(2)}) collective-permute-start(bf16[128,2048]{1,0:T(8,128)(2,1)} %merge_parts.1.refs_0_.hidden_ref), channel_id=1, source_target_pairs={{0,4},{1,5},{2,6},{3,7},{4,0},{5,1},{6,2},{7,3},{8,12},{9,13},{10,... | collective-permute-start | bytes 1572872 | tf_op jit(solution)/shard_map/ppermute | solution.py:391
  194.3 14.8 %collective-permute-start.17 = (bf16[128,2048]{1,0:T(8,128)(2,1)S(1)}, bf16[128,2048]{1,0:T(8,128)(2,1)S(1)}, u32[]{:S(2)}, u32[]{:S(2)}) collective-permute-start(bf16[128,2048]{1,0:T(8,128)(2,1)S(1)} %collective-permute-done.16.refs_0_), channel_id=1, source_target_pairs={{0,16},{1,17},{2,18},{3,19},{4,20},{5,21},{6,22},{7,23},{8,24},{9,... | collective-permute-start | bytes 1572872 | tf_op jit(solution)/shard_map/ppermute | solution.py:391
  195.8 24.3 %collective-permute-start.14 = (bf16[128,2048]{1,0:T(8,128)(2,1)}, bf16[128,2048]{1,0:T(8,128)(2,1)S(1)}, u32[]{:S(2)}, u32[]{:S(2)}) collective-permute-start(bf16[128,2048]{1,0:T(8,128)(2,1)} %merge_parts.1.refs_0_.hidden_ref), channel_id=1, source_target_pairs={{0,16},{1,17},{2,18},{3,19},{4,20},{5,21},{6,22},{7,23},{8,24},{9,... | collective-permute-start | bytes 1572872 | tf_op jit(solution)/shard_map/ppermute | solution.py:391
  218.5 20.7 %collective-permute-start.18 = (bf16[128,2048]{1,0:T(8,128)(2,1)}, bf16[128,2048]{1,0:T(8,128)(2,1)S(1)}, u32[]{:S(2)}, u32[]{:S(2)}) collective-permute-start(bf16[128,2048]{1,0:T(8,128)(2,1)} %feed_forward.7), channel_id=1, source_target_pairs={{0,16},{1,17},{2,18},{3,19},{4,20},{5,21},{6,22},{7,23},{8,24},{9,... | collective-permute-start | bytes 1572872 | tf_op jit(solution)/shard_map/ppermute | solution.py:391
  229.5 21.3 %collective-permute-start.15 = (bf16[128,2048]{1,0:T(8,128)(2,1)}, bf16[128,2048]{1,0:T(8,128)(2,1)S(1)}, u32[]{:S(2)}, u32[]{:S(2)}) collective-permute-start(bf16[128,2048]{1,0:T(8,128)(2,1)} %feed_forward.5), channel_id=1, source_target_pairs={{0,16},{1,17},{2,18},{3,19},{4,20},{5,21},{6,22},{7,23},{8,24},{9,... | collective-permute-start | bytes 1572872 | tf_op jit(solution)/shard_map/ppermute | solution.py:391
  242.1 23.3 %collective-permute-start.19 = (bf16[128,2048]{1,0:T(8,128)(2,1)}, bf16[128,2048]{1,0:T(8,128)(2,1)S(1)}, u32[]{:S(2)}, u32[]{:S(2)}) collective-permute-start(bf16[128,2048]{1,0:T(8,128)(2,1)} %add_rows.1), channel_id=1, source_target_pairs={{0,4},{1,5},{2,6},{3,7},{4,0},{5,1},{6,2},{7,3},{8,12},{9,13},{10,... | collective-permute-start | bytes 1572872 | tf_op jit(solution)/shard_map/ppermute | solution.py:391
  (16 other events, 161.2 us)

commit v3 on v2

--- a/solution.py
+++ b/solution.py
@@ -391,10 +391,12 @@
     return lax.ppermute(value, ("grp", "dev"), [(here, here ^ mask) for here in range(total)])
 
 
-def spread(block, masks):
-    held = {0: block}
+def complete(held, masks):
+    held = dict(held)
     for mask in masks:
-        held.update({mask ^ at: swap(held[at], mask) for at in list(held)})
+        for at in list(held):
+            if mask ^ at not in held:
+                held[mask ^ at] = swap(held[at], mask)
     return held
 
 
@@ -521,9 +523,18 @@
     capacity = 2 * slot_count // group_count
     sources = group_count * column_count
 
+    near_mask = group_count // 2 * column_count
+    far_mask = column_count // 2
+    column_masks = [1 << bit for bit in range(far_mask.bit_length() - 1)]
+    group_masks = [column_count << bit for bit in range((group_count // 2).bit_length() - 1)]
+
     outgoing = pack_queries(
         suffix_lengths, request_group, suffix_queries, group_count, column_count, capacity
     )
+    bias_rows = jnp.broadcast_to(up_bias[None, :], (16, up_bias.shape[0]))
+    ups = {0: jnp.concatenate([up_weight, bias_rows], axis=0)}
+    downs = {0: down_weight}
+
     arrived = lax.all_to_all(
         outgoing.reshape(sources, capacity + STAT_ROWS, part_width),
         ("grp", "dev"),
@@ -531,17 +542,29 @@
         concat_axis=0,
         tiled=True,
     )
+    for mask in column_masks:
+        ups[mask] = swap(ups[0], mask)
+    arrived, ups, downs = lax.optimization_barrier((arrived, ups, downs))
+
     counts = arrived[:, capacity, 0].astype(jnp.int32)
     turned_keys = prefix_keys[0].T
     value_heads = prefix_values[0].reshape(-1, local_heads, HD).transpose(1, 0, 2)
     wide_values = jnp.concatenate([value_heads, jnp.ones_like(value_heads)], axis=2)
     answer_part = attend_prefix(counts, arrived, turned_keys, wide_values)
+    for mask in column_masks:
+        downs[mask] = swap(downs[0], mask)
+    answer_part, ups, downs = lax.optimization_barrier((answer_part, ups, downs))
+
     answer = lax.all_to_all(
         answer_part, ("grp", "dev"), split_axis=0, concat_axis=0, tiled=True
     ).reshape(group_count, column_count, capacity + STAT_ROWS, part_width)
+    ups = complete(ups, column_masks[::-1])
+    downs = complete(downs, column_masks)
     own_mixed, own_top, own_sum = attend_suffix(
         suffix_lengths, suffix_queries, suffix_keys, suffix_values, local_heads
     )
+    answer, ups, downs, own_mixed = lax.optimization_barrier((answer, ups, downs, own_mixed))
+
     hidden_state = merge_parts(
         suffix_lengths,
         request_group,
@@ -553,25 +576,22 @@
         attn_gain,
         attn_shift,
     )
-    near_mask = group_count // 2 * column_count
-    far_mask = column_count // 2
-    column_masks = [1 << bit for bit in range(far_mask.bit_length() - 1)]
-    group_masks = [column_count << bit for bit in range((group_count // 2).bit_length() - 1)]
-    bias_rows = jnp.broadcast_to(up_bias[None, :], (16, up_bias.shape[0]))
-    ups = spread(jnp.concatenate([up_weight, bias_rows], axis=0), column_masks[::-1] + group_masks)
-    downs = spread(down_weight, column_masks + group_masks)
+
+    far_hidden = swap(hidden_state, far_mask)
+    near_hidden = swap(hidden_state, near_mask)
+    ups = complete(ups, group_masks)
+    downs = complete(downs, group_masks)
     order = sorted(ups)
     ups = [ups[mask] for mask in order]
     downs = [downs[mask] for mask in order]
-
-    far_hidden = swap(hidden_state, far_mask)
-    near_hidden = swap(hidden_state, near_mask)
-    cross_hidden = swap(far_hidden, near_mask)
     own_part = feed_forward(hidden_state, ups, downs)
     near_part = feed_forward(near_hidden, ups, downs)
+    far_hidden, own_part, near_part = lax.optimization_barrier((far_hidden, own_part, near_part))
+    cross_hidden = swap(far_hidden, near_mask)
+    near_sum = swap(near_part, near_mask)
     far_part = feed_forward(far_hidden, ups, downs)
+    cross_hidden, far_part = lax.optimization_barrier((cross_hidden, far_part))
     cross_part = feed_forward(cross_hidden, ups, downs)
-    near_sum = swap(near_part, near_mask)
     cross_sum = swap(cross_part, near_mask)
     far_sum = swap(add_rows(far_part, cross_sum), far_mask)
     return finish_rows(

time: 270 us -> 253 us (0.937)
  waiting for transfers between devices: 152 us -> 124 us
  local copies, waits for them, and re-layouts: 17 us -> 23 us
  Pallas kernels: 70.3 us -> 75.4 us
    all_to_all x1, waiting for transfers between devices: 15.8 us -> 0.01 us  [on_device(): lax.all_to_all(outgoing.reshape(sources, capacity + STAT_ROWS, part_width...]
    ppermute x20, waiting for transfers between devices: 136 us -> 124 us  [swap(): lax.ppermute(value, ('grp', 'dev'), [(here, here ^ mask) for here in rang...]
    pallas_call x1, Pallas kernels: 17.9 us -> 23.2 us  [attend_prefix(): pl.pallas_call(far_kernel, out_shape=jax.ShapeDtypeStruct((sources, capac...]
    unnamed x38 -> x40, local copies, waits for them, and re-layouts: 11.4 us -> 15 us
  transfers between devices with their start and end apart: 22 -> 22, of which waited for: 7 -> 12; matrix products, arithmetic and copies ran while one was open for 5% -> 7% of each run, Pallas kernels for 24% -> 24%
where the time goes in v3:
time: 253 us
  waiting for transfers between devices  124 us (49%)
  Pallas kernels  75.4 us (30%)
  starting transfers between devices  27.8 us (11%)
  local copies, waits for them, and re-layouts  23 us (9%)
    ppermute x20, waiting for transfers between devices, swap(): lax.ppermute(value, ('grp', 'dev'), [(here, here ^ mask) for here in rang...  124 us
    pallas_call x4, Pallas kernels, feed_forward(): pl.pallas_call(functools.partial(mlp_kernel, parts), out_shape=jax.ShapeD...  34.7 us
    pallas_call x1, Pallas kernels, attend_prefix(): pl.pallas_call(far_kernel, out_shape=jax.ShapeDtypeStruct((sources, capac...  23.2 us
    ppermute x20, starting transfers between devices, swap(): lax.ppermute(value, ('grp', 'dev'), [(here, here ^ mask) for here in rang...  16.4 us
    unnamed x40, local copies, waits for them, and re-layouts  15 us
    all_to_all x1, starting transfers between devices, on_device(): lax.all_to_all(outgoing.reshape(sources, capacity + STAT_ROWS, part_width...  7.41 us
    pallas_call x1, Pallas kernels, attend_suffix(): pl.pallas_call(functools.partial(own_kernel, local_heads), out_shape=(jax...  6.28 us
  transfers between devices with their start and end apart: 22, of which 12 were waited for; matrix products, arithmetic and copies ran while one was open for 7% of the time, Pallas kernels for 24%

profile of v3, /device:TPU:0, one launch (start us, length us, event | category | flops | bytes accessed | tf_op | source)
XLA Modules:
  0.0 252.9 jit_solution(4164214260628904132)
XLA Ops:
  2.3 7.4 %all-to-all-start = ((bf16[32,72,256]{2,1,0:T(8,128)(2,1)}), bf16[32,72,256]{2,1,0:T(8,128)(2,1)}, u32[]{:S(2)}, u32[]{:S(2)}) async-start(bf16[32,72,256]{2,1,0:T(8,128)(2,1)} %bitcast.14), calls=%async_computation | async-start | bytes 2359296 | tf_op jit(solution)/shard_map/all_to_all | solution.py:538
  13.1 34.7 %collective-permute-done.refs_2_ = bf16[2064,256]{1,0:T(8,128)(2,1)S(1)} collective-permute-done((bf16[2064,256]{1,0:T(8,128)(2,1)S(1)}, bf16[2064,256]{1,0:T(8,128)(2,1)S(1)}, u32[]{:S(2)}, u32[]{:S(2)}) %collective-permute-start) | collective-permute-done | bytes 1056800 | tf_op jit(solution)/shard_map/ppermute | solution.py:391
  47.8 6.3 %collective-permute-done.1.refs_3_ = bf16[2064,256]{1,0:T(8,128)(2,1)S(1)} collective-permute-done((bf16[2064,256]{1,0:T(8,128)(2,1)S(1)}, bf16[2064,256]{1,0:T(8,128)(2,1)S(1)}, u32[]{:S(2)}, u32[]{:S(2)}) %collective-permute-start.1) | collective-permute-done | bytes 1056800 | tf_op jit(solution)/shard_map/ppermute | solution.py:391
  56.2 4.1 %copy.18 = bf16[1,4096,256]{1,2,0:T(8,128)(2,1)} copy(bf16[1,4096,256]{2,1,0:T(8,128)(2,1)} %param.22) | data formatting | bytes 4194304 | tf_op args[6]
  60.3 4.1 %copy.19 = bf16[1,4096,256]{1,2,0:T(8,128)(2,1)} copy(bf16[1,4096,256]{2,1,0:T(8,128)(2,1)} %param.23) | data formatting | bytes 4194304 | tf_op args[7]
  64.4 4.1 %copy.20 = bf16[4096,2,128]{2,0,1:T(8,128)(2,1)} copy(bf16[4096,2,128]{0,2,1:T(8,128)(2,1)} %bitcast.13) | data formatting | bytes 4194304 | tf_op jit(solution)/shard_map/reshape;squeeze | solution.py:551
  68.5 3.9 %concatenate.7.values_ref = bf16[2,4096,256]{2,1,0:T(8,128)(2,1)} pad(bf16[2,4096,128]{2,1,0:T(8,128)(2,1)} %bitcast.12, bf16[]{:T(256)} %constant.0.clone.1), padding=0_0x0_0x0_128 | pad | bytes 6291458 | tf_op jit(solution)/shard_map/concatenate | solution.py:552
  74.5 23.2 %attend_prefix.1 = bf16[32,72,256]{2,1,0:T(8,128)(2,1)} custom-call(s32[32]{0:T(128)} %convert_reduce_fusion.counts_ref, bf16[32,72,256]{2,1,0:T(8,128)(2,1)} %all-to-all-done.arrived_ref, bf16[256,4096]{1,0:T(8,128)(2,1)} %bitcast.15, bf16[2,4096,256]{2,1,0:T(8,128)(2,1)} %concatenate.7.values_ref), custom_call_target="tpu_custom_call" | custom-call | flops 8589934592 | bytes 8388608 | tf_op jit(solution)/shard_map/attend_prefix/pallas_call | solution.py:207
  97.7 4.0 %all-to-all-start.1 = ((bf16[32,72,256]{2,1,0:T(8,128)(2,1)}), bf16[32,72,256]{2,1,0:T(8,128)(2,1)}, u32[]{:S(2)}, u32[]{:S(2)}) async-start(bf16[32,72,256]{2,1,0:T(8,128)(2,1)} %attend_prefix.1), calls=%async_computation.1 | async-start | bytes 2359296 | tf_op jit(solution)/shard_map/all_to_all | solution.py:558
  104.9 6.3 %attend_suffix.1 = (f32[128,2048]{1,0:T(8,128)}, f32[128,128]{1,0:T(8,128)}, f32[128,128]{1,0:T(8,128)}) custom-call(s32[1,4]{1,0:T(1,128)} %lengths_ref.5, bf16[128,2048]{1,0:T(8,128)(2,1)} %query_ref.3, bf16[128,2048]{1,0:T(8,128)(2,1)} %key_ref.1, bf16[128,2048]{1,0:T(8,128)(2,1)} %value_ref.1), custom_call_target="tpu_custom_call" | custom-call | flops 1342177280 | bytes 2097152 | tf_op jit(solution)/shard_map/attend_suffix/pallas_call | solution.py:277
  111.2 28.3 %collective-permute-done.5.refs_12_ = bf16[256,2048]{1,0:T(8,128)(2,1)} collective-permute-done((bf16[256,2048]{1,0:T(8,128)(2,1)}, bf16[256,2048]{1,0:T(8,128)(2,1)}, u32[]{:S(2)}, u32[]{:S(2)}) %collective-permute-start.5) | collective-permute-done | bytes 1048608 | tf_op jit(solution)/shard_map/ppermute | solution.py:391
  139.4 6.5 %collective-permute-done.4.refs_4_ = bf16[2064,256]{1,0:T(8,128)(2,1)} collective-permute-done((bf16[2064,256]{1,0:T(8,128)(2,1)S(1)}, bf16[2064,256]{1,0:T(8,128)(2,1)}, u32[]{:S(2)}, u32[]{:S(2)}) %collective-permute-start.4) | collective-permute-done | bytes 1056800 | tf_op jit(solution)/shard_map/ppermute | solution.py:391
  148.9 4.4 %collective-permute-done.12.refs_14_ = bf16[256,2048]{1,0:T(8,128)(2,1)S(1)} collective-permute-done((bf16[256,2048]{1,0:T(8,128)(2,1)}, bf16[256,2048]{1,0:T(8,128)(2,1)S(1)}, u32[]{:S(2)}, u32[]{:S(2)}) %collective-permute-start.12) | collective-permute-done | bytes 1048608 | tf_op jit(solution)/shard_map/ppermute | solution.py:391
  157.3 3.8 %merge_parts.1.refs_0_.hidden_ref = bf16[128,2048]{1,0:T(8,128)(2,1)} custom-call(s32[1,4]{1,0:T(1,128)} %lengths_ref.5, s32[1,4]{1,0:T(1,128)} %groups_ref.3, bf16[4,8,72,256]{3,2,1,0:T(8,128)(2,1)} %bitcast.5.arrived_ref, f32[128,2048]{1,0:T(8,128)} %get-tuple-element.49.own_mixed_ref, f32[128,128]{1,0:T(8,128)} %get-tuple-element.50.own_top_ref, ...), custom_call_target="tpu_custom_call" | custom-call | tf_op jit(solution)/shard_map/merge_parts/pallas_call | solution.py:365
  167.4 8.6 %feed_forward.4.own_ref = bf16[128,2048]{1,0:T(8,128)(2,1)} custom-call(bf16[128,2048]{1,0:T(8,128)(2,1)} %merge_parts.1.refs_0_.hidden_ref, bf16[2064,256]{1,0:T(8,128)(2,1)} %copy-done, bf16[2064,256]{1,0:T(8,128)(2,1)} %copy-done.1, bf16[2064,256]{1,0:T(8,128)(2,1)} %copy-done.2, bf16[2064,256]{1,0:T(8,128)(2,1)} %collective-permute-done.4.refs_4_, ...), custom_call_target="tpu_custom_call" | custom-call | flops 2147483648 | bytes 16777216 | tf_op jit(solution)/shard_map/feed_forward/pallas_call | solution.py:434
  176.8 8.6 %feed_forward.5 = bf16[128,2048]{1,0:T(8,128)(2,1)} custom-call(bf16[128,2048]{1,0:T(8,128)(2,1)} %copy-done.14, bf16[2064,256]{1,0:T(8,128)(2,1)} %copy-done, bf16[2064,256]{1,0:T(8,128)(2,1)} %copy-done.1, bf16[2064,256]{1,0:T(8,128)(2,1)} %copy-done.2, bf16[2064,256]{1,0:T(8,128)(2,1)} %collective-permute-done.4.refs_4_, bf16[2064,256]{1,0:T(8,128)(2,1)} %copy-done.3, ...), custom_call_target="tpu_custom_call" | custom-call | flops 2147483648 | bytes 16777216 | tf_op jit(solution)/shard_map/feed_forward/pallas_call | solution.py:434
  185.5 3.2 %collective-permute-done.6.refs_0_ = bf16[128,2048]{1,0:T(8,128)(2,1)S(1)} collective-permute-done((bf16[128,2048]{1,0:T(8,128)(2,1)}, bf16[128,2048]{1,0:T(8,128)(2,1)S(1)}, u32[]{:S(2)}, u32[]{:S(2)}) %collective-permute-start.6) | collective-permute-done | bytes 524320 | tf_op jit(solution)/shard_map/ppermute | solution.py:391
  189.4 8.8 %feed_forward.6.here_ref = bf16[128,2048]{1,0:T(8,128)(2,1)} custom-call(bf16[128,2048]{1,0:T(8,128)(2,1)} %copy-done.12, bf16[2064,256]{1,0:T(8,128)(2,1)} %copy-done, bf16[2064,256]{1,0:T(8,128)(2,1)} %copy-done.1, bf16[2064,256]{1,0:T(8,128)(2,1)} %copy-done.2, bf16[2064,256]{1,0:T(8,128)(2,1)} %collective-permute-done.4.refs_4_, ...), custom_call_target="tpu_custom_call" | custom-call | flops 2147483648 | bytes 16777216 | tf_op jit(solution)/shard_map/feed_forward/pallas_call | solution.py:434
  198.3 4.2 %collective-permute-done.17.refs_0_ = bf16[128,2048]{1,0:T(8,128)(2,1)S(1)} collective-permute-done((bf16[128,2048]{1,0:T(8,128)(2,1)S(1)}, bf16[128,2048]{1,0:T(8,128)(2,1)S(1)}, u32[]{:S(2)}, u32[]{:S(2)}) %collective-permute-start.17) | collective-permute-done | bytes 524320 | tf_op jit(solution)/shard_map/ppermute | solution.py:391
  203.3 8.6 %feed_forward.7 = bf16[128,2048]{1,0:T(8,128)(2,1)} custom-call(bf16[128,2048]{1,0:T(8,128)(2,1)} %copy-done.15, bf16[2064,256]{1,0:T(8,128)(2,1)} %copy-done, bf16[2064,256]{1,0:T(8,128)(2,1)} %copy-done.1, bf16[2064,256]{1,0:T(8,128)(2,1)} %copy-done.2, bf16[2064,256]{1,0:T(8,128)(2,1)} %collective-permute-done.4.refs_4_, bf16[2064,256]{1,0:T(8,128)(2,1)} %copy-done.3, ...), custom_call_target="tpu_custom_call" | custom-call | flops 2147483648 | bytes 16777216 | tf_op jit(solution)/shard_map/feed_forward/pallas_call | solution.py:434
  214.0 13.0 %collective-permute-done.18.there_ref = bf16[128,2048]{1,0:T(8,128)(2,1)S(1)} collective-permute-done((bf16[128,2048]{1,0:T(8,128)(2,1)}, bf16[128,2048]{1,0:T(8,128)(2,1)S(1)}, u32[]{:S(2)}, u32[]{:S(2)}) %collective-permute-start.18) | collective-permute-done | bytes 524320 | tf_op jit(solution)/shard_map/ppermute | solution.py:391
  230.0 6.4 %collective-permute-done.16.near_ref = bf16[128,2048]{1,0:T(8,128)(2,1)S(1)} collective-permute-done((bf16[128,2048]{1,0:T(8,128)(2,1)S(1)}, bf16[128,2048]{1,0:T(8,128)(2,1)S(1)}, u32[]{:S(2)}, u32[]{:S(2)}) %collective-permute-start.16) | collective-permute-done | bytes 524320 | tf_op jit(solution)/shard_map/ppermute | solution.py:391
  236.4 12.7 %collective-permute-done.19.far_ref = bf16[128,2048]{1,0:T(8,128)(2,1)S(1)} collective-permute-done((bf16[128,2048]{1,0:T(8,128)(2,1)}, bf16[128,2048]{1,0:T(8,128)(2,1)S(1)}, u32[]{:S(2)}, u32[]{:S(2)}) %collective-permute-start.19) | collective-permute-done | bytes 524320 | tf_op jit(solution)/shard_map/ppermute | solution.py:391
  249.9 3.0 %finish_rows.1 = bf16[128,2048]{1,0:T(8,128)(2,1)} custom-call(bf16[128,2048]{1,0:T(8,128)(2,1)} %merge_parts.1.refs_0_.hidden_ref, bf16[128,2048]{1,0:T(8,128)(2,1)} %feed_forward.4.own_ref, bf16[128,2048]{1,0:T(8,128)(2,1)} %copy-done.13, bf16[128,2048]{1,0:T(8,128)(2,1)} %copy-done.16, f32[1,2048]{1,0:T(1,128)} %bitcast.18, f32[1,2048]{1,0:T(1,128)} %bitcast.19, ...), custom_call_target="tpu_custom_call" | custom-call | tf_op jit(solution)/shard_map/finish_rows/pallas_call | solution.py:482
  (75 shorter events, 34.4 us)
Async XLA Ops:
  2.3 51.8 %all-to-all-start = ((bf16[32,72,256]{2,1,0:T(8,128)(2,1)}), bf16[32,72,256]{2,1,0:T(8,128)(2,1)}, u32[]{:S(2)}, u32[]{:S(2)}) async-start(bf16[32,72,256]{2,1,0:T(8,128)(2,1)} %bitcast.14), calls=%async_computation | async-start | bytes 2359296 | tf_op jit(solution)/shard_map/all_to_all | solution.py:538
  9.9 137.1 %copy-start = (bf16[2064,256]{1,0:T(8,128)(2,1)}, bf16[2064,256]{1,0:T(8,128)(2,1)S(1)}, u32[]{:S(2)}) copy-start(bf16[2064,256]{1,0:T(8,128)(2,1)S(1)} %pad_maximum_fusion.refs_1_) | copy-start | bytes 3170308
  9.9 37.9 %collective-permute-start = (bf16[2064,256]{1,0:T(8,128)(2,1)S(1)}, bf16[2064,256]{1,0:T(8,128)(2,1)S(1)}, u32[]{:S(2)}, u32[]{:S(2)}) collective-permute-start(bf16[2064,256]{1,0:T(8,128)(2,1)S(1)} %pad_maximum_fusion.refs_1_), channel_id=1, source_target_pairs={{0,1},{1,0},{2,3},{3,2},{4,5},{5,4},{6,7},{7,6},{8,9},{9,8},{10,11... | collective-permute-start | bytes 3170312 | tf_op jit(solution)/shard_map/ppermute | solution.py:391
  11.6 42.5 %collective-permute-start.1 = (bf16[2064,256]{1,0:T(8,128)(2,1)S(1)}, bf16[2064,256]{1,0:T(8,128)(2,1)S(1)}, u32[]{:S(2)}, u32[]{:S(2)}) collective-permute-start(bf16[2064,256]{1,0:T(8,128)(2,1)S(1)} %pad_maximum_fusion.refs_1_), channel_id=1, source_target_pairs={{0,2},{1,3},{2,0},{3,1},{4,6},{5,7},{6,4},{7,5},{8,10},{9,11},{10,... | collective-permute-start | bytes 3170312 | tf_op jit(solution)/shard_map/ppermute | solution.py:391
  47.8 101.0 %copy-start.1 = (bf16[2064,256]{1,0:T(8,128)(2,1)}, bf16[2064,256]{1,0:T(8,128)(2,1)S(1)}, u32[]{:S(2)}) copy-start(bf16[2064,256]{1,0:T(8,128)(2,1)S(1)} %collective-permute-done.refs_2_) | copy-start | bytes 3170308
  54.1 43.5 %collective-permute-start.2 = (bf16[256,2048]{1,0:T(8,128)(2,1)}, bf16[256,2048]{1,0:T(8,128)(2,1)}, u32[]{:S(2)}, u32[]{:S(2)}) collective-permute-start(bf16[256,2048]{1,0:T(8,128)(2,1)} %refs_9_.3), channel_id=1, source_target_pairs={{0,1},{1,0},{2,3},{3,2},{4,5},{5,4},{6,7},{7,6},{8,9},{9,8},{10,11... | collective-permute-start | bytes 3145736 | tf_op jit(solution)/shard_map/ppermute | solution.py:391
  55.6 42.1 %collective-permute-start.3 = (bf16[256,2048]{1,0:T(8,128)(2,1)}, bf16[256,2048]{1,0:T(8,128)(2,1)}, u32[]{:S(2)}, u32[]{:S(2)}) collective-permute-start(bf16[256,2048]{1,0:T(8,128)(2,1)} %refs_9_.3), channel_id=1, source_target_pairs={{0,2},{1,3},{2,0},{3,1},{4,6},{5,7},{6,4},{7,5},{8,10},{9,11},{10,... | collective-permute-start | bytes 3145736 | tf_op jit(solution)/shard_map/ppermute | solution.py:391
  97.7 48.3 %all-to-all-start.1 = ((bf16[32,72,256]{2,1,0:T(8,128)(2,1)}), bf16[32,72,256]{2,1,0:T(8,128)(2,1)}, u32[]{:S(2)}, u32[]{:S(2)}) async-start(bf16[32,72,256]{2,1,0:T(8,128)(2,1)} %attend_prefix.1), calls=%async_computation.1 | async-start | bytes 2359296 | tf_op jit(solution)/shard_map/all_to_all | solution.py:558
  101.6 44.3 %collective-permute-start.4 = (bf16[2064,256]{1,0:T(8,128)(2,1)S(1)}, bf16[2064,256]{1,0:T(8,128)(2,1)}, u32[]{:S(2)}, u32[]{:S(2)}) collective-permute-start(bf16[2064,256]{1,0:T(8,128)(2,1)S(1)} %collective-permute-done.refs_2_), channel_id=1, source_target_pairs={{0,2},{1,3},{2,0},{3,1},{4,6},{5,7},{6,4},{7,5},{8,10},{9,11},{10,... | collective-permute-start | bytes 3170312 | tf_op jit(solution)/shard_map/ppermute | solution.py:391
  103.4 36.0 %collective-permute-start.5 = (bf16[256,2048]{1,0:T(8,128)(2,1)}, bf16[256,2048]{1,0:T(8,128)(2,1)}, u32[]{:S(2)}, u32[]{:S(2)}) collective-permute-start(bf16[256,2048]{1,0:T(8,128)(2,1)} %collective-permute-done.3.refs_11_), channel_id=1, source_target_pairs={{0,1},{1,0},{2,3},{3,2},{4,5},{5,4},{6,7},{7,6},{8,9},{9,8},{10,11... | collective-permute-start | bytes 3145736 | tf_op jit(solution)/shard_map/ppermute | solution.py:391
  145.9 2.9 %collective-permute-start.11 = (bf16[256,2048]{1,0:T(8,128)(2,1)}, bf16[256,2048]{1,0:T(8,128)(2,1)S(1)}, u32[]{:S(2)}, u32[]{:S(2)}) collective-permute-start(bf16[256,2048]{1,0:T(8,128)(2,1)} %refs_9_.3), channel_id=1, source_target_pairs={{0,8},{1,9},{2,10},{3,11},{4,12},{5,13},{6,14},{7,15},{8,0},{9,1},... | collective-permute-start | bytes 3145736 | tf_op jit(solution)/shard_map/ppermute | solution.py:391
  145.9 7.4 %collective-permute-start.12 = (bf16[256,2048]{1,0:T(8,128)(2,1)}, bf16[256,2048]{1,0:T(8,128)(2,1)S(1)}, u32[]{:S(2)}, u32[]{:S(2)}) collective-permute-start(bf16[256,2048]{1,0:T(8,128)(2,1)} %collective-permute-done.2.refs_10_), channel_id=1, source_target_pairs={{0,8},{1,9},{2,10},{3,11},{4,12},{5,13},{6,14},{7,15},{8,0},{9,1},... | collective-permute-start | bytes 3145736 | tf_op jit(solution)/shard_map/ppermute | solution.py:391
  146.4 9.9 %collective-permute-start.13 = (bf16[256,2048]{1,0:T(8,128)(2,1)}, bf16[256,2048]{1,0:T(8,128)(2,1)S(1)}, u32[]{:S(2)}, u32[]{:S(2)}) collective-permute-start(bf16[256,2048]{1,0:T(8,128)(2,1)} %collective-permute-done.3.refs_11_), channel_id=1, source_target_pairs={{0,8},{1,9},{2,10},{3,11},{4,12},{5,13},{6,14},{7,15},{8,0},{9,1},... | collective-permute-start | bytes 3145736 | tf_op jit(solution)/shard_map/ppermute | solution.py:391
  146.4 14.7 %collective-permute-start.14 = (bf16[256,2048]{1,0:T(8,128)(2,1)}, bf16[256,2048]{1,0:T(8,128)(2,1)}, u32[]{:S(2)}, u32[]{:S(2)}) collective-permute-start(bf16[256,2048]{1,0:T(8,128)(2,1)} %collective-permute-done.5.refs_12_), channel_id=1, source_target_pairs={{0,8},{1,9},{2,10},{3,11},{4,12},{5,13},{6,14},{7,15},{8,0},{9,1},... | collective-permute-start | bytes 3145736 | tf_op jit(solution)/shard_map/ppermute | solution.py:391
  147.0 15.6 %collective-permute-start.7 = (bf16[2064,256]{1,0:T(8,128)(2,1)S(1)}, bf16[2064,256]{1,0:T(8,128)(2,1)S(1)}, u32[]{:S(2)}, u32[]{:S(2)}) collective-permute-start(bf16[2064,256]{1,0:T(8,128)(2,1)S(1)} %pad_maximum_fusion.refs_1_), channel_id=1, source_target_pairs={{0,8},{1,9},{2,10},{3,11},{4,12},{5,13},{6,14},{7,15},{8,0},{9,1},... | collective-permute-start | bytes 3170312 | tf_op jit(solution)/shard_map/ppermute | solution.py:391
  148.8 16.3 %collective-permute-start.8 = (bf16[2064,256]{1,0:T(8,128)(2,1)S(1)}, bf16[2064,256]{1,0:T(8,128)(2,1)S(1)}, u32[]{:S(2)}, u32[]{:S(2)}) collective-permute-start(bf16[2064,256]{1,0:T(8,128)(2,1)S(1)} %collective-permute-done.refs_2_), channel_id=1, source_target_pairs={{0,8},{1,9},{2,10},{3,11},{4,12},{5,13},{6,14},{7,15},{8,0},{9,1},... | collective-permute-start | bytes 3170312 | tf_op jit(solution)/shard_map/ppermute | solution.py:391
  153.3 11.8 %collective-permute-start.9 = (bf16[2064,256]{1,0:T(8,128)(2,1)S(1)}, bf16[2064,256]{1,0:T(8,128)(2,1)S(1)}, u32[]{:S(2)}, u32[]{:S(2)}) collective-permute-start(bf16[2064,256]{1,0:T(8,128)(2,1)S(1)} %collective-permute-done.1.refs_3_), channel_id=1, source_target_pairs={{0,8},{1,9},{2,10},{3,11},{4,12},{5,13},{6,14},{7,15},{8,0},{9,1},... | collective-permute-start | bytes 3170312 | tf_op jit(solution)/shard_map/ppermute | solution.py:391
  156.3 8.8 %collective-permute-start.10 = (bf16[2064,256]{1,0:T(8,128)(2,1)}, bf16[2064,256]{1,0:T(8,128)(2,1)S(1)}, u32[]{:S(2)}, u32[]{:S(2)}) collective-permute-start(bf16[2064,256]{1,0:T(8,128)(2,1)} %collective-permute-done.4.refs_4_), channel_id=1, source_target_pairs={{0,8},{1,9},{2,10},{3,11},{4,12},{5,13},{6,14},{7,15},{8,0},{9,1},... | collective-permute-start | bytes 3170312 | tf_op jit(solution)/shard_map/ppermute | solution.py:391
  161.1 14.9 %collective-permute-start.15 = (bf16[128,2048]{1,0:T(8,128)(2,1)}, bf16[128,2048]{1,0:T(8,128)(2,1)S(1)}, u32[]{:S(2)}, u32[]{:S(2)}) collective-permute-start(bf16[128,2048]{1,0:T(8,128)(2,1)} %merge_parts.1.refs_0_.hidden_ref), channel_id=1, source_target_pairs={{0,16},{1,17},{2,18},{3,19},{4,20},{5,21},{6,22},{7,23},{8,24},{9,... | collective-permute-start | bytes 1572872 | tf_op jit(solution)/shard_map/ppermute | solution.py:391
  162.6 26.0 %collective-permute-start.6 = (bf16[128,2048]{1,0:T(8,128)(2,1)}, bf16[128,2048]{1,0:T(8,128)(2,1)S(1)}, u32[]{:S(2)}, u32[]{:S(2)}) collective-permute-start(bf16[128,2048]{1,0:T(8,128)(2,1)} %merge_parts.1.refs_0_.hidden_ref), channel_id=1, source_target_pairs={{0,4},{1,5},{2,6},{3,7},{4,0},{5,1},{6,2},{7,3},{8,12},{9,13},{10,... | collective-permute-start | bytes 1572872 | tf_op jit(solution)/shard_map/ppermute | solution.py:391
  188.6 13.8 %collective-permute-start.17 = (bf16[128,2048]{1,0:T(8,128)(2,1)S(1)}, bf16[128,2048]{1,0:T(8,128)(2,1)S(1)}, u32[]{:S(2)}, u32[]{:S(2)}) collective-permute-start(bf16[128,2048]{1,0:T(8,128)(2,1)S(1)} %collective-permute-done.6.refs_0_), channel_id=1, source_target_pairs={{0,16},{1,17},{2,18},{3,19},{4,20},{5,21},{6,22},{7,23},{8,24},{9,... | collective-permute-start | bytes 1572872 | tf_op jit(solution)/shard_map/ppermute | solution.py:391
  211.9 15.1 %collective-permute-start.18 = (bf16[128,2048]{1,0:T(8,128)(2,1)}, bf16[128,2048]{1,0:T(8,128)(2,1)S(1)}, u32[]{:S(2)}, u32[]{:S(2)}) collective-permute-start(bf16[128,2048]{1,0:T(8,128)(2,1)} %feed_forward.7), channel_id=1, source_target_pairs={{0,16},{1,17},{2,18},{3,19},{4,20},{5,21},{6,22},{7,23},{8,24},{9,... | collective-permute-start | bytes 1572872 | tf_op jit(solution)/shard_map/ppermute | solution.py:391
  212.3 24.1 %collective-permute-start.16 = (bf16[128,2048]{1,0:T(8,128)(2,1)S(1)}, bf16[128,2048]{1,0:T(8,128)(2,1)S(1)}, u32[]{:S(2)}, u32[]{:S(2)}) collective-permute-start(bf16[128,2048]{1,0:T(8,128)(2,1)S(1)} %copy-done.11), channel_id=1, source_target_pairs={{0,16},{1,17},{2,18},{3,19},{4,20},{5,21},{6,22},{7,23},{8,24},{9,... | collective-permute-start | bytes 1572872 | tf_op jit(solution)/shard_map/ppermute | solution.py:391
  230.0 19.1 %collective-permute-start.19 = (bf16[128,2048]{1,0:T(8,128)(2,1)}, bf16[128,2048]{1,0:T(8,128)(2,1)S(1)}, u32[]{:S(2)}, u32[]{:S(2)}) collective-permute-start(bf16[128,2048]{1,0:T(8,128)(2,1)} %add_rows.1), channel_id=1, source_target_pairs={{0,4},{1,5},{2,6},{3,7},{4,0},{5,1},{6,2},{7,3},{8,12},{9,13},{10,... | collective-permute-start | bytes 1572872 | tf_op jit(solution)/shard_map/ppermute | solution.py:391
  (17 other events, 159.2 us)

commit v4 on v3

--- a/solution.py
+++ b/solution.py
@@ -17,7 +17,7 @@
 norm_eps = 1e-12
 score_scale = HD ** (-0.5)
 log2_e = math.log2(math.e)
-kernel_vmem = 56 * 1024 * 1024
+mebibyte = 1024 * 1024
 
 
 def layer_norm(summed, norm_gain, norm_shift):
@@ -75,7 +75,7 @@
         scratch_shapes=[
             pltpu.VMEM((model_width // LANES, slot_count + capacity, LANES), jnp.float32)
         ],
-        compiler_params=pltpu.CompilerParams(vmem_limit_bytes=kernel_vmem),
+        compiler_params=pltpu.CompilerParams(vmem_limit_bytes=16 * mebibyte),
         name="pack_queries",
     )(lengths, groups, queries)
 
@@ -216,7 +216,7 @@
             pltpu.VMEM((2, ROW_BLOCK, key_total), jnp.float32),
             pltpu.VMEM((2, ROW_BLOCK, LANES), jnp.float32),
         ],
-        compiler_params=pltpu.CompilerParams(vmem_limit_bytes=kernel_vmem),
+        compiler_params=pltpu.CompilerParams(vmem_limit_bytes=40 * mebibyte),
         cost_estimate=pl.CostEstimate(
             flops=4 * sources * capacity * key_total * part_width,
             bytes_accessed=8 * key_total * part_width,
@@ -279,7 +279,7 @@
         out_shape=(jax.ShapeDtypeStruct((slot_count, model_width), jnp.float32), stats, stats),
         in_specs=[smem_spec()] + [vmem_spec()] * 3,
         out_specs=(vmem_spec(), vmem_spec(), vmem_spec()),
-        compiler_params=pltpu.CompilerParams(vmem_limit_bytes=kernel_vmem),
+        compiler_params=pltpu.CompilerParams(vmem_limit_bytes=16 * mebibyte),
         cost_estimate=pl.CostEstimate(
             flops=40 * slot_count * slot_count * model_width,
             bytes_accessed=8 * slot_count * model_width,
@@ -299,7 +299,8 @@
     input_ref,
     gain_ref,
     shift_ref,
-    hidden_ref,
+    first_ref,
+    second_ref,
     far_ref,
     stat_ref,
 ):
@@ -354,24 +355,27 @@
     for head in range(head_count):
         columns = slice(head * HD, (head + 1) * HD)
         centred = far_ref[head, :slot_count, :] - row_mean
-        hidden_ref[:, columns] = (
-            centred * factor * gain_ref[:, columns] + shift_ref[:, columns]
-        ).astype(jnp.bfloat16)
+        hidden = (centred * factor * gain_ref[:, columns] + shift_ref[:, columns]).astype(
+            jnp.bfloat16
+        )
+        first_ref[:, columns] = hidden[: slot_count // 2]
+        second_ref[:, columns] = hidden[slot_count // 2 :]
 
 
 def merge_parts(lengths, groups, arrived, own_mixed, own_top, own_sum, layer_input, gain, shift):
     slot_count, model_width = layer_input.shape
     capacity = arrived.shape[2] - STAT_ROWS
+    half = jax.ShapeDtypeStruct((slot_count // 2, model_width), jnp.bfloat16)
     return pl.pallas_call(
         merge_kernel,
-        out_shape=jax.ShapeDtypeStruct((slot_count, model_width), jnp.bfloat16),
+        out_shape=(half, half),
         in_specs=[smem_spec(), smem_spec()] + [vmem_spec()] * 7,
-        out_specs=vmem_spec(),
+        out_specs=(vmem_spec(), vmem_spec()),
         scratch_shapes=[
             pltpu.VMEM((model_width // HD, slot_count + capacity, HD), jnp.float32),
             pltpu.VMEM((slot_count + capacity, LANES), jnp.float32),
         ],
-        compiler_params=pltpu.CompilerParams(vmem_limit_bytes=kernel_vmem),
+        compiler_params=pltpu.CompilerParams(vmem_limit_bytes=16 * mebibyte),
         name="merge_parts",
     )(
         lengths,
@@ -400,55 +404,76 @@
     return held
 
 
-def mlp_kernel(parts, *refs):
-    rows_ref, refs = refs[0], refs[1:]
-    ups, downs = refs[:parts], refs[parts : 2 * parts]
-    out_ref, up_ref, down_ref, sems = refs[2 * parts :]
-    model_width = rows_ref.shape[1]
-    copies = []
+def tie(values, after):
+    return lax.optimization_barrier((values, after))[0]
+
+
+def mlp_kernel(pieces, parts, *refs):
+    row_refs, refs = refs[:pieces], refs[pieces:]
+    ups, refs = refs[:parts], refs[parts:]
+    downs, refs = refs[:parts], refs[parts:]
+    out_refs, (up_ref, down_ref, sems) = refs[:pieces], refs[pieces:]
+    model_width = row_refs[0].shape[1]
+    units = downs[0].shape[0]
+    up_copies = [
+        pltpu.make_async_copy(ups[part], up_ref.at[part], sems.at[part, 0])
+        for part in range(parts)
+    ]
+    down_copies = [
+        pltpu.make_async_copy(
+            downs[part], down_ref.at[pl.ds(part * units, units)], sems.at[part, 1]
+        )
+        for part in range(parts)
+    ]
+    copies = up_copies + down_copies
+    ahead = 4
+    for copy in copies[:ahead]:
+        copy.start()
+    rows = jnp.concatenate([ref[...] for ref in row_refs], axis=0)
+    activations = []
     for part in range(parts):
-        up_copy = pltpu.make_async_copy(ups[part], up_ref.at[part], sems.at[part, 0])
-        down_copy = pltpu.make_async_copy(downs[part], down_ref.at[part], sems.at[part, 1])
-        up_copy.start()
-        down_copy.start()
-        copies.append((up_copy, down_copy))
-    rows = rows_ref[...]
-    total = None
-    for part in range(parts):
-        copies[part][0].wait()
+        copies[part].wait()
+        if part + ahead < len(copies):
+            copies[part + ahead].start()
         product = jnp.dot(
             rows, up_ref[part, :model_width, :], preferred_element_type=jnp.float32
         )
         offset = up_ref[part, model_width:, :].astype(jnp.float32)[0:1]
-        activation = jax.nn.gelu(product + offset, approximate=True).astype(jnp.bfloat16)
-        copies[part][1].wait()
-        term = jnp.dot(activation, down_ref[part], preferred_element_type=jnp.float32)
-        total = term if total is None else total + term
-    out_ref[...] = total.astype(jnp.bfloat16)
+        activations.append(jax.nn.gelu(product + offset, approximate=True).astype(jnp.bfloat16))
+    for part in range(parts, 2 * parts):
+        copies[part].wait()
+        if part + ahead < len(copies):
+            copies[part + ahead].start()
+    total = jnp.dot(
+        jnp.concatenate(activations, axis=1), down_ref[...], preferred_element_type=jnp.float32
+    ).astype(jnp.bfloat16)
+    height = row_refs[0].shape[0]
+    for piece in range(pieces):
+        out_refs[piece][...] = total[piece * height : (piece + 1) * height]
 
 
 def feed_forward(rows, ups, downs):
-    parts = len(ups)
-    row_count, model_width = rows.shape
+    pieces, parts = len(rows), len(ups)
+    height, model_width = rows[0].shape
     up_rows, units = ups[0].shape
     return pl.pallas_call(
-        functools.partial(mlp_kernel, parts),
-        out_shape=jax.ShapeDtypeStruct((row_count, model_width), jnp.bfloat16),
-        in_specs=[vmem_spec()] + [pl.BlockSpec(memory_space=pl.ANY)] * (2 * parts),
-        out_specs=vmem_spec(),
+        functools.partial(mlp_kernel, pieces, parts),
+        out_shape=tuple(jax.ShapeDtypeStruct(piece.shape, jnp.bfloat16) for piece in rows),
+        in_specs=[vmem_spec()] * pieces + [pl.BlockSpec(memory_space=pl.ANY)] * (2 * parts),
+        out_specs=tuple(vmem_spec() for _ in rows),
         scratch_shapes=[
             pltpu.VMEM((parts, up_rows, units), jnp.bfloat16),
-            pltpu.VMEM((parts, units, model_width), jnp.bfloat16),
+            pltpu.VMEM((parts * units, model_width), jnp.bfloat16),
             pltpu.SemaphoreType.DMA((parts, 2)),
         ],
-        compiler_params=pltpu.CompilerParams(vmem_limit_bytes=kernel_vmem),
+        compiler_params=pltpu.CompilerParams(vmem_limit_bytes=32 * mebibyte),
         cost_estimate=pl.CostEstimate(
-            flops=4 * row_count * model_width * parts * units,
+            flops=4 * pieces * height * model_width * parts * units,
             bytes_accessed=4 * parts * model_width * units,
-            transcendentals=row_count * parts * units,
+            transcendentals=pieces * height * parts * units,
         ),
         name="feed_forward",
-    )(rows, *ups, *downs)
+    )(*rows, *ups, *downs)
 
 
 def add_kernel(here_ref, there_ref, out_ref):
@@ -467,30 +492,34 @@
     )(here, there)
 
 
-def finish_kernel(hidden_ref, own_ref, near_ref, far_ref, bias_ref, gain_ref, shift_ref, out_ref):
-    summed = hidden_ref[...].astype(jnp.float32) + (
-        own_ref[...].astype(jnp.float32)
-        + near_ref[...].astype(jnp.float32)
-        + far_ref[...].astype(jnp.float32)
-    )
-    summed = summed + bias_ref[...]
-    out_ref[...] = layer_norm(summed, gain_ref[...], shift_ref[...]).astype(jnp.bfloat16)
+def finish_kernel(pieces, *refs):
+    bias_ref, gain_ref, shift_ref, out_ref = refs[4 * pieces :]
+    height = out_ref.shape[0] // pieces
+    for piece in range(pieces):
+        hidden, own, near, far = (
+            refs[kind * pieces + piece][...].astype(jnp.float32) for kind in range(4)
+        )
+        summed = hidden + (own + near + far) + bias_ref[...]
+        out_ref[piece * height : (piece + 1) * height, :] = layer_norm(
+            summed, gain_ref[...], shift_ref[...]
+        ).astype(jnp.bfloat16)
 
 
 def finish_rows(hidden, own, near, far, bias, gain, shift):
-    model_width = hidden.shape[1]
+    pieces = len(hidden)
+    height, model_width = hidden[0].shape
     return pl.pallas_call(
-        finish_kernel,
-        out_shape=jax.ShapeDtypeStruct(hidden.shape, jnp.bfloat16),
-        in_specs=[vmem_spec()] * 7,
+        functools.partial(finish_kernel, pieces),
+        out_shape=jax.ShapeDtypeStruct((pieces * height, model_width), jnp.bfloat16),
+        in_specs=[vmem_spec()] * (4 * pieces + 3),
         out_specs=vmem_spec(),
-        compiler_params=pltpu.CompilerParams(vmem_limit_bytes=kernel_vmem),
+        compiler_params=pltpu.CompilerParams(vmem_limit_bytes=16 * mebibyte),
         name="finish_rows",
     )(
-        hidden,
-        own,
-        near,
-        far,
+        *hidden,
+        *own,
+        *near,
+        *far,
         bias.reshape(1, model_width),
         gain.reshape(1, model_width),
         shift.reshape(1, model_width),
@@ -544,12 +573,17 @@
     )
     for mask in column_masks:
         ups[mask] = swap(ups[0], mask)
-    arrived, ups, downs = lax.optimization_barrier((arrived, ups, downs))
-
-    counts = arrived[:, capacity, 0].astype(jnp.int32)
     turned_keys = prefix_keys[0].T
     value_heads = prefix_values[0].reshape(-1, local_heads, HD).transpose(1, 0, 2)
     wide_values = jnp.concatenate([value_heads, jnp.ones_like(value_heads)], axis=2)
+    own = attend_suffix(
+        suffix_lengths, suffix_queries, suffix_keys, suffix_values, local_heads
+    )
+    arrived, ups, downs, turned_keys, wide_values, own = lax.optimization_barrier(
+        (arrived, ups, downs, turned_keys, wide_values, own)
+    )
+
+    counts = arrived[:, capacity, 0].astype(jnp.int32)
     answer_part = attend_prefix(counts, arrived, turned_keys, wide_values)
     for mask in column_masks:
         downs[mask] = swap(downs[0], mask)
@@ -558,44 +592,49 @@
     answer = lax.all_to_all(
         answer_part, ("grp", "dev"), split_axis=0, concat_axis=0, tiled=True
     ).reshape(group_count, column_count, capacity + STAT_ROWS, part_width)
+    core_mask = group_masks[0]
+    early_ups = {core_mask ^ at: swap(block, core_mask) for at, block in ups.items()}
+    early_downs = {core_mask ^ at: swap(block, core_mask) for at, block in downs.items()}
     ups = complete(ups, column_masks[::-1])
     downs = complete(downs, column_masks)
-    own_mixed, own_top, own_sum = attend_suffix(
-        suffix_lengths, suffix_queries, suffix_keys, suffix_values, local_heads
-    )
-    answer, ups, downs, own_mixed = lax.optimization_barrier((answer, ups, downs, own_mixed))
-
-    hidden_state = merge_parts(
-        suffix_lengths,
-        request_group,
-        answer,
-        own_mixed,
-        own_top,
-        own_sum,
-        layer_input,
-        attn_gain,
-        attn_shift,
-    )
-
-    far_hidden = swap(hidden_state, far_mask)
-    near_hidden = swap(hidden_state, near_mask)
+    ups.update(early_ups)
+    downs.update(early_downs)
+    answer, ups, downs = lax.optimization_barrier((answer, ups, downs))
+
+    hidden = merge_parts(
+        suffix_lengths, request_group, answer, *own, layer_input, attn_gain, attn_shift
+    )
+
+    hidden, ups, downs = lax.optimization_barrier((hidden, ups, downs))
+    far_a = swap(hidden[0], far_mask)
+    near = [swap(piece, near_mask) for piece in hidden]
     ups = complete(ups, group_masks)
     downs = complete(downs, group_masks)
     order = sorted(ups)
     ups = [ups[mask] for mask in order]
     downs = [downs[mask] for mask in order]
-    own_part = feed_forward(hidden_state, ups, downs)
-    near_part = feed_forward(near_hidden, ups, downs)
-    far_hidden, own_part, near_part = lax.optimization_barrier((far_hidden, own_part, near_part))
-    cross_hidden = swap(far_hidden, near_mask)
-    near_sum = swap(near_part, near_mask)
-    far_part = feed_forward(far_hidden, ups, downs)
-    cross_hidden, far_part = lax.optimization_barrier((cross_hidden, far_part))
-    cross_part = feed_forward(cross_hidden, ups, downs)
-    cross_sum = swap(cross_part, near_mask)
-    far_sum = swap(add_rows(far_part, cross_sum), far_mask)
+    own_part = feed_forward(hidden, ups, downs)
+    far_a, own_part = lax.optimization_barrier((far_a, own_part))
+    far_b = swap(tie(hidden[1], far_a), far_mask)
+    cross_a = swap(far_a, near_mask)
+    near_part = feed_forward(tie(near, far_a), ups, downs)
+    far_b, cross_a, near_part = lax.optimization_barrier((far_b, cross_a, near_part))
+    cross_b = swap(far_b, near_mask)
+    far_part_a, cross_part_a = feed_forward([far_a, cross_a], ups, downs)
+    cross_b, far_part_a, cross_part_a = lax.optimization_barrier(
+        (cross_b, far_part_a, cross_part_a)
+    )
+    cross_sum_a = swap(cross_part_a, near_mask)
+    far_part_b, cross_part_b = feed_forward([far_b, cross_b], ups, downs)
+    cross_sum_a, far_part_b, cross_part_b = lax.optimization_barrier(
+        (cross_sum_a, far_part_b, cross_part_b)
+    )
+    cross_sum_b = swap(cross_part_b, near_mask)
+    far_sum_a = swap(add_rows(far_part_a, cross_sum_a), far_mask)
+    near_sum = [swap(piece, near_mask) for piece in tie(near_part, cross_sum_b)]
+    far_sum_b = swap(add_rows(far_part_b, cross_sum_b), far_mask)
     return finish_rows(
-        hidden_state, own_part, near_sum, far_sum, down_bias, out_gain, out_shift
+        hidden, own_part, near_sum, [far_sum_a, far_sum_b], down_bias, out_gain, out_shift
     )
 
 

time: 253 us -> 220 us (0.87)
  waiting for transfers between devices: 124 us -> 77.5 us
  local copies, waits for them, and re-layouts: 23 us -> 44.6 us
  Pallas kernels: 75.4 us -> 60.6 us
  starting transfers between devices: 27.8 us -> 35 us
    ppermute x20 -> x26, waiting for transfers between devices: 124 us -> 77.5 us  [swap(): lax.ppermute(value, ('grp', 'dev'), [(here, here ^ mask) for here in rang...]
    unnamed x40 -> x112, local copies, waits for them, and re-layouts: 15 us -> 36.4 us
    pallas_call x6, Pallas kernels: 41.5 us -> 29.7 us  [the longest x4 25.5 us: feed_forward(): pl.pallas_call(functools.partial(mlp_kernel, pieces, parts), out_shape=tu...]
    ppermute x20 -> x26, starting transfers between devices: 16.4 us -> 23.6 us  [swap(): lax.ppermute(value, ('grp', 'dev'), [(here, here ^ mask) for here in rang...]
  transfers between devices with their start and end apart: 22 -> 28, of which waited for: 12 -> 10; matrix products, arithmetic and copies ran while one was open for 7% -> 8% of each run, Pallas kernels for 24% -> 25%
where the time goes in v4:
time: 220 us
  waiting for transfers between devices  77.5 us (35%)
  Pallas kernels  60.6 us (28%)
  local copies, waits for them, and re-layouts  44.6 us (20%)
  starting transfers between devices  35 us (16%)
    ppermute x26, waiting for transfers between devices, swap(): lax.ppermute(value, ('grp', 'dev'), [(here, here ^ mask) for here in rang...  77.5 us
    unnamed x112, local copies, waits for them, and re-layouts  36.4 us
    pallas_call x4, Pallas kernels, feed_forward(): pl.pallas_call(functools.partial(mlp_kernel, pieces, parts), out_shape=tu...  25.5 us
    ppermute x26, starting transfers between devices, swap(): lax.ppermute(value, ('grp', 'dev'), [(here, here ^ mask) for here in rang...  23.6 us
    pallas_call x1, Pallas kernels, attend_prefix(): pl.pallas_call(far_kernel, out_shape=jax.ShapeDtypeStruct((sources, capac...  20.9 us
    all_to_all x1, starting transfers between devices, on_device(): lax.all_to_all(outgoing.reshape(sources, capacity + STAT_ROWS, part_width...  7.41 us
    pallas_call x1, Pallas kernels, attend_suffix(): pl.pallas_call(functools.partial(own_kernel, local_heads), out_shape=(jax...  4.49 us
  transfers between devices with their start and end apart: 28, of which 10 were waited for; matrix products, arithmetic and copies ran while one was open for 8% of the time, Pallas kernels for 25%

profile of v4, /device:TPU:0, one launch (start us, length us, event | category | flops | bytes accessed | tf_op | source)
XLA Modules:
  0.0 219.7 jit_solution(10412391246175135745)
XLA Ops:
  4.2 7.4 %all-to-all-start = ((bf16[32,72,256]{2,1,0:T(8,128)(2,1)}), bf16[32,72,256]{2,1,0:T(8,128)(2,1)}, u32[]{:S(2)}, u32[]{:S(2)}) async-start(bf16[32,72,256]{2,1,0:T(8,128)(2,1)} %bitcast), calls=%async_computation | async-start | bytes 2359296 | tf_op jit(solution)/shard_map/all_to_all | solution.py:567
  14.9 4.1 %copy.18 = bf16[1,4096,256]{1,2,0:T(8,128)(2,1)} copy(bf16[1,4096,256]{2,1,0:T(8,128)(2,1)} %param.22) | data formatting | bytes 4194304 | tf_op args[6]
  19.1 4.1 %copy.19 = bf16[1,4096,256]{1,2,0:T(8,128)(2,1)} copy(bf16[1,4096,256]{2,1,0:T(8,128)(2,1)} %param.23) | data formatting | bytes 4194304 | tf_op args[7]
  23.2 4.1 %copy.20 = bf16[4096,2,128]{2,0,1:T(8,128)(2,1)} copy(bf16[4096,2,128]{0,2,1:T(8,128)(2,1)} %bitcast.19) | data formatting | bytes 4194304 | tf_op jit(solution)/shard_map/reshape;squeeze | solution.py:577
  27.3 4.1 %concatenate.7.values_ref = bf16[2,4096,256]{2,1,0:T(8,128)(2,1)} pad(bf16[2,4096,128]{2,1,0:T(8,128)(2,1)} %bitcast.18, bf16[]{:T(256)} %constant.0.clone.1), padding=0_0x0_0x0_128 | pad | bytes 6291458 | tf_op jit(solution)/shard_map/concatenate | solution.py:578
  31.4 4.5 %attend_suffix.1 = (f32[128,2048]{1,0:T(8,128)S(1)}, f32[128,128]{1,0:T(8,128)S(1)}, f32[128,128]{1,0:T(8,128)S(1)}) custom-call(s32[1,4]{1,0:T(1,128)S(1)} %copy-done.44, bf16[128,2048]{1,0:T(8,128)(2,1)S(1)} %copy-done.28, bf16[128,2048]{1,0:T(8,128)(2,1)S(1)} %copy-done.47, bf16[128,2048]{1,0:T(8,128)(2,1)S(1)} %copy-done.48), custom_call_target="tpu_custom_call" | custom-call | flops 1342177280 | bytes 2097152 | tf_op jit(solution)/shard_map/attend_suffix/pallas_call | solution.py:277
  37.5 18.5 %collective-permute-done.1.refs_4_ = bf16[2064,256]{1,0:T(8,128)(2,1)S(1)} collective-permute-done((bf16[2064,256]{1,0:T(8,128)(2,1)S(1)}, bf16[2064,256]{1,0:T(8,128)(2,1)S(1)}, u32[]{:S(2)}, u32[]{:S(2)}) %collective-permute-start.1) | collective-permute-done | bytes 1056800 | tf_op jit(solution)/shard_map/ppermute | solution.py:395
  59.5 2.2 copy-done.20
  63.3 20.9 %attend_prefix.1 = bf16[32,72,256]{2,1,0:T(8,128)(2,1)S(1)} custom-call(s32[32]{0:T(128)S(1)} %convert_reduce_fusion.counts_ref, bf16[32,72,256]{2,1,0:T(8,128)(2,1)} %all-to-all-done.arrived_ref, bf16[256,4096]{1,0:T(8,128)(2,1)S(1)} %bitcast.12, bf16[2,4096,256]{2,1,0:T(8,128)(2,1)S(1)} %copy-done.20), custom_call_target="tpu_custom_call" | custom-call | flops 8589934592 | bytes 8388608 | tf_op jit(solution)/shard_map/attend_prefix/pallas_call | solution.py:207
  85.3 4.0 %all-to-all-start.1 = ((bf16[32,72,256]{2,1,0:T(8,128)(2,1)}), bf16[32,72,256]{2,1,0:T(8,128)(2,1)}, u32[]{:S(2)}, u32[]{:S(2)}) async-start(bf16[32,72,256]{2,1,0:T(8,128)(2,1)} %copy-done.22), calls=%async_computation.1 | async-start | bytes 2359296 | tf_op jit(solution)/shard_map/all_to_all | solution.py:592
  93.4 1.9 collective-permute-done.10.refs_15_
  100.8 27.1 %collective-permute-done.8.refs_13_ = bf16[256,2048]{1,0:T(8,128)(2,1)S(1)} collective-permute-done((bf16[256,2048]{1,0:T(8,128)(2,1)}, bf16[256,2048]{1,0:T(8,128)(2,1)S(1)}, u32[]{:S(2)}, u32[]{:S(2)}) %collective-permute-start.8) | collective-permute-done | bytes 1048608 | tf_op jit(solution)/shard_map/ppermute | solution.py:395
  130.9 2.6 %collective-permute-done.4.refs_5_ = bf16[2064,256]{1,0:T(8,128)(2,1)} collective-permute-done((bf16[2064,256]{1,0:T(8,128)(2,1)S(1)}, bf16[2064,256]{1,0:T(8,128)(2,1)}, u32[]{:S(2)}, u32[]{:S(2)}) %collective-permute-start.4) | collective-permute-done | bytes 1056800 | tf_op jit(solution)/shard_map/ppermute | solution.py:395
  136.7 2.7 %merge_parts.1 = (bf16[64,2048]{1,0:T(8,128)(2,1)S(1)}, bf16[64,2048]{1,0:T(8,128)(2,1)S(1)}) custom-call(s32[1,4]{1,0:T(1,128)S(1)} %copy-done.44, s32[1,4]{1,0:T(1,128)S(1)} %copy-done.46, bf16[4,8,72,256]{3,2,1,0:T(8,128)(2,1)} %bitcast.5.arrived_ref, f32[128,2048]{1,0:T(8,128)S(1)} %copy-done.26, f32[128,128]{1,0:T(8,128)S(1)} %get-tuple-element.103.own_top_ref, ...), custom_call_target="tpu_custom_call" | custom-call | tf_op jit(solution)/shard_map/merge_parts/pallas_call | solution.py:369
  140.1 2.5 %collective-permute-start.12 = (bf16[64,2048]{1,0:T(8,128)(2,1)S(1)}, bf16[64,2048]{1,0:T(8,128)(2,1)S(1)}, u32[]{:S(2)}, u32[]{:S(2)}) collective-permute-start(bf16[64,2048]{1,0:T(8,128)(2,1)S(1)} %get-tuple-element.121.refs_0_), channel_id=1, source_target_pairs={{0,4},{1,5},{2,6},{3,7},{4,0},{5,1},{6,2},{7,3},{8,12},{9,13},{10,... | collective-permute-start | bytes 786440 | tf_op jit(solution)/shard_map/ppermute | solution.py:395
  151.9 6.2 %feed_forward.4 = (bf16[64,2048]{1,0:T(8,128)(2,1)S(1)}, bf16[64,2048]{1,0:T(8,128)(2,1)S(1)}) custom-call(bf16[64,2048]{1,0:T(8,128)(2,1)S(1)} %get-tuple-element.121.refs_0_, bf16[64,2048]{1,0:T(8,128)(2,1)S(1)} %get-tuple-element.142.refs_1_, bf16[2064,256]{1,0:T(8,128)(2,1)S(1)} %pad_maximum_fusion.refs_2_, ...), custom_call_target="tpu_custom_call" | custom-call | flops 2147483648 | bytes 16777216 | tf_op jit(solution)/shard_map/feed_forward/pallas_call | solution.py:459
  158.9 1.9 collective-permute-start.15
  162.3 6.2 %feed_forward.5 = (bf16[64,2048]{1,0:T(8,128)(2,1)S(1)}, bf16[64,2048]{1,0:T(8,128)(2,1)S(1)}) custom-call(bf16[64,2048]{1,0:T(8,128)(2,1)S(1)} %collective-permute-done.17.refs_0_, bf16[64,2048]{1,0:T(8,128)(2,1)S(1)} %collective-permute-done.18.refs_1_, bf16[2064,256]{1,0:T(8,128)(2,1)S(1)} %pad_maximum_fusion.refs_2_, ...), custom_call_target="tpu_custom_call" | custom-call | flops 2147483648 | bytes 16777216 | tf_op jit(solution)/shard_map/feed_forward/pallas_call | solution.py:459
  168.6 4.6 %collective-permute-done.15.refs_0_ = bf16[64,2048]{1,0:T(8,128)(2,1)S(1)} collective-permute-done((bf16[64,2048]{1,0:T(8,128)(2,1)S(1)}, bf16[64,2048]{1,0:T(8,128)(2,1)S(1)}, u32[]{:S(2)}, u32[]{:S(2)}) %collective-permute-start.15) | collective-permute-done | bytes 262176 | tf_op jit(solution)/shard_map/ppermute | solution.py:395
  174.6 6.2 %feed_forward.6 = (bf16[64,2048]{1,0:T(8,128)(2,1)S(1)}, bf16[64,2048]{1,0:T(8,128)(2,1)S(1)}) custom-call(bf16[64,2048]{1,0:T(8,128)(2,1)S(1)} %collective-permute-done.12.refs_0_, bf16[64,2048]{1,0:T(8,128)(2,1)S(1)} %collective-permute-done.16.refs_1_, bf16[2064,256]{1,0:T(8,128)(2,1)S(1)} %pad_maximum_fusion.refs_2_, ...), custom_call_target="tpu_custom_call" | custom-call | flops 2147483648 | bytes 16777216 | tf_op jit(solution)/shard_map/feed_forward/pallas_call | solution.py:459
  182.3 6.9 %feed_forward.7 = (bf16[64,2048]{1,0:T(8,128)(2,1)S(1)}, bf16[64,2048]{1,0:T(8,128)(2,1)}) custom-call(bf16[64,2048]{1,0:T(8,128)(2,1)S(1)} %collective-permute-done.15.refs_0_, bf16[64,2048]{1,0:T(8,128)(2,1)S(1)} %collective-permute-done.19.refs_1_, bf16[2064,256]{1,0:T(8,128)(2,1)S(1)} %pad_maximum_fusion.refs_2_, ...), custom_call_target="tpu_custom_call" | custom-call | flops 2147483648 | bytes 16777216 | tf_op jit(solution)/shard_map/feed_forward/pallas_call | solution.py:459
  193.8 4.0 %collective-permute-done.21.there_ref = bf16[64,2048]{1,0:T(8,128)(2,1)S(1)} collective-permute-done((bf16[64,2048]{1,0:T(8,128)(2,1)}, bf16[64,2048]{1,0:T(8,128)(2,1)S(1)}, u32[]{:S(2)}, u32[]{:S(2)}) %collective-permute-start.21) | collective-permute-done | bytes 262176 | tf_op jit(solution)/shard_map/ppermute | solution.py:395
  201.6 11.0 %collective-permute-done.24.refs_6_ = bf16[64,2048]{1,0:T(8,128)(2,1)S(1)} collective-permute-done((bf16[64,2048]{1,0:T(8,128)(2,1)}, bf16[64,2048]{1,0:T(8,128)(2,1)S(1)}, u32[]{:S(2)}, u32[]{:S(2)}) %collective-permute-start.24) | collective-permute-done | bytes 262176 | tf_op jit(solution)/shard_map/ppermute | solution.py:395
  212.6 5.5 %collective-permute-done.25.refs_7_ = bf16[64,2048]{1,0:T(8,128)(2,1)S(1)} collective-permute-done((bf16[64,2048]{1,0:T(8,128)(2,1)}, bf16[64,2048]{1,0:T(8,128)(2,1)S(1)}, u32[]{:S(2)}, u32[]{:S(2)}) %collective-permute-start.25) | collective-permute-done | bytes 262176 | tf_op jit(solution)/shard_map/ppermute | solution.py:395
  (160 shorter events, 56.0 us)
Async XLA Ops:
  4.2 51.8 %all-to-all-start = ((bf16[32,72,256]{2,1,0:T(8,128)(2,1)}), bf16[32,72,256]{2,1,0:T(8,128)(2,1)}, u32[]{:S(2)}, u32[]{:S(2)}) async-start(bf16[32,72,256]{2,1,0:T(8,128)(2,1)} %bitcast), calls=%async_computation | async-start | bytes 2359296 | tf_op jit(solution)/shard_map/all_to_all | solution.py:567
  11.7 44.2 %collective-permute-start.1 = (bf16[2064,256]{1,0:T(8,128)(2,1)S(1)}, bf16[2064,256]{1,0:T(8,128)(2,1)S(1)}, u32[]{:S(2)}, u32[]{:S(2)}) collective-permute-start(bf16[2064,256]{1,0:T(8,128)(2,1)S(1)} %pad_maximum_fusion.refs_2_), channel_id=1, source_target_pairs={{0,2},{1,3},{2,0},{3,1},{4,6},{5,7},{6,4},{7,5},{8,10},{9,11},{10,... | collective-permute-start | bytes 3170312 | tf_op jit(solution)/shard_map/ppermute | solution.py:395
  13.5 42.5 %collective-permute-start = (bf16[2064,256]{1,0:T(8,128)(2,1)S(1)}, bf16[2064,256]{1,0:T(8,128)(2,1)S(1)}, u32[]{:S(2)}, u32[]{:S(2)}) collective-permute-start(bf16[2064,256]{1,0:T(8,128)(2,1)S(1)} %pad_maximum_fusion.refs_2_), channel_id=1, source_target_pairs={{0,1},{1,0},{2,3},{3,2},{4,5},{5,4},{6,7},{7,6},{8,9},{9,8},{10,11... | collective-permute-start | bytes 3170312 | tf_op jit(solution)/shard_map/ppermute | solution.py:395
  56.0 29.3 %collective-permute-start.3 = (bf16[256,2048]{1,0:T(8,128)(2,1)}, bf16[256,2048]{1,0:T(8,128)(2,1)}, u32[]{:S(2)}, u32[]{:S(2)}) collective-permute-start(bf16[256,2048]{1,0:T(8,128)(2,1)} %refs_10_.3), channel_id=1, source_target_pairs={{0,2},{1,3},{2,0},{3,1},{4,6},{5,7},{6,4},{7,5},{8,10},{9,11},{10,... | collective-permute-start | bytes 3145736 | tf_op jit(solution)/shard_map/ppermute | solution.py:395
  56.3 29.0 %collective-permute-start.2 = (bf16[256,2048]{1,0:T(8,128)(2,1)}, bf16[256,2048]{1,0:T(8,128)(2,1)}, u32[]{:S(2)}, u32[]{:S(2)}) collective-permute-start(bf16[256,2048]{1,0:T(8,128)(2,1)} %refs_10_.3), channel_id=1, source_target_pairs={{0,1},{1,0},{2,3},{3,2},{4,5},{5,4},{6,7},{7,6},{8,9},{9,8},{10,11... | collective-permute-start | bytes 3145736 | tf_op jit(solution)/shard_map/ppermute | solution.py:395
  85.3 48.3 %all-to-all-start.1 = ((bf16[32,72,256]{2,1,0:T(8,128)(2,1)}), bf16[32,72,256]{2,1,0:T(8,128)(2,1)}, u32[]{:S(2)}, u32[]{:S(2)}) async-start(bf16[32,72,256]{2,1,0:T(8,128)(2,1)} %copy-done.22), calls=%async_computation.1 | async-start | bytes 2359296 | tf_op jit(solution)/shard_map/all_to_all | solution.py:592
  89.9 8.4 %collective-permute-start.11 = (bf16[256,2048]{1,0:T(8,128)(2,1)}, bf16[256,2048]{1,0:T(8,128)(2,1)S(1)}, u32[]{:S(2)}, u32[]{:S(2)}) collective-permute-start(bf16[256,2048]{1,0:T(8,128)(2,1)} %collective-permute-done.3.refs_12_), channel_id=1, source_target_pairs={{0,8},{1,9},{2,10},{3,11},{4,12},{5,13},{6,14},{7,15},{8,0},{9,1},... | collective-permute-start | bytes 3145736 | tf_op jit(solution)/shard_map/ppermute | solution.py:395
  90.0 37.9 %collective-permute-start.5 = (bf16[2064,256]{1,0:T(8,128)(2,1)S(1)}, bf16[2064,256]{1,0:T(8,128)(2,1)S(1)}, u32[]{:S(2)}, u32[]{:S(2)}) collective-permute-start(bf16[2064,256]{1,0:T(8,128)(2,1)S(1)} %pad_maximum_fusion.refs_2_), channel_id=1, source_target_pairs={{0,8},{1,9},{2,10},{3,11},{4,12},{5,13},{6,14},{7,15},{8,0},{9,1},... | collective-permute-start | bytes 3170312 | tf_op jit(solution)/shard_map/ppermute | solution.py:395
  90.4 38.5 %collective-permute-start.7 = (bf16[2064,256]{1,0:T(8,128)(2,1)S(1)}, bf16[2064,256]{1,0:T(8,128)(2,1)S(1)}, u32[]{:S(2)}, u32[]{:S(2)}) collective-permute-start(bf16[2064,256]{1,0:T(8,128)(2,1)S(1)} %collective-permute-done.1.refs_4_), channel_id=1, source_target_pairs={{0,8},{1,9},{2,10},{3,11},{4,12},{5,13},{6,14},{7,15},{8,0},{9,1},... | collective-permute-start | bytes 3170312 | tf_op jit(solution)/shard_map/ppermute | solution.py:395
  93.2 36.7 %collective-permute-start.6 = (bf16[2064,256]{1,0:T(8,128)(2,1)S(1)}, bf16[2064,256]{1,0:T(8,128)(2,1)S(1)}, u32[]{:S(2)}, u32[]{:S(2)}) collective-permute-start(bf16[2064,256]{1,0:T(8,128)(2,1)S(1)} %collective-permute-done.refs_3_), channel_id=1, source_target_pairs={{0,8},{1,9},{2,10},{3,11},{4,12},{5,13},{6,14},{7,15},{8,0},{9,1},... | collective-permute-start | bytes 3170312 | tf_op jit(solution)/shard_map/ppermute | solution.py:395
  96.2 37.4 %collective-permute-start.4 = (bf16[2064,256]{1,0:T(8,128)(2,1)S(1)}, bf16[2064,256]{1,0:T(8,128)(2,1)}, u32[]{:S(2)}, u32[]{:S(2)}) collective-permute-start(bf16[2064,256]{1,0:T(8,128)(2,1)S(1)} %collective-permute-done.refs_3_), channel_id=1, source_target_pairs={{0,2},{1,3},{2,0},{3,1},{4,6},{5,7},{6,4},{7,5},{8,10},{9,11},{10,... | collective-permute-start | bytes 3170312 | tf_op jit(solution)/shard_map/ppermute | solution.py:395
  99.3 28.6 %collective-permute-start.8 = (bf16[256,2048]{1,0:T(8,128)(2,1)}, bf16[256,2048]{1,0:T(8,128)(2,1)S(1)}, u32[]{:S(2)}, u32[]{:S(2)}) collective-permute-start(bf16[256,2048]{1,0:T(8,128)(2,1)} %collective-permute-done.3.refs_12_), channel_id=1, source_target_pairs={{0,1},{1,0},{2,3},{3,2},{4,5},{5,4},{6,7},{7,6},{8,9},{9,8},{10,11... | collective-permute-start | bytes 3145736 | tf_op jit(solution)/shard_map/ppermute | solution.py:395
  140.1 18.8 %collective-permute-start.12 = (bf16[64,2048]{1,0:T(8,128)(2,1)S(1)}, bf16[64,2048]{1,0:T(8,128)(2,1)S(1)}, u32[]{:S(2)}, u32[]{:S(2)}) collective-permute-start(bf16[64,2048]{1,0:T(8,128)(2,1)S(1)} %get-tuple-element.121.refs_0_), channel_id=1, source_target_pairs={{0,4},{1,5},{2,6},{3,7},{4,0},{5,1},{6,2},{7,3},{8,12},{9,13},{10,... | collective-permute-start | bytes 786440 | tf_op jit(solution)/shard_map/ppermute | solution.py:395
  142.5 19.8 %collective-permute-start.17 = (bf16[64,2048]{1,0:T(8,128)(2,1)S(1)}, bf16[64,2048]{1,0:T(8,128)(2,1)S(1)}, u32[]{:S(2)}, u32[]{:S(2)}) collective-permute-start(bf16[64,2048]{1,0:T(8,128)(2,1)S(1)} %get-tuple-element.121.refs_0_), channel_id=1, source_target_pairs={{0,16},{1,17},{2,18},{3,19},{4,20},{5,21},{6,22},{7,23},{8,24},{9,... | collective-permute-start | bytes 786440 | tf_op jit(solution)/shard_map/ppermute | solution.py:395
  144.0 18.3 %collective-permute-start.18 = (bf16[64,2048]{1,0:T(8,128)(2,1)S(1)}, bf16[64,2048]{1,0:T(8,128)(2,1)S(1)}, u32[]{:S(2)}, u32[]{:S(2)}) collective-permute-start(bf16[64,2048]{1,0:T(8,128)(2,1)S(1)} %get-tuple-element.142.refs_1_), channel_id=1, source_target_pairs={{0,16},{1,17},{2,18},{3,19},{4,20},{5,21},{6,22},{7,23},{8,24},{9,... | collective-permute-start | bytes 786440 | tf_op jit(solution)/shard_map/ppermute | solution.py:395
  158.9 14.3 %collective-permute-start.15 = (bf16[64,2048]{1,0:T(8,128)(2,1)S(1)}, bf16[64,2048]{1,0:T(8,128)(2,1)S(1)}, u32[]{:S(2)}, u32[]{:S(2)}) collective-permute-start(bf16[64,2048]{1,0:T(8,128)(2,1)S(1)} %get-tuple-element.142.refs_1_), channel_id=1, source_target_pairs={{0,4},{1,5},{2,6},{3,7},{4,0},{5,1},{6,2},{7,3},{8,12},{9,13},{10,... | collective-permute-start | bytes 786440 | tf_op jit(solution)/shard_map/ppermute | solution.py:395
  160.8 12.4 %collective-permute-start.16 = (bf16[64,2048]{1,0:T(8,128)(2,1)S(1)}, bf16[64,2048]{1,0:T(8,128)(2,1)S(1)}, u32[]{:S(2)}, u32[]{:S(2)}) collective-permute-start(bf16[64,2048]{1,0:T(8,128)(2,1)S(1)} %collective-permute-done.12.refs_0_), channel_id=1, source_target_pairs={{0,16},{1,17},{2,18},{3,19},{4,20},{5,21},{6,22},{7,23},{8,24},{9,... | collective-permute-start | bytes 786440 | tf_op jit(solution)/shard_map/ppermute | solution.py:395
  173.2 8.4 %collective-permute-start.19 = (bf16[64,2048]{1,0:T(8,128)(2,1)S(1)}, bf16[64,2048]{1,0:T(8,128)(2,1)S(1)}, u32[]{:S(2)}, u32[]{:S(2)}) collective-permute-start(bf16[64,2048]{1,0:T(8,128)(2,1)S(1)} %collective-permute-done.15.refs_0_), channel_id=1, source_target_pairs={{0,16},{1,17},{2,18},{3,19},{4,20},{5,21},{6,22},{7,23},{8,24},{9,... | collective-permute-start | bytes 786440 | tf_op jit(solution)/shard_map/ppermute | solution.py:395
  181.6 8.3 %collective-permute-start.20 = (bf16[64,2048]{1,0:T(8,128)(2,1)S(1)}, bf16[64,2048]{1,0:T(8,128)(2,1)S(1)}, u32[]{:S(2)}, u32[]{:S(2)}) collective-permute-start(bf16[64,2048]{1,0:T(8,128)(2,1)S(1)} %get-tuple-element.153), channel_id=1, source_target_pairs={{0,16},{1,17},{2,18},{3,19},{4,20},{5,21},{6,22},{7,23},{8,24},{9,... | collective-permute-start | bytes 786440 | tf_op jit(solution)/shard_map/ppermute | solution.py:395
  190.6 7.2 %collective-permute-start.21 = (bf16[64,2048]{1,0:T(8,128)(2,1)}, bf16[64,2048]{1,0:T(8,128)(2,1)S(1)}, u32[]{:S(2)}, u32[]{:S(2)}) collective-permute-start(bf16[64,2048]{1,0:T(8,128)(2,1)} %get-tuple-element.157), channel_id=1, source_target_pairs={{0,16},{1,17},{2,18},{3,19},{4,20},{5,21},{6,22},{7,23},{8,24},{9,... | collective-permute-start | bytes 786440 | tf_op jit(solution)/shard_map/ppermute | solution.py:395
  193.8 18.8 %collective-permute-start.24 = (bf16[64,2048]{1,0:T(8,128)(2,1)}, bf16[64,2048]{1,0:T(8,128)(2,1)S(1)}, u32[]{:S(2)}, u32[]{:S(2)}) collective-permute-start(bf16[64,2048]{1,0:T(8,128)(2,1)} %add_rows.2), channel_id=1, source_target_pairs={{0,4},{1,5},{2,6},{3,7},{4,0},{5,1},{6,2},{7,3},{8,12},{9,13},{10,... | collective-permute-start | bytes 786440 | tf_op jit(solution)/shard_map/ppermute | solution.py:395
  197.8 14.8 %collective-permute-start.22 = (bf16[64,2048]{1,0:T(8,128)(2,1)}, bf16[64,2048]{1,0:T(8,128)(2,1)S(1)}, u32[]{:S(2)}, u32[]{:S(2)}) collective-permute-start(bf16[64,2048]{1,0:T(8,128)(2,1)} %copy-done.50), channel_id=1, source_target_pairs={{0,16},{1,17},{2,18},{3,19},{4,20},{5,21},{6,22},{7,23},{8,24},{9,... | collective-permute-start | bytes 786440 | tf_op jit(solution)/shard_map/ppermute | solution.py:395
  199.3 13.4 %collective-permute-start.23 = (bf16[64,2048]{1,0:T(8,128)(2,1)}, bf16[64,2048]{1,0:T(8,128)(2,1)S(1)}, u32[]{:S(2)}, u32[]{:S(2)}) collective-permute-start(bf16[64,2048]{1,0:T(8,128)(2,1)} %copy-done.49), channel_id=1, source_target_pairs={{0,16},{1,17},{2,18},{3,19},{4,20},{5,21},{6,22},{7,23},{8,24},{9,... | collective-permute-start | bytes 786440 | tf_op jit(solution)/shard_map/ppermute | solution.py:395
  201.6 16.5 %collective-permute-start.25 = (bf16[64,2048]{1,0:T(8,128)(2,1)}, bf16[64,2048]{1,0:T(8,128)(2,1)S(1)}, u32[]{:S(2)}, u32[]{:S(2)}) collective-permute-start(bf16[64,2048]{1,0:T(8,128)(2,1)} %add_rows.3), channel_id=1, source_target_pairs={{0,4},{1,5},{2,6},{3,7},{4,0},{5,1},{6,2},{7,3},{8,12},{9,13},{10,... | collective-permute-start | bytes 786440 | tf_op jit(solution)/shard_map/ppermute | solution.py:395
  (59 other events, 518.0 us)

commit v5 on v4

--- a/solution.py
+++ b/solution.py
@@ -29,6 +29,10 @@
 
 def vmem_spec():
     return pl.BlockSpec(memory_space=pltpu.VMEM)
+
+
+def hbm_spec():
+    return pl.BlockSpec(memory_space=pltpu.HBM)
 
 
 def smem_spec():
@@ -83,15 +87,24 @@
 def far_kernel(
     counts_ref,
     arrived_ref,
-    keys_ref,
-    values_ref,
+    keys_hbm,
+    values_hbm,
     out_ref,
     query_ref,
     answer_ref,
     stat_ref,
     score_ref,
     top_ref,
+    keys_ref,
+    values_ref,
+    sems,
 ):
+    copies = [
+        pltpu.make_async_copy(keys_hbm, keys_ref, sems.at[0]),
+        pltpu.make_async_copy(values_hbm, values_ref, sems.at[1]),
+    ]
+    for copy in copies:
+        copy.start()
     sources, chunk_rows, part_width = arrived_ref.shape
     capacity = chunk_rows - STAT_ROWS
     local_heads = part_width // HD
@@ -156,6 +169,8 @@
     def slot_of(block, head):
         return (block * local_heads + head) % 2 if local_heads % 2 else head % 2
 
+    for copy in copies:
+        copy.wait()
     first_rows = load_queries(0, 0)
     part_top = None
     for chunk in range(chunks):
@@ -207,7 +222,7 @@
     return pl.pallas_call(
         far_kernel,
         out_shape=jax.ShapeDtypeStruct((sources, capacity + STAT_ROWS, part_width), jnp.bfloat16),
-        in_specs=[smem_spec(), vmem_spec(), vmem_spec(), vmem_spec()],
+        in_specs=[smem_spec(), vmem_spec(), hbm_spec(), hbm_spec()],
         out_specs=vmem_spec(),
         scratch_shapes=[
             pltpu.VMEM((local_heads, row_total, HD), jnp.float32),
@@ -215,6 +230,9 @@
             pltpu.VMEM((row_total, LANES), jnp.float32),
             pltpu.VMEM((2, ROW_BLOCK, key_total), jnp.float32),
             pltpu.VMEM((2, ROW_BLOCK, LANES), jnp.float32),
+            pltpu.VMEM(turned_keys.shape, jnp.bfloat16),
+            pltpu.VMEM(wide_values.shape, jnp.bfloat16),
+            pltpu.SemaphoreType.DMA((2,)),
         ],
         compiler_params=pltpu.CompilerParams(vmem_limit_bytes=40 * mebibyte),
         cost_estimate=pl.CostEstimate(
@@ -301,6 +319,7 @@
     shift_ref,
     first_ref,
     second_ref,
+    hidden_ref,
     far_ref,
     stat_ref,
 ):
@@ -360,6 +379,7 @@
         )
         first_ref[:, columns] = hidden[: slot_count // 2]
         second_ref[:, columns] = hidden[slot_count // 2 :]
+        hidden_ref[:, columns] = hidden
 
 
 def merge_parts(lengths, groups, arrived, own_mixed, own_top, own_sum, layer_input, gain, shift):
@@ -368,9 +388,9 @@
     half = jax.ShapeDtypeStruct((slot_count // 2, model_width), jnp.bfloat16)
     return pl.pallas_call(
         merge_kernel,
-        out_shape=(half, half),
+        out_shape=(half, half, jax.ShapeDtypeStruct(layer_input.shape, jnp.bfloat16)),
         in_specs=[smem_spec(), smem_spec()] + [vmem_spec()] * 7,
-        out_specs=(vmem_spec(), vmem_spec()),
+        out_specs=(vmem_spec(), vmem_spec(), vmem_spec()),
         scratch_shapes=[
             pltpu.VMEM((model_width // HD, slot_count + capacity, HD), jnp.float32),
             pltpu.VMEM((slot_count + capacity, LANES), jnp.float32),
@@ -392,7 +412,8 @@
 
 def swap(value, mask):
     total = lax.axis_size("grp") * lax.axis_size("dev")
-    return lax.ppermute(value, ("grp", "dev"), [(here, here ^ mask) for here in range(total)])
+    pairs = [(here, here ^ mask) for here in range(total)]
+    return jax.tree.map(lambda leaf: lax.ppermute(leaf, ("grp", "dev"), pairs), value)
 
 
 def complete(held, masks):
@@ -408,42 +429,55 @@
     return lax.optimization_barrier((values, after))[0]
 
 
-def mlp_kernel(pieces, parts, *refs):
+def mlp_kernel(pieces, up_plan, down_plan, *refs):
+    parts = len(up_plan)
     row_refs, refs = refs[:pieces], refs[pieces:]
-    ups, refs = refs[:parts], refs[parts:]
-    downs, refs = refs[:parts], refs[parts:]
+    up_total, down_total = sum(map(len, up_plan)), sum(map(len, down_plan))
+    ups, refs = list(refs[:up_total]), refs[up_total:]
+    downs, refs = list(refs[:down_total]), refs[down_total:]
     out_refs, (up_ref, down_ref, sems) = refs[:pieces], refs[pieces:]
     model_width = row_refs[0].shape[1]
-    units = downs[0].shape[0]
-    up_copies = [
-        pltpu.make_async_copy(ups[part], up_ref.at[part], sems.at[part, 0])
-        for part in range(parts)
-    ]
-    down_copies = [
-        pltpu.make_async_copy(
-            downs[part], down_ref.at[pl.ds(part * units, units)], sems.at[part, 1]
-        )
-        for part in range(parts)
-    ]
-    copies = up_copies + down_copies
+    copies = []
+    for part, heights in enumerate(up_plan):
+        begin, held = 0, []
+        for piece, height in enumerate(heights):
+            target = up_ref.at[part, pl.ds(begin, height)]
+            held.append(pltpu.make_async_copy(ups.pop(0), target, sems.at[part, 0, piece]))
+            begin += height
+        copies.append(held)
+    begin = 0
+    for part, heights in enumerate(down_plan):
+        held = []
+        for piece, height in enumerate(heights):
+            target = down_ref.at[pl.ds(begin, height)]
+            held.append(pltpu.make_async_copy(downs.pop(0), target, sems.at[part, 1, piece]))
+            begin += height
+        copies.append(held)
     ahead = 4
-    for copy in copies[:ahead]:
-        copy.start()
+
+    def start(at):
+        if at < len(copies):
+            for copy in copies[at]:
+                copy.start()
+
+    def arrive(at):
+        for copy in copies[at]:
+            copy.wait()
+        start(at + ahead)
+
+    for at in range(ahead):
+        start(at)
     rows = jnp.concatenate([ref[...] for ref in row_refs], axis=0)
     activations = []
     for part in range(parts):
-        copies[part].wait()
-        if part + ahead < len(copies):
-            copies[part + ahead].start()
+        arrive(part)
         product = jnp.dot(
             rows, up_ref[part, :model_width, :], preferred_element_type=jnp.float32
         )
         offset = up_ref[part, model_width:, :].astype(jnp.float32)[0:1]
         activations.append(jax.nn.gelu(product + offset, approximate=True).astype(jnp.bfloat16))
-    for part in range(parts, 2 * parts):
-        copies[part].wait()
-        if part + ahead < len(copies):
-            copies[part + ahead].start()
+    for part in range(parts):
+        arrive(parts + part)
     total = jnp.dot(
         jnp.concatenate(activations, axis=1), down_ref[...], preferred_element_type=jnp.float32
     ).astype(jnp.bfloat16)
@@ -455,16 +489,21 @@
 def feed_forward(rows, ups, downs):
     pieces, parts = len(rows), len(ups)
     height, model_width = rows[0].shape
-    up_rows, units = ups[0].shape
+    up_plan = [[piece.shape[0] for piece in block] for block in ups]
+    down_plan = [[piece.shape[0] for piece in block] for block in downs]
+    up_rows, down_rows = sum(up_plan[0]), sum(down_plan[0])
+    units = ups[0][0].shape[1]
+    flat = [piece for block in ups + downs for piece in block]
+    most = max(map(len, up_plan + down_plan))
     return pl.pallas_call(
-        functools.partial(mlp_kernel, pieces, parts),
+        functools.partial(mlp_kernel, pieces, up_plan, down_plan),
         out_shape=tuple(jax.ShapeDtypeStruct(piece.shape, jnp.bfloat16) for piece in rows),
-        in_specs=[vmem_spec()] * pieces + [pl.BlockSpec(memory_space=pl.ANY)] * (2 * parts),
+        in_specs=[vmem_spec()] * pieces + [hbm_spec()] * len(flat),
         out_specs=tuple(vmem_spec() for _ in rows),
         scratch_shapes=[
             pltpu.VMEM((parts, up_rows, units), jnp.bfloat16),
-            pltpu.VMEM((parts * units, model_width), jnp.bfloat16),
-            pltpu.SemaphoreType.DMA((parts, 2)),
+            pltpu.VMEM((parts * down_rows, model_width), jnp.bfloat16),
+            pltpu.SemaphoreType.DMA((parts, 2, most)),
         ],
         compiler_params=pltpu.CompilerParams(vmem_limit_bytes=32 * mebibyte),
         cost_estimate=pl.CostEstimate(
@@ -473,7 +512,7 @@
             transcendentals=pieces * height * parts * units,
         ),
         name="feed_forward",
-    )(*rows, *ups, *downs)
+    )(*rows, *flat)
 
 
 def add_kernel(here_ref, there_ref, out_ref):
@@ -492,34 +531,37 @@
     )(here, there)
 
 
-def finish_kernel(pieces, *refs):
-    bias_ref, gain_ref, shift_ref, out_ref = refs[4 * pieces :]
-    height = out_ref.shape[0] // pieces
-    for piece in range(pieces):
-        hidden, own, near, far = (
-            refs[kind * pieces + piece][...].astype(jnp.float32) for kind in range(4)
-        )
-        summed = hidden + (own + near + far) + bias_ref[...]
-        out_ref[piece * height : (piece + 1) * height, :] = layer_norm(
-            summed, gain_ref[...], shift_ref[...]
+def finish_kernel(
+    hidden_ref, own_ref, near_ref, far_a_ref, far_b_ref, bias_ref, gain_ref, shift_ref, out_ref
+):
+    height = far_a_ref.shape[0]
+    for begin, far_ref in ((0, far_a_ref), (height, far_b_ref)):
+        rows = slice(begin, begin + height)
+        summed = hidden_ref[rows, :].astype(jnp.float32) + (
+            own_ref[rows, :].astype(jnp.float32)
+            + near_ref[rows, :].astype(jnp.float32)
+            + far_ref[...].astype(jnp.float32)
+        )
+        out_ref[rows, :] = layer_norm(
+            summed + bias_ref[...], gain_ref[...], shift_ref[...]
         ).astype(jnp.bfloat16)
 
 
-def finish_rows(hidden, own, near, far, bias, gain, shift):
-    pieces = len(hidden)
-    height, model_width = hidden[0].shape
+def finish_rows(hidden, own, near, far_a, far_b, bias, gain, shift):
+    model_width = hidden.shape[1]
     return pl.pallas_call(
-        functools.partial(finish_kernel, pieces),
-        out_shape=jax.ShapeDtypeStruct((pieces * height, model_width), jnp.bfloat16),
-        in_specs=[vmem_spec()] * (4 * pieces + 3),
+        finish_kernel,
+        out_shape=jax.ShapeDtypeStruct(hidden.shape, jnp.bfloat16),
+        in_specs=[vmem_spec()] * 8,
         out_specs=vmem_spec(),
         compiler_params=pltpu.CompilerParams(vmem_limit_bytes=16 * mebibyte),
         name="finish_rows",
     )(
-        *hidden,
-        *own,
-        *near,
-        *far,
+        hidden,
+        own,
+        near,
+        far_a,
+        far_b,
         bias.reshape(1, model_width),
         gain.reshape(1, model_width),
         shift.reshape(1, model_width),
@@ -557,12 +599,19 @@
     column_masks = [1 << bit for bit in range(far_mask.bit_length() - 1)]
     group_masks = [column_count << bit for bit in range((group_count // 2).bit_length() - 1)]
 
+    low_mask, high_masks = column_masks[0], column_masks[1:]
+    core_mask = group_masks[0]
+
     outgoing = pack_queries(
         suffix_lengths, request_group, suffix_queries, group_count, column_count, capacity
     )
     bias_rows = jnp.broadcast_to(up_bias[None, :], (16, up_bias.shape[0]))
-    ups = {0: jnp.concatenate([up_weight, bias_rows], axis=0)}
-    downs = {0: down_weight}
+    up_block = jnp.concatenate([up_weight, bias_rows], axis=0)
+    up_cut, down_cut = up_weight.shape[0] // 2, down_weight.shape[0] // 2
+    up_pieces = (up_block[:up_cut], up_block[up_cut:])
+    down_pieces = (down_weight[:down_cut], down_weight[down_cut:])
+    ups, downs = {0: (up_block,)}, {0: (down_weight,)}
+    high_mask = high_masks[0]
 
     arrived = lax.all_to_all(
         outgoing.reshape(sources, capacity + STAT_ROWS, part_width),
@@ -571,55 +620,65 @@
         concat_axis=0,
         tiled=True,
     )
-    for mask in column_masks:
-        ups[mask] = swap(ups[0], mask)
+    ups[low_mask] = swap(ups[0], low_mask)
+    up_first = swap(up_pieces[0], high_mask)
     turned_keys = prefix_keys[0].T
     value_heads = prefix_values[0].reshape(-1, local_heads, HD).transpose(1, 0, 2)
     wide_values = jnp.concatenate([value_heads, jnp.ones_like(value_heads)], axis=2)
     own = attend_suffix(
         suffix_lengths, suffix_queries, suffix_keys, suffix_values, local_heads
     )
-    arrived, ups, downs, turned_keys, wide_values, own = lax.optimization_barrier(
-        (arrived, ups, downs, turned_keys, wide_values, own)
+    arrived, ups, up_first, up_pieces, downs, down_pieces, turned_keys, wide_values, own = (
+        lax.optimization_barrier(
+            (arrived, ups, up_first, up_pieces, downs, down_pieces, turned_keys, wide_values, own)
+        )
     )
 
     counts = arrived[:, capacity, 0].astype(jnp.int32)
     answer_part = attend_prefix(counts, arrived, turned_keys, wide_values)
-    for mask in column_masks:
-        downs[mask] = swap(downs[0], mask)
-    answer_part, ups, downs = lax.optimization_barrier((answer_part, ups, downs))
+    downs[low_mask] = swap(downs[0], low_mask)
+    up_second = swap(up_pieces[1], high_mask)
+    down_first = swap(down_pieces[0], high_mask)
+    answer_part, ups, up_first, up_second, downs, down_first, down_pieces = (
+        lax.optimization_barrier(
+            (answer_part, ups, up_first, up_second, downs, down_first, down_pieces)
+        )
+    )
 
     answer = lax.all_to_all(
         answer_part, ("grp", "dev"), split_axis=0, concat_axis=0, tiled=True
     ).reshape(group_count, column_count, capacity + STAT_ROWS, part_width)
-    core_mask = group_masks[0]
+    ups[high_mask] = (jnp.concatenate([up_first, up_second], axis=0),)
     early_ups = {core_mask ^ at: swap(block, core_mask) for at, block in ups.items()}
     early_downs = {core_mask ^ at: swap(block, core_mask) for at, block in downs.items()}
-    ups = complete(ups, column_masks[::-1])
-    downs = complete(downs, column_masks)
+    down_second = swap(down_pieces[1], high_mask)
+    downs[high_mask] = (jnp.concatenate([down_first, down_second], axis=0),)
+    ups[low_mask ^ high_mask] = swap(ups[high_mask], low_mask)
     ups.update(early_ups)
     downs.update(early_downs)
     answer, ups, downs = lax.optimization_barrier((answer, ups, downs))
 
-    hidden = merge_parts(
+    hidden_a, hidden_b, hidden = merge_parts(
         suffix_lengths, request_group, answer, *own, layer_input, attn_gain, attn_shift
     )
 
-    hidden, ups, downs = lax.optimization_barrier((hidden, ups, downs))
-    far_a = swap(hidden[0], far_mask)
-    near = [swap(piece, near_mask) for piece in hidden]
-    ups = complete(ups, group_masks)
-    downs = complete(downs, group_masks)
+    (hidden_a, hidden_b, hidden), ups, downs = lax.optimization_barrier(
+        ((hidden_a, hidden_b, hidden), ups, downs)
+    )
+    far_a = swap(hidden_a, far_mask)
+    near = swap(hidden, near_mask)
+    downs[low_mask ^ high_mask] = swap(downs[high_mask], low_mask)
+    ups = complete(ups, group_masks + column_masks)
+    far_b = swap(tie(hidden_b, far_a), far_mask)
+    cross_a = swap(far_a, near_mask)
+    far_b, cross_a, near, ups, downs = lax.optimization_barrier(
+        (far_b, cross_a, near, ups, downs)
+    )
+    cross_b = swap(far_b, near_mask)
+    downs = complete(downs, group_masks + column_masks)
     order = sorted(ups)
     ups = [ups[mask] for mask in order]
     downs = [downs[mask] for mask in order]
-    own_part = feed_forward(hidden, ups, downs)
-    far_a, own_part = lax.optimization_barrier((far_a, own_part))
-    far_b = swap(tie(hidden[1], far_a), far_mask)
-    cross_a = swap(far_a, near_mask)
-    near_part = feed_forward(tie(near, far_a), ups, downs)
-    far_b, cross_a, near_part = lax.optimization_barrier((far_b, cross_a, near_part))
-    cross_b = swap(far_b, near_mask)
     far_part_a, cross_part_a = feed_forward([far_a, cross_a], ups, downs)
     cross_b, far_part_a, cross_part_a = lax.optimization_barrier(
         (cross_b, far_part_a, cross_part_a)
@@ -629,12 +688,15 @@
     cross_sum_a, far_part_b, cross_part_b = lax.optimization_barrier(
         (cross_sum_a, far_part_b, cross_part_b)
     )
+    far_sum_a = swap(add_rows(far_part_a, cross_sum_a), far_mask)
     cross_sum_b = swap(cross_part_b, near_mask)
-    far_sum_a = swap(add_rows(far_part_a, cross_sum_a), far_mask)
-    near_sum = [swap(piece, near_mask) for piece in tie(near_part, cross_sum_b)]
+    (near_part,) = feed_forward([tie(near, cross_part_b)], ups, downs)
+    near_sum = swap(near_part, near_mask)
+    cross_sum_b, near_part = lax.optimization_barrier((cross_sum_b, near_part))
     far_sum_b = swap(add_rows(far_part_b, cross_sum_b), far_mask)
+    (own_part,) = feed_forward([tie(hidden, near_part)], ups, downs)
     return finish_rows(
-        hidden, own_part, near_sum, [far_sum_a, far_sum_b], down_bias, out_gain, out_shift
+        hidden, own_part, near_sum, far_sum_a, far_sum_b, down_bias, out_gain, out_shift
     )
 
 

time: 220 us -> 227 us (1.032)
  local copies, waits for them, and re-layouts: 44.6 us -> 58.1 us
  waiting for transfers between devices: 77.5 us -> 66.8 us
  starting transfers between devices: 35 us -> 39.1 us
  Pallas kernels: 60.6 us -> 58.3 us
    ppermute x26, waiting for transfers between devices: 77.5 us -> 66.8 us  [swap(): lax.ppermute(leaf, ('grp', 'dev'), pairs)]
    unnamed x112 -> x117, local copies, waits for them, and re-layouts: 36.4 us -> 46.8 us
    pallas_call x1, Pallas kernels: 20.9 us -> 14.7 us  [attend_prefix(): pl.pallas_call(far_kernel, out_shape=jax.ShapeDtypeStruct((sources, capac...]
    pallas_call x6, Pallas kernels: 29.7 us -> 33.5 us  [the longest x4 28.3 us: feed_forward(): pl.pallas_call(functools.partial(mlp_kernel, pieces, up_plan, down_plan),...]
    all_to_all x1, starting transfers between devices: 3.98 us -> 6.37 us  [on_device(): lax.all_to_all(answer_part, ('grp', 'dev'), split_axis=0, concat_axis=0,...]
  transfers between devices with their start and end apart: 28 -> 28, of which waited for: 10 -> 9; matrix products, arithmetic and copies ran while one was open for 8% -> 11% of each run, Pallas kernels for 25% -> 23%
where the time goes in v5:
time: 227 us; the launch traced here: 225 us
  waiting for transfers between devices  66.8 us (29%)
  Pallas kernels  58.3 us (26%)
  local copies, waits for them, and re-layouts  58.1 us (26%)
  starting transfers between devices  39.1 us (17%)
  other arithmetic  2.71 us (1%)
    ppermute x26, waiting for transfers between devices, swap(): lax.ppermute(leaf, ('grp', 'dev'), pairs)  66.8 us
    unnamed x117, local copies, waits for them, and re-layouts  46.8 us
    pallas_call x4, Pallas kernels, feed_forward(): pl.pallas_call(functools.partial(mlp_kernel, pieces, up_plan, down_plan),...  28.3 us
    ppermute x26, starting transfers between devices, swap(): lax.ppermute(leaf, ('grp', 'dev'), pairs)  25.4 us
    pallas_call x1, Pallas kernels, attend_prefix(): pl.pallas_call(far_kernel, out_shape=jax.ShapeDtypeStruct((sources, capac...  14.7 us
    all_to_all x1, starting transfers between devices, on_device(): lax.all_to_all(outgoing.reshape(sources, capacity + STAT_ROWS, part_width...  7.3 us
    all_to_all x1, starting transfers between devices, on_device(): lax.all_to_all(answer_part, ('grp', 'dev'), split_axis=0, concat_axis=0,...  6.37 us
  transfers between devices with their start and end apart: 28, of which 9 were waited for; matrix products, arithmetic and copies ran while one was open for 11% of the time, Pallas kernels for 23%

profile of v5, /device:TPU:0, one launch (start us, length us, event | category | flops | bytes accessed | tf_op | source)
XLA Modules:
  0.0 225.4 jit_solution(9719418751411105524)
XLA Ops:
  2.4 1.9 pack_queries.1
  4.3 7.3 %all-to-all-start = ((bf16[32,72,256]{2,1,0:T(8,128)(2,1)}), bf16[32,72,256]{2,1,0:T(8,128)(2,1)S(1)}, u32[]{:S(2)}, u32[]{:S(2)}) async-start(bf16[32,72,256]{2,1,0:T(8,128)(2,1)} %bitcast), calls=%async_computation | async-start | bytes 2359296 | tf_op jit(solution)/shard_map/all_to_all | solution.py:616
  16.7 4.5 %attend_suffix.1 = (f32[128,2048]{1,0:T(8,128)S(1)}, f32[128,128]{1,0:T(8,128)S(1)}, f32[128,128]{1,0:T(8,128)S(1)}) custom-call(s32[1,4]{1,0:T(1,128)S(1)} %copy-done.48, bf16[128,2048]{1,0:T(8,128)(2,1)S(1)} %copy-done.38, bf16[128,2048]{1,0:T(8,128)(2,1)S(1)} %copy-done.51, bf16[128,2048]{1,0:T(8,128)(2,1)S(1)} %copy-done.52), custom_call_target="tpu_custom_call" | custom-call | flops 1342177280 | bytes 2097152 | tf_op jit(solution)/shard_map/attend_suffix/pallas_call | solution.py:295
  21.2 4.6 %copy.18 = bf16[1,4096,256]{1,2,0:T(8,128)(2,1)} copy(bf16[1,4096,256]{2,1,0:T(8,128)(2,1)} %param.22) | data formatting | bytes 4194304 | tf_op args[6]
  25.8 4.1 %copy.19 = bf16[1,4096,256]{1,2,0:T(8,128)(2,1)} copy(bf16[1,4096,256]{2,1,0:T(8,128)(2,1)} %param.23) | data formatting | bytes 4194304 | tf_op args[7]
  29.9 4.1 %copy.20 = bf16[4096,2,128]{2,0,1:T(8,128)(2,1)} copy(bf16[4096,2,128]{0,2,1:T(8,128)(2,1)} %bitcast.19) | data formatting | bytes 4194304 | tf_op jit(solution)/shard_map/reshape;squeeze | solution.py:626
  34.0 4.1 %concatenate.13.values_hbm = bf16[2,4096,256]{2,1,0:T(8,128)(2,1)} pad(bf16[2,4096,128]{2,1,0:T(8,128)(2,1)} %bitcast.18, bf16[]{:T(256)} %constant.0.clone.1), padding=0_0x0_0x0_128 | pad | bytes 6291458 | tf_op jit(solution)/shard_map/concatenate | solution.py:627
  39.2 5.5 %collective-permute-done.1 = bf16[1024,256]{1,0:T(8,128)(2,1)} collective-permute-done((bf16[1024,256]{1,0:T(8,128)(2,1)}, bf16[1024,256]{1,0:T(8,128)(2,1)}, u32[]{:S(2)}, u32[]{:S(2)}) %collective-permute-start.1) | collective-permute-done | bytes 524320 | tf_op jit(solution)/shard_map/ppermute | solution.py:416
  44.7 5.1 %collective-permute-done.refs_2_.refs_3_ = bf16[2064,256]{1,0:T(8,128)(2,1)} collective-permute-done((bf16[2064,256]{1,0:T(8,128)(2,1)S(1)}, bf16[2064,256]{1,0:T(8,128)(2,1)}, u32[]{:S(2)}, u32[]{:S(2)}) %collective-permute-start) | collective-permute-done | bytes 1056800 | tf_op jit(solution)/shard_map/ppermute | solution.py:416
  52.9 2.2 copy-done.30
  56.7 14.7 %attend_prefix.1 = bf16[32,72,256]{2,1,0:T(8,128)(2,1)S(1)} custom-call(s32[32]{0:T(128)S(1)} %convert_reduce_fusion.counts_ref, bf16[32,72,256]{2,1,0:T(8,128)(2,1)S(1)} %all-to-all-done.arrived_ref, bf16[256,4096]{1,0:T(8,128)(2,1)S(1)} %bitcast.12, bf16[2,4096,256]{2,1,0:T(8,128)(2,1)S(1)} %copy-done.30), custom_call_target="tpu_custom_call" | custom-call | flops 8589934592 | bytes 8388608 | tf_op jit(solution)/shard_map/attend_prefix/pallas_call | solution.py:222
  72.5 2.8 %collective-permute-done.2 = bf16[1040,256]{1,0:T(8,128)(2,1)} collective-permute-done((bf16[1040,256]{1,0:T(8,128)(2,1)}, bf16[1040,256]{1,0:T(8,128)(2,1)}, u32[]{:S(2)}, u32[]{:S(2)}) %collective-permute-start.2) | collective-permute-done | bytes 532512 | tf_op jit(solution)/shard_map/ppermute | solution.py:416
  75.3 6.4 %all-to-all-start.1 = ((bf16[32,72,256]{2,1,0:T(8,128)(2,1)}), bf16[32,72,256]{2,1,0:T(8,128)(2,1)}, u32[]{:S(2)}, u32[]{:S(2)}) async-start(bf16[32,72,256]{2,1,0:T(8,128)(2,1)} %copy-done.34), calls=%async_computation.1 | async-start | bytes 2359296 | tf_op jit(solution)/shard_map/all_to_all | solution.py:648
  87.5 27.0 %collective-permute-done.9 = bf16[128,2048]{1,0:T(8,128)(2,1)S(1)} collective-permute-done((bf16[128,2048]{1,0:T(8,128)(2,1)S(1)}, bf16[128,2048]{1,0:T(8,128)(2,1)S(1)}, u32[]{:S(2)}, u32[]{:S(2)}) %collective-permute-start.9) | collective-permute-done | bytes 524320 | tf_op jit(solution)/shard_map/ppermute | solution.py:416
  126.3 2.7 %merge_parts.1 = (bf16[64,2048]{1,0:T(8,128)(2,1)S(1)}, bf16[64,2048]{1,0:T(8,128)(2,1)S(1)}, bf16[128,2048]{1,0:T(8,128)(2,1)S(1)}) custom-call(s32[1,4]{1,0:T(1,128)S(1)} %copy-done.48, s32[1,4]{1,0:T(1,128)S(1)} %copy-done.50, bf16[4,8,72,256]{3,2,1,0:T(8,128)(2,1)} %bitcast.5.arrived_ref, f32[128,2048]{1,0:T(8,128)S(1)} %copy-done.36, ...), custom_call_target="tpu_custom_call" | custom-call | tf_op jit(solution)/shard_map/merge_parts/pallas_call | solution.py:389
  130.7 2.4 %collective-permute-start.12 = (bf16[64,2048]{1,0:T(8,128)(2,1)S(1)}, bf16[64,2048]{1,0:T(8,128)(2,1)S(1)}, u32[]{:S(2)}, u32[]{:S(2)}) collective-permute-start(bf16[64,2048]{1,0:T(8,128)(2,1)S(1)} %get-tuple-element.134), channel_id=1, source_target_pairs={{0,4},{1,5},{2,6},{3,7},{4,0},{5,1},{6,2},{7,3},{8,12},{9,13},{10,... | collective-permute-start | bytes 786440 | tf_op jit(solution)/shard_map/ppermute | solution.py:416
  135.4 10.1 %collective-permute-done.12.refs_0_ = bf16[64,2048]{1,0:T(8,128)(2,1)S(1)} collective-permute-done((bf16[64,2048]{1,0:T(8,128)(2,1)S(1)}, bf16[64,2048]{1,0:T(8,128)(2,1)S(1)}, u32[]{:S(2)}, u32[]{:S(2)}) %collective-permute-start.12) | collective-permute-done | bytes 262176 | tf_op jit(solution)/shard_map/ppermute | solution.py:416
  147.0 12.2 %collective-permute-done.13.refs_0_ = bf16[64,2048]{1,0:T(8,128)(2,1)S(1)} collective-permute-done((bf16[64,2048]{1,0:T(8,128)(2,1)S(1)}, bf16[64,2048]{1,0:T(8,128)(2,1)S(1)}, u32[]{:S(2)}, u32[]{:S(2)}) %collective-permute-start.13) | collective-permute-done | bytes 262176 | tf_op jit(solution)/shard_map/ppermute | solution.py:416
  169.6 6.9 %feed_forward.5 = (bf16[64,2048]{1,0:T(8,128)(2,1)S(1)}, bf16[64,2048]{1,0:T(8,128)(2,1)S(1)}) custom-call(bf16[64,2048]{1,0:T(8,128)(2,1)S(1)} %collective-permute-done.12.refs_0_, bf16[64,2048]{1,0:T(8,128)(2,1)S(1)} %collective-permute-done.14.refs_1_, bf16[2064,256]{1,0:T(8,128)(2,1)S(1)} %pad_maximum_fusion.refs_1_.refs_2_, ...), custom_call_target="tpu_custom_call" | custom-call | flops 2147483648 | bytes 16777216 | tf_op jit(solution)/shard_map/feed_forward/pallas_call | solution.py:498
  178.0 7.3 %feed_forward.6 = (bf16[64,2048]{1,0:T(8,128)(2,1)S(1)}, bf16[64,2048]{1,0:T(8,128)(2,1)}) custom-call(bf16[64,2048]{1,0:T(8,128)(2,1)S(1)} %collective-permute-done.13.refs_0_, bf16[64,2048]{1,0:T(8,128)(2,1)S(1)} %collective-permute-done.20.refs_1_, bf16[2064,256]{1,0:T(8,128)(2,1)S(1)} %pad_maximum_fusion.refs_1_.refs_2_, ...), custom_call_target="tpu_custom_call" | custom-call | flops 2147483648 | bytes 16777216 | tf_op jit(solution)/shard_map/feed_forward/pallas_call | solution.py:498
  186.4 7.6 %feed_forward.7 = bf16[128,2048]{1,0:T(8,128)(2,1)} custom-call(bf16[128,2048]{1,0:T(8,128)(2,1)S(1)} %collective-permute-done.15.refs_0_, bf16[2064,256]{1,0:T(8,128)(2,1)S(1)} %pad_maximum_fusion.refs_1_.refs_2_, bf16[2064,256]{1,0:T(8,128)(2,1)} %collective-permute-done.refs_2_.refs_3_, bf16[2064,256]{1,0:T(8,128)(2,1)S(1)} %copy-done.2, ...), custom_call_target="tpu_custom_call" | custom-call | flops 2147483648 | bytes 16777216 | tf_op jit(solution)/shard_map/feed_forward/pallas_call | solution.py:498
  198.7 2.9 %collective-permute-start.25 = (bf16[64,2048]{1,0:T(8,128)(2,1)}, bf16[64,2048]{1,0:T(8,128)(2,1)S(1)}, u32[]{:S(2)}, u32[]{:S(2)}) collective-permute-start(bf16[64,2048]{1,0:T(8,128)(2,1)} %add_rows.3), channel_id=1, source_target_pairs={{0,4},{1,5},{2,6},{3,7},{4,0},{5,1},{6,2},{7,3},{8,12},{9,13},{10,... | collective-permute-start | bytes 786440 | tf_op jit(solution)/shard_map/ppermute | solution.py:416
  216.2 6.6 %feed_forward.4.own_ref = bf16[128,2048]{1,0:T(8,128)(2,1)S(1)} custom-call(bf16[128,2048]{1,0:T(8,128)(2,1)S(1)} %copy-done.32, bf16[2064,256]{1,0:T(8,128)(2,1)S(1)} %pad_maximum_fusion.refs_1_.refs_2_, bf16[2064,256]{1,0:T(8,128)(2,1)} %collective-permute-done.refs_2_.refs_3_, bf16[2064,256]{1,0:T(8,128)(2,1)S(1)} %copy-done.3, ...), custom_call_target="tpu_custom_call" | custom-call | flops 2147483648 | bytes 16777216 | tf_op jit(solution)/shard_map/feed_forward/pallas_call | solution.py:498
  222.8 2.5 %finish_rows.1 = bf16[128,2048]{1,0:T(8,128)(2,1)} custom-call(bf16[128,2048]{1,0:T(8,128)(2,1)S(1)} %copy-done.32, bf16[128,2048]{1,0:T(8,128)(2,1)S(1)} %feed_forward.4.own_ref, bf16[128,2048]{1,0:T(8,128)(2,1)} %collective-permute-done.22.near_ref, bf16[64,2048]{1,0:T(8,128)(2,1)S(1)} %collective-permute-done.23.far_a_ref, ...), custom_call_target="tpu_custom_call" | custom-call | tf_op jit(solution)/shard_map/finish_rows/pallas_call | solution.py:552
  (170 shorter events, 69.4 us)
Async XLA Ops:
  4.3 45.6 %all-to-all-start = ((bf16[32,72,256]{2,1,0:T(8,128)(2,1)}), bf16[32,72,256]{2,1,0:T(8,128)(2,1)S(1)}, u32[]{:S(2)}, u32[]{:S(2)}) async-start(bf16[32,72,256]{2,1,0:T(8,128)(2,1)} %bitcast), calls=%async_computation | async-start | bytes 2359296 | tf_op jit(solution)/shard_map/all_to_all | solution.py:616
  11.7 38.1 %collective-permute-start = (bf16[2064,256]{1,0:T(8,128)(2,1)S(1)}, bf16[2064,256]{1,0:T(8,128)(2,1)}, u32[]{:S(2)}, u32[]{:S(2)}) collective-permute-start(bf16[2064,256]{1,0:T(8,128)(2,1)S(1)} %pad_maximum_fusion.refs_1_.refs_2_), channel_id=1, source_target_pairs={{0,1},{1,0},{2,3},{3,2},{4,5},{5,4},{6,7},{7,6},{8,9},{9,8},{10,11... | collective-permute-start | bytes 3170312 | tf_op jit(solution)/shard_map/ppermute | solution.py:416
  14.4 30.3 %collective-permute-start.1 = (bf16[1024,256]{1,0:T(8,128)(2,1)}, bf16[1024,256]{1,0:T(8,128)(2,1)}, u32[]{:S(2)}, u32[]{:S(2)}) collective-permute-start(bf16[1024,256]{1,0:T(8,128)(2,1)} %slice.15), channel_id=1, source_target_pairs={{0,2},{1,3},{2,0},{3,1},{4,6},{5,7},{6,4},{7,5},{8,10},{9,11},{10,... | collective-permute-start | bytes 1572872 | tf_op jit(solution)/shard_map/ppermute | solution.py:416
  49.8 25.5 %collective-permute-start.3 = (bf16[256,2048]{1,0:T(8,128)(2,1)S(1)}, bf16[256,2048]{1,0:T(8,128)(2,1)}, u32[]{:S(2)}, u32[]{:S(2)}) collective-permute-start(bf16[256,2048]{1,0:T(8,128)(2,1)S(1)} %copy-done), channel_id=1, source_target_pairs={{0,1},{1,0},{2,3},{3,2},{4,5},{5,4},{6,7},{7,6},{8,9},{9,8},{10,11... | collective-permute-start | bytes 3145736 | tf_op jit(solution)/shard_map/ppermute | solution.py:416
  50.2 22.3 %collective-permute-start.4 = (bf16[128,2048]{1,0:T(8,128)(2,1)}, bf16[128,2048]{1,0:T(8,128)(2,1)}, u32[]{:S(2)}, u32[]{:S(2)}) collective-permute-start(bf16[128,2048]{1,0:T(8,128)(2,1)} %get-tuple-element.102), channel_id=1, source_target_pairs={{0,2},{1,3},{2,0},{3,1},{4,6},{5,7},{6,4},{7,5},{8,10},{9,11},{10,... | collective-permute-start | bytes 1572872 | tf_op jit(solution)/shard_map/ppermute | solution.py:416
  51.9 23.5 %collective-permute-start.2 = (bf16[1040,256]{1,0:T(8,128)(2,1)}, bf16[1040,256]{1,0:T(8,128)(2,1)}, u32[]{:S(2)}, u32[]{:S(2)}) collective-permute-start(bf16[1040,256]{1,0:T(8,128)(2,1)} %fusion), channel_id=1, source_target_pairs={{0,2},{1,3},{2,0},{3,1},{4,6},{5,7},{6,4},{7,5},{8,10},{9,11},{10,... | collective-permute-start | bytes 1597448 | tf_op jit(solution)/shard_map/ppermute | solution.py:416
  75.3 48.7 %all-to-all-start.1 = ((bf16[32,72,256]{2,1,0:T(8,128)(2,1)}), bf16[32,72,256]{2,1,0:T(8,128)(2,1)}, u32[]{:S(2)}, u32[]{:S(2)}) async-start(bf16[32,72,256]{2,1,0:T(8,128)(2,1)} %copy-done.34), calls=%async_computation.1 | async-start | bytes 2359296 | tf_op jit(solution)/shard_map/all_to_all | solution.py:648
  81.7 32.8 %collective-permute-start.10 = (bf16[256,2048]{1,0:T(8,128)(2,1)S(1)}, bf16[256,2048]{1,0:T(8,128)(2,1)S(1)}, u32[]{:S(2)}, u32[]{:S(2)}) collective-permute-start(bf16[256,2048]{1,0:T(8,128)(2,1)S(1)} %copy-done), channel_id=1, source_target_pairs={{0,8},{1,9},{2,10},{3,11},{4,12},{5,13},{6,14},{7,15},{8,0},{9,1},... | collective-permute-start | bytes 3145736 | tf_op jit(solution)/shard_map/ppermute | solution.py:416
  81.8 32.7 %collective-permute-start.9 = (bf16[128,2048]{1,0:T(8,128)(2,1)S(1)}, bf16[128,2048]{1,0:T(8,128)(2,1)S(1)}, u32[]{:S(2)}, u32[]{:S(2)}) collective-permute-start(bf16[128,2048]{1,0:T(8,128)(2,1)S(1)} %copy-done.54), channel_id=1, source_target_pairs={{0,2},{1,3},{2,0},{3,1},{4,6},{5,7},{6,4},{7,5},{8,10},{9,11},{10,... | collective-permute-start | bytes 1572872 | tf_op jit(solution)/shard_map/ppermute | solution.py:416
  85.7 34.2 %collective-permute-start.8 = (bf16[2064,256]{1,0:T(8,128)(2,1)S(1)}, bf16[2064,256]{1,0:T(8,128)(2,1)S(1)}, u32[]{:S(2)}, u32[]{:S(2)}) collective-permute-start(bf16[2064,256]{1,0:T(8,128)(2,1)S(1)} %constant_dynamic-update-slice_fusion.refs_3_.refs_4_), channel_id=1, source_target_pairs={{0,8},{1,9},{2,10},{3,11},{4,12},{5,13},{6,14},{7,15},{8,0},{9,1},... | collective-permute-start | bytes 3170312 | tf_op jit(solution)/shard_map/ppermute | solution.py:416
  85.8 35.0 %collective-permute-start.5 = (bf16[2064,256]{1,0:T(8,128)(2,1)S(1)}, bf16[2064,256]{1,0:T(8,128)(2,1)S(1)}, u32[]{:S(2)}, u32[]{:S(2)}) collective-permute-start(bf16[2064,256]{1,0:T(8,128)(2,1)S(1)} %constant_dynamic-update-slice_fusion.refs_3_.refs_4_), channel_id=1, source_target_pairs={{0,1},{1,0},{2,3},{3,2},{4,5},{5,4},{6,7},{7,6},{8,9},{9,8},{10,11... | collective-permute-start | bytes 3170312 | tf_op jit(solution)/shard_map/ppermute | solution.py:416
  87.3 33.6 %collective-permute-start.6 = (bf16[2064,256]{1,0:T(8,128)(2,1)S(1)}, bf16[2064,256]{1,0:T(8,128)(2,1)S(1)}, u32[]{:S(2)}, u32[]{:S(2)}) collective-permute-start(bf16[2064,256]{1,0:T(8,128)(2,1)S(1)} %pad_maximum_fusion.refs_1_.refs_2_), channel_id=1, source_target_pairs={{0,8},{1,9},{2,10},{3,11},{4,12},{5,13},{6,14},{7,15},{8,0},{9,1},... | collective-permute-start | bytes 3170312 | tf_op jit(solution)/shard_map/ppermute | solution.py:416
  129.0 30.2 %collective-permute-start.16 = (bf16[2064,256]{1,0:T(8,128)(2,1)}, bf16[2064,256]{1,0:T(8,128)(2,1)S(1)}, u32[]{:S(2)}, u32[]{:S(2)}) collective-permute-start(bf16[2064,256]{1,0:T(8,128)(2,1)} %copy-done.7), channel_id=1, source_target_pairs={{0,8},{1,9},{2,10},{3,11},{4,12},{5,13},{6,14},{7,15},{8,0},{9,1},... | collective-permute-start | bytes 3170312 | tf_op jit(solution)/shard_map/ppermute | solution.py:416
  129.2 30.0 %collective-permute-start.17 = (bf16[256,2048]{1,0:T(8,128)(2,1)S(1)}, bf16[256,2048]{1,0:T(8,128)(2,1)S(1)}, u32[]{:S(2)}, u32[]{:S(2)}) collective-permute-start(bf16[256,2048]{1,0:T(8,128)(2,1)S(1)} %pad_maximum_fusion.1.refs_11_.refs_12_), channel_id=1, source_target_pairs={{0,1},{1,0},{2,3},{3,2},{4,5},{5,4},{6,7},{7,6},{8,9},{9,8},{10,11... | collective-permute-start | bytes 3145736 | tf_op jit(solution)/shard_map/ppermute | solution.py:416
  130.7 14.8 %collective-permute-start.12 = (bf16[64,2048]{1,0:T(8,128)(2,1)S(1)}, bf16[64,2048]{1,0:T(8,128)(2,1)S(1)}, u32[]{:S(2)}, u32[]{:S(2)}) collective-permute-start(bf16[64,2048]{1,0:T(8,128)(2,1)S(1)} %get-tuple-element.134), channel_id=1, source_target_pairs={{0,4},{1,5},{2,6},{3,7},{4,0},{5,1},{6,2},{7,3},{8,12},{9,13},{10,... | collective-permute-start | bytes 786440 | tf_op jit(solution)/shard_map/ppermute | solution.py:416
  133.1 13.9 %collective-permute-start.15 = (bf16[128,2048]{1,0:T(8,128)(2,1)S(1)}, bf16[128,2048]{1,0:T(8,128)(2,1)S(1)}, u32[]{:S(2)}, u32[]{:S(2)}) collective-permute-start(bf16[128,2048]{1,0:T(8,128)(2,1)S(1)} %get-tuple-element.132.refs_0_.hidden_ref), channel_id=1, source_target_pairs={{0,16},{1,17},{2,18},{3,19},{4,20},{5,21},{6,22},{7,23},{8,24},{9,... | collective-permute-start | bytes 1572872 | tf_op jit(solution)/shard_map/ppermute | solution.py:416
  145.5 13.7 %collective-permute-start.13 = (bf16[64,2048]{1,0:T(8,128)(2,1)S(1)}, bf16[64,2048]{1,0:T(8,128)(2,1)S(1)}, u32[]{:S(2)}, u32[]{:S(2)}) collective-permute-start(bf16[64,2048]{1,0:T(8,128)(2,1)S(1)} %get-tuple-element.135), channel_id=1, source_target_pairs={{0,4},{1,5},{2,6},{3,7},{4,0},{5,1},{6,2},{7,3},{8,12},{9,13},{10,... | collective-permute-start | bytes 786440 | tf_op jit(solution)/shard_map/ppermute | solution.py:416
  145.5 13.7 %collective-permute-start.14 = (bf16[64,2048]{1,0:T(8,128)(2,1)S(1)}, bf16[64,2048]{1,0:T(8,128)(2,1)S(1)}, u32[]{:S(2)}, u32[]{:S(2)}) collective-permute-start(bf16[64,2048]{1,0:T(8,128)(2,1)S(1)} %collective-permute-done.12.refs_0_), channel_id=1, source_target_pairs={{0,16},{1,17},{2,18},{3,19},{4,20},{5,21},{6,22},{7,23},{8,24},{9,... | collective-permute-start | bytes 786440 | tf_op jit(solution)/shard_map/ppermute | solution.py:416
  159.8 16.7 %collective-permute-start.20 = (bf16[64,2048]{1,0:T(8,128)(2,1)S(1)}, bf16[64,2048]{1,0:T(8,128)(2,1)S(1)}, u32[]{:S(2)}, u32[]{:S(2)}) collective-permute-start(bf16[64,2048]{1,0:T(8,128)(2,1)S(1)} %collective-permute-done.13.refs_0_), channel_id=1, source_target_pairs={{0,16},{1,17},{2,18},{3,19},{4,20},{5,21},{6,22},{7,23},{8,24},{9,... | collective-permute-start | bytes 786440 | tf_op jit(solution)/shard_map/ppermute | solution.py:416
  176.5 8.8 %collective-permute-start.21 = (bf16[64,2048]{1,0:T(8,128)(2,1)S(1)}, bf16[64,2048]{1,0:T(8,128)(2,1)S(1)}, u32[]{:S(2)}, u32[]{:S(2)}) collective-permute-start(bf16[64,2048]{1,0:T(8,128)(2,1)S(1)} %get-tuple-element.167), channel_id=1, source_target_pairs={{0,16},{1,17},{2,18},{3,19},{4,20},{5,21},{6,22},{7,23},{8,24},{9,... | collective-permute-start | bytes 786440 | tf_op jit(solution)/shard_map/ppermute | solution.py:416
  185.4 11.6 %collective-permute-start.24 = (bf16[64,2048]{1,0:T(8,128)(2,1)}, bf16[64,2048]{1,0:T(8,128)(2,1)}, u32[]{:S(2)}, u32[]{:S(2)}) collective-permute-start(bf16[64,2048]{1,0:T(8,128)(2,1)} %get-tuple-element.171), channel_id=1, source_target_pairs={{0,16},{1,17},{2,18},{3,19},{4,20},{5,21},{6,22},{7,23},{8,24},{9,... | collective-permute-start | bytes 786440 | tf_op jit(solution)/shard_map/ppermute | solution.py:416
  194.0 28.8 %collective-permute-start.22 = (bf16[128,2048]{1,0:T(8,128)(2,1)}, bf16[128,2048]{1,0:T(8,128)(2,1)}, u32[]{:S(2)}, u32[]{:S(2)}) collective-permute-start(bf16[128,2048]{1,0:T(8,128)(2,1)} %feed_forward.7), channel_id=1, source_target_pairs={{0,16},{1,17},{2,18},{3,19},{4,20},{5,21},{6,22},{7,23},{8,24},{9,... | collective-permute-start | bytes 1572872 | tf_op jit(solution)/shard_map/ppermute | solution.py:416
  196.9 25.8 %collective-permute-start.23 = (bf16[64,2048]{1,0:T(8,128)(2,1)}, bf16[64,2048]{1,0:T(8,128)(2,1)S(1)}, u32[]{:S(2)}, u32[]{:S(2)}) collective-permute-start(bf16[64,2048]{1,0:T(8,128)(2,1)} %add_rows.2), channel_id=1, source_target_pairs={{0,4},{1,5},{2,6},{3,7},{4,0},{5,1},{6,2},{7,3},{8,12},{9,13},{10,... | collective-permute-start | bytes 786440 | tf_op jit(solution)/shard_map/ppermute | solution.py:416
  198.7 24.0 %collective-permute-start.25 = (bf16[64,2048]{1,0:T(8,128)(2,1)}, bf16[64,2048]{1,0:T(8,128)(2,1)S(1)}, u32[]{:S(2)}, u32[]{:S(2)}) collective-permute-start(bf16[64,2048]{1,0:T(8,128)(2,1)} %add_rows.3), channel_id=1, source_target_pairs={{0,4},{1,5},{2,6},{3,7},{4,0},{5,1},{6,2},{7,3},{8,12},{9,13},{10,... | collective-permute-start | bytes 786440 | tf_op jit(solution)/shard_map/ppermute | solution.py:416
  (61 other events, 474.6 us)

commit v6 on v5

--- a/solution.py
+++ b/solution.py
@@ -234,7 +234,7 @@
             pltpu.VMEM(wide_values.shape, jnp.bfloat16),
             pltpu.SemaphoreType.DMA((2,)),
         ],
-        compiler_params=pltpu.CompilerParams(vmem_limit_bytes=40 * mebibyte),
+        compiler_params=pltpu.CompilerParams(vmem_limit_bytes=58 * mebibyte),
         cost_estimate=pl.CostEstimate(
             flops=4 * sources * capacity * key_total * part_width,
             bytes_accessed=8 * key_total * part_width,
@@ -505,7 +505,7 @@
             pltpu.VMEM((parts * down_rows, model_width), jnp.bfloat16),
             pltpu.SemaphoreType.DMA((parts, 2, most)),
         ],
-        compiler_params=pltpu.CompilerParams(vmem_limit_bytes=32 * mebibyte),
+        compiler_params=pltpu.CompilerParams(vmem_limit_bytes=58 * mebibyte),
         cost_estimate=pl.CostEstimate(
             flops=4 * pieces * height * model_width * parts * units,
             bytes_accessed=4 * parts * model_width * units,
@@ -622,6 +622,8 @@
     )
     ups[low_mask] = swap(ups[0], low_mask)
     up_first = swap(up_pieces[0], high_mask)
+    ups[core_mask] = swap(ups[0], core_mask)
+    downs[core_mask] = swap(downs[0], core_mask)
     turned_keys = prefix_keys[0].T
     value_heads = prefix_values[0].reshape(-1, local_heads, HD).transpose(1, 0, 2)
     wide_values = jnp.concatenate([value_heads, jnp.ones_like(value_heads)], axis=2)
@@ -639,6 +641,7 @@
     downs[low_mask] = swap(downs[0], low_mask)
     up_second = swap(up_pieces[1], high_mask)
     down_first = swap(down_pieces[0], high_mask)
+    ups[core_mask ^ low_mask] = swap(ups[low_mask], core_mask)
     answer_part, ups, up_first, up_second, downs, down_first, down_pieces = (
         lax.optimization_barrier(
             (answer_part, ups, up_first, up_second, downs, down_first, down_pieces)
@@ -649,13 +652,11 @@
         answer_part, ("grp", "dev"), split_axis=0, concat_axis=0, tiled=True
     ).reshape(group_count, column_count, capacity + STAT_ROWS, part_width)
     ups[high_mask] = (jnp.concatenate([up_first, up_second], axis=0),)
-    early_ups = {core_mask ^ at: swap(block, core_mask) for at, block in ups.items()}
-    early_downs = {core_mask ^ at: swap(block, core_mask) for at, block in downs.items()}
+    ups[core_mask ^ high_mask] = swap(ups[high_mask], core_mask)
+    downs[core_mask ^ low_mask] = swap(downs[low_mask], core_mask)
     down_second = swap(down_pieces[1], high_mask)
     downs[high_mask] = (jnp.concatenate([down_first, down_second], axis=0),)
     ups[low_mask ^ high_mask] = swap(ups[high_mask], low_mask)
-    ups.update(early_ups)
-    downs.update(early_downs)
     answer, ups, downs = lax.optimization_barrier((answer, ups, downs))
 
     hidden_a, hidden_b, hidden = merge_parts(
@@ -666,8 +667,9 @@
         ((hidden_a, hidden_b, hidden), ups, downs)
     )
     far_a = swap(hidden_a, far_mask)
-    near = swap(hidden, near_mask)
+    near = swap(tie(hidden, far_a), near_mask)
     downs[low_mask ^ high_mask] = swap(downs[high_mask], low_mask)
+    downs[core_mask ^ high_mask] = swap(downs[high_mask], core_mask)
     ups = complete(ups, group_masks + column_masks)
     far_b = swap(tie(hidden_b, far_a), far_mask)
     cross_a = swap(far_a, near_mask)

time: 227 us -> 228 us (level)
  local copies, waits for them, and re-layouts: 58.1 us -> 28.7 us
  waiting for transfers between devices: 66.8 us -> 83 us
  Pallas kernels: 58.3 us -> 73.8 us
    unnamed x117 -> x83, local copies, waits for them, and re-layouts: 46.8 us -> 17.5 us
    ppermute x26, waiting for transfers between devices: 66.8 us -> 83 us  [swap(): lax.ppermute(leaf, ('grp', 'dev'), pairs)]
    pallas_call x4, Pallas kernels: 28.3 us -> 41.9 us  [feed_forward(): pl.pallas_call(functools.partial(mlp_kernel, pieces, up_plan, down_plan),...]
    pallas_call x1, Pallas kernels: 14.7 us -> 18.7 us  [attend_prefix(): pl.pallas_call(far_kernel, out_shape=jax.ShapeDtypeStruct((sources, capac...]
  transfers between devices with their start and end apart: 28 -> 28, of which waited for: 9 -> 11; matrix products, arithmetic and copies ran while one was open for 11% -> 10% of each run, Pallas kernels for 23% -> 30%
where the time goes in v6:
time: 228 us
  waiting for transfers between devices  83 us (36%)
  Pallas kernels  73.8 us (32%)
  starting transfers between devices  38.4 us (17%)
  local copies, waits for them, and re-layouts  28.7 us (13%)
  other arithmetic  3.14 us (1%)
    ppermute x26, waiting for transfers between devices, swap(): lax.ppermute(leaf, ('grp', 'dev'), pairs)  83 us
    pallas_call x4, Pallas kernels, feed_forward(): pl.pallas_call(functools.partial(mlp_kernel, pieces, up_plan, down_plan),...  41.9 us
    ppermute x26, starting transfers between devices, swap(): lax.ppermute(leaf, ('grp', 'dev'), pairs)  25.1 us
    pallas_call x1, Pallas kernels, attend_prefix(): pl.pallas_call(far_kernel, out_shape=jax.ShapeDtypeStruct((sources, capac...  18.7 us
    unnamed x83, local copies, waits for them, and re-layouts  17.5 us
    all_to_all x1, starting transfers between devices, on_device(): lax.all_to_all(outgoing.reshape(sources, capacity + STAT_ROWS, part_width...  7.3 us
    all_to_all x1, starting transfers between devices, on_device(): lax.all_to_all(answer_part, ('grp', 'dev'), split_axis=0, concat_axis=0,...  6.04 us
  transfers between devices with their start and end apart: 28, of which 11 were waited for; matrix products, arithmetic and copies ran while one was open for 10% of the time, Pallas kernels for 30%

profile of v6, /device:TPU:0, one launch (start us, length us, event | category | flops | bytes accessed | tf_op | source)
XLA Modules:
  0.0 227.6 jit_solution(2488132325829473447)
XLA Ops:
  4.2 7.3 %all-to-all-start = ((bf16[32,72,256]{2,1,0:T(8,128)(2,1)}), bf16[32,72,256]{2,1,0:T(8,128)(2,1)S(1)}, u32[]{:S(2)}, u32[]{:S(2)}) async-start(bf16[32,72,256]{2,1,0:T(8,128)(2,1)} %bitcast), calls=%async_computation | async-start | bytes 2359296 | tf_op jit(solution)/shard_map/all_to_all | solution.py:616
  16.9 4.5 %attend_suffix.1 = (f32[128,2048]{1,0:T(8,128)S(1)}, f32[128,128]{1,0:T(8,128)S(1)}, f32[128,128]{1,0:T(8,128)S(1)}) custom-call(s32[1,4]{1,0:T(1,128)S(1)} %copy-done.12, bf16[128,2048]{1,0:T(8,128)(2,1)S(1)} %copy-done.4, bf16[128,2048]{1,0:T(8,128)(2,1)S(1)} %copy-done.15, bf16[128,2048]{1,0:T(8,128)(2,1)S(1)} %copy-done.16), custom_call_target="tpu_custom_call" | custom-call | flops 1342177280 | bytes 2097152 | tf_op jit(solution)/shard_map/attend_suffix/pallas_call | solution.py:295
  21.4 4.2 %copy.18 = bf16[1,4096,256]{1,2,0:T(8,128)(2,1)} copy(bf16[1,4096,256]{2,1,0:T(8,128)(2,1)} %param.22) | data formatting | bytes 4194304 | tf_op args[6]
  25.5 4.1 %copy.19 = bf16[1,4096,256]{1,2,0:T(8,128)(2,1)} copy(bf16[1,4096,256]{2,1,0:T(8,128)(2,1)} %param.23) | data formatting | bytes 4194304 | tf_op args[7]
  29.7 4.1 %copy.20 = bf16[4096,2,128]{2,0,1:T(8,128)(2,1)} copy(bf16[4096,2,128]{0,2,1:T(8,128)(2,1)} %bitcast.19) | data formatting | bytes 4194304 | tf_op jit(solution)/shard_map/reshape;squeeze | solution.py:628
  33.8 4.0 %concatenate.13.values_hbm = bf16[2,4096,256]{2,1,0:T(8,128)(2,1)} pad(bf16[2,4096,128]{2,1,0:T(8,128)(2,1)} %bitcast.18, bf16[]{:T(256)} %constant.0.clone.1), padding=0_0x0_0x0_128 | pad | bytes 6291458 | tf_op jit(solution)/shard_map/concatenate | solution.py:629
  37.8 2.3 fusion.1
  40.0 4.6 %collective-permute-done.2 = bf16[1024,256]{1,0:T(8,128)(2,1)} collective-permute-done((bf16[1024,256]{1,0:T(8,128)(2,1)}, bf16[1024,256]{1,0:T(8,128)(2,1)}, u32[]{:S(2)}, u32[]{:S(2)}) %collective-permute-start.2) | collective-permute-done | bytes 524320 | tf_op jit(solution)/shard_map/ppermute | solution.py:416
  44.7 5.1 %collective-permute-done.refs_2_.refs_3_ = bf16[2064,256]{1,0:T(8,128)(2,1)} collective-permute-done((bf16[2064,256]{1,0:T(8,128)(2,1)S(1)}, bf16[2064,256]{1,0:T(8,128)(2,1)}, u32[]{:S(2)}, u32[]{:S(2)}) %collective-permute-start) | collective-permute-done | bytes 1056800 | tf_op jit(solution)/shard_map/ppermute | solution.py:416
  53.4 18.7 %attend_prefix.1 = bf16[32,72,256]{2,1,0:T(8,128)(2,1)} custom-call(s32[32]{0:T(128)} %convert_reduce_fusion.counts_ref, bf16[32,72,256]{2,1,0:T(8,128)(2,1)} %copy-done.27, bf16[256,4096]{1,0:T(8,128)(2,1)} %bitcast.20, bf16[2,4096,256]{2,1,0:T(8,128)(2,1)} %concatenate.13.values_hbm), custom_call_target="tpu_custom_call" | custom-call | flops 8589934592 | bytes 8388608 | tf_op jit(solution)/shard_map/attend_prefix/pallas_call | solution.py:222
  72.1 3.7 %collective-permute-done.5 = bf16[1040,256]{1,0:T(8,128)(2,1)S(1)} collective-permute-done((bf16[1040,256]{1,0:T(8,128)(2,1)}, bf16[1040,256]{1,0:T(8,128)(2,1)S(1)}, u32[]{:S(2)}, u32[]{:S(2)}) %collective-permute-start.5) | collective-permute-done | bytes 532512 | tf_op jit(solution)/shard_map/ppermute | solution.py:416
  76.6 6.0 %all-to-all-start.1 = ((bf16[32,72,256]{2,1,0:T(8,128)(2,1)}), bf16[32,72,256]{2,1,0:T(8,128)(2,1)S(1)}, u32[]{:S(2)}, u32[]{:S(2)}) async-start(bf16[32,72,256]{2,1,0:T(8,128)(2,1)} %attend_prefix.1), calls=%async_computation.1 | async-start | bytes 2359296 | tf_op jit(solution)/shard_map/all_to_all | solution.py:651
  87.5 28.0 %collective-permute-done.10 = bf16[128,2048]{1,0:T(8,128)(2,1)S(1)} collective-permute-done((bf16[128,2048]{1,0:T(8,128)(2,1)S(1)}, bf16[128,2048]{1,0:T(8,128)(2,1)S(1)}, u32[]{:S(2)}, u32[]{:S(2)}) %collective-permute-start.10) | collective-permute-done | bytes 524320 | tf_op jit(solution)/shard_map/ppermute | solution.py:416
  123.6 2.4 %collective-permute-start.12 = (bf16[64,2048]{1,0:T(8,128)(2,1)S(1)}, bf16[64,2048]{1,0:T(8,128)(2,1)S(1)}, u32[]{:S(2)}, u32[]{:S(2)}) collective-permute-start(bf16[64,2048]{1,0:T(8,128)(2,1)S(1)} %get-tuple-element.146), channel_id=1, source_target_pairs={{0,4},{1,5},{2,6},{3,7},{4,0},{5,1},{6,2},{7,3},{8,12},{9,13},{10,... | collective-permute-start | bytes 786440 | tf_op jit(solution)/shard_map/ppermute | solution.py:416
  126.0 12.2 %collective-permute-done.12.refs_0_ = bf16[64,2048]{1,0:T(8,128)(2,1)S(1)} collective-permute-done((bf16[64,2048]{1,0:T(8,128)(2,1)S(1)}, bf16[64,2048]{1,0:T(8,128)(2,1)S(1)}, u32[]{:S(2)}, u32[]{:S(2)}) %collective-permute-start.12) | collective-permute-done | bytes 262176 | tf_op jit(solution)/shard_map/ppermute | solution.py:416
  139.8 12.0 %collective-permute-done.13.refs_0_ = bf16[64,2048]{1,0:T(8,128)(2,1)S(1)} collective-permute-done((bf16[64,2048]{1,0:T(8,128)(2,1)S(1)}, bf16[64,2048]{1,0:T(8,128)(2,1)S(1)}, u32[]{:S(2)}, u32[]{:S(2)}) %collective-permute-start.13) | collective-permute-done | bytes 262176 | tf_op jit(solution)/shard_map/ppermute | solution.py:416
  153.6 4.9 %collective-permute-done.14.refs_1_ = bf16[64,2048]{1,0:T(8,128)(2,1)S(1)} collective-permute-done((bf16[64,2048]{1,0:T(8,128)(2,1)S(1)}, bf16[64,2048]{1,0:T(8,128)(2,1)S(1)}, u32[]{:S(2)}, u32[]{:S(2)}) %collective-permute-start.14) | collective-permute-done | bytes 262176 | tf_op jit(solution)/shard_map/ppermute | solution.py:416
  162.3 10.4 %feed_forward.5 = (bf16[64,2048]{1,0:T(8,128)(2,1)}, bf16[64,2048]{1,0:T(8,128)(2,1)}) custom-call(bf16[64,2048]{1,0:T(8,128)(2,1)} %copy-done.35, bf16[64,2048]{1,0:T(8,128)(2,1)} %copy-done.36, bf16[2064,256]{1,0:T(8,128)(2,1)} %copy-done.17, bf16[2064,256]{1,0:T(8,128)(2,1)} %collective-permute-done.refs_2_.refs_3_, bf16[2064,256]{1,0:T(8,128)(2,1)} %copy-done.19, ...), custom_call_target="tpu_custom_call" | custom-call | flops 2147483648 | bytes 16777216 | tf_op jit(solution)/shard_map/feed_forward/pallas_call | solution.py:498
  174.6 10.4 %feed_forward.6 = (bf16[64,2048]{1,0:T(8,128)(2,1)}, bf16[64,2048]{1,0:T(8,128)(2,1)}) custom-call(bf16[64,2048]{1,0:T(8,128)(2,1)} %copy-done.34, bf16[64,2048]{1,0:T(8,128)(2,1)} %collective-permute-done.20.refs_1_, bf16[2064,256]{1,0:T(8,128)(2,1)} %copy-done.17, bf16[2064,256]{1,0:T(8,128)(2,1)} %collective-permute-done.refs_2_.refs_3_, ...), custom_call_target="tpu_custom_call" | custom-call | flops 2147483648 | bytes 16777216 | tf_op jit(solution)/shard_map/feed_forward/pallas_call | solution.py:498
  185.3 10.7 %feed_forward.7 = bf16[128,2048]{1,0:T(8,128)(2,1)} custom-call(bf16[128,2048]{1,0:T(8,128)(2,1)} %copy-done.30, bf16[2064,256]{1,0:T(8,128)(2,1)} %copy-done.17, bf16[2064,256]{1,0:T(8,128)(2,1)} %collective-permute-done.refs_2_.refs_3_, bf16[2064,256]{1,0:T(8,128)(2,1)} %copy-done.19, bf16[2064,256]{1,0:T(8,128)(2,1)} %collective-permute-done.8.refs_4_.refs_5_, ...), custom_call_target="tpu_custom_call" | custom-call | flops 2147483648 | bytes 16777216 | tf_op jit(solution)/shard_map/feed_forward/pallas_call | solution.py:498
  202.9 2.2 collective-permute-start.25
  205.1 10.4 %feed_forward.4.own_ref = bf16[128,2048]{1,0:T(8,128)(2,1)} custom-call(bf16[128,2048]{1,0:T(8,128)(2,1)} %copy-done, bf16[2064,256]{1,0:T(8,128)(2,1)} %copy-done.17, bf16[2064,256]{1,0:T(8,128)(2,1)} %collective-permute-done.refs_2_.refs_3_, bf16[2064,256]{1,0:T(8,128)(2,1)} %copy-done.19, bf16[2064,256]{1,0:T(8,128)(2,1)} %collective-permute-done.8.refs_4_.refs_5_, ...), custom_call_target="tpu_custom_call" | custom-call | flops 2147483648 | bytes 16777216 | tf_op jit(solution)/shard_map/feed_forward/pallas_call | solution.py:498
  215.6 5.6 %collective-permute-done.23.far_a_ref = bf16[64,2048]{1,0:T(8,128)(2,1)S(1)} collective-permute-done((bf16[64,2048]{1,0:T(8,128)(2,1)}, bf16[64,2048]{1,0:T(8,128)(2,1)S(1)}, u32[]{:S(2)}, u32[]{:S(2)}) %collective-permute-start.23) | collective-permute-done | bytes 262176 | tf_op jit(solution)/shard_map/ppermute | solution.py:416
  221.2 3.9 %collective-permute-done.25.far_b_ref = bf16[64,2048]{1,0:T(8,128)(2,1)S(1)} collective-permute-done((bf16[64,2048]{1,0:T(8,128)(2,1)}, bf16[64,2048]{1,0:T(8,128)(2,1)S(1)}, u32[]{:S(2)}, u32[]{:S(2)}) %collective-permute-start.25) | collective-permute-done | bytes 262176 | tf_op jit(solution)/shard_map/ppermute | solution.py:416
  (136 shorter events, 45.5 us)
Async XLA Ops:
  4.2 45.6 %all-to-all-start = ((bf16[32,72,256]{2,1,0:T(8,128)(2,1)}), bf16[32,72,256]{2,1,0:T(8,128)(2,1)S(1)}, u32[]{:S(2)}, u32[]{:S(2)}) async-start(bf16[32,72,256]{2,1,0:T(8,128)(2,1)} %bitcast), calls=%async_computation | async-start | bytes 2359296 | tf_op jit(solution)/shard_map/all_to_all | solution.py:616
  11.7 33.0 %collective-permute-start.1 = (bf16[2064,256]{1,0:T(8,128)(2,1)S(1)}, bf16[2064,256]{1,0:T(8,128)(2,1)}, u32[]{:S(2)}, u32[]{:S(2)}) collective-permute-start(bf16[2064,256]{1,0:T(8,128)(2,1)S(1)} %pad_maximum_fusion.refs_1_.refs_2_), channel_id=1, source_target_pairs={{0,8},{1,9},{2,10},{3,11},{4,12},{5,13},{6,14},{7,15},{8,0},{9,1},... | collective-permute-start | bytes 3170312 | tf_op jit(solution)/shard_map/ppermute | solution.py:416
  12.0 37.8 %collective-permute-start = (bf16[2064,256]{1,0:T(8,128)(2,1)S(1)}, bf16[2064,256]{1,0:T(8,128)(2,1)}, u32[]{:S(2)}, u32[]{:S(2)}) collective-permute-start(bf16[2064,256]{1,0:T(8,128)(2,1)S(1)} %pad_maximum_fusion.refs_1_.refs_2_), channel_id=1, source_target_pairs={{0,1},{1,0},{2,3},{3,2},{4,5},{5,4},{6,7},{7,6},{8,9},{9,8},{10,11... | collective-permute-start | bytes 3170312 | tf_op jit(solution)/shard_map/ppermute | solution.py:416
  13.7 31.0 %collective-permute-start.3 = (bf16[256,2048]{1,0:T(8,128)(2,1)}, bf16[256,2048]{1,0:T(8,128)(2,1)}, u32[]{:S(2)}, u32[]{:S(2)}) collective-permute-start(bf16[256,2048]{1,0:T(8,128)(2,1)} %refs_9_.1), channel_id=1, source_target_pairs={{0,8},{1,9},{2,10},{3,11},{4,12},{5,13},{6,14},{7,15},{8,0},{9,1},... | collective-permute-start | bytes 3145736 | tf_op jit(solution)/shard_map/ppermute | solution.py:416
  14.5 30.1 %collective-permute-start.2 = (bf16[1024,256]{1,0:T(8,128)(2,1)}, bf16[1024,256]{1,0:T(8,128)(2,1)}, u32[]{:S(2)}, u32[]{:S(2)}) collective-permute-start(bf16[1024,256]{1,0:T(8,128)(2,1)} %slice.15), channel_id=1, source_target_pairs={{0,2},{1,3},{2,0},{3,1},{4,6},{5,7},{6,4},{7,5},{8,10},{9,11},{10,... | collective-permute-start | bytes 1572872 | tf_op jit(solution)/shard_map/ppermute | solution.py:416
  49.8 26.0 %collective-permute-start.4 = (bf16[2064,256]{1,0:T(8,128)(2,1)}, bf16[2064,256]{1,0:T(8,128)(2,1)}, u32[]{:S(2)}, u32[]{:S(2)}) collective-permute-start(bf16[2064,256]{1,0:T(8,128)(2,1)} %collective-permute-done.refs_2_.refs_3_), channel_id=1, source_target_pairs={{0,8},{1,9},{2,10},{3,11},{4,12},{5,13},{6,14},{7,15},{8,0},{9,1},... | collective-permute-start | bytes 3170312 | tf_op jit(solution)/shard_map/ppermute | solution.py:416
  49.8 26.0 %collective-permute-start.6 = (bf16[256,2048]{1,0:T(8,128)(2,1)}, bf16[256,2048]{1,0:T(8,128)(2,1)}, u32[]{:S(2)}, u32[]{:S(2)}) collective-permute-start(bf16[256,2048]{1,0:T(8,128)(2,1)} %refs_9_.1), channel_id=1, source_target_pairs={{0,1},{1,0},{2,3},{3,2},{4,5},{5,4},{6,7},{7,6},{8,9},{9,8},{10,11... | collective-permute-start | bytes 3145736 | tf_op jit(solution)/shard_map/ppermute | solution.py:416
  50.2 21.9 %collective-permute-start.7 = (bf16[128,2048]{1,0:T(8,128)(2,1)}, bf16[128,2048]{1,0:T(8,128)(2,1)S(1)}, u32[]{:S(2)}, u32[]{:S(2)}) collective-permute-start(bf16[128,2048]{1,0:T(8,128)(2,1)} %get-tuple-element.111), channel_id=1, source_target_pairs={{0,2},{1,3},{2,0},{3,1},{4,6},{5,7},{6,4},{7,5},{8,10},{9,11},{10,... | collective-permute-start | bytes 1572872 | tf_op jit(solution)/shard_map/ppermute | solution.py:416
  51.8 23.9 %collective-permute-start.5 = (bf16[1040,256]{1,0:T(8,128)(2,1)}, bf16[1040,256]{1,0:T(8,128)(2,1)S(1)}, u32[]{:S(2)}, u32[]{:S(2)}) collective-permute-start(bf16[1040,256]{1,0:T(8,128)(2,1)} %fusion), channel_id=1, source_target_pairs={{0,2},{1,3},{2,0},{3,1},{4,6},{5,7},{6,4},{7,5},{8,10},{9,11},{10,... | collective-permute-start | bytes 1597448 | tf_op jit(solution)/shard_map/ppermute | solution.py:416
  76.6 44.1 %all-to-all-start.1 = ((bf16[32,72,256]{2,1,0:T(8,128)(2,1)}), bf16[32,72,256]{2,1,0:T(8,128)(2,1)S(1)}, u32[]{:S(2)}, u32[]{:S(2)}) async-start(bf16[32,72,256]{2,1,0:T(8,128)(2,1)} %attend_prefix.1), calls=%async_computation.1 | async-start | bytes 2359296 | tf_op jit(solution)/shard_map/all_to_all | solution.py:651
  84.0 32.6 %collective-permute-start.9 = (bf16[2064,256]{1,0:T(8,128)(2,1)S(1)}, bf16[2064,256]{1,0:T(8,128)(2,1)S(1)}, u32[]{:S(2)}, u32[]{:S(2)}) collective-permute-start(bf16[2064,256]{1,0:T(8,128)(2,1)S(1)} %constant_dynamic-update-slice_fusion.refs_3_.refs_4_), channel_id=1, source_target_pairs={{0,8},{1,9},{2,10},{3,11},{4,12},{5,13},{6,14},{7,15},{8,0},{9,1},... | collective-permute-start | bytes 3170312 | tf_op jit(solution)/shard_map/ppermute | solution.py:416
  84.3 36.4 %collective-permute-start.8 = (bf16[2064,256]{1,0:T(8,128)(2,1)S(1)}, bf16[2064,256]{1,0:T(8,128)(2,1)}, u32[]{:S(2)}, u32[]{:S(2)}) collective-permute-start(bf16[2064,256]{1,0:T(8,128)(2,1)S(1)} %constant_dynamic-update-slice_fusion.refs_3_.refs_4_), channel_id=1, source_target_pairs={{0,1},{1,0},{2,3},{3,2},{4,5},{5,4},{6,7},{7,6},{8,9},{9,8},{10,11... | collective-permute-start | bytes 3170312 | tf_op jit(solution)/shard_map/ppermute | solution.py:416
  86.0 30.6 %collective-permute-start.11 = (bf16[256,2048]{1,0:T(8,128)(2,1)}, bf16[256,2048]{1,0:T(8,128)(2,1)S(1)}, u32[]{:S(2)}, u32[]{:S(2)}) collective-permute-start(bf16[256,2048]{1,0:T(8,128)(2,1)} %collective-permute-done.6.refs_10_.refs_11_), channel_id=1, source_target_pairs={{0,8},{1,9},{2,10},{3,11},{4,12},{5,13},{6,14},{7,15},{8,0},{9,1},... | collective-permute-start | bytes 3145736 | tf_op jit(solution)/shard_map/ppermute | solution.py:416
  86.1 29.5 %collective-permute-start.10 = (bf16[128,2048]{1,0:T(8,128)(2,1)S(1)}, bf16[128,2048]{1,0:T(8,128)(2,1)S(1)}, u32[]{:S(2)}, u32[]{:S(2)}) collective-permute-start(bf16[128,2048]{1,0:T(8,128)(2,1)S(1)} %copy-done.31), channel_id=1, source_target_pairs={{0,2},{1,3},{2,0},{3,1},{4,6},{5,7},{6,4},{7,5},{8,10},{9,11},{10,... | collective-permute-start | bytes 1572872 | tf_op jit(solution)/shard_map/ppermute | solution.py:416
  122.7 35.9 %collective-permute-start.16 = (bf16[2064,256]{1,0:T(8,128)(2,1)}, bf16[2064,256]{1,0:T(8,128)(2,1)S(1)}, u32[]{:S(2)}, u32[]{:S(2)}) collective-permute-start(bf16[2064,256]{1,0:T(8,128)(2,1)} %collective-permute-done.8.refs_4_.refs_5_), channel_id=1, source_target_pairs={{0,8},{1,9},{2,10},{3,11},{4,12},{5,13},{6,14},{7,15},{8,0},{9,1},... | collective-permute-start | bytes 3170312 | tf_op jit(solution)/shard_map/ppermute | solution.py:416
  122.8 35.8 %collective-permute-start.18 = (bf16[256,2048]{1,0:T(8,128)(2,1)S(1)}, bf16[256,2048]{1,0:T(8,128)(2,1)S(1)}, u32[]{:S(2)}, u32[]{:S(2)}) collective-permute-start(bf16[256,2048]{1,0:T(8,128)(2,1)S(1)} %copy-done.18), channel_id=1, source_target_pairs={{0,8},{1,9},{2,10},{3,11},{4,12},{5,13},{6,14},{7,15},{8,0},{9,1},... | collective-permute-start | bytes 3145736 | tf_op jit(solution)/shard_map/ppermute | solution.py:416
  123.2 35.3 %collective-permute-start.17 = (bf16[256,2048]{1,0:T(8,128)(2,1)S(1)}, bf16[256,2048]{1,0:T(8,128)(2,1)S(1)}, u32[]{:S(2)}, u32[]{:S(2)}) collective-permute-start(bf16[256,2048]{1,0:T(8,128)(2,1)S(1)} %copy-done.18), channel_id=1, source_target_pairs={{0,1},{1,0},{2,3},{3,2},{4,5},{5,4},{6,7},{7,6},{8,9},{9,8},{10,11... | collective-permute-start | bytes 3145736 | tf_op jit(solution)/shard_map/ppermute | solution.py:416
  123.6 14.5 %collective-permute-start.12 = (bf16[64,2048]{1,0:T(8,128)(2,1)S(1)}, bf16[64,2048]{1,0:T(8,128)(2,1)S(1)}, u32[]{:S(2)}, u32[]{:S(2)}) collective-permute-start(bf16[64,2048]{1,0:T(8,128)(2,1)S(1)} %get-tuple-element.146), channel_id=1, source_target_pairs={{0,4},{1,5},{2,6},{3,7},{4,0},{5,1},{6,2},{7,3},{8,12},{9,13},{10,... | collective-permute-start | bytes 786440 | tf_op jit(solution)/shard_map/ppermute | solution.py:416
  138.1 20.4 %collective-permute-start.15 = (bf16[128,2048]{1,0:T(8,128)(2,1)S(1)}, bf16[128,2048]{1,0:T(8,128)(2,1)S(1)}, u32[]{:S(2)}, u32[]{:S(2)}) collective-permute-start(bf16[128,2048]{1,0:T(8,128)(2,1)S(1)} %get-tuple-element.148.refs_0_.hidden_ref), channel_id=1, source_target_pairs={{0,16},{1,17},{2,18},{3,19},{4,20},{5,21},{6,22},{7,23},{8,24},{9,... | collective-permute-start | bytes 1572872 | tf_op jit(solution)/shard_map/ppermute | solution.py:416
  158.6 14.1 %collective-permute-start.20 = (bf16[64,2048]{1,0:T(8,128)(2,1)S(1)}, bf16[64,2048]{1,0:T(8,128)(2,1)}, u32[]{:S(2)}, u32[]{:S(2)}) collective-permute-start(bf16[64,2048]{1,0:T(8,128)(2,1)S(1)} %collective-permute-done.13.refs_0_), channel_id=1, source_target_pairs={{0,16},{1,17},{2,18},{3,19},{4,20},{5,21},{6,22},{7,23},{8,24},{9,... | collective-permute-start | bytes 786440 | tf_op jit(solution)/shard_map/ppermute | solution.py:416
  185.0 15.4 %collective-permute-start.24 = (bf16[64,2048]{1,0:T(8,128)(2,1)}, bf16[64,2048]{1,0:T(8,128)(2,1)S(1)}, u32[]{:S(2)}, u32[]{:S(2)}) collective-permute-start(bf16[64,2048]{1,0:T(8,128)(2,1)} %get-tuple-element.185), channel_id=1, source_target_pairs={{0,16},{1,17},{2,18},{3,19},{4,20},{5,21},{6,22},{7,23},{8,24},{9,... | collective-permute-start | bytes 786440 | tf_op jit(solution)/shard_map/ppermute | solution.py:416
  196.0 29.1 %collective-permute-start.22 = (bf16[128,2048]{1,0:T(8,128)(2,1)}, bf16[128,2048]{1,0:T(8,128)(2,1)S(1)}, u32[]{:S(2)}, u32[]{:S(2)}) collective-permute-start(bf16[128,2048]{1,0:T(8,128)(2,1)} %feed_forward.7), channel_id=1, source_target_pairs={{0,16},{1,17},{2,18},{3,19},{4,20},{5,21},{6,22},{7,23},{8,24},{9,... | collective-permute-start | bytes 1572872 | tf_op jit(solution)/shard_map/ppermute | solution.py:416
  199.6 21.6 %collective-permute-start.23 = (bf16[64,2048]{1,0:T(8,128)(2,1)}, bf16[64,2048]{1,0:T(8,128)(2,1)S(1)}, u32[]{:S(2)}, u32[]{:S(2)}) collective-permute-start(bf16[64,2048]{1,0:T(8,128)(2,1)} %add_rows.2), channel_id=1, source_target_pairs={{0,4},{1,5},{2,6},{3,7},{4,0},{5,1},{6,2},{7,3},{8,12},{9,13},{10,... | collective-permute-start | bytes 786440 | tf_op jit(solution)/shard_map/ppermute | solution.py:416
  202.9 22.2 %collective-permute-start.25 = (bf16[64,2048]{1,0:T(8,128)(2,1)}, bf16[64,2048]{1,0:T(8,128)(2,1)S(1)}, u32[]{:S(2)}, u32[]{:S(2)}) collective-permute-start(bf16[64,2048]{1,0:T(8,128)(2,1)} %add_rows.3), channel_id=1, source_target_pairs={{0,4},{1,5},{2,6},{3,7},{4,0},{5,1},{6,2},{7,3},{8,12},{9,13},{10,... | collective-permute-start | bytes 786440 | tf_op jit(solution)/shard_map/ppermute | solution.py:416
  (44 other events, 530.1 us)

commit v7 on v6

--- a/solution.py
+++ b/solution.py
@@ -453,42 +453,35 @@
             held.append(pltpu.make_async_copy(downs.pop(0), target, sems.at[part, 1, piece]))
             begin += height
         copies.append(held)
-    ahead = 4
-
-    def start(at):
-        if at < len(copies):
-            for copy in copies[at]:
-                copy.start()
-
-    def arrive(at):
-        for copy in copies[at]:
-            copy.wait()
-        start(at + ahead)
-
-    for at in range(ahead):
-        start(at)
+    for held in copies:
+        for copy in held:
+            copy.start()
     rows = jnp.concatenate([ref[...] for ref in row_refs], axis=0)
     activations = []
     for part in range(parts):
-        arrive(part)
+        for copy in copies[part]:
+            copy.wait()
         product = jnp.dot(
             rows, up_ref[part, :model_width, :], preferred_element_type=jnp.float32
         )
         offset = up_ref[part, model_width:, :].astype(jnp.float32)[0:1]
         activations.append(jax.nn.gelu(product + offset, approximate=True).astype(jnp.bfloat16))
-    for part in range(parts):
-        arrive(parts + part)
+    for held in copies[parts:]:
+        for copy in held:
+            copy.wait()
     total = jnp.dot(
         jnp.concatenate(activations, axis=1), down_ref[...], preferred_element_type=jnp.float32
     ).astype(jnp.bfloat16)
-    height = row_refs[0].shape[0]
-    for piece in range(pieces):
-        out_refs[piece][...] = total[piece * height : (piece + 1) * height]
+    begin = 0
+    for out_ref in out_refs:
+        height = out_ref.shape[0]
+        out_ref[...] = total[begin : begin + height]
+        begin += height
 
 
 def feed_forward(rows, ups, downs):
     pieces, parts = len(rows), len(ups)
-    height, model_width = rows[0].shape
+    row_total, model_width = sum(piece.shape[0] for piece in rows), rows[0].shape[1]
     up_plan = [[piece.shape[0] for piece in block] for block in ups]
     down_plan = [[piece.shape[0] for piece in block] for block in downs]
     up_rows, down_rows = sum(up_plan[0]), sum(down_plan[0])
@@ -507,9 +500,9 @@
         ],
         compiler_params=pltpu.CompilerParams(vmem_limit_bytes=58 * mebibyte),
         cost_estimate=pl.CostEstimate(
-            flops=4 * pieces * height * model_width * parts * units,
+            flops=4 * row_total * model_width * parts * units,
             bytes_accessed=4 * parts * model_width * units,
-            transcendentals=pieces * height * parts * units,
+            transcendentals=row_total * parts * units,
         ),
         name="feed_forward",
     )(*rows, *flat)
@@ -656,6 +649,7 @@
     downs[core_mask ^ low_mask] = swap(downs[low_mask], core_mask)
     down_second = swap(down_pieces[1], high_mask)
     downs[high_mask] = (jnp.concatenate([down_first, down_second], axis=0),)
+    downs[core_mask ^ high_mask] = swap(downs[high_mask], core_mask)
     ups[low_mask ^ high_mask] = swap(ups[high_mask], low_mask)
     answer, ups, downs = lax.optimization_barrier((answer, ups, downs))
 
@@ -667,9 +661,8 @@
         ((hidden_a, hidden_b, hidden), ups, downs)
     )
     far_a = swap(hidden_a, far_mask)
-    near = swap(tie(hidden, far_a), near_mask)
+    near = swap(hidden, near_mask)
     downs[low_mask ^ high_mask] = swap(downs[high_mask], low_mask)
-    downs[core_mask ^ high_mask] = swap(downs[high_mask], core_mask)
     ups = complete(ups, group_masks + column_masks)
     far_b = swap(tie(hidden_b, far_a), far_mask)
     cross_a = swap(far_a, near_mask)
@@ -690,13 +683,14 @@
     cross_sum_a, far_part_b, cross_part_b = lax.optimization_barrier(
         (cross_sum_a, far_part_b, cross_part_b)
     )
-    far_sum_a = swap(add_rows(far_part_a, cross_sum_a), far_mask)
     cross_sum_b = swap(cross_part_b, near_mask)
-    (near_part,) = feed_forward([tie(near, cross_part_b)], ups, downs)
+    joined_a = add_rows(far_part_a, cross_sum_a)
+    far_sum_a = swap(joined_a, far_mask)
+    near, hidden = tie((near, hidden), joined_a)
+    near_part, own_part = feed_forward([near, hidden], ups, downs)
     near_sum = swap(near_part, near_mask)
     cross_sum_b, near_part = lax.optimization_barrier((cross_sum_b, near_part))
     far_sum_b = swap(add_rows(far_part_b, cross_sum_b), far_mask)
-    (own_part,) = feed_forward([tie(hidden, near_part)], ups, downs)
     return finish_rows(
         hidden, own_part, near_sum, far_sum_a, far_sum_b, down_bias, out_gain, out_shift
     )

time: 228 us -> 220 us (0.965)
  Pallas kernels: 73.8 us -> 61.7 us
  waiting for transfers between devices: 83 us -> 89.4 us
    pallas_call x4 -> x3, Pallas kernels: 41.9 us -> 29.9 us  [feed_forward(): pl.pallas_call(functools.partial(mlp_kernel, pieces, up_plan, down_plan),...]
    ppermute x26, waiting for transfers between devices: 83 us -> 89.4 us  [swap(): lax.ppermute(leaf, ('grp', 'dev'), pairs)]
    unnamed x83 -> x92, local copies, waits for them, and re-layouts: 17.5 us -> 17.1 us
  transfers between devices with their start and end apart: 28 -> 28, of which waited for: 11 -> 10; matrix products, arithmetic and copies ran while one was open for 10% -> 10% of each run, Pallas kernels for 30% -> 25%
where the time goes in v7:
time: 220 us
  waiting for transfers between devices  89.4 us (41%)
  Pallas kernels  61.7 us (28%)
  starting transfers between devices  37.4 us (17%)
  local copies, waits for them, and re-layouts  28.4 us (13%)
    ppermute x26, waiting for transfers between devices, swap(): lax.ppermute(leaf, ('grp', 'dev'), pairs)  89.4 us
    pallas_call x3, Pallas kernels, feed_forward(): pl.pallas_call(functools.partial(mlp_kernel, pieces, up_plan, down_plan),...  29.9 us
    ppermute x26, starting transfers between devices, swap(): lax.ppermute(leaf, ('grp', 'dev'), pairs)  24.1 us
    pallas_call x1, Pallas kernels, attend_prefix(): pl.pallas_call(far_kernel, out_shape=jax.ShapeDtypeStruct((sources, capac...  18.6 us
    unnamed x92, local copies, waits for them, and re-layouts  17.1 us
    all_to_all x1, starting transfers between devices, on_device(): lax.all_to_all(outgoing.reshape(sources, capacity + STAT_ROWS, part_width...  7.3 us
    all_to_all x1, starting transfers between devices, on_device(): lax.all_to_all(answer_part, ('grp', 'dev'), split_axis=0, concat_axis=0,...  6.04 us
    pallas_call x1, Pallas kernels, attend_suffix(): pl.pallas_call(functools.partial(own_kernel, local_heads), out_shape=(jax...  4.48 us
  transfers between devices with their start and end apart: 28, of which 10 were waited for; matrix products, arithmetic and copies ran while one was open for 10% of the time, Pallas kernels for 25%

profile of v7, /device:TPU:0, one launch (start us, length us, event | category | flops | bytes accessed | tf_op | source)
XLA Modules:
  0.0 219.6 jit_solution(15087034385996312676)
XLA Ops:
  4.2 7.3 %all-to-all-start = ((bf16[32,72,256]{2,1,0:T(8,128)(2,1)}), bf16[32,72,256]{2,1,0:T(8,128)(2,1)S(1)}, u32[]{:S(2)}, u32[]{:S(2)}) async-start(bf16[32,72,256]{2,1,0:T(8,128)(2,1)} %bitcast), calls=%async_computation | async-start | bytes 2359296 | tf_op jit(solution)/shard_map/all_to_all | solution.py:609
  16.9 4.5 %attend_suffix.1 = (f32[128,2048]{1,0:T(8,128)S(1)}, f32[128,128]{1,0:T(8,128)S(1)}, f32[128,128]{1,0:T(8,128)S(1)}) custom-call(s32[1,4]{1,0:T(1,128)S(1)} %copy-done.12, bf16[128,2048]{1,0:T(8,128)(2,1)S(1)} %copy-done.3, bf16[128,2048]{1,0:T(8,128)(2,1)S(1)} %copy-done.15, bf16[128,2048]{1,0:T(8,128)(2,1)S(1)} %copy-done.16), custom_call_target="tpu_custom_call" | custom-call | flops 1342177280 | bytes 2097152 | tf_op jit(solution)/shard_map/attend_suffix/pallas_call | solution.py:295
  21.4 4.1 %copy.18 = bf16[1,4096,256]{1,2,0:T(8,128)(2,1)} copy(bf16[1,4096,256]{2,1,0:T(8,128)(2,1)} %param.22) | data formatting | bytes 4194304 | tf_op args[6]
  25.5 4.1 %copy.19 = bf16[1,4096,256]{1,2,0:T(8,128)(2,1)} copy(bf16[1,4096,256]{2,1,0:T(8,128)(2,1)} %param.23) | data formatting | bytes 4194304 | tf_op args[7]
  29.6 4.1 %copy.20 = bf16[4096,2,128]{2,0,1:T(8,128)(2,1)} copy(bf16[4096,2,128]{0,2,1:T(8,128)(2,1)} %bitcast.19) | data formatting | bytes 4194304 | tf_op jit(solution)/shard_map/reshape;squeeze | solution.py:621
  33.7 4.0 %concatenate.13.values_hbm = bf16[2,4096,256]{2,1,0:T(8,128)(2,1)} pad(bf16[2,4096,128]{2,1,0:T(8,128)(2,1)} %bitcast.18, bf16[]{:T(256)} %constant.0.clone.1), padding=0_0x0_0x0_128 | pad | bytes 6291458 | tf_op jit(solution)/shard_map/concatenate | solution.py:622
  37.7 2.3 %fusion.1 = (bf16[128,2048]{1,0:T(8,128)(2,1)}, bf16[128,2048]{1,0:T(8,128)(2,1)}) fusion(bf16[256,2048]{1,0:T(8,128)(2,1)} %refs_10_.2), kind=kLoop, calls=%fused_computation.9 | loop fusion | bytes 2097152 | tf_op jit(solution)/shard_map/slice | solution.py:605
  40.0 4.7 %collective-permute-done.2 = bf16[1024,256]{1,0:T(8,128)(2,1)} collective-permute-done((bf16[1024,256]{1,0:T(8,128)(2,1)}, bf16[1024,256]{1,0:T(8,128)(2,1)}, u32[]{:S(2)}, u32[]{:S(2)}) %collective-permute-start.2) | collective-permute-done | bytes 524320 | tf_op jit(solution)/shard_map/ppermute | solution.py:416
  44.7 5.1 %collective-permute-done.refs_3_ = bf16[2064,256]{1,0:T(8,128)(2,1)} collective-permute-done((bf16[2064,256]{1,0:T(8,128)(2,1)S(1)}, bf16[2064,256]{1,0:T(8,128)(2,1)}, u32[]{:S(2)}, u32[]{:S(2)}) %collective-permute-start) | collective-permute-done | bytes 1056800 | tf_op jit(solution)/shard_map/ppermute | solution.py:416
  53.4 18.6 %attend_prefix.1 = bf16[32,72,256]{2,1,0:T(8,128)(2,1)} custom-call(s32[32]{0:T(128)} %convert_reduce_fusion.counts_ref, bf16[32,72,256]{2,1,0:T(8,128)(2,1)} %copy-done.29, bf16[256,4096]{1,0:T(8,128)(2,1)} %bitcast.20, bf16[2,4096,256]{2,1,0:T(8,128)(2,1)} %concatenate.13.values_hbm), custom_call_target="tpu_custom_call" | custom-call | flops 8589934592 | bytes 8388608 | tf_op jit(solution)/shard_map/attend_prefix/pallas_call | solution.py:222
  72.1 3.7 %collective-permute-done.5 = bf16[1040,256]{1,0:T(8,128)(2,1)S(1)} collective-permute-done((bf16[1040,256]{1,0:T(8,128)(2,1)}, bf16[1040,256]{1,0:T(8,128)(2,1)S(1)}, u32[]{:S(2)}, u32[]{:S(2)}) %collective-permute-start.5) | collective-permute-done | bytes 532512 | tf_op jit(solution)/shard_map/ppermute | solution.py:416
  76.7 6.0 %all-to-all-start.1 = ((bf16[32,72,256]{2,1,0:T(8,128)(2,1)}), bf16[32,72,256]{2,1,0:T(8,128)(2,1)S(1)}, u32[]{:S(2)}, u32[]{:S(2)}) async-start(bf16[32,72,256]{2,1,0:T(8,128)(2,1)} %attend_prefix.1), calls=%async_computation.1 | async-start | bytes 2359296 | tf_op jit(solution)/shard_map/all_to_all | solution.py:644
  87.6 28.0 %collective-permute-done.10 = bf16[128,2048]{1,0:T(8,128)(2,1)S(1)} collective-permute-done((bf16[128,2048]{1,0:T(8,128)(2,1)S(1)}, bf16[128,2048]{1,0:T(8,128)(2,1)S(1)}, u32[]{:S(2)}, u32[]{:S(2)}) %collective-permute-start.10) | collective-permute-done | bytes 524320 | tf_op jit(solution)/shard_map/ppermute | solution.py:416
  115.8 4.9 %collective-permute-done.8.refs_5_ = bf16[2064,256]{1,0:T(8,128)(2,1)S(1)} collective-permute-done((bf16[2064,256]{1,0:T(8,128)(2,1)S(1)}, bf16[2064,256]{1,0:T(8,128)(2,1)S(1)}, u32[]{:S(2)}, u32[]{:S(2)}) %collective-permute-start.8) | collective-permute-done | bytes 1056800 | tf_op jit(solution)/shard_map/ppermute | solution.py:416
  121.8 1.9 merge_parts.1
  124.3 2.2 %collective-permute-start.13 = (bf16[64,2048]{1,0:T(8,128)(2,1)S(1)}, bf16[64,2048]{1,0:T(8,128)(2,1)S(1)}, u32[]{:S(2)}, u32[]{:S(2)}) collective-permute-start(bf16[64,2048]{1,0:T(8,128)(2,1)S(1)} %get-tuple-element.150), channel_id=1, source_target_pairs={{0,4},{1,5},{2,6},{3,7},{4,0},{5,1},{6,2},{7,3},{8,12},{9,13},{10,... | collective-permute-start | bytes 786440 | tf_op jit(solution)/shard_map/ppermute | solution.py:416
  128.2 11.0 %collective-permute-done.13.refs_0_ = bf16[64,2048]{1,0:T(8,128)(2,1)S(1)} collective-permute-done((bf16[64,2048]{1,0:T(8,128)(2,1)S(1)}, bf16[64,2048]{1,0:T(8,128)(2,1)S(1)}, u32[]{:S(2)}, u32[]{:S(2)}) %collective-permute-start.13) | collective-permute-done | bytes 262176 | tf_op jit(solution)/shard_map/ppermute | solution.py:416
  140.8 12.5 %collective-permute-done.14.refs_0_ = bf16[64,2048]{1,0:T(8,128)(2,1)S(1)} collective-permute-done((bf16[64,2048]{1,0:T(8,128)(2,1)S(1)}, bf16[64,2048]{1,0:T(8,128)(2,1)S(1)}, u32[]{:S(2)}, u32[]{:S(2)}) %collective-permute-start.14) | collective-permute-done | bytes 262176 | tf_op jit(solution)/shard_map/ppermute | solution.py:416
  157.1 9.0 %feed_forward.3 = (bf16[64,2048]{1,0:T(8,128)(2,1)}, bf16[64,2048]{1,0:T(8,128)(2,1)}) custom-call(bf16[64,2048]{1,0:T(8,128)(2,1)} %copy-done.37, bf16[64,2048]{1,0:T(8,128)(2,1)} %copy-done.38, bf16[2064,256]{1,0:T(8,128)(2,1)} %copy-done.17, bf16[2064,256]{1,0:T(8,128)(2,1)} %collective-permute-done.refs_3_, bf16[2064,256]{1,0:T(8,128)(2,1)} %copy-done.18, ...), custom_call_target="tpu_custom_call" | custom-call | flops 2147483648 | bytes 16777216 | tf_op jit(solution)/shard_map/feed_forward/pallas_call | solution.py:491
  167.7 9.0 %feed_forward.4 = (bf16[64,2048]{1,0:T(8,128)(2,1)}, bf16[64,2048]{1,0:T(8,128)(2,1)}) custom-call(bf16[64,2048]{1,0:T(8,128)(2,1)} %copy-done.36, bf16[64,2048]{1,0:T(8,128)(2,1)} %copy-done.39, bf16[2064,256]{1,0:T(8,128)(2,1)} %copy-done.17, bf16[2064,256]{1,0:T(8,128)(2,1)} %collective-permute-done.refs_3_, bf16[2064,256]{1,0:T(8,128)(2,1)} %copy-done.18, ...), custom_call_target="tpu_custom_call" | custom-call | flops 2147483648 | bytes 16777216 | tf_op jit(solution)/shard_map/feed_forward/pallas_call | solution.py:491
  180.0 11.8 %feed_forward.5 = (bf16[128,2048]{1,0:T(8,128)(2,1)}, bf16[128,2048]{1,0:T(8,128)(2,1)}) custom-call(bf16[128,2048]{1,0:T(8,128)(2,1)} %copy-done.32, bf16[128,2048]{1,0:T(8,128)(2,1)} %copy-done, bf16[2064,256]{1,0:T(8,128)(2,1)} %copy-done.17, bf16[2064,256]{1,0:T(8,128)(2,1)} %collective-permute-done.refs_3_, bf16[2064,256]{1,0:T(8,128)(2,1)} %copy-done.18, ...), custom_call_target="tpu_custom_call" | custom-call | flops 4294967296 | bytes 16777216 | tf_op jit(solution)/shard_map/feed_forward/pallas_call | solution.py:491
  195.8 2.9 %collective-permute-start.25 = (bf16[64,2048]{1,0:T(8,128)(2,1)}, bf16[64,2048]{1,0:T(8,128)(2,1)S(1)}, u32[]{:S(2)}, u32[]{:S(2)}) collective-permute-start(bf16[64,2048]{1,0:T(8,128)(2,1)} %add_rows.3), channel_id=1, source_target_pairs={{0,4},{1,5},{2,6},{3,7},{4,0},{5,1},{6,2},{7,3},{8,12},{9,13},{10,... | collective-permute-start | bytes 786440 | tf_op jit(solution)/shard_map/ppermute | solution.py:416
  198.7 12.8 %collective-permute-done.23.far_a_ref = bf16[64,2048]{1,0:T(8,128)(2,1)S(1)} collective-permute-done((bf16[64,2048]{1,0:T(8,128)(2,1)S(1)}, bf16[64,2048]{1,0:T(8,128)(2,1)S(1)}, u32[]{:S(2)}, u32[]{:S(2)}) %collective-permute-start.23) | collective-permute-done | bytes 262176 | tf_op jit(solution)/shard_map/ppermute | solution.py:416
  211.6 5.5 %collective-permute-done.25.far_b_ref = bf16[64,2048]{1,0:T(8,128)(2,1)S(1)} collective-permute-done((bf16[64,2048]{1,0:T(8,128)(2,1)}, bf16[64,2048]{1,0:T(8,128)(2,1)S(1)}, u32[]{:S(2)}, u32[]{:S(2)}) %collective-permute-start.25) | collective-permute-done | bytes 262176 | tf_op jit(solution)/shard_map/ppermute | solution.py:416
  (144 shorter events, 38.9 us)
Async XLA Ops:
  4.2 45.6 %all-to-all-start = ((bf16[32,72,256]{2,1,0:T(8,128)(2,1)}), bf16[32,72,256]{2,1,0:T(8,128)(2,1)S(1)}, u32[]{:S(2)}, u32[]{:S(2)}) async-start(bf16[32,72,256]{2,1,0:T(8,128)(2,1)} %bitcast), calls=%async_computation | async-start | bytes 2359296 | tf_op jit(solution)/shard_map/all_to_all | solution.py:609
  11.7 33.0 %collective-permute-start.1 = (bf16[2064,256]{1,0:T(8,128)(2,1)S(1)}, bf16[2064,256]{1,0:T(8,128)(2,1)}, u32[]{:S(2)}, u32[]{:S(2)}) collective-permute-start(bf16[2064,256]{1,0:T(8,128)(2,1)S(1)} %pad_maximum_fusion.refs_2_), channel_id=1, source_target_pairs={{0,8},{1,9},{2,10},{3,11},{4,12},{5,13},{6,14},{7,15},{8,0},{9,1},... | collective-permute-start | bytes 3170312 | tf_op jit(solution)/shard_map/ppermute | solution.py:416
  12.0 37.8 %collective-permute-start = (bf16[2064,256]{1,0:T(8,128)(2,1)S(1)}, bf16[2064,256]{1,0:T(8,128)(2,1)}, u32[]{:S(2)}, u32[]{:S(2)}) collective-permute-start(bf16[2064,256]{1,0:T(8,128)(2,1)S(1)} %pad_maximum_fusion.refs_2_), channel_id=1, source_target_pairs={{0,1},{1,0},{2,3},{3,2},{4,5},{5,4},{6,7},{7,6},{8,9},{9,8},{10,11... | collective-permute-start | bytes 3170312 | tf_op jit(solution)/shard_map/ppermute | solution.py:416
  13.7 31.0 %collective-permute-start.3 = (bf16[256,2048]{1,0:T(8,128)(2,1)}, bf16[256,2048]{1,0:T(8,128)(2,1)}, u32[]{:S(2)}, u32[]{:S(2)}) collective-permute-start(bf16[256,2048]{1,0:T(8,128)(2,1)} %refs_10_.2), channel_id=1, source_target_pairs={{0,8},{1,9},{2,10},{3,11},{4,12},{5,13},{6,14},{7,15},{8,0},{9,1},... | collective-permute-start | bytes 3145736 | tf_op jit(solution)/shard_map/ppermute | solution.py:416
  14.6 30.1 %collective-permute-start.2 = (bf16[1024,256]{1,0:T(8,128)(2,1)}, bf16[1024,256]{1,0:T(8,128)(2,1)}, u32[]{:S(2)}, u32[]{:S(2)}) collective-permute-start(bf16[1024,256]{1,0:T(8,128)(2,1)} %slice.15), channel_id=1, source_target_pairs={{0,2},{1,3},{2,0},{3,1},{4,6},{5,7},{6,4},{7,5},{8,10},{9,11},{10,... | collective-permute-start | bytes 1572872 | tf_op jit(solution)/shard_map/ppermute | solution.py:416
  49.8 26.0 %collective-permute-start.4 = (bf16[2064,256]{1,0:T(8,128)(2,1)}, bf16[2064,256]{1,0:T(8,128)(2,1)}, u32[]{:S(2)}, u32[]{:S(2)}) collective-permute-start(bf16[2064,256]{1,0:T(8,128)(2,1)} %collective-permute-done.refs_3_), channel_id=1, source_target_pairs={{0,8},{1,9},{2,10},{3,11},{4,12},{5,13},{6,14},{7,15},{8,0},{9,1},... | collective-permute-start | bytes 3170312 | tf_op jit(solution)/shard_map/ppermute | solution.py:416
  49.8 26.0 %collective-permute-start.6 = (bf16[256,2048]{1,0:T(8,128)(2,1)}, bf16[256,2048]{1,0:T(8,128)(2,1)}, u32[]{:S(2)}, u32[]{:S(2)}) collective-permute-start(bf16[256,2048]{1,0:T(8,128)(2,1)} %refs_10_.2), channel_id=1, source_target_pairs={{0,1},{1,0},{2,3},{3,2},{4,5},{5,4},{6,7},{7,6},{8,9},{9,8},{10,11... | collective-permute-start | bytes 3145736 | tf_op jit(solution)/shard_map/ppermute | solution.py:416
  50.2 21.8 %collective-permute-start.7 = (bf16[128,2048]{1,0:T(8,128)(2,1)}, bf16[128,2048]{1,0:T(8,128)(2,1)S(1)}, u32[]{:S(2)}, u32[]{:S(2)}) collective-permute-start(bf16[128,2048]{1,0:T(8,128)(2,1)} %get-tuple-element.115), channel_id=1, source_target_pairs={{0,2},{1,3},{2,0},{3,1},{4,6},{5,7},{6,4},{7,5},{8,10},{9,11},{10,... | collective-permute-start | bytes 1572872 | tf_op jit(solution)/shard_map/ppermute | solution.py:416
  51.9 23.9 %collective-permute-start.5 = (bf16[1040,256]{1,0:T(8,128)(2,1)}, bf16[1040,256]{1,0:T(8,128)(2,1)S(1)}, u32[]{:S(2)}, u32[]{:S(2)}) collective-permute-start(bf16[1040,256]{1,0:T(8,128)(2,1)} %fusion), channel_id=1, source_target_pairs={{0,2},{1,3},{2,0},{3,1},{4,6},{5,7},{6,4},{7,5},{8,10},{9,11},{10,... | collective-permute-start | bytes 1597448 | tf_op jit(solution)/shard_map/ppermute | solution.py:416
  76.7 45.1 %all-to-all-start.1 = ((bf16[32,72,256]{2,1,0:T(8,128)(2,1)}), bf16[32,72,256]{2,1,0:T(8,128)(2,1)S(1)}, u32[]{:S(2)}, u32[]{:S(2)}) async-start(bf16[32,72,256]{2,1,0:T(8,128)(2,1)} %attend_prefix.1), calls=%async_computation.1 | async-start | bytes 2359296 | tf_op jit(solution)/shard_map/all_to_all | solution.py:644
  82.7 32.8 %collective-permute-start.10 = (bf16[128,2048]{1,0:T(8,128)(2,1)S(1)}, bf16[128,2048]{1,0:T(8,128)(2,1)S(1)}, u32[]{:S(2)}, u32[]{:S(2)}) collective-permute-start(bf16[128,2048]{1,0:T(8,128)(2,1)S(1)} %copy-done.35), channel_id=1, source_target_pairs={{0,2},{1,3},{2,0},{3,1},{4,6},{5,7},{6,4},{7,5},{8,10},{9,11},{10,... | collective-permute-start | bytes 1572872 | tf_op jit(solution)/shard_map/ppermute | solution.py:416
  85.8 30.0 %collective-permute-start.9 = (bf16[2064,256]{1,0:T(8,128)(2,1)S(1)}, bf16[2064,256]{1,0:T(8,128)(2,1)S(1)}, u32[]{:S(2)}, u32[]{:S(2)}) collective-permute-start(bf16[2064,256]{1,0:T(8,128)(2,1)S(1)} %constant_dynamic-update-slice_fusion.refs_4_), channel_id=1, source_target_pairs={{0,8},{1,9},{2,10},{3,11},{4,12},{5,13},{6,14},{7,15},{8,0},{9,1},... | collective-permute-start | bytes 3170312 | tf_op jit(solution)/shard_map/ppermute | solution.py:416
  85.8 34.8 %collective-permute-start.8 = (bf16[2064,256]{1,0:T(8,128)(2,1)S(1)}, bf16[2064,256]{1,0:T(8,128)(2,1)S(1)}, u32[]{:S(2)}, u32[]{:S(2)}) collective-permute-start(bf16[2064,256]{1,0:T(8,128)(2,1)S(1)} %constant_dynamic-update-slice_fusion.refs_4_), channel_id=1, source_target_pairs={{0,1},{1,0},{2,3},{3,2},{4,5},{5,4},{6,7},{7,6},{8,9},{9,8},{10,11... | collective-permute-start | bytes 3170312 | tf_op jit(solution)/shard_map/ppermute | solution.py:416
  87.4 28.4 %collective-permute-start.11 = (bf16[256,2048]{1,0:T(8,128)(2,1)}, bf16[256,2048]{1,0:T(8,128)(2,1)S(1)}, u32[]{:S(2)}, u32[]{:S(2)}) collective-permute-start(bf16[256,2048]{1,0:T(8,128)(2,1)} %collective-permute-done.6.refs_11_), channel_id=1, source_target_pairs={{0,8},{1,9},{2,10},{3,11},{4,12},{5,13},{6,14},{7,15},{8,0},{9,1},... | collective-permute-start | bytes 3145736 | tf_op jit(solution)/shard_map/ppermute | solution.py:416
  123.7 29.6 %collective-permute-start.17 = (bf16[2064,256]{1,0:T(8,128)(2,1)S(1)}, bf16[2064,256]{1,0:T(8,128)(2,1)S(1)}, u32[]{:S(2)}, u32[]{:S(2)}) collective-permute-start(bf16[2064,256]{1,0:T(8,128)(2,1)S(1)} %copy-done.23), channel_id=1, source_target_pairs={{0,8},{1,9},{2,10},{3,11},{4,12},{5,13},{6,14},{7,15},{8,0},{9,1},... | collective-permute-start | bytes 3170312 | tf_op jit(solution)/shard_map/ppermute | solution.py:416
  123.8 29.5 %collective-permute-start.18 = (bf16[256,2048]{1,0:T(8,128)(2,1)S(1)}, bf16[256,2048]{1,0:T(8,128)(2,1)S(1)}, u32[]{:S(2)}, u32[]{:S(2)}) collective-permute-start(bf16[256,2048]{1,0:T(8,128)(2,1)S(1)} %copy-done.20), channel_id=1, source_target_pairs={{0,1},{1,0},{2,3},{3,2},{4,5},{5,4},{6,7},{7,6},{8,9},{9,8},{10,11... | collective-permute-start | bytes 3145736 | tf_op jit(solution)/shard_map/ppermute | solution.py:416
  124.3 14.9 %collective-permute-start.13 = (bf16[64,2048]{1,0:T(8,128)(2,1)S(1)}, bf16[64,2048]{1,0:T(8,128)(2,1)S(1)}, u32[]{:S(2)}, u32[]{:S(2)}) collective-permute-start(bf16[64,2048]{1,0:T(8,128)(2,1)S(1)} %get-tuple-element.150), channel_id=1, source_target_pairs={{0,4},{1,5},{2,6},{3,7},{4,0},{5,1},{6,2},{7,3},{8,12},{9,13},{10,... | collective-permute-start | bytes 786440 | tf_op jit(solution)/shard_map/ppermute | solution.py:416
  126.6 14.2 %collective-permute-start.16 = (bf16[128,2048]{1,0:T(8,128)(2,1)S(1)}, bf16[128,2048]{1,0:T(8,128)(2,1)S(1)}, u32[]{:S(2)}, u32[]{:S(2)}) collective-permute-start(bf16[128,2048]{1,0:T(8,128)(2,1)S(1)} %get-tuple-element.192.refs_1_.hidden_ref), channel_id=1, source_target_pairs={{0,16},{1,17},{2,18},{3,19},{4,20},{5,21},{6,22},{7,23},{8,24},{9,... | collective-permute-start | bytes 1572872 | tf_op jit(solution)/shard_map/ppermute | solution.py:416
  139.2 14.1 %collective-permute-start.14 = (bf16[64,2048]{1,0:T(8,128)(2,1)S(1)}, bf16[64,2048]{1,0:T(8,128)(2,1)S(1)}, u32[]{:S(2)}, u32[]{:S(2)}) collective-permute-start(bf16[64,2048]{1,0:T(8,128)(2,1)S(1)} %get-tuple-element.151), channel_id=1, source_target_pairs={{0,4},{1,5},{2,6},{3,7},{4,0},{5,1},{6,2},{7,3},{8,12},{9,13},{10,... | collective-permute-start | bytes 786440 | tf_op jit(solution)/shard_map/ppermute | solution.py:416
  139.2 14.1 %collective-permute-start.15 = (bf16[64,2048]{1,0:T(8,128)(2,1)S(1)}, bf16[64,2048]{1,0:T(8,128)(2,1)S(1)}, u32[]{:S(2)}, u32[]{:S(2)}) collective-permute-start(bf16[64,2048]{1,0:T(8,128)(2,1)S(1)} %collective-permute-done.13.refs_0_), channel_id=1, source_target_pairs={{0,16},{1,17},{2,18},{3,19},{4,20},{5,21},{6,22},{7,23},{8,24},{9,... | collective-permute-start | bytes 786440 | tf_op jit(solution)/shard_map/ppermute | solution.py:416
  179.3 14.0 %collective-permute-start.24 = (bf16[64,2048]{1,0:T(8,128)(2,1)}, bf16[64,2048]{1,0:T(8,128)(2,1)S(1)}, u32[]{:S(2)}, u32[]{:S(2)}) collective-permute-start(bf16[64,2048]{1,0:T(8,128)(2,1)} %get-tuple-element.197), channel_id=1, source_target_pairs={{0,16},{1,17},{2,18},{3,19},{4,20},{5,21},{6,22},{7,23},{8,24},{9,... | collective-permute-start | bytes 786440 | tf_op jit(solution)/shard_map/ppermute | solution.py:416
  191.8 25.3 %collective-permute-start.22 = (bf16[128,2048]{1,0:T(8,128)(2,1)}, bf16[128,2048]{1,0:T(8,128)(2,1)S(1)}, u32[]{:S(2)}, u32[]{:S(2)}) collective-permute-start(bf16[128,2048]{1,0:T(8,128)(2,1)} %get-tuple-element.195), channel_id=1, source_target_pairs={{0,16},{1,17},{2,18},{3,19},{4,20},{5,21},{6,22},{7,23},{8,24},{9,... | collective-permute-start | bytes 1572872 | tf_op jit(solution)/shard_map/ppermute | solution.py:416
  193.3 18.3 %collective-permute-start.23 = (bf16[64,2048]{1,0:T(8,128)(2,1)S(1)}, bf16[64,2048]{1,0:T(8,128)(2,1)S(1)}, u32[]{:S(2)}, u32[]{:S(2)}) collective-permute-start(bf16[64,2048]{1,0:T(8,128)(2,1)S(1)} %copy-done.40), channel_id=1, source_target_pairs={{0,4},{1,5},{2,6},{3,7},{4,0},{5,1},{6,2},{7,3},{8,12},{9,13},{10,... | collective-permute-start | bytes 786440 | tf_op jit(solution)/shard_map/ppermute | solution.py:416
  195.8 21.3 %collective-permute-start.25 = (bf16[64,2048]{1,0:T(8,128)(2,1)}, bf16[64,2048]{1,0:T(8,128)(2,1)S(1)}, u32[]{:S(2)}, u32[]{:S(2)}) collective-permute-start(bf16[64,2048]{1,0:T(8,128)(2,1)} %add_rows.3), channel_id=1, source_target_pairs={{0,4},{1,5},{2,6},{3,7},{4,0},{5,1},{6,2},{7,3},{8,12},{9,13},{10,... | collective-permute-start | bytes 786440 | tf_op jit(solution)/shard_map/ppermute | solution.py:416
  (48 other events, 564.8 us)

commit v8 on v7

--- a/solution.py
+++ b/solution.py
@@ -234,7 +234,7 @@
             pltpu.VMEM(wide_values.shape, jnp.bfloat16),
             pltpu.SemaphoreType.DMA((2,)),
         ],
-        compiler_params=pltpu.CompilerParams(vmem_limit_bytes=58 * mebibyte),
+        compiler_params=pltpu.CompilerParams(vmem_limit_bytes=40 * mebibyte),
         cost_estimate=pl.CostEstimate(
             flops=4 * sources * capacity * key_total * part_width,
             bytes_accessed=8 * key_total * part_width,
@@ -429,49 +429,21 @@
     return lax.optimization_barrier((values, after))[0]
 
 
-def mlp_kernel(pieces, up_plan, down_plan, *refs):
-    parts = len(up_plan)
+def mlp_kernel(pieces, parts, *refs):
     row_refs, refs = refs[:pieces], refs[pieces:]
-    up_total, down_total = sum(map(len, up_plan)), sum(map(len, down_plan))
-    ups, refs = list(refs[:up_total]), refs[up_total:]
-    downs, refs = list(refs[:down_total]), refs[down_total:]
-    out_refs, (up_ref, down_ref, sems) = refs[:pieces], refs[pieces:]
+    ups, downs, out_refs = refs[:parts], refs[parts : 2 * parts], refs[2 * parts :]
     model_width = row_refs[0].shape[1]
-    copies = []
-    for part, heights in enumerate(up_plan):
-        begin, held = 0, []
-        for piece, height in enumerate(heights):
-            target = up_ref.at[part, pl.ds(begin, height)]
-            held.append(pltpu.make_async_copy(ups.pop(0), target, sems.at[part, 0, piece]))
-            begin += height
-        copies.append(held)
-    begin = 0
-    for part, heights in enumerate(down_plan):
-        held = []
-        for piece, height in enumerate(heights):
-            target = down_ref.at[pl.ds(begin, height)]
-            held.append(pltpu.make_async_copy(downs.pop(0), target, sems.at[part, 1, piece]))
-            begin += height
-        copies.append(held)
-    for held in copies:
-        for copy in held:
-            copy.start()
     rows = jnp.concatenate([ref[...] for ref in row_refs], axis=0)
-    activations = []
-    for part in range(parts):
-        for copy in copies[part]:
-            copy.wait()
+    total = None
+    for up_ref, down_ref in zip(ups, downs):
         product = jnp.dot(
-            rows, up_ref[part, :model_width, :], preferred_element_type=jnp.float32
-        )
-        offset = up_ref[part, model_width:, :].astype(jnp.float32)[0:1]
-        activations.append(jax.nn.gelu(product + offset, approximate=True).astype(jnp.bfloat16))
-    for held in copies[parts:]:
-        for copy in held:
-            copy.wait()
-    total = jnp.dot(
-        jnp.concatenate(activations, axis=1), down_ref[...], preferred_element_type=jnp.float32
-    ).astype(jnp.bfloat16)
+            rows, up_ref[:model_width, :], preferred_element_type=jnp.float32
+        )
+        offset = up_ref[model_width:, :].astype(jnp.float32)[0:1]
+        activation = jax.nn.gelu(product + offset, approximate=True).astype(jnp.bfloat16)
+        term = jnp.dot(activation, down_ref[...], preferred_element_type=jnp.float32)
+        total = term if total is None else total + term
+    total = total.astype(jnp.bfloat16)
     begin = 0
     for out_ref in out_refs:
         height = out_ref.shape[0]
@@ -482,30 +454,20 @@
 def feed_forward(rows, ups, downs):
     pieces, parts = len(rows), len(ups)
     row_total, model_width = sum(piece.shape[0] for piece in rows), rows[0].shape[1]
-    up_plan = [[piece.shape[0] for piece in block] for block in ups]
-    down_plan = [[piece.shape[0] for piece in block] for block in downs]
-    up_rows, down_rows = sum(up_plan[0]), sum(down_plan[0])
-    units = ups[0][0].shape[1]
-    flat = [piece for block in ups + downs for piece in block]
-    most = max(map(len, up_plan + down_plan))
+    units = ups[0].shape[1]
     return pl.pallas_call(
-        functools.partial(mlp_kernel, pieces, up_plan, down_plan),
+        functools.partial(mlp_kernel, pieces, parts),
         out_shape=tuple(jax.ShapeDtypeStruct(piece.shape, jnp.bfloat16) for piece in rows),
-        in_specs=[vmem_spec()] * pieces + [hbm_spec()] * len(flat),
+        in_specs=[vmem_spec()] * (pieces + 2 * parts),
         out_specs=tuple(vmem_spec() for _ in rows),
-        scratch_shapes=[
-            pltpu.VMEM((parts, up_rows, units), jnp.bfloat16),
-            pltpu.VMEM((parts * down_rows, model_width), jnp.bfloat16),
-            pltpu.SemaphoreType.DMA((parts, 2, most)),
-        ],
-        compiler_params=pltpu.CompilerParams(vmem_limit_bytes=58 * mebibyte),
+        compiler_params=pltpu.CompilerParams(vmem_limit_bytes=34 * mebibyte),
         cost_estimate=pl.CostEstimate(
             flops=4 * row_total * model_width * parts * units,
             bytes_accessed=4 * parts * model_width * units,
             transcendentals=row_total * parts * units,
         ),
         name="feed_forward",
-    )(*rows, *flat)
+    )(*rows, *ups, *downs)
 
 
 def add_kernel(here_ref, there_ref, out_ref):
@@ -672,8 +634,8 @@
     cross_b = swap(far_b, near_mask)
     downs = complete(downs, group_masks + column_masks)
     order = sorted(ups)
-    ups = [ups[mask] for mask in order]
-    downs = [downs[mask] for mask in order]
+    ups = [ups[mask][0] for mask in order]
+    downs = [downs[mask][0] for mask in order]
     far_part_a, cross_part_a = feed_forward([far_a, cross_a], ups, downs)
     cross_b, far_part_a, cross_part_a = lax.optimization_barrier(
         (cross_b, far_part_a, cross_part_a)
@@ -689,7 +651,9 @@
     near, hidden = tie((near, hidden), joined_a)
     near_part, own_part = feed_forward([near, hidden], ups, downs)
     near_sum = swap(near_part, near_mask)
-    cross_sum_b, near_part = lax.optimization_barrier((cross_sum_b, near_part))
+    cross_sum_b, near_part, far_sum_a = lax.optimization_barrier(
+        (cross_sum_b, near_part, far_sum_a)
+    )
     far_sum_b = swap(add_rows(far_part_b, cross_sum_b), far_mask)
     return finish_rows(
         hidden, own_part, near_sum, far_sum_a, far_sum_b, down_bias, out_gain, out_shift

time: 220 us -> 236 us (1.073)
  local copies, waits for them, and re-layouts: 28.4 us -> 65.7 us
  waiting for transfers between devices: 89.4 us -> 74.7 us
  Pallas kernels: 61.7 us -> 53.6 us
    unnamed x92 -> x140, local copies, waits for them, and re-layouts: 17.1 us -> 54.6 us
    ppermute x26, waiting for transfers between devices: 89.4 us -> 74.7 us  [swap(): lax.ppermute(leaf, ('grp', 'dev'), pairs)]
    pallas_call x3, Pallas kernels: 29.9 us -> 21.4 us  [feed_forward(): pl.pallas_call(functools.partial(mlp_kernel, pieces, parts), out_shape=tu...]
  transfers between devices with their start and end apart: 28 -> 28, of which waited for: 10 -> 9; matrix products, arithmetic and copies ran while one was open for 10% -> 10% of each run, Pallas kernels for 25% -> 20%
where the time goes in v8:
time: 236 us; the launch traced here: 233 us
  waiting for transfers between devices  74.7 us (32%)
  local copies, waits for them, and re-layouts  65.7 us (28%)
  Pallas kernels  53.6 us (23%)
  starting transfers between devices  36.5 us (15%)
  other arithmetic  2.42 us (1%)
    ppermute x26, waiting for transfers between devices, swap(): lax.ppermute(leaf, ('grp', 'dev'), pairs)  74.7 us
    unnamed x140, local copies, waits for them, and re-layouts  54.6 us
    ppermute x26, starting transfers between devices, swap(): lax.ppermute(leaf, ('grp', 'dev'), pairs)  23.6 us
    pallas_call x3, Pallas kernels, feed_forward(): pl.pallas_call(functools.partial(mlp_kernel, pieces, parts), out_shape=tu...  21.4 us
    pallas_call x1, Pallas kernels, attend_prefix(): pl.pallas_call(far_kernel, out_shape=jax.ShapeDtypeStruct((sources, capac...  18.1 us
    all_to_all x1, starting transfers between devices, on_device(): lax.all_to_all(outgoing.reshape(sources, capacity + STAT_ROWS, part_width...  7.41 us
    all_to_all x1, starting transfers between devices, on_device(): lax.all_to_all(answer_part, ('grp', 'dev'), split_axis=0, concat_axis=0,...  5.43 us
  transfers between devices with their start and end apart: 28, of which 9 were waited for; matrix products, arithmetic and copies ran while one was open for 10% of the time, Pallas kernels for 20%

profile of v8, /device:TPU:0, one launch (start us, length us, event | category | flops | bytes accessed | tf_op | source)
XLA Modules:
  0.0 233.5 jit_solution(11332988914916475691)
XLA Ops:
  2.4 1.8 pack_queries.1
  4.2 7.4 %all-to-all-start = ((bf16[32,72,256]{2,1,0:T(8,128)(2,1)}), bf16[32,72,256]{2,1,0:T(8,128)(2,1)}, u32[]{:S(2)}, u32[]{:S(2)}) async-start(bf16[32,72,256]{2,1,0:T(8,128)(2,1)} %bitcast), calls=%async_computation | async-start | bytes 2359296 | tf_op jit(solution)/shard_map/all_to_all | solution.py:571
  16.9 4.5 %attend_suffix.1 = (f32[128,2048]{1,0:T(8,128)S(1)}, f32[128,128]{1,0:T(8,128)S(1)}, f32[128,128]{1,0:T(8,128)S(1)}) custom-call(s32[1,4]{1,0:T(1,128)S(1)} %copy-done.55, bf16[128,2048]{1,0:T(8,128)(2,1)S(1)} %copy-done.41, bf16[128,2048]{1,0:T(8,128)(2,1)S(1)} %copy-done.58, bf16[128,2048]{1,0:T(8,128)(2,1)S(1)} %copy-done.59), custom_call_target="tpu_custom_call" | custom-call | flops 1342177280 | bytes 2097152 | tf_op jit(solution)/shard_map/attend_suffix/pallas_call | solution.py:295
  22.4 4.1 %copy.18 = bf16[1,4096,256]{1,2,0:T(8,128)(2,1)} copy(bf16[1,4096,256]{2,1,0:T(8,128)(2,1)} %param.22) | data formatting | bytes 4194304 | tf_op args[6]
  26.5 4.1 %copy.19 = bf16[1,4096,256]{1,2,0:T(8,128)(2,1)} copy(bf16[1,4096,256]{2,1,0:T(8,128)(2,1)} %param.23) | data formatting | bytes 4194304 | tf_op args[7]
  30.6 4.1 %copy.20 = bf16[4096,2,128]{2,0,1:T(8,128)(2,1)} copy(bf16[4096,2,128]{0,2,1:T(8,128)(2,1)} %bitcast.19) | data formatting | bytes 4194304 | tf_op jit(solution)/shard_map/reshape;squeeze | solution.py:583
  34.7 4.0 %concatenate.13.values_hbm = bf16[2,4096,256]{2,1,0:T(8,128)(2,1)} pad(bf16[2,4096,128]{2,1,0:T(8,128)(2,1)} %bitcast.18, bf16[]{:T(256)} %constant.0.clone.1), padding=0_0x0_0x0_128 | pad | bytes 6291458 | tf_op jit(solution)/shard_map/concatenate | solution.py:584
  39.8 4.8 %collective-permute-done.2 = bf16[1024,256]{1,0:T(8,128)(2,1)} collective-permute-done((bf16[1024,256]{1,0:T(8,128)(2,1)}, bf16[1024,256]{1,0:T(8,128)(2,1)}, u32[]{:S(2)}, u32[]{:S(2)}) %collective-permute-start.2) | collective-permute-done | bytes 524320 | tf_op jit(solution)/shard_map/ppermute | solution.py:416
  44.6 5.1 %collective-permute-done.refs_3_ = bf16[2064,256]{1,0:T(8,128)(2,1)} collective-permute-done((bf16[2064,256]{1,0:T(8,128)(2,1)S(1)}, bf16[2064,256]{1,0:T(8,128)(2,1)}, u32[]{:S(2)}, u32[]{:S(2)}) %collective-permute-start) | collective-permute-done | bytes 1056800 | tf_op jit(solution)/shard_map/ppermute | solution.py:416
  53.6 2.2 copy-done.32
  57.4 18.1 %attend_prefix.1 = bf16[32,72,256]{2,1,0:T(8,128)(2,1)S(1)} custom-call(s32[32]{0:T(128)S(1)} %convert_reduce_fusion.counts_ref, bf16[32,72,256]{2,1,0:T(8,128)(2,1)} %all-to-all-done.arrived_ref, bf16[256,4096]{1,0:T(8,128)(2,1)S(1)} %bitcast.12, bf16[2,4096,256]{2,1,0:T(8,128)(2,1)S(1)} %copy-done.32), custom_call_target="tpu_custom_call" | custom-call | flops 8589934592 | bytes 8388608 | tf_op jit(solution)/shard_map/attend_prefix/pallas_call | solution.py:222
  79.5 5.4 %all-to-all-start.1 = ((bf16[32,72,256]{2,1,0:T(8,128)(2,1)}), bf16[32,72,256]{2,1,0:T(8,128)(2,1)}, u32[]{:S(2)}, u32[]{:S(2)}) async-start(bf16[32,72,256]{2,1,0:T(8,128)(2,1)} %copy-done.37), calls=%async_computation.1 | async-start | bytes 2359296 | tf_op jit(solution)/shard_map/all_to_all | solution.py:606
  90.8 26.9 %collective-permute-done.10 = bf16[128,2048]{1,0:T(8,128)(2,1)S(1)} collective-permute-done((bf16[128,2048]{1,0:T(8,128)(2,1)}, bf16[128,2048]{1,0:T(8,128)(2,1)S(1)}, u32[]{:S(2)}, u32[]{:S(2)}) %collective-permute-start.10) | collective-permute-done | bytes 524320 | tf_op jit(solution)/shard_map/ppermute | solution.py:416
  120.0 2.8 %collective-permute-done.8.refs_5_ = bf16[2064,256]{1,0:T(8,128)(2,1)S(1)} collective-permute-done((bf16[2064,256]{1,0:T(8,128)(2,1)S(1)}, bf16[2064,256]{1,0:T(8,128)(2,1)S(1)}, u32[]{:S(2)}, u32[]{:S(2)}) %collective-permute-start.8) | collective-permute-done | bytes 1056800 | tf_op jit(solution)/shard_map/ppermute | solution.py:416
  127.1 2.7 %merge_parts.1 = (bf16[64,2048]{1,0:T(8,128)(2,1)S(1)}, bf16[64,2048]{1,0:T(8,128)(2,1)S(1)}, bf16[128,2048]{1,0:T(8,128)(2,1)S(1)}) custom-call(s32[1,4]{1,0:T(1,128)S(1)} %copy-done.55, s32[1,4]{1,0:T(1,128)S(1)} %copy-done.57, bf16[4,8,72,256]{3,2,1,0:T(8,128)(2,1)} %bitcast.5.arrived_ref, f32[128,2048]{1,0:T(8,128)S(1)} %copy-done.39, ...), custom_call_target="tpu_custom_call" | custom-call | tf_op jit(solution)/shard_map/merge_parts/pallas_call | solution.py:389
  130.9 2.0 collective-permute-start.13
  135.2 10.6 %collective-permute-done.13.refs_0_ = bf16[64,2048]{1,0:T(8,128)(2,1)S(1)} collective-permute-done((bf16[64,2048]{1,0:T(8,128)(2,1)S(1)}, bf16[64,2048]{1,0:T(8,128)(2,1)S(1)}, u32[]{:S(2)}, u32[]{:S(2)}) %collective-permute-start.13) | collective-permute-done | bytes 262176 | tf_op jit(solution)/shard_map/ppermute | solution.py:416
  148.1 12.0 %collective-permute-done.14.refs_0_ = bf16[64,2048]{1,0:T(8,128)(2,1)S(1)} collective-permute-done((bf16[64,2048]{1,0:T(8,128)(2,1)S(1)}, bf16[64,2048]{1,0:T(8,128)(2,1)S(1)}, u32[]{:S(2)}, u32[]{:S(2)}) %collective-permute-start.14) | collective-permute-done | bytes 262176 | tf_op jit(solution)/shard_map/ppermute | solution.py:416
  170.2 6.2 %feed_forward.3 = (bf16[64,2048]{1,0:T(8,128)(2,1)S(1)}, bf16[64,2048]{1,0:T(8,128)(2,1)S(1)}) custom-call(bf16[64,2048]{1,0:T(8,128)(2,1)S(1)} %collective-permute-done.13.refs_0_, bf16[64,2048]{1,0:T(8,128)(2,1)S(1)} %collective-permute-done.15.refs_1_, bf16[2064,256]{1,0:T(8,128)(2,1)S(1)} %pad_maximum_fusion.refs_2_, ...), custom_call_target="tpu_custom_call" | custom-call | flops 2147483648 | bytes 16777216 | tf_op jit(solution)/shard_map/feed_forward/pallas_call | solution.py:458
  177.9 5.8 %feed_forward.4 = (bf16[64,2048]{1,0:T(8,128)(2,1)S(1)}, bf16[64,2048]{1,0:T(8,128)(2,1)S(1)}) custom-call(bf16[64,2048]{1,0:T(8,128)(2,1)S(1)} %collective-permute-done.14.refs_0_, bf16[64,2048]{1,0:T(8,128)(2,1)S(1)} %collective-permute-done.19.refs_1_, bf16[2064,256]{1,0:T(8,128)(2,1)S(1)} %pad_maximum_fusion.refs_2_, ...), custom_call_target="tpu_custom_call" | custom-call | flops 2147483648 | bytes 16777216 | tf_op jit(solution)/shard_map/feed_forward/pallas_call | solution.py:458
  185.5 1.8 add_rows.2
  204.4 9.4 %feed_forward.5 = (bf16[128,2048]{1,0:T(8,128)(2,1)}, bf16[128,2048]{1,0:T(8,128)(2,1)S(1)}) custom-call(bf16[128,2048]{1,0:T(8,128)(2,1)S(1)} %copy-done.43, bf16[128,2048]{1,0:T(8,128)(2,1)S(1)} %copy-done.34, bf16[2064,256]{1,0:T(8,128)(2,1)S(1)} %pad_maximum_fusion.refs_2_, bf16[2064,256]{1,0:T(8,128)(2,1)} %collective-permute-done.refs_3_, ...), custom_call_target="tpu_custom_call" | custom-call | flops 4294967296 | bytes 16777216 | tf_op jit(solution)/shard_map/feed_forward/pallas_call | solution.py:458
  217.0 2.9 %collective-permute-start.25 = (bf16[64,2048]{1,0:T(8,128)(2,1)}, bf16[64,2048]{1,0:T(8,128)(2,1)S(1)}, u32[]{:S(2)}, u32[]{:S(2)}) collective-permute-start(bf16[64,2048]{1,0:T(8,128)(2,1)} %add_rows.3), channel_id=1, source_target_pairs={{0,4},{1,5},{2,6},{3,7},{4,0},{5,1},{6,2},{7,3},{8,12},{9,13},{10,... | collective-permute-start | bytes 786440 | tf_op jit(solution)/shard_map/ppermute | solution.py:416
  219.9 11.1 %collective-permute-done.25.far_b_ref = bf16[64,2048]{1,0:T(8,128)(2,1)S(1)} collective-permute-done((bf16[64,2048]{1,0:T(8,128)(2,1)}, bf16[64,2048]{1,0:T(8,128)(2,1)S(1)}, u32[]{:S(2)}, u32[]{:S(2)}) %collective-permute-start.25) | collective-permute-done | bytes 262176 | tf_op jit(solution)/shard_map/ppermute | solution.py:416
  (192 shorter events, 73.1 us)
Async XLA Ops:
  4.2 45.6 %all-to-all-start = ((bf16[32,72,256]{2,1,0:T(8,128)(2,1)}), bf16[32,72,256]{2,1,0:T(8,128)(2,1)}, u32[]{:S(2)}, u32[]{:S(2)}) async-start(bf16[32,72,256]{2,1,0:T(8,128)(2,1)} %bitcast), calls=%async_computation | async-start | bytes 2359296 | tf_op jit(solution)/shard_map/all_to_all | solution.py:571
  11.8 32.9 %collective-permute-start.1 = (bf16[2064,256]{1,0:T(8,128)(2,1)S(1)}, bf16[2064,256]{1,0:T(8,128)(2,1)S(1)}, u32[]{:S(2)}, u32[]{:S(2)}) collective-permute-start(bf16[2064,256]{1,0:T(8,128)(2,1)S(1)} %pad_maximum_fusion.refs_2_), channel_id=1, source_target_pairs={{0,8},{1,9},{2,10},{3,11},{4,12},{5,13},{6,14},{7,15},{8,0},{9,1},... | collective-permute-start | bytes 3170312 | tf_op jit(solution)/shard_map/ppermute | solution.py:416
  12.0 37.7 %collective-permute-start = (bf16[2064,256]{1,0:T(8,128)(2,1)S(1)}, bf16[2064,256]{1,0:T(8,128)(2,1)}, u32[]{:S(2)}, u32[]{:S(2)}) collective-permute-start(bf16[2064,256]{1,0:T(8,128)(2,1)S(1)} %pad_maximum_fusion.refs_2_), channel_id=1, source_target_pairs={{0,1},{1,0},{2,3},{3,2},{4,5},{5,4},{6,7},{7,6},{8,9},{9,8},{10,11... | collective-permute-start | bytes 3170312 | tf_op jit(solution)/shard_map/ppermute | solution.py:416
  13.7 30.9 %collective-permute-start.3 = (bf16[256,2048]{1,0:T(8,128)(2,1)S(1)}, bf16[256,2048]{1,0:T(8,128)(2,1)}, u32[]{:S(2)}, u32[]{:S(2)}) collective-permute-start(bf16[256,2048]{1,0:T(8,128)(2,1)S(1)} %copy-done), channel_id=1, source_target_pairs={{0,8},{1,9},{2,10},{3,11},{4,12},{5,13},{6,14},{7,15},{8,0},{9,1},... | collective-permute-start | bytes 3145736 | tf_op jit(solution)/shard_map/ppermute | solution.py:416
  14.6 30.0 %collective-permute-start.2 = (bf16[1024,256]{1,0:T(8,128)(2,1)}, bf16[1024,256]{1,0:T(8,128)(2,1)}, u32[]{:S(2)}, u32[]{:S(2)}) collective-permute-start(bf16[1024,256]{1,0:T(8,128)(2,1)} %slice.15), channel_id=1, source_target_pairs={{0,2},{1,3},{2,0},{3,1},{4,6},{5,7},{6,4},{7,5},{8,10},{9,11},{10,... | collective-permute-start | bytes 1572872 | tf_op jit(solution)/shard_map/ppermute | solution.py:416
  49.7 28.8 %collective-permute-start.4 = (bf16[2064,256]{1,0:T(8,128)(2,1)}, bf16[2064,256]{1,0:T(8,128)(2,1)S(1)}, u32[]{:S(2)}, u32[]{:S(2)}) collective-permute-start(bf16[2064,256]{1,0:T(8,128)(2,1)} %collective-permute-done.refs_3_), channel_id=1, source_target_pairs={{0,8},{1,9},{2,10},{3,11},{4,12},{5,13},{6,14},{7,15},{8,0},{9,1},... | collective-permute-start | bytes 3170312 | tf_op jit(solution)/shard_map/ppermute | solution.py:416
  49.7 26.8 %collective-permute-start.6 = (bf16[256,2048]{1,0:T(8,128)(2,1)S(1)}, bf16[256,2048]{1,0:T(8,128)(2,1)S(1)}, u32[]{:S(2)}, u32[]{:S(2)}) collective-permute-start(bf16[256,2048]{1,0:T(8,128)(2,1)S(1)} %copy-done), channel_id=1, source_target_pairs={{0,1},{1,0},{2,3},{3,2},{4,5},{5,4},{6,7},{7,6},{8,9},{9,8},{10,11... | collective-permute-start | bytes 3145736 | tf_op jit(solution)/shard_map/ppermute | solution.py:416
  50.1 26.4 %collective-permute-start.7 = (bf16[128,2048]{1,0:T(8,128)(2,1)}, bf16[128,2048]{1,0:T(8,128)(2,1)S(1)}, u32[]{:S(2)}, u32[]{:S(2)}) collective-permute-start(bf16[128,2048]{1,0:T(8,128)(2,1)} %get-tuple-element.116), channel_id=1, source_target_pairs={{0,2},{1,3},{2,0},{3,1},{4,6},{5,7},{6,4},{7,5},{8,10},{9,11},{10,... | collective-permute-start | bytes 1572872 | tf_op jit(solution)/shard_map/ppermute | solution.py:416
  51.8 24.8 %collective-permute-start.5 = (bf16[1040,256]{1,0:T(8,128)(2,1)}, bf16[1040,256]{1,0:T(8,128)(2,1)S(1)}, u32[]{:S(2)}, u32[]{:S(2)}) collective-permute-start(bf16[1040,256]{1,0:T(8,128)(2,1)} %fusion), channel_id=1, source_target_pairs={{0,2},{1,3},{2,0},{3,1},{4,6},{5,7},{6,4},{7,5},{8,10},{9,11},{10,... | collective-permute-start | bytes 1597448 | tf_op jit(solution)/shard_map/ppermute | solution.py:416
  79.5 45.3 %all-to-all-start.1 = ((bf16[32,72,256]{2,1,0:T(8,128)(2,1)}), bf16[32,72,256]{2,1,0:T(8,128)(2,1)}, u32[]{:S(2)}, u32[]{:S(2)}) async-start(bf16[32,72,256]{2,1,0:T(8,128)(2,1)} %copy-done.37), calls=%async_computation.1 | async-start | bytes 2359296 | tf_op jit(solution)/shard_map/all_to_all | solution.py:606
  85.0 32.7 %collective-permute-start.10 = (bf16[128,2048]{1,0:T(8,128)(2,1)}, bf16[128,2048]{1,0:T(8,128)(2,1)S(1)}, u32[]{:S(2)}, u32[]{:S(2)}) collective-permute-start(bf16[128,2048]{1,0:T(8,128)(2,1)} %get-tuple-element.128), channel_id=1, source_target_pairs={{0,2},{1,3},{2,0},{3,1},{4,6},{5,7},{6,4},{7,5},{8,10},{9,11},{10,... | collective-permute-start | bytes 1572872 | tf_op jit(solution)/shard_map/ppermute | solution.py:416
  88.9 30.1 %collective-permute-start.9 = (bf16[2064,256]{1,0:T(8,128)(2,1)S(1)}, bf16[2064,256]{1,0:T(8,128)(2,1)S(1)}, u32[]{:S(2)}, u32[]{:S(2)}) collective-permute-start(bf16[2064,256]{1,0:T(8,128)(2,1)S(1)} %constant_dynamic-update-slice_fusion.refs_4_), channel_id=1, source_target_pairs={{0,8},{1,9},{2,10},{3,11},{4,12},{5,13},{6,14},{7,15},{8,0},{9,1},... | collective-permute-start | bytes 3170312 | tf_op jit(solution)/shard_map/ppermute | solution.py:416
  89.0 33.8 %collective-permute-start.8 = (bf16[2064,256]{1,0:T(8,128)(2,1)S(1)}, bf16[2064,256]{1,0:T(8,128)(2,1)S(1)}, u32[]{:S(2)}, u32[]{:S(2)}) collective-permute-start(bf16[2064,256]{1,0:T(8,128)(2,1)S(1)} %constant_dynamic-update-slice_fusion.refs_4_), channel_id=1, source_target_pairs={{0,1},{1,0},{2,3},{3,2},{4,5},{5,4},{6,7},{7,6},{8,9},{9,8},{10,11... | collective-permute-start | bytes 3170312 | tf_op jit(solution)/shard_map/ppermute | solution.py:416
  90.5 27.3 %collective-permute-start.11 = (bf16[256,2048]{1,0:T(8,128)(2,1)S(1)}, bf16[256,2048]{1,0:T(8,128)(2,1)S(1)}, u32[]{:S(2)}, u32[]{:S(2)}) collective-permute-start(bf16[256,2048]{1,0:T(8,128)(2,1)S(1)} %copy-done.19), channel_id=1, source_target_pairs={{0,8},{1,9},{2,10},{3,11},{4,12},{5,13},{6,14},{7,15},{8,0},{9,1},... | collective-permute-start | bytes 3145736 | tf_op jit(solution)/shard_map/ppermute | solution.py:416
  129.8 30.2 %collective-permute-start.17 = (bf16[2064,256]{1,0:T(8,128)(2,1)}, bf16[2064,256]{1,0:T(8,128)(2,1)S(1)}, u32[]{:S(2)}, u32[]{:S(2)}) collective-permute-start(bf16[2064,256]{1,0:T(8,128)(2,1)} %copy-done.13), channel_id=1, source_target_pairs={{0,8},{1,9},{2,10},{3,11},{4,12},{5,13},{6,14},{7,15},{8,0},{9,1},... | collective-permute-start | bytes 3170312 | tf_op jit(solution)/shard_map/ppermute | solution.py:416
  129.9 30.1 %collective-permute-start.18 = (bf16[256,2048]{1,0:T(8,128)(2,1)S(1)}, bf16[256,2048]{1,0:T(8,128)(2,1)S(1)}, u32[]{:S(2)}, u32[]{:S(2)}) collective-permute-start(bf16[256,2048]{1,0:T(8,128)(2,1)S(1)} %copy-done.2), channel_id=1, source_target_pairs={{0,1},{1,0},{2,3},{3,2},{4,5},{5,4},{6,7},{7,6},{8,9},{9,8},{10,11... | collective-permute-start | bytes 3145736 | tf_op jit(solution)/shard_map/ppermute | solution.py:416
  130.9 14.9 %collective-permute-start.13 = (bf16[64,2048]{1,0:T(8,128)(2,1)S(1)}, bf16[64,2048]{1,0:T(8,128)(2,1)S(1)}, u32[]{:S(2)}, u32[]{:S(2)}) collective-permute-start(bf16[64,2048]{1,0:T(8,128)(2,1)S(1)} %get-tuple-element.151), channel_id=1, source_target_pairs={{0,4},{1,5},{2,6},{3,7},{4,0},{5,1},{6,2},{7,3},{8,12},{9,13},{10,... | collective-permute-start | bytes 786440 | tf_op jit(solution)/shard_map/ppermute | solution.py:416
  132.9 14.3 %collective-permute-start.16 = (bf16[128,2048]{1,0:T(8,128)(2,1)S(1)}, bf16[128,2048]{1,0:T(8,128)(2,1)S(1)}, u32[]{:S(2)}, u32[]{:S(2)}) collective-permute-start(bf16[128,2048]{1,0:T(8,128)(2,1)S(1)} %get-tuple-element.193.refs_1_.hidden_ref), channel_id=1, source_target_pairs={{0,16},{1,17},{2,18},{3,19},{4,20},{5,21},{6,22},{7,23},{8,24},{9,... | collective-permute-start | bytes 1572872 | tf_op jit(solution)/shard_map/ppermute | solution.py:416
  145.8 14.2 %collective-permute-start.14 = (bf16[64,2048]{1,0:T(8,128)(2,1)S(1)}, bf16[64,2048]{1,0:T(8,128)(2,1)S(1)}, u32[]{:S(2)}, u32[]{:S(2)}) collective-permute-start(bf16[64,2048]{1,0:T(8,128)(2,1)S(1)} %get-tuple-element.152), channel_id=1, source_target_pairs={{0,4},{1,5},{2,6},{3,7},{4,0},{5,1},{6,2},{7,3},{8,12},{9,13},{10,... | collective-permute-start | bytes 786440 | tf_op jit(solution)/shard_map/ppermute | solution.py:416
  145.8 14.2 %collective-permute-start.15 = (bf16[64,2048]{1,0:T(8,128)(2,1)S(1)}, bf16[64,2048]{1,0:T(8,128)(2,1)S(1)}, u32[]{:S(2)}, u32[]{:S(2)}) collective-permute-start(bf16[64,2048]{1,0:T(8,128)(2,1)S(1)} %collective-permute-done.13.refs_0_), channel_id=1, source_target_pairs={{0,16},{1,17},{2,18},{3,19},{4,20},{5,21},{6,22},{7,23},{8,24},{9,... | collective-permute-start | bytes 786440 | tf_op jit(solution)/shard_map/ppermute | solution.py:416
  160.2 16.2 %collective-permute-start.19 = (bf16[64,2048]{1,0:T(8,128)(2,1)S(1)}, bf16[64,2048]{1,0:T(8,128)(2,1)S(1)}, u32[]{:S(2)}, u32[]{:S(2)}) collective-permute-start(bf16[64,2048]{1,0:T(8,128)(2,1)S(1)} %collective-permute-done.14.refs_0_), channel_id=1, source_target_pairs={{0,16},{1,17},{2,18},{3,19},{4,20},{5,21},{6,22},{7,23},{8,24},{9,... | collective-permute-start | bytes 786440 | tf_op jit(solution)/shard_map/ppermute | solution.py:416
  187.3 27.8 %collective-permute-start.24 = (bf16[64,2048]{1,0:T(8,128)(2,1)}, bf16[64,2048]{1,0:T(8,128)(2,1)S(1)}, u32[]{:S(2)}, u32[]{:S(2)}) collective-permute-start(bf16[64,2048]{1,0:T(8,128)(2,1)} %add_rows.2), channel_id=1, source_target_pairs={{0,4},{1,5},{2,6},{3,7},{4,0},{5,1},{6,2},{7,3},{8,12},{9,13},{10,... | collective-permute-start | bytes 786440 | tf_op jit(solution)/shard_map/ppermute | solution.py:416
  187.3 27.8 %collective-permute-start.23 = (bf16[64,2048]{1,0:T(8,128)(2,1)}, bf16[64,2048]{1,0:T(8,128)(2,1)}, u32[]{:S(2)}, u32[]{:S(2)}) collective-permute-start(bf16[64,2048]{1,0:T(8,128)(2,1)} %copy-done.60), channel_id=1, source_target_pairs={{0,16},{1,17},{2,18},{3,19},{4,20},{5,21},{6,22},{7,23},{8,24},{9,... | collective-permute-start | bytes 786440 | tf_op jit(solution)/shard_map/ppermute | solution.py:416
  214.6 16.3 %collective-permute-start.22 = (bf16[128,2048]{1,0:T(8,128)(2,1)}, bf16[128,2048]{1,0:T(8,128)(2,1)S(1)}, u32[]{:S(2)}, u32[]{:S(2)}) collective-permute-start(bf16[128,2048]{1,0:T(8,128)(2,1)} %get-tuple-element.196), channel_id=1, source_target_pairs={{0,16},{1,17},{2,18},{3,19},{4,20},{5,21},{6,22},{7,23},{8,24},{9,... | collective-permute-start | bytes 1572872 | tf_op jit(solution)/shard_map/ppermute | solution.py:416
  (72 other events, 515.0 us)

commit v9 on v7

--- a/solution.py
+++ b/solution.py
@@ -11,6 +11,8 @@
 HD = 128
 LANES = 128
 STAT_ROWS = 8
+STREAMS = 4
+EMPTY = 64.0
 ROW_BLOCK = 256
 KEY_CHUNK = 1024
 
@@ -41,9 +43,9 @@
 
 def pack_kernel(lengths_ref, groups_ref, query_ref, out_ref, wide_ref):
     request_total = lengths_ref.shape[1]
-    _, column_count, chunk_rows, part_width = out_ref.shape
-    capacity = chunk_rows - STAT_ROWS
+    _, column_count, capacity, part_width = out_ref.shape
     slot_count = query_ref.shape[0]
+    slot = lax.broadcasted_iota(jnp.int32, (capacity, LANES), 0)
     tiles = part_width // LANES
     for tile in range(wide_ref.shape[0]):
         wide_ref[tile, 0:slot_count, :] = query_ref[
@@ -55,11 +57,11 @@
     start = 0
     for request in range(request_total):
         group = groups_ref[0, request]
-        count = jnp.full((STAT_ROWS, LANES), lengths_ref[0, request], jnp.int32).astype(jnp.float32)
+        filled = slot < lengths_ref[0, request]
         for column in range(column_count):
             for tile in range(tiles):
                 rows = wide_ref[column * tiles + tile, pl.ds(start, capacity), :]
-                rows = jnp.concatenate([rows, count], axis=0)
+                rows = jnp.where(filled, rows, EMPTY)
                 out_ref[group, column, :, tile * LANES : (tile + 1) * LANES] = rows.astype(
                     jnp.bfloat16
                 )
@@ -72,14 +74,14 @@
     return pl.pallas_call(
         pack_kernel,
         out_shape=jax.ShapeDtypeStruct(
-            (group_count, column_count, capacity + STAT_ROWS, part_width), jnp.bfloat16
+            (group_count, column_count, capacity, part_width), jnp.bfloat16
         ),
         in_specs=[smem_spec(), smem_spec(), vmem_spec()],
         out_specs=vmem_spec(),
         scratch_shapes=[
             pltpu.VMEM((model_width // LANES, slot_count + capacity, LANES), jnp.float32)
         ],
-        compiler_params=pltpu.CompilerParams(vmem_limit_bytes=16 * mebibyte),
+        compiler_params=pltpu.CompilerParams(vmem_limit_bytes=58 * mebibyte),
         name="pack_queries",
     )(lengths, groups, queries)
 
@@ -105,8 +107,7 @@
     ]
     for copy in copies:
         copy.start()
-    sources, chunk_rows, part_width = arrived_ref.shape
-    capacity = chunk_rows - STAT_ROWS
+    sources, capacity, part_width = arrived_ref.shape
     local_heads = part_width // HD
     key_total = keys_ref.shape[1]
     chunks = key_total // KEY_CHUNK
@@ -114,7 +115,7 @@
     def take(source, offset):
         for head in range(local_heads):
             rows = arrived_ref[source, :, head * HD : (head + 1) * HD].astype(jnp.float32)
-            query_ref[head, pl.ds(offset, capacity), :] = rows[:capacity]
+            query_ref[head, pl.ds(offset, capacity), :] = rows
         return offset + counts_ref[source]
 
     total = lax.fori_loop(0, sources, take, jnp.int32(0))
@@ -214,8 +215,7 @@
 
 
 def attend_prefix(counts, arrived, turned_keys, wide_values):
-    sources, chunk_rows, part_width = arrived.shape
-    capacity = chunk_rows - STAT_ROWS
+    sources, capacity, part_width = arrived.shape
     local_heads = part_width // HD
     key_total = turned_keys.shape[1]
     row_total = -(-sources * capacity // ROW_BLOCK) * ROW_BLOCK + LANES
@@ -429,6 +429,14 @@
     return lax.optimization_barrier((values, after))[0]
 
 
+def cut(height):
+    step = max(height // STREAMS // 16, 1) * 16
+    begins = [first for first in range(0, height, step)][:STREAMS]
+    return [
+        (first, (begins + [height])[at + 1] - first) for at, first in enumerate(begins)
+    ]
+
+
 def mlp_kernel(pieces, up_plan, down_plan, *refs):
     parts = len(up_plan)
     row_refs, refs = refs[:pieces], refs[pieces:]
@@ -441,16 +449,30 @@
     for part, heights in enumerate(up_plan):
         begin, held = 0, []
         for piece, height in enumerate(heights):
-            target = up_ref.at[part, pl.ds(begin, height)]
-            held.append(pltpu.make_async_copy(ups.pop(0), target, sems.at[part, 0, piece]))
+            source = ups.pop(0)
+            for stream, (first, rows) in enumerate(cut(height)):
+                held.append(
+                    pltpu.make_async_copy(
+                        source.at[pl.ds(first, rows)],
+                        up_ref.at[part, pl.ds(begin + first, rows)],
+                        sems.at[part, 0, piece * STREAMS + stream],
+                    )
+                )
             begin += height
         copies.append(held)
     begin = 0
     for part, heights in enumerate(down_plan):
         held = []
         for piece, height in enumerate(heights):
-            target = down_ref.at[pl.ds(begin, height)]
-            held.append(pltpu.make_async_copy(downs.pop(0), target, sems.at[part, 1, piece]))
+            source = downs.pop(0)
+            for stream, (first, rows) in enumerate(cut(height)):
+                held.append(
+                    pltpu.make_async_copy(
+                        source.at[pl.ds(first, rows)],
+                        down_ref.at[pl.ds(begin + first, rows)],
+                        sems.at[part, 1, piece * STREAMS + stream],
+                    )
+                )
             begin += height
         copies.append(held)
     for held in copies:
@@ -496,7 +518,7 @@
         scratch_shapes=[
             pltpu.VMEM((parts, up_rows, units), jnp.bfloat16),
             pltpu.VMEM((parts * down_rows, model_width), jnp.bfloat16),
-            pltpu.SemaphoreType.DMA((parts, 2, most)),
+            pltpu.SemaphoreType.DMA((parts, 2, most * STREAMS)),
         ],
         compiler_params=pltpu.CompilerParams(vmem_limit_bytes=58 * mebibyte),
         cost_estimate=pl.CostEstimate(
@@ -508,20 +530,8 @@
     )(*rows, *flat)
 
 
-def add_kernel(here_ref, there_ref, out_ref):
-    out_ref[...] = (
-        here_ref[...].astype(jnp.float32) + there_ref[...].astype(jnp.float32)
-    ).astype(jnp.bfloat16)
-
-
 def add_rows(here, there):
-    return pl.pallas_call(
-        add_kernel,
-        out_shape=jax.ShapeDtypeStruct(here.shape, jnp.bfloat16),
-        in_specs=[vmem_spec(), vmem_spec()],
-        out_specs=vmem_spec(),
-        name="add_rows",
-    )(here, there)
+    return (here.astype(jnp.float32) + there.astype(jnp.float32)).astype(jnp.bfloat16)
 
 
 def finish_kernel(
@@ -600,14 +610,14 @@
     )
     bias_rows = jnp.broadcast_to(up_bias[None, :], (16, up_bias.shape[0]))
     up_block = jnp.concatenate([up_weight, bias_rows], axis=0)
-    up_cut, down_cut = up_weight.shape[0] // 2, down_weight.shape[0] // 2
+    up_cut, down_cut = up_weight.shape[0] * 5 // 8, down_weight.shape[0] // 2
     up_pieces = (up_block[:up_cut], up_block[up_cut:])
     down_pieces = (down_weight[:down_cut], down_weight[down_cut:])
     ups, downs = {0: (up_block,)}, {0: (down_weight,)}
     high_mask = high_masks[0]
 
     arrived = lax.all_to_all(
-        outgoing.reshape(sources, capacity + STAT_ROWS, part_width),
+        outgoing.reshape(sources, capacity, part_width),
         ("grp", "dev"),
         split_axis=0,
         concat_axis=0,
@@ -629,7 +639,7 @@
         )
     )
 
-    counts = arrived[:, capacity, 0].astype(jnp.int32)
+    counts = jnp.sum((arrived[:, :, 0] < EMPTY / 2).astype(jnp.int32), axis=1)
     answer_part = attend_prefix(counts, arrived, turned_keys, wide_values)
     downs[low_mask] = swap(downs[0], low_mask)
     up_second = swap(up_pieces[1], high_mask)
@@ -689,7 +699,9 @@
     near, hidden = tie((near, hidden), joined_a)
     near_part, own_part = feed_forward([near, hidden], ups, downs)
     near_sum = swap(near_part, near_mask)
-    cross_sum_b, near_part = lax.optimization_barrier((cross_sum_b, near_part))
+    cross_sum_b, near_part, far_sum_a = lax.optimization_barrier(
+        (cross_sum_b, near_part, far_sum_a)
+    )
     far_sum_b = swap(add_rows(far_part_b, cross_sum_b), far_mask)
     return finish_rows(
         hidden, own_part, near_sum, far_sum_a, far_sum_b, down_bias, out_gain, out_shift

time: 220 us -> 204 us (0.927)
  waiting for transfers between devices: 89.4 us -> 80.5 us
  local copies, waits for them, and re-layouts: 28.4 us -> 24 us
    ppermute x26, waiting for transfers between devices: 89.4 us -> 80.5 us  [swap(): lax.ppermute(leaf, ('grp', 'dev'), pairs)]
    unnamed x92 -> x74, local copies, waits for them, and re-layouts: 17.1 us -> 12.6 us
    pallas_call x2 -> x0, Pallas kernels: 3.6 us -> none  [add_rows(): pl.pallas_call(add_kernel, out_shape=jax.ShapeDtypeStruct(here.shape, jnp...]
  transfers between devices with their start and end apart: 28 -> 28, of which waited for: 10 -> 10; matrix products, arithmetic and copies ran while one was open for 10% -> 11% of each run, Pallas kernels for 25% -> 27%
where the time goes in v9:
time: 204 us
  waiting for transfers between devices  80.5 us (39%)
  Pallas kernels  59.8 us (29%)
  starting transfers between devices  36.3 us (18%)
  local copies, waits for them, and re-layouts  24 us (12%)
  other arithmetic  2.29 us (1%)
    ppermute x26, waiting for transfers between devices, swap(): lax.ppermute(leaf, ('grp', 'dev'), pairs)  80.5 us
    pallas_call x3, Pallas kernels, feed_forward(): pl.pallas_call(functools.partial(mlp_kernel, pieces, up_plan, down_plan),...  31.1 us
    ppermute x26, starting transfers between devices, swap(): lax.ppermute(leaf, ('grp', 'dev'), pairs)  24.1 us
    pallas_call x1, Pallas kernels, attend_prefix(): pl.pallas_call(far_kernel, out_shape=jax.ShapeDtypeStruct((sources, capac...  18.6 us
    unnamed x74, local copies, waits for them, and re-layouts  12.6 us
    all_to_all x1, starting transfers between devices, on_device(): lax.all_to_all(outgoing.reshape(sources, capacity, part_width), ('grp', '...  7.3 us
    all_to_all x1, starting transfers between devices, on_device(): lax.all_to_all(answer_part, ('grp', 'dev'), split_axis=0, concat_axis=0,...  4.87 us
    pallas_call x1, Pallas kernels, attend_suffix(): pl.pallas_call(functools.partial(own_kernel, local_heads), out_shape=(jax...  4.48 us
  transfers between devices with their start and end apart: 28, of which 10 were waited for; matrix products, arithmetic and copies ran while one was open for 11% of the time, Pallas kernels for 27%

profile of v9, /device:TPU:0, one launch (start us, length us, event | category | flops | bytes accessed | tf_op | source)
XLA Modules:
  0.0 203.6 jit_solution(9686098217312553173)
XLA Ops:
  0.0 2.3 %pack_queries.1 = bf16[4,8,64,256]{3,2,1,0:T(8,128)(2,1)} custom-call(s32[1,4]{1,0:T(1,128)} %lengths_ref.5, s32[1,4]{1,0:T(1,128)} %groups_ref.3, bf16[128,2048]{1,0:T(8,128)(2,1)} %query_ref.3), custom_call_target="tpu_custom_call" | custom-call | tf_op jit(solution)/shard_map/pack_queries/pallas_call | solution.py:74
  2.3 7.3 %all-to-all-start = ((bf16[32,64,256]{2,1,0:T(8,128)(2,1)}), bf16[32,64,256]{2,1,0:T(8,128)(2,1)S(1)}, u32[]{:S(2)}, u32[]{:S(2)}) async-start(bf16[32,64,256]{2,1,0:T(8,128)(2,1)} %bitcast.20), calls=%async_computation | async-start | bytes 2097152 | tf_op jit(solution)/shard_map/all_to_all | solution.py:619
  15.0 4.1 %copy.18 = bf16[1,4096,256]{1,2,0:T(8,128)(2,1)} copy(bf16[1,4096,256]{2,1,0:T(8,128)(2,1)} %param.22) | data formatting | bytes 4194304 | tf_op args[6]
  19.1 4.1 %copy.19 = bf16[1,4096,256]{1,2,0:T(8,128)(2,1)} copy(bf16[1,4096,256]{2,1,0:T(8,128)(2,1)} %param.23) | data formatting | bytes 4194304 | tf_op args[7]
  23.2 4.1 %copy.20 = bf16[4096,2,128]{2,0,1:T(8,128)(2,1)} copy(bf16[4096,2,128]{0,2,1:T(8,128)(2,1)} %bitcast.19) | data formatting | bytes 4194304 | tf_op jit(solution)/shard_map/reshape;squeeze | solution.py:631
  27.3 4.1 %concatenate.13.values_hbm = bf16[2,4096,256]{2,1,0:T(8,128)(2,1)} pad(bf16[2,4096,128]{2,1,0:T(8,128)(2,1)} %bitcast.18, bf16[]{:T(256)} %constant.0.clone.1), padding=0_0x0_0x0_128 | pad | bytes 6291458 | tf_op jit(solution)/shard_map/concatenate | solution.py:632
  31.5 4.5 %attend_suffix.1 = (f32[128,2048]{1,0:T(8,128)S(1)}, f32[128,128]{1,0:T(8,128)S(1)}, f32[128,128]{1,0:T(8,128)S(1)}) custom-call(s32[1,4]{1,0:T(1,128)S(1)} %copy-done.10, bf16[128,2048]{1,0:T(8,128)(2,1)S(1)} %copy-done.3, bf16[128,2048]{1,0:T(8,128)(2,1)S(1)} %copy-done.12, bf16[128,2048]{1,0:T(8,128)(2,1)S(1)} %copy-done.13), custom_call_target="tpu_custom_call" | custom-call | flops 1342177280 | bytes 2097152 | tf_op jit(solution)/shard_map/attend_suffix/pallas_call | solution.py:295
  35.9 2.3 %fusion.1 = (bf16[128,2048]{1,0:T(8,128)(2,1)}, bf16[128,2048]{1,0:T(8,128)(2,1)}) fusion(bf16[256,2048]{1,0:T(8,128)(2,1)} %refs_10_.2), kind=kLoop, calls=%fused_computation.11 | loop fusion | bytes 2097152 | tf_op jit(solution)/shard_map/slice | solution.py:615
  38.2 5.3 %collective-permute-done.2 = bf16[1280,256]{1,0:T(8,128)(2,1)} collective-permute-done((bf16[1280,256]{1,0:T(8,128)(2,1)}, bf16[1280,256]{1,0:T(8,128)(2,1)}, u32[]{:S(2)}, u32[]{:S(2)}) %collective-permute-start.2) | collective-permute-done | bytes 655392 | tf_op jit(solution)/shard_map/ppermute | solution.py:416
  43.5 3.0 %collective-permute-done.refs_3_ = bf16[2064,256]{1,0:T(8,128)(2,1)} collective-permute-done((bf16[2064,256]{1,0:T(8,128)(2,1)S(1)}, bf16[2064,256]{1,0:T(8,128)(2,1)}, u32[]{:S(2)}, u32[]{:S(2)}) %collective-permute-start) | collective-permute-done | bytes 1056800 | tf_op jit(solution)/shard_map/ppermute | solution.py:416
  50.2 18.6 %attend_prefix.1 = bf16[32,72,256]{2,1,0:T(8,128)(2,1)} custom-call(s32[32]{0:T(128)} %convert_reduce_fusion.counts_ref, bf16[32,64,256]{2,1,0:T(8,128)(2,1)} %copy-done.26, bf16[256,4096]{1,0:T(8,128)(2,1)} %bitcast.21, bf16[2,4096,256]{2,1,0:T(8,128)(2,1)} %concatenate.13.values_hbm), custom_call_target="tpu_custom_call" | custom-call | flops 8589934592 | bytes 8388608 | tf_op jit(solution)/shard_map/attend_prefix/pallas_call | solution.py:222
  69.7 2.7 %collective-permute-done.6.refs_11_ = bf16[256,2048]{1,0:T(8,128)(2,1)} collective-permute-done((bf16[256,2048]{1,0:T(8,128)(2,1)}, bf16[256,2048]{1,0:T(8,128)(2,1)}, u32[]{:S(2)}, u32[]{:S(2)}) %collective-permute-start.6) | collective-permute-done | bytes 1048608 | tf_op jit(solution)/shard_map/ppermute | solution.py:416
  72.4 4.9 %all-to-all-start.1 = ((bf16[32,72,256]{2,1,0:T(8,128)(2,1)}), bf16[32,72,256]{2,1,0:T(8,128)(2,1)S(1)}, u32[]{:S(2)}, u32[]{:S(2)}) async-start(bf16[32,72,256]{2,1,0:T(8,128)(2,1)} %attend_prefix.1), calls=%async_computation.1 | async-start | bytes 2359296 | tf_op jit(solution)/shard_map/all_to_all | solution.py:654
  82.2 28.0 %collective-permute-done.10 = bf16[128,2048]{1,0:T(8,128)(2,1)S(1)} collective-permute-done((bf16[128,2048]{1,0:T(8,128)(2,1)}, bf16[128,2048]{1,0:T(8,128)(2,1)S(1)}, u32[]{:S(2)}, u32[]{:S(2)}) %collective-permute-start.10) | collective-permute-done | bytes 524320 | tf_op jit(solution)/shard_map/ppermute | solution.py:416
  110.3 4.9 %collective-permute-done.8.refs_5_ = bf16[2064,256]{1,0:T(8,128)(2,1)S(1)} collective-permute-done((bf16[2064,256]{1,0:T(8,128)(2,1)S(1)}, bf16[2064,256]{1,0:T(8,128)(2,1)S(1)}, u32[]{:S(2)}, u32[]{:S(2)}) %collective-permute-start.8) | collective-permute-done | bytes 1056800 | tf_op jit(solution)/shard_map/ppermute | solution.py:416
  116.4 1.9 merge_parts.1
  118.9 2.2 %collective-permute-start.13 = (bf16[64,2048]{1,0:T(8,128)(2,1)S(1)}, bf16[64,2048]{1,0:T(8,128)(2,1)S(1)}, u32[]{:S(2)}, u32[]{:S(2)}) collective-permute-start(bf16[64,2048]{1,0:T(8,128)(2,1)S(1)} %get-tuple-element.151), channel_id=1, source_target_pairs={{0,4},{1,5},{2,6},{3,7},{4,0},{5,1},{6,2},{7,3},{8,12},{9,13},{10,... | collective-permute-start | bytes 786440 | tf_op jit(solution)/shard_map/ppermute | solution.py:416
  122.8 11.0 %collective-permute-done.13.refs_0_ = bf16[64,2048]{1,0:T(8,128)(2,1)S(1)} collective-permute-done((bf16[64,2048]{1,0:T(8,128)(2,1)S(1)}, bf16[64,2048]{1,0:T(8,128)(2,1)S(1)}, u32[]{:S(2)}, u32[]{:S(2)}) %collective-permute-start.13) | collective-permute-done | bytes 262176 | tf_op jit(solution)/shard_map/ppermute | solution.py:416
  135.4 12.5 %collective-permute-done.14.refs_0_ = bf16[64,2048]{1,0:T(8,128)(2,1)S(1)} collective-permute-done((bf16[64,2048]{1,0:T(8,128)(2,1)S(1)}, bf16[64,2048]{1,0:T(8,128)(2,1)S(1)}, u32[]{:S(2)}, u32[]{:S(2)}) %collective-permute-start.14) | collective-permute-done | bytes 262176 | tf_op jit(solution)/shard_map/ppermute | solution.py:416
  151.7 9.4 %feed_forward.3 = (bf16[64,2048]{1,0:T(8,128)(2,1)}, bf16[64,2048]{1,0:T(8,128)(2,1)}) custom-call(bf16[64,2048]{1,0:T(8,128)(2,1)} %copy-done.29, bf16[64,2048]{1,0:T(8,128)(2,1)} %copy-done.30, bf16[2064,256]{1,0:T(8,128)(2,1)} %copy-done.14, bf16[2064,256]{1,0:T(8,128)(2,1)} %collective-permute-done.refs_3_, bf16[2064,256]{1,0:T(8,128)(2,1)} %copy-done.15, ...), custom_call_target="tpu_custom_call" | custom-call | flops 2147483648 | bytes 16777216 | tf_op jit(solution)/shard_map/feed_forward/pallas_call | solution.py:513
  162.7 9.4 %feed_forward.4 = (bf16[64,2048]{1,0:T(8,128)(2,1)}, bf16[64,2048]{1,0:T(8,128)(2,1)}) custom-call(bf16[64,2048]{1,0:T(8,128)(2,1)} %copy-done.28, bf16[64,2048]{1,0:T(8,128)(2,1)} %copy-done.31, bf16[2064,256]{1,0:T(8,128)(2,1)} %copy-done.14, bf16[2064,256]{1,0:T(8,128)(2,1)} %collective-permute-done.refs_3_, bf16[2064,256]{1,0:T(8,128)(2,1)} %copy-done.15, ...), custom_call_target="tpu_custom_call" | custom-call | flops 2147483648 | bytes 16777216 | tf_op jit(solution)/shard_map/feed_forward/pallas_call | solution.py:513
  173.1 12.3 %feed_forward.5 = (bf16[128,2048]{1,0:T(8,128)(2,1)}, bf16[128,2048]{1,0:T(8,128)(2,1)}) custom-call(bf16[128,2048]{1,0:T(8,128)(2,1)} %copy-done.27, bf16[128,2048]{1,0:T(8,128)(2,1)} %copy-done, bf16[2064,256]{1,0:T(8,128)(2,1)} %copy-done.14, bf16[2064,256]{1,0:T(8,128)(2,1)} %collective-permute-done.refs_3_, bf16[2064,256]{1,0:T(8,128)(2,1)} %copy-done.15, ...), custom_call_target="tpu_custom_call" | custom-call | flops 4294967296 | bytes 16777216 | tf_op jit(solution)/shard_map/feed_forward/pallas_call | solution.py:513
  187.0 2.9 %collective-permute-start.25 = (bf16[64,2048]{1,0:T(8,128)(2,1)S(1)}, bf16[64,2048]{1,0:T(8,128)(2,1)S(1)}, u32[]{:S(2)}, u32[]{:S(2)}) collective-permute-start(bf16[64,2048]{1,0:T(8,128)(2,1)S(1)} %add_convert_fusion), channel_id=1, source_target_pairs={{0,4},{1,5},{2,6},{3,7},{4,0},{5,1},{6,2},{7,3},{8,12},{9,13},{10,... | collective-permute-start | bytes 786440 | tf_op jit(solution)/shard_map/ppermute | solution.py:416
  189.9 11.2 %collective-permute-done.25.far_b_ref = bf16[64,2048]{1,0:T(8,128)(2,1)S(1)} collective-permute-done((bf16[64,2048]{1,0:T(8,128)(2,1)S(1)}, bf16[64,2048]{1,0:T(8,128)(2,1)S(1)}, u32[]{:S(2)}, u32[]{:S(2)}) %collective-permute-start.25) | collective-permute-done | bytes 262176 | tf_op jit(solution)/shard_map/ppermute | solution.py:416
  (126 shorter events, 30.1 us)
Async XLA Ops:
  2.3 44.2 %all-to-all-start = ((bf16[32,64,256]{2,1,0:T(8,128)(2,1)}), bf16[32,64,256]{2,1,0:T(8,128)(2,1)S(1)}, u32[]{:S(2)}, u32[]{:S(2)}) async-start(bf16[32,64,256]{2,1,0:T(8,128)(2,1)} %bitcast.20), calls=%async_computation | async-start | bytes 2097152 | tf_op jit(solution)/shard_map/all_to_all | solution.py:619
  9.8 33.8 %collective-permute-start.1 = (bf16[2064,256]{1,0:T(8,128)(2,1)S(1)}, bf16[2064,256]{1,0:T(8,128)(2,1)}, u32[]{:S(2)}, u32[]{:S(2)}) collective-permute-start(bf16[2064,256]{1,0:T(8,128)(2,1)S(1)} %pad_maximum_fusion.refs_2_), channel_id=1, source_target_pairs={{0,8},{1,9},{2,10},{3,11},{4,12},{5,13},{6,14},{7,15},{8,0},{9,1},... | collective-permute-start | bytes 3170312 | tf_op jit(solution)/shard_map/ppermute | solution.py:416
  10.1 36.4 %collective-permute-start = (bf16[2064,256]{1,0:T(8,128)(2,1)S(1)}, bf16[2064,256]{1,0:T(8,128)(2,1)}, u32[]{:S(2)}, u32[]{:S(2)}) collective-permute-start(bf16[2064,256]{1,0:T(8,128)(2,1)S(1)} %pad_maximum_fusion.refs_2_), channel_id=1, source_target_pairs={{0,1},{1,0},{2,3},{3,2},{4,5},{5,4},{6,7},{7,6},{8,9},{9,8},{10,11... | collective-permute-start | bytes 3170312 | tf_op jit(solution)/shard_map/ppermute | solution.py:416
  11.8 31.8 %collective-permute-start.3 = (bf16[256,2048]{1,0:T(8,128)(2,1)}, bf16[256,2048]{1,0:T(8,128)(2,1)}, u32[]{:S(2)}, u32[]{:S(2)}) collective-permute-start(bf16[256,2048]{1,0:T(8,128)(2,1)} %refs_10_.2), channel_id=1, source_target_pairs={{0,8},{1,9},{2,10},{3,11},{4,12},{5,13},{6,14},{7,15},{8,0},{9,1},... | collective-permute-start | bytes 3145736 | tf_op jit(solution)/shard_map/ppermute | solution.py:416
  12.7 30.8 %collective-permute-start.2 = (bf16[1280,256]{1,0:T(8,128)(2,1)}, bf16[1280,256]{1,0:T(8,128)(2,1)}, u32[]{:S(2)}, u32[]{:S(2)}) collective-permute-start(bf16[1280,256]{1,0:T(8,128)(2,1)} %slice.15), channel_id=1, source_target_pairs={{0,2},{1,3},{2,0},{3,1},{4,6},{5,7},{6,4},{7,5},{8,10},{9,11},{10,... | collective-permute-start | bytes 1966088 | tf_op jit(solution)/shard_map/ppermute | solution.py:416
  46.5 25.9 %collective-permute-start.4 = (bf16[2064,256]{1,0:T(8,128)(2,1)}, bf16[2064,256]{1,0:T(8,128)(2,1)}, u32[]{:S(2)}, u32[]{:S(2)}) collective-permute-start(bf16[2064,256]{1,0:T(8,128)(2,1)} %collective-permute-done.refs_3_), channel_id=1, source_target_pairs={{0,8},{1,9},{2,10},{3,11},{4,12},{5,13},{6,14},{7,15},{8,0},{9,1},... | collective-permute-start | bytes 3170312 | tf_op jit(solution)/shard_map/ppermute | solution.py:416
  46.5 25.9 %collective-permute-start.6 = (bf16[256,2048]{1,0:T(8,128)(2,1)}, bf16[256,2048]{1,0:T(8,128)(2,1)}, u32[]{:S(2)}, u32[]{:S(2)}) collective-permute-start(bf16[256,2048]{1,0:T(8,128)(2,1)} %refs_10_.2), channel_id=1, source_target_pairs={{0,1},{1,0},{2,3},{3,2},{4,5},{5,4},{6,7},{7,6},{8,9},{9,8},{10,11... | collective-permute-start | bytes 3145736 | tf_op jit(solution)/shard_map/ppermute | solution.py:416
  46.9 21.9 %collective-permute-start.5 = (bf16[784,256]{1,0:T(8,128)(2,1)}, bf16[784,256]{1,0:T(8,128)(2,1)S(1)}, u32[]{:S(2)}, u32[]{:S(2)}) collective-permute-start(bf16[784,256]{1,0:T(8,128)(2,1)} %fusion), channel_id=1, source_target_pairs={{0,2},{1,3},{2,0},{3,1},{4,6},{5,7},{6,4},{7,5},{8,10},{9,11},{10,... | collective-permute-start | bytes 1204232 | tf_op jit(solution)/shard_map/ppermute | solution.py:416
  48.6 21.1 %collective-permute-start.7 = (bf16[128,2048]{1,0:T(8,128)(2,1)}, bf16[128,2048]{1,0:T(8,128)(2,1)S(1)}, u32[]{:S(2)}, u32[]{:S(2)}) collective-permute-start(bf16[128,2048]{1,0:T(8,128)(2,1)} %get-tuple-element.116), channel_id=1, source_target_pairs={{0,2},{1,3},{2,0},{3,1},{4,6},{5,7},{6,4},{7,5},{8,10},{9,11},{10,... | collective-permute-start | bytes 1572872 | tf_op jit(solution)/shard_map/ppermute | solution.py:416
  72.4 43.9 %all-to-all-start.1 = ((bf16[32,72,256]{2,1,0:T(8,128)(2,1)}), bf16[32,72,256]{2,1,0:T(8,128)(2,1)S(1)}, u32[]{:S(2)}, u32[]{:S(2)}) async-start(bf16[32,72,256]{2,1,0:T(8,128)(2,1)} %attend_prefix.1), calls=%async_computation.1 | async-start | bytes 2359296 | tf_op jit(solution)/shard_map/all_to_all | solution.py:654
  77.3 32.9 %collective-permute-start.10 = (bf16[128,2048]{1,0:T(8,128)(2,1)}, bf16[128,2048]{1,0:T(8,128)(2,1)S(1)}, u32[]{:S(2)}, u32[]{:S(2)}) collective-permute-start(bf16[128,2048]{1,0:T(8,128)(2,1)} %get-tuple-element.128), channel_id=1, source_target_pairs={{0,2},{1,3},{2,0},{3,1},{4,6},{5,7},{6,4},{7,5},{8,10},{9,11},{10,... | collective-permute-start | bytes 1572872 | tf_op jit(solution)/shard_map/ppermute | solution.py:416
  80.3 30.0 %collective-permute-start.9 = (bf16[2064,256]{1,0:T(8,128)(2,1)S(1)}, bf16[2064,256]{1,0:T(8,128)(2,1)S(1)}, u32[]{:S(2)}, u32[]{:S(2)}) collective-permute-start(bf16[2064,256]{1,0:T(8,128)(2,1)S(1)} %constant_dynamic-update-slice_fusion.refs_4_), channel_id=1, source_target_pairs={{0,8},{1,9},{2,10},{3,11},{4,12},{5,13},{6,14},{7,15},{8,0},{9,1},... | collective-permute-start | bytes 3170312 | tf_op jit(solution)/shard_map/ppermute | solution.py:416
  80.4 34.8 %collective-permute-start.8 = (bf16[2064,256]{1,0:T(8,128)(2,1)S(1)}, bf16[2064,256]{1,0:T(8,128)(2,1)S(1)}, u32[]{:S(2)}, u32[]{:S(2)}) collective-permute-start(bf16[2064,256]{1,0:T(8,128)(2,1)S(1)} %constant_dynamic-update-slice_fusion.refs_4_), channel_id=1, source_target_pairs={{0,1},{1,0},{2,3},{3,2},{4,5},{5,4},{6,7},{7,6},{8,9},{9,8},{10,11... | collective-permute-start | bytes 3170312 | tf_op jit(solution)/shard_map/ppermute | solution.py:416
  82.0 28.3 %collective-permute-start.11 = (bf16[256,2048]{1,0:T(8,128)(2,1)}, bf16[256,2048]{1,0:T(8,128)(2,1)S(1)}, u32[]{:S(2)}, u32[]{:S(2)}) collective-permute-start(bf16[256,2048]{1,0:T(8,128)(2,1)} %collective-permute-done.6.refs_11_), channel_id=1, source_target_pairs={{0,8},{1,9},{2,10},{3,11},{4,12},{5,13},{6,14},{7,15},{8,0},{9,1},... | collective-permute-start | bytes 3145736 | tf_op jit(solution)/shard_map/ppermute | solution.py:416
  118.3 29.6 %collective-permute-start.17 = (bf16[2064,256]{1,0:T(8,128)(2,1)S(1)}, bf16[2064,256]{1,0:T(8,128)(2,1)S(1)}, u32[]{:S(2)}, u32[]{:S(2)}) collective-permute-start(bf16[2064,256]{1,0:T(8,128)(2,1)S(1)} %copy-done.20), channel_id=1, source_target_pairs={{0,8},{1,9},{2,10},{3,11},{4,12},{5,13},{6,14},{7,15},{8,0},{9,1},... | collective-permute-start | bytes 3170312 | tf_op jit(solution)/shard_map/ppermute | solution.py:416
  118.4 29.5 %collective-permute-start.18 = (bf16[256,2048]{1,0:T(8,128)(2,1)S(1)}, bf16[256,2048]{1,0:T(8,128)(2,1)S(1)}, u32[]{:S(2)}, u32[]{:S(2)}) collective-permute-start(bf16[256,2048]{1,0:T(8,128)(2,1)S(1)} %copy-done.17), channel_id=1, source_target_pairs={{0,1},{1,0},{2,3},{3,2},{4,5},{5,4},{6,7},{7,6},{8,9},{9,8},{10,11... | collective-permute-start | bytes 3145736 | tf_op jit(solution)/shard_map/ppermute | solution.py:416
  118.9 14.9 %collective-permute-start.13 = (bf16[64,2048]{1,0:T(8,128)(2,1)S(1)}, bf16[64,2048]{1,0:T(8,128)(2,1)S(1)}, u32[]{:S(2)}, u32[]{:S(2)}) collective-permute-start(bf16[64,2048]{1,0:T(8,128)(2,1)S(1)} %get-tuple-element.151), channel_id=1, source_target_pairs={{0,4},{1,5},{2,6},{3,7},{4,0},{5,1},{6,2},{7,3},{8,12},{9,13},{10,... | collective-permute-start | bytes 786440 | tf_op jit(solution)/shard_map/ppermute | solution.py:416
  121.2 14.2 %collective-permute-start.16 = (bf16[128,2048]{1,0:T(8,128)(2,1)S(1)}, bf16[128,2048]{1,0:T(8,128)(2,1)S(1)}, u32[]{:S(2)}, u32[]{:S(2)}) collective-permute-start(bf16[128,2048]{1,0:T(8,128)(2,1)S(1)} %get-tuple-element.193.refs_1_.hidden_ref), channel_id=1, source_target_pairs={{0,16},{1,17},{2,18},{3,19},{4,20},{5,21},{6,22},{7,23},{8,24},{9,... | collective-permute-start | bytes 1572872 | tf_op jit(solution)/shard_map/ppermute | solution.py:416
  133.8 14.1 %collective-permute-start.14 = (bf16[64,2048]{1,0:T(8,128)(2,1)S(1)}, bf16[64,2048]{1,0:T(8,128)(2,1)S(1)}, u32[]{:S(2)}, u32[]{:S(2)}) collective-permute-start(bf16[64,2048]{1,0:T(8,128)(2,1)S(1)} %get-tuple-element.152), channel_id=1, source_target_pairs={{0,4},{1,5},{2,6},{3,7},{4,0},{5,1},{6,2},{7,3},{8,12},{9,13},{10,... | collective-permute-start | bytes 786440 | tf_op jit(solution)/shard_map/ppermute | solution.py:416
  133.8 14.1 %collective-permute-start.15 = (bf16[64,2048]{1,0:T(8,128)(2,1)S(1)}, bf16[64,2048]{1,0:T(8,128)(2,1)S(1)}, u32[]{:S(2)}, u32[]{:S(2)}) collective-permute-start(bf16[64,2048]{1,0:T(8,128)(2,1)S(1)} %collective-permute-done.13.refs_0_), channel_id=1, source_target_pairs={{0,16},{1,17},{2,18},{3,19},{4,20},{5,21},{6,22},{7,23},{8,24},{9,... | collective-permute-start | bytes 786440 | tf_op jit(solution)/shard_map/ppermute | solution.py:416
  172.3 14.6 %collective-permute-start.24 = (bf16[64,2048]{1,0:T(8,128)(2,1)S(1)}, bf16[64,2048]{1,0:T(8,128)(2,1)S(1)}, u32[]{:S(2)}, u32[]{:S(2)}) collective-permute-start(bf16[64,2048]{1,0:T(8,128)(2,1)S(1)} %add_convert_fusion.1), channel_id=1, source_target_pairs={{0,4},{1,5},{2,6},{3,7},{4,0},{5,1},{6,2},{7,3},{8,12},{9,13},{10,... | collective-permute-start | bytes 786440 | tf_op jit(solution)/shard_map/ppermute | solution.py:416
  172.4 14.5 %collective-permute-start.23 = (bf16[64,2048]{1,0:T(8,128)(2,1)}, bf16[64,2048]{1,0:T(8,128)(2,1)S(1)}, u32[]{:S(2)}, u32[]{:S(2)}) collective-permute-start(bf16[64,2048]{1,0:T(8,128)(2,1)} %get-tuple-element.197), channel_id=1, source_target_pairs={{0,16},{1,17},{2,18},{3,19},{4,20},{5,21},{6,22},{7,23},{8,24},{9,... | collective-permute-start | bytes 786440 | tf_op jit(solution)/shard_map/ppermute | solution.py:416
  185.4 15.6 %collective-permute-start.22 = (bf16[128,2048]{1,0:T(8,128)(2,1)}, bf16[128,2048]{1,0:T(8,128)(2,1)S(1)}, u32[]{:S(2)}, u32[]{:S(2)}) collective-permute-start(bf16[128,2048]{1,0:T(8,128)(2,1)} %get-tuple-element.196), channel_id=1, source_target_pairs={{0,16},{1,17},{2,18},{3,19},{4,20},{5,21},{6,22},{7,23},{8,24},{9,... | collective-permute-start | bytes 1572872 | tf_op jit(solution)/shard_map/ppermute | solution.py:416
  187.0 14.1 %collective-permute-start.25 = (bf16[64,2048]{1,0:T(8,128)(2,1)S(1)}, bf16[64,2048]{1,0:T(8,128)(2,1)S(1)}, u32[]{:S(2)}, u32[]{:S(2)}) collective-permute-start(bf16[64,2048]{1,0:T(8,128)(2,1)S(1)} %add_convert_fusion), channel_id=1, source_target_pairs={{0,4},{1,5},{2,6},{3,7},{4,0},{5,1},{6,2},{7,3},{8,12},{9,13},{10,... | collective-permute-start | bytes 786440 | tf_op jit(solution)/shard_map/ppermute | solution.py:416
  (39 other events, 510.3 us)

commit v10 on v9

--- a/solution.py
+++ b/solution.py
@@ -12,6 +12,7 @@
 LANES = 128
 STAT_ROWS = 8
 STREAMS = 4
+FETCHES = 8
 EMPTY = 64.0
 ROW_BLOCK = 256
 KEY_CHUNK = 1024
@@ -101,11 +102,22 @@
     values_ref,
     sems,
 ):
-    copies = [
-        pltpu.make_async_copy(keys_hbm, keys_ref, sems.at[0]),
-        pltpu.make_async_copy(values_hbm, values_ref, sems.at[1]),
-    ]
-    for copy in copies:
+    key_step = keys_ref.shape[0] // FETCHES
+    value_step = values_ref.shape[1] // FETCHES
+    key_copies, value_copies = [], []
+    for fetch in range(FETCHES):
+        rows = pl.ds(fetch * key_step, key_step)
+        key_copies.append(
+            pltpu.make_async_copy(keys_hbm.at[rows], keys_ref.at[rows], sems.at[0, fetch])
+        )
+        rows = pl.ds(fetch * value_step, value_step)
+        for head in range(values_ref.shape[0]):
+            value_copies.append(
+                pltpu.make_async_copy(
+                    values_hbm.at[head, rows], values_ref.at[head, rows], sems.at[1 + head, fetch]
+                )
+            )
+    for copy in key_copies + value_copies:
         copy.start()
     sources, capacity, part_width = arrived_ref.shape
     local_heads = part_width // HD
@@ -170,13 +182,15 @@
     def slot_of(block, head):
         return (block * local_heads + head) % 2 if local_heads % 2 else head % 2
 
-    for copy in copies:
+    for copy in key_copies:
         copy.wait()
     first_rows = load_queries(0, 0)
     part_top = None
     for chunk in range(chunks):
         part_top = score_chunk(first_rows, 0, 0, chunk, part_top)
     finish_top(part_top, 0)
+    for copy in value_copies:
+        copy.wait()
 
     def one_block(block, carry):
         for head in range(local_heads):
@@ -232,7 +246,7 @@
             pltpu.VMEM((2, ROW_BLOCK, LANES), jnp.float32),
             pltpu.VMEM(turned_keys.shape, jnp.bfloat16),
             pltpu.VMEM(wide_values.shape, jnp.bfloat16),
-            pltpu.SemaphoreType.DMA((2,)),
+            pltpu.SemaphoreType.DMA((1 + local_heads, FETCHES)),
         ],
         compiler_params=pltpu.CompilerParams(vmem_limit_bytes=58 * mebibyte),
         cost_estimate=pl.CostEstimate(
@@ -475,22 +489,28 @@
                 )
             begin += height
         copies.append(held)
-    for held in copies:
+    ahead = min(4, len(copies))
+
+    def arrive(at):
+        for copy in copies[at]:
+            copy.wait()
+        for copy in copies[at + ahead] if at + ahead < len(copies) else ():
+            copy.start()
+
+    for held in copies[:ahead]:
         for copy in held:
             copy.start()
     rows = jnp.concatenate([ref[...] for ref in row_refs], axis=0)
     activations = []
     for part in range(parts):
-        for copy in copies[part]:
-            copy.wait()
+        arrive(part)
         product = jnp.dot(
             rows, up_ref[part, :model_width, :], preferred_element_type=jnp.float32
         )
         offset = up_ref[part, model_width:, :].astype(jnp.float32)[0:1]
         activations.append(jax.nn.gelu(product + offset, approximate=True).astype(jnp.bfloat16))
-    for held in copies[parts:]:
-        for copy in held:
-            copy.wait()
+    for part in range(parts):
+        arrive(parts + part)
     total = jnp.dot(
         jnp.concatenate(activations, axis=1), down_ref[...], preferred_element_type=jnp.float32
     ).astype(jnp.bfloat16)
@@ -672,18 +692,24 @@
     )
     far_a = swap(hidden_a, far_mask)
     near = swap(hidden, near_mask)
-    downs[low_mask ^ high_mask] = swap(downs[high_mask], low_mask)
+    crossing = (
+        swap(downs[high_mask][0][:down_cut], low_mask),
+        swap(downs[low_mask][0][down_cut:], high_mask),
+    )
+    far_a, near, crossing, hidden_b, ups = lax.optimization_barrier(
+        (far_a, near, crossing, hidden_b, ups)
+    )
+    far_b = swap(hidden_b, far_mask)
+    cross_a = swap(far_a, near_mask)
+    downs[low_mask ^ high_mask] = crossing
     ups = complete(ups, group_masks + column_masks)
-    far_b = swap(tie(hidden_b, far_a), far_mask)
-    cross_a = swap(far_a, near_mask)
-    far_b, cross_a, near, ups, downs = lax.optimization_barrier(
-        (far_b, cross_a, near, ups, downs)
-    )
-    cross_b = swap(far_b, near_mask)
     downs = complete(downs, group_masks + column_masks)
     order = sorted(ups)
     ups = [ups[mask] for mask in order]
     downs = [downs[mask] for mask in order]
+    near_part, own_part = feed_forward([near, hidden], ups, downs)
+    far_b, cross_a, near_part = lax.optimization_barrier((far_b, cross_a, near_part))
+    cross_b = swap(far_b, near_mask)
     far_part_a, cross_part_a = feed_forward([far_a, cross_a], ups, downs)
     cross_b, far_part_a, cross_part_a = lax.optimization_barrier(
         (cross_b, far_part_a, cross_part_a)
@@ -693,16 +719,10 @@
     cross_sum_a, far_part_b, cross_part_b = lax.optimization_barrier(
         (cross_sum_a, far_part_b, cross_part_b)
     )
+    far_sum_a = swap(add_rows(far_part_a, cross_sum_a), far_mask)
     cross_sum_b = swap(cross_part_b, near_mask)
-    joined_a = add_rows(far_part_a, cross_sum_a)
-    far_sum_a = swap(joined_a, far_mask)
-    near, hidden = tie((near, hidden), joined_a)
-    near_part, own_part = feed_forward([near, hidden], ups, downs)
-    near_sum = swap(near_part, near_mask)
-    cross_sum_b, near_part, far_sum_a = lax.optimization_barrier(
-        (cross_sum_b, near_part, far_sum_a)
-    )
     far_sum_b = swap(add_rows(far_part_b, cross_sum_b), far_mask)
+    near_sum = swap(tie(near_part, cross_part_b), near_mask)
     return finish_rows(
         hidden, own_part, near_sum, far_sum_a, far_sum_b, down_bias, out_gain, out_shift
     )

time: 204 us -> 214 us (1.049)
  Pallas kernels: 59.8 us -> 65.9 us
  starting transfers between devices: 36.3 us -> 40.4 us
  waiting for transfers between devices: 80.5 us -> 77.8 us
    pallas_call x3, Pallas kernels: 31.1 us -> 37.8 us  [feed_forward(): pl.pallas_call(functools.partial(mlp_kernel, pieces, up_plan, down_plan),...]
    ppermute x26 -> x28, starting transfers between devices: 24.1 us -> 28.4 us  [swap(): lax.ppermute(leaf, ('grp', 'dev'), pairs)]
    ppermute x26 -> x28, waiting for transfers between devices: 80.5 us -> 77.7 us  [swap(): lax.ppermute(leaf, ('grp', 'dev'), pairs)]
    unnamed x74 -> x78, local copies, waits for them, and re-layouts: 12.6 us -> 12.5 us
  transfers between devices with their start and end apart: 28 -> 30, of which waited for: 10 -> 11; matrix products, arithmetic and copies ran while one was open for 11% -> 11% of each run, Pallas kernels for 27% -> 28%
where the time goes in v10:
time: 214 us; the launch traced here: 213 us
  waiting for transfers between devices  77.8 us (36%)
  Pallas kernels  65.9 us (31%)
  starting transfers between devices  40.4 us (19%)
  local copies, waits for them, and re-layouts  25.4 us (12%)
  other arithmetic  3.17 us (1%)
    ppermute x28, waiting for transfers between devices, swap(): lax.ppermute(leaf, ('grp', 'dev'), pairs)  77.7 us
    pallas_call x3, Pallas kernels, feed_forward(): pl.pallas_call(functools.partial(mlp_kernel, pieces, up_plan, down_plan),...  37.8 us
    ppermute x28, starting transfers between devices, swap(): lax.ppermute(leaf, ('grp', 'dev'), pairs)  28.4 us
    pallas_call x1, Pallas kernels, attend_prefix(): pl.pallas_call(far_kernel, out_shape=jax.ShapeDtypeStruct((sources, capac...  18 us
    unnamed x78, local copies, waits for them, and re-layouts  12.5 us
    all_to_all x1, starting transfers between devices, on_device(): lax.all_to_all(outgoing.reshape(sources, capacity, part_width), ('grp', '...  7.3 us
    all_to_all x1, starting transfers between devices, on_device(): lax.all_to_all(answer_part, ('grp', 'dev'), split_axis=0, concat_axis=0,...  4.72 us
    pallas_call x1, Pallas kernels, attend_suffix(): pl.pallas_call(functools.partial(own_kernel, local_heads), out_shape=(jax...  4.49 us
  transfers between devices with their start and end apart: 30, of which 11 were waited for; matrix products, arithmetic and copies ran while one was open for 11% of the time, Pallas kernels for 28%

profile of v10, /device:TPU:0, one launch (start us, length us, event | category | flops | bytes accessed | tf_op | source)
XLA Modules:
  0.0 213.2 jit_solution(1579835966689718165)
XLA Ops:
  0.0 2.4 %pack_queries.1 = bf16[4,8,64,256]{3,2,1,0:T(8,128)(2,1)} custom-call(s32[1,4]{1,0:T(1,128)} %lengths_ref.5, s32[1,4]{1,0:T(1,128)} %groups_ref.3, bf16[128,2048]{1,0:T(8,128)(2,1)} %query_ref.3), custom_call_target="tpu_custom_call" | custom-call | tf_op jit(solution)/shard_map/pack_queries/pallas_call | solution.py:75
  2.4 7.3 %all-to-all-start = ((bf16[32,64,256]{2,1,0:T(8,128)(2,1)}), bf16[32,64,256]{2,1,0:T(8,128)(2,1)S(1)}, u32[]{:S(2)}, u32[]{:S(2)}) async-start(bf16[32,64,256]{2,1,0:T(8,128)(2,1)} %bitcast.20), calls=%async_computation | async-start | bytes 2097152 | tf_op jit(solution)/shard_map/all_to_all | solution.py:639
  15.0 4.2 %copy.18 = bf16[1,4096,256]{1,2,0:T(8,128)(2,1)} copy(bf16[1,4096,256]{2,1,0:T(8,128)(2,1)} %param.22) | data formatting | bytes 4194304 | tf_op args[6]
  19.2 4.1 %copy.19 = bf16[1,4096,256]{1,2,0:T(8,128)(2,1)} copy(bf16[1,4096,256]{2,1,0:T(8,128)(2,1)} %param.23) | data formatting | bytes 4194304 | tf_op args[7]
  23.3 4.1 %copy.20 = bf16[4096,2,128]{2,0,1:T(8,128)(2,1)} copy(bf16[4096,2,128]{0,2,1:T(8,128)(2,1)} %bitcast.19) | data formatting | bytes 4194304 | tf_op jit(solution)/shard_map/reshape;squeeze | solution.py:651
  27.4 4.1 %concatenate.13.values_hbm = bf16[2,4096,256]{2,1,0:T(8,128)(2,1)} pad(bf16[2,4096,128]{2,1,0:T(8,128)(2,1)} %bitcast.18, bf16[]{:T(256)} %constant.0.clone.1), padding=0_0x0_0x0_128 | pad | bytes 6291458 | tf_op jit(solution)/shard_map/concatenate | solution.py:652
  31.5 4.5 %attend_suffix.1 = (f32[128,2048]{1,0:T(8,128)S(1)}, f32[128,128]{1,0:T(8,128)S(1)}, f32[128,128]{1,0:T(8,128)S(1)}) custom-call(s32[1,4]{1,0:T(1,128)S(1)} %copy-done.10, bf16[128,2048]{1,0:T(8,128)(2,1)S(1)} %copy-done.3, bf16[128,2048]{1,0:T(8,128)(2,1)S(1)} %copy-done.12, bf16[128,2048]{1,0:T(8,128)(2,1)S(1)} %copy-done.13), custom_call_target="tpu_custom_call" | custom-call | flops 1342177280 | bytes 2097152 | tf_op jit(solution)/shard_map/attend_suffix/pallas_call | solution.py:309
  38.3 5.2 %collective-permute-done.2 = bf16[1280,256]{1,0:T(8,128)(2,1)} collective-permute-done((bf16[1280,256]{1,0:T(8,128)(2,1)}, bf16[1280,256]{1,0:T(8,128)(2,1)}, u32[]{:S(2)}, u32[]{:S(2)}) %collective-permute-start.2) | collective-permute-done | bytes 655392 | tf_op jit(solution)/shard_map/ppermute | solution.py:430
  43.6 3.0 %collective-permute-done.refs_3_ = bf16[2064,256]{1,0:T(8,128)(2,1)} collective-permute-done((bf16[2064,256]{1,0:T(8,128)(2,1)S(1)}, bf16[2064,256]{1,0:T(8,128)(2,1)}, u32[]{:S(2)}, u32[]{:S(2)}) %collective-permute-start) | collective-permute-done | bytes 1056800 | tf_op jit(solution)/shard_map/ppermute | solution.py:430
  50.2 18.0 %attend_prefix.1 = bf16[32,72,256]{2,1,0:T(8,128)(2,1)} custom-call(s32[32]{0:T(128)} %convert_reduce_fusion.counts_ref, bf16[32,64,256]{2,1,0:T(8,128)(2,1)} %copy-done.28, bf16[256,4096]{1,0:T(8,128)(2,1)} %bitcast.21, bf16[2,4096,256]{2,1,0:T(8,128)(2,1)} %concatenate.13.values_hbm), custom_call_target="tpu_custom_call" | custom-call | flops 8589934592 | bytes 8388608 | tf_op jit(solution)/shard_map/attend_prefix/pallas_call | solution.py:236
  69.8 2.7 %collective-permute-done.6.refs_11_ = bf16[256,2048]{1,0:T(8,128)(2,1)} collective-permute-done((bf16[256,2048]{1,0:T(8,128)(2,1)}, bf16[256,2048]{1,0:T(8,128)(2,1)}, u32[]{:S(2)}, u32[]{:S(2)}) %collective-permute-start.6) | collective-permute-done | bytes 1048608 | tf_op jit(solution)/shard_map/ppermute | solution.py:430
  72.4 4.7 %all-to-all-start.1 = ((bf16[32,72,256]{2,1,0:T(8,128)(2,1)}), bf16[32,72,256]{2,1,0:T(8,128)(2,1)S(1)}, u32[]{:S(2)}, u32[]{:S(2)}) async-start(bf16[32,72,256]{2,1,0:T(8,128)(2,1)} %attend_prefix.1), calls=%async_computation.1 | async-start | bytes 2359296 | tf_op jit(solution)/shard_map/all_to_all | solution.py:674
  82.1 28.0 %collective-permute-done.10 = bf16[128,2048]{1,0:T(8,128)(2,1)S(1)} collective-permute-done((bf16[128,2048]{1,0:T(8,128)(2,1)}, bf16[128,2048]{1,0:T(8,128)(2,1)S(1)}, u32[]{:S(2)}, u32[]{:S(2)}) %collective-permute-start.10) | collective-permute-done | bytes 524320 | tf_op jit(solution)/shard_map/ppermute | solution.py:430
  110.2 4.9 %collective-permute-done.8.refs_5_ = bf16[2064,256]{1,0:T(8,128)(2,1)S(1)} collective-permute-done((bf16[2064,256]{1,0:T(8,128)(2,1)S(1)}, bf16[2064,256]{1,0:T(8,128)(2,1)S(1)}, u32[]{:S(2)}, u32[]{:S(2)}) %collective-permute-start.8) | collective-permute-done | bytes 1056800 | tf_op jit(solution)/shard_map/ppermute | solution.py:430
  123.0 2.4 %collective-permute-start.13 = (bf16[64,2048]{1,0:T(8,128)(2,1)S(1)}, bf16[64,2048]{1,0:T(8,128)(2,1)S(1)}, u32[]{:S(2)}, u32[]{:S(2)}) collective-permute-start(bf16[64,2048]{1,0:T(8,128)(2,1)S(1)} %get-tuple-element.144), channel_id=1, source_target_pairs={{0,4},{1,5},{2,6},{3,7},{4,0},{5,1},{6,2},{7,3},{8,12},{9,13},{10,... | collective-permute-start | bytes 786440 | tf_op jit(solution)/shard_map/ppermute | solution.py:430
  125.4 12.2 %collective-permute-done.13.refs_0_ = bf16[64,2048]{1,0:T(8,128)(2,1)S(1)} collective-permute-done((bf16[64,2048]{1,0:T(8,128)(2,1)S(1)}, bf16[64,2048]{1,0:T(8,128)(2,1)S(1)}, u32[]{:S(2)}, u32[]{:S(2)}) %collective-permute-start.13) | collective-permute-done | bytes 262176 | tf_op jit(solution)/shard_map/ppermute | solution.py:430
  139.3 2.4 %collective-permute-start.20 = (bf16[64,2048]{1,0:T(8,128)(2,1)S(1)}, bf16[64,2048]{1,0:T(8,128)(2,1)S(1)}, u32[]{:S(2)}, u32[]{:S(2)}) collective-permute-start(bf16[64,2048]{1,0:T(8,128)(2,1)S(1)} %get-tuple-element.170), channel_id=1, source_target_pairs={{0,4},{1,5},{2,6},{3,7},{4,0},{5,1},{6,2},{7,3},{8,12},{9,13},{10,... | collective-permute-start | bytes 786440 | tf_op jit(solution)/shard_map/ppermute | solution.py:430
  145.2 14.9 %feed_forward.3 = (bf16[128,2048]{1,0:T(8,128)(2,1)}, bf16[128,2048]{1,0:T(8,128)(2,1)}) custom-call(bf16[128,2048]{1,0:T(8,128)(2,1)} %copy-done.29, bf16[128,2048]{1,0:T(8,128)(2,1)} %copy-done, bf16[2064,256]{1,0:T(8,128)(2,1)} %copy-done.14, bf16[2064,256]{1,0:T(8,128)(2,1)} %collective-permute-done.refs_3_, bf16[2064,256]{1,0:T(8,128)(2,1)} %copy-done.17, ...), custom_call_target="tpu_custom_call" | custom-call | flops 4294967296 | bytes 16777216 | tf_op jit(solution)/shard_map/feed_forward/pallas_call | solution.py:533
  161.2 11.3 %feed_forward.4 = (bf16[64,2048]{1,0:T(8,128)(2,1)}, bf16[64,2048]{1,0:T(8,128)(2,1)}) custom-call(bf16[64,2048]{1,0:T(8,128)(2,1)} %copy-done.30, bf16[64,2048]{1,0:T(8,128)(2,1)} %copy-done.33, bf16[2064,256]{1,0:T(8,128)(2,1)} %copy-done.14, bf16[2064,256]{1,0:T(8,128)(2,1)} %collective-permute-done.refs_3_, bf16[2064,256]{1,0:T(8,128)(2,1)} %copy-done.17, ...), custom_call_target="tpu_custom_call" | custom-call | flops 2147483648 | bytes 16777216 | tf_op jit(solution)/shard_map/feed_forward/pallas_call | solution.py:533
  173.7 11.5 %feed_forward.5 = (bf16[64,2048]{1,0:T(8,128)(2,1)}, bf16[64,2048]{1,0:T(8,128)(2,1)}) custom-call(bf16[64,2048]{1,0:T(8,128)(2,1)} %copy-done.31, bf16[64,2048]{1,0:T(8,128)(2,1)} %copy-done.32, bf16[2064,256]{1,0:T(8,128)(2,1)} %copy-done.14, bf16[2064,256]{1,0:T(8,128)(2,1)} %collective-permute-done.refs_3_, bf16[2064,256]{1,0:T(8,128)(2,1)} %copy-done.17, ...), custom_call_target="tpu_custom_call" | custom-call | flops 2147483648 | bytes 16777216 | tf_op jit(solution)/shard_map/feed_forward/pallas_call | solution.py:533
  186.4 2.4 %collective-permute-start.25 = (bf16[64,2048]{1,0:T(8,128)(2,1)S(1)}, bf16[64,2048]{1,0:T(8,128)(2,1)S(1)}, u32[]{:S(2)}, u32[]{:S(2)}) collective-permute-start(bf16[64,2048]{1,0:T(8,128)(2,1)S(1)} %add_convert_fusion.1), channel_id=1, source_target_pairs={{0,4},{1,5},{2,6},{3,7},{4,0},{5,1},{6,2},{7,3},{8,12},{9,13},{10,... | collective-permute-start | bytes 786440 | tf_op jit(solution)/shard_map/ppermute | solution.py:430
  189.5 5.3 %collective-permute-done.26 = bf16[64,2048]{1,0:T(8,128)(2,1)S(1)} collective-permute-done((bf16[64,2048]{1,0:T(8,128)(2,1)}, bf16[64,2048]{1,0:T(8,128)(2,1)S(1)}, u32[]{:S(2)}, u32[]{:S(2)}) %collective-permute-start.26) | collective-permute-done | bytes 262176 | tf_op jit(solution)/shard_map/ppermute | solution.py:430
  197.8 10.0 %collective-permute-done.25.far_a_ref = bf16[64,2048]{1,0:T(8,128)(2,1)S(1)} collective-permute-done((bf16[64,2048]{1,0:T(8,128)(2,1)S(1)}, bf16[64,2048]{1,0:T(8,128)(2,1)S(1)}, u32[]{:S(2)}, u32[]{:S(2)}) %collective-permute-start.25) | collective-permute-done | bytes 262176 | tf_op jit(solution)/shard_map/ppermute | solution.py:430
  207.8 3.9 %collective-permute-done.27.far_b_ref = bf16[64,2048]{1,0:T(8,128)(2,1)S(1)} collective-permute-done((bf16[64,2048]{1,0:T(8,128)(2,1)S(1)}, bf16[64,2048]{1,0:T(8,128)(2,1)S(1)}, u32[]{:S(2)}, u32[]{:S(2)}) %collective-permute-start.27) | collective-permute-done | bytes 262176 | tf_op jit(solution)/shard_map/ppermute | solution.py:430
  (136 shorter events, 39.1 us)
Async XLA Ops:
  2.4 44.2 %all-to-all-start = ((bf16[32,64,256]{2,1,0:T(8,128)(2,1)}), bf16[32,64,256]{2,1,0:T(8,128)(2,1)S(1)}, u32[]{:S(2)}, u32[]{:S(2)}) async-start(bf16[32,64,256]{2,1,0:T(8,128)(2,1)} %bitcast.20), calls=%async_computation | async-start | bytes 2097152 | tf_op jit(solution)/shard_map/all_to_all | solution.py:639
  9.8 33.8 %collective-permute-start.1 = (bf16[2064,256]{1,0:T(8,128)(2,1)S(1)}, bf16[2064,256]{1,0:T(8,128)(2,1)}, u32[]{:S(2)}, u32[]{:S(2)}) collective-permute-start(bf16[2064,256]{1,0:T(8,128)(2,1)S(1)} %pad_maximum_fusion.refs_2_), channel_id=1, source_target_pairs={{0,8},{1,9},{2,10},{3,11},{4,12},{5,13},{6,14},{7,15},{8,0},{9,1},... | collective-permute-start | bytes 3170312 | tf_op jit(solution)/shard_map/ppermute | solution.py:430
  10.1 36.4 %collective-permute-start = (bf16[2064,256]{1,0:T(8,128)(2,1)S(1)}, bf16[2064,256]{1,0:T(8,128)(2,1)}, u32[]{:S(2)}, u32[]{:S(2)}) collective-permute-start(bf16[2064,256]{1,0:T(8,128)(2,1)S(1)} %pad_maximum_fusion.refs_2_), channel_id=1, source_target_pairs={{0,1},{1,0},{2,3},{3,2},{4,5},{5,4},{6,7},{7,6},{8,9},{9,8},{10,11... | collective-permute-start | bytes 3170312 | tf_op jit(solution)/shard_map/ppermute | solution.py:430
  11.8 31.8 %collective-permute-start.3 = (bf16[256,2048]{1,0:T(8,128)(2,1)}, bf16[256,2048]{1,0:T(8,128)(2,1)}, u32[]{:S(2)}, u32[]{:S(2)}) collective-permute-start(bf16[256,2048]{1,0:T(8,128)(2,1)} %refs_10_.2), channel_id=1, source_target_pairs={{0,8},{1,9},{2,10},{3,11},{4,12},{5,13},{6,14},{7,15},{8,0},{9,1},... | collective-permute-start | bytes 3145736 | tf_op jit(solution)/shard_map/ppermute | solution.py:430
  12.8 30.8 %collective-permute-start.2 = (bf16[1280,256]{1,0:T(8,128)(2,1)}, bf16[1280,256]{1,0:T(8,128)(2,1)}, u32[]{:S(2)}, u32[]{:S(2)}) collective-permute-start(bf16[1280,256]{1,0:T(8,128)(2,1)} %slice.21), channel_id=1, source_target_pairs={{0,2},{1,3},{2,0},{3,1},{4,6},{5,7},{6,4},{7,5},{8,10},{9,11},{10,... | collective-permute-start | bytes 1966088 | tf_op jit(solution)/shard_map/ppermute | solution.py:430
  46.6 25.9 %collective-permute-start.4 = (bf16[2064,256]{1,0:T(8,128)(2,1)}, bf16[2064,256]{1,0:T(8,128)(2,1)}, u32[]{:S(2)}, u32[]{:S(2)}) collective-permute-start(bf16[2064,256]{1,0:T(8,128)(2,1)} %collective-permute-done.refs_3_), channel_id=1, source_target_pairs={{0,8},{1,9},{2,10},{3,11},{4,12},{5,13},{6,14},{7,15},{8,0},{9,1},... | collective-permute-start | bytes 3170312 | tf_op jit(solution)/shard_map/ppermute | solution.py:430
  46.6 25.9 %collective-permute-start.6 = (bf16[256,2048]{1,0:T(8,128)(2,1)}, bf16[256,2048]{1,0:T(8,128)(2,1)}, u32[]{:S(2)}, u32[]{:S(2)}) collective-permute-start(bf16[256,2048]{1,0:T(8,128)(2,1)} %refs_10_.2), channel_id=1, source_target_pairs={{0,1},{1,0},{2,3},{3,2},{4,5},{5,4},{6,7},{7,6},{8,9},{9,8},{10,11... | collective-permute-start | bytes 3145736 | tf_op jit(solution)/shard_map/ppermute | solution.py:430
  47.0 21.3 %collective-permute-start.5 = (bf16[784,256]{1,0:T(8,128)(2,1)}, bf16[784,256]{1,0:T(8,128)(2,1)S(1)}, u32[]{:S(2)}, u32[]{:S(2)}) collective-permute-start(bf16[784,256]{1,0:T(8,128)(2,1)} %fusion), channel_id=1, source_target_pairs={{0,2},{1,3},{2,0},{3,1},{4,6},{5,7},{6,4},{7,5},{8,10},{9,11},{10,... | collective-permute-start | bytes 1204232 | tf_op jit(solution)/shard_map/ppermute | solution.py:430
  48.6 21.1 %collective-permute-start.7 = (bf16[128,2048]{1,0:T(8,128)(2,1)}, bf16[128,2048]{1,0:T(8,128)(2,1)S(1)}, u32[]{:S(2)}, u32[]{:S(2)}) collective-permute-start(bf16[128,2048]{1,0:T(8,128)(2,1)} %get-tuple-element.109), channel_id=1, source_target_pairs={{0,2},{1,3},{2,0},{3,1},{4,6},{5,7},{6,4},{7,5},{8,10},{9,11},{10,... | collective-permute-start | bytes 1572872 | tf_op jit(solution)/shard_map/ppermute | solution.py:430
  72.4 43.7 %all-to-all-start.1 = ((bf16[32,72,256]{2,1,0:T(8,128)(2,1)}), bf16[32,72,256]{2,1,0:T(8,128)(2,1)S(1)}, u32[]{:S(2)}, u32[]{:S(2)}) async-start(bf16[32,72,256]{2,1,0:T(8,128)(2,1)} %attend_prefix.1), calls=%async_computation.1 | async-start | bytes 2359296 | tf_op jit(solution)/shard_map/all_to_all | solution.py:674
  77.2 32.9 %collective-permute-start.10 = (bf16[128,2048]{1,0:T(8,128)(2,1)}, bf16[128,2048]{1,0:T(8,128)(2,1)S(1)}, u32[]{:S(2)}, u32[]{:S(2)}) collective-permute-start(bf16[128,2048]{1,0:T(8,128)(2,1)} %get-tuple-element.121), channel_id=1, source_target_pairs={{0,2},{1,3},{2,0},{3,1},{4,6},{5,7},{6,4},{7,5},{8,10},{9,11},{10,... | collective-permute-start | bytes 1572872 | tf_op jit(solution)/shard_map/ppermute | solution.py:430
  80.2 30.0 %collective-permute-start.9 = (bf16[2064,256]{1,0:T(8,128)(2,1)S(1)}, bf16[2064,256]{1,0:T(8,128)(2,1)S(1)}, u32[]{:S(2)}, u32[]{:S(2)}) collective-permute-start(bf16[2064,256]{1,0:T(8,128)(2,1)S(1)} %constant_dynamic-update-slice_fusion.refs_4_), channel_id=1, source_target_pairs={{0,8},{1,9},{2,10},{3,11},{4,12},{5,13},{6,14},{7,15},{8,0},{9,1},... | collective-permute-start | bytes 3170312 | tf_op jit(solution)/shard_map/ppermute | solution.py:430
  80.3 34.8 %collective-permute-start.8 = (bf16[2064,256]{1,0:T(8,128)(2,1)S(1)}, bf16[2064,256]{1,0:T(8,128)(2,1)S(1)}, u32[]{:S(2)}, u32[]{:S(2)}) collective-permute-start(bf16[2064,256]{1,0:T(8,128)(2,1)S(1)} %constant_dynamic-update-slice_fusion.refs_4_), channel_id=1, source_target_pairs={{0,1},{1,0},{2,3},{3,2},{4,5},{5,4},{6,7},{7,6},{8,9},{9,8},{10,11... | collective-permute-start | bytes 3170312 | tf_op jit(solution)/shard_map/ppermute | solution.py:430
  81.8 28.3 %collective-permute-start.11 = (bf16[256,2048]{1,0:T(8,128)(2,1)}, bf16[256,2048]{1,0:T(8,128)(2,1)S(1)}, u32[]{:S(2)}, u32[]{:S(2)}) collective-permute-start(bf16[256,2048]{1,0:T(8,128)(2,1)} %collective-permute-done.6.refs_11_), channel_id=1, source_target_pairs={{0,8},{1,9},{2,10},{3,11},{4,12},{5,13},{6,14},{7,15},{8,0},{9,1},... | collective-permute-start | bytes 3145736 | tf_op jit(solution)/shard_map/ppermute | solution.py:430
  119.5 19.1 %collective-permute-start.16 = (bf16[128,2048]{1,0:T(8,128)(2,1)S(1)}, bf16[128,2048]{1,0:T(8,128)(2,1)S(1)}, u32[]{:S(2)}, u32[]{:S(2)}) collective-permute-start(bf16[128,2048]{1,0:T(8,128)(2,1)S(1)} %slice.27), channel_id=1, source_target_pairs={{0,2},{1,3},{2,0},{3,1},{4,6},{5,7},{6,4},{7,5},{8,10},{9,11},{10,... | collective-permute-start | bytes 1572872 | tf_op jit(solution)/shard_map/ppermute | solution.py:430
  121.0 17.6 %collective-permute-start.15 = (bf16[128,2048]{1,0:T(8,128)(2,1)S(1)}, bf16[128,2048]{1,0:T(8,128)(2,1)S(1)}, u32[]{:S(2)}, u32[]{:S(2)}) collective-permute-start(bf16[128,2048]{1,0:T(8,128)(2,1)S(1)} %slice.26), channel_id=1, source_target_pairs={{0,1},{1,0},{2,3},{3,2},{4,5},{5,4},{6,7},{7,6},{8,9},{9,8},{10,11... | collective-permute-start | bytes 1572872 | tf_op jit(solution)/shard_map/ppermute | solution.py:430
  121.6 17.1 %collective-permute-start.14 = (bf16[128,2048]{1,0:T(8,128)(2,1)S(1)}, bf16[128,2048]{1,0:T(8,128)(2,1)S(1)}, u32[]{:S(2)}, u32[]{:S(2)}) collective-permute-start(bf16[128,2048]{1,0:T(8,128)(2,1)S(1)} %get-tuple-element.143.refs_1_.hidden_ref), channel_id=1, source_target_pairs={{0,16},{1,17},{2,18},{3,19},{4,20},{5,21},{6,22},{7,23},{8,24},{9,... | collective-permute-start | bytes 1572872 | tf_op jit(solution)/shard_map/ppermute | solution.py:430
  123.0 14.6 %collective-permute-start.13 = (bf16[64,2048]{1,0:T(8,128)(2,1)S(1)}, bf16[64,2048]{1,0:T(8,128)(2,1)S(1)}, u32[]{:S(2)}, u32[]{:S(2)}) collective-permute-start(bf16[64,2048]{1,0:T(8,128)(2,1)S(1)} %get-tuple-element.144), channel_id=1, source_target_pairs={{0,4},{1,5},{2,6},{3,7},{4,0},{5,1},{6,2},{7,3},{8,12},{9,13},{10,... | collective-permute-start | bytes 786440 | tf_op jit(solution)/shard_map/ppermute | solution.py:430
  139.3 20.8 %collective-permute-start.20 = (bf16[64,2048]{1,0:T(8,128)(2,1)S(1)}, bf16[64,2048]{1,0:T(8,128)(2,1)S(1)}, u32[]{:S(2)}, u32[]{:S(2)}) collective-permute-start(bf16[64,2048]{1,0:T(8,128)(2,1)S(1)} %get-tuple-element.170), channel_id=1, source_target_pairs={{0,4},{1,5},{2,6},{3,7},{4,0},{5,1},{6,2},{7,3},{8,12},{9,13},{10,... | collective-permute-start | bytes 786440 | tf_op jit(solution)/shard_map/ppermute | solution.py:430
  141.7 18.4 %collective-permute-start.21 = (bf16[64,2048]{1,0:T(8,128)(2,1)S(1)}, bf16[64,2048]{1,0:T(8,128)(2,1)S(1)}, u32[]{:S(2)}, u32[]{:S(2)}) collective-permute-start(bf16[64,2048]{1,0:T(8,128)(2,1)S(1)} %collective-permute-done.13.refs_0_), channel_id=1, source_target_pairs={{0,16},{1,17},{2,18},{3,19},{4,20},{5,21},{6,22},{7,23},{8,24},{9,... | collective-permute-start | bytes 786440 | tf_op jit(solution)/shard_map/ppermute | solution.py:430
  172.5 12.7 %collective-permute-start.23 = (bf16[64,2048]{1,0:T(8,128)(2,1)}, bf16[64,2048]{1,0:T(8,128)(2,1)S(1)}, u32[]{:S(2)}, u32[]{:S(2)}) collective-permute-start(bf16[64,2048]{1,0:T(8,128)(2,1)} %get-tuple-element.178), channel_id=1, source_target_pairs={{0,16},{1,17},{2,18},{3,19},{4,20},{5,21},{6,22},{7,23},{8,24},{9,... | collective-permute-start | bytes 786440 | tf_op jit(solution)/shard_map/ppermute | solution.py:430
  186.4 21.4 %collective-permute-start.25 = (bf16[64,2048]{1,0:T(8,128)(2,1)S(1)}, bf16[64,2048]{1,0:T(8,128)(2,1)S(1)}, u32[]{:S(2)}, u32[]{:S(2)}) collective-permute-start(bf16[64,2048]{1,0:T(8,128)(2,1)S(1)} %add_convert_fusion.1), channel_id=1, source_target_pairs={{0,4},{1,5},{2,6},{3,7},{4,0},{5,1},{6,2},{7,3},{8,12},{9,13},{10,... | collective-permute-start | bytes 786440 | tf_op jit(solution)/shard_map/ppermute | solution.py:430
  188.8 22.9 %collective-permute-start.24 = (bf16[128,2048]{1,0:T(8,128)(2,1)S(1)}, bf16[128,2048]{1,0:T(8,128)(2,1)S(1)}, u32[]{:S(2)}, u32[]{:S(2)}) collective-permute-start(bf16[128,2048]{1,0:T(8,128)(2,1)S(1)} %copy-done.36), channel_id=1, source_target_pairs={{0,16},{1,17},{2,18},{3,19},{4,20},{5,21},{6,22},{7,23},{8,24},{9,... | collective-permute-start | bytes 1572872 | tf_op jit(solution)/shard_map/ppermute | solution.py:430
  195.8 15.9 %collective-permute-start.27 = (bf16[64,2048]{1,0:T(8,128)(2,1)S(1)}, bf16[64,2048]{1,0:T(8,128)(2,1)S(1)}, u32[]{:S(2)}, u32[]{:S(2)}) collective-permute-start(bf16[64,2048]{1,0:T(8,128)(2,1)S(1)} %add_convert_fusion), channel_id=1, source_target_pairs={{0,4},{1,5},{2,6},{3,7},{4,0},{5,1},{6,2},{7,3},{8,12},{9,13},{10,... | collective-permute-start | bytes 786440 | tf_op jit(solution)/shard_map/ppermute | solution.py:430
  (43 other events, 539.3 us)

commit v11 on v9

--- a/solution.py
+++ b/solution.py
@@ -12,6 +12,8 @@
 LANES = 128
 STAT_ROWS = 8
 STREAMS = 4
+FETCHES = 8
+UNROLL = 4
 EMPTY = 64.0
 ROW_BLOCK = 256
 KEY_CHUNK = 1024
@@ -95,17 +97,29 @@
     query_ref,
     answer_ref,
     stat_ref,
+    turned_ref,
     score_ref,
     top_ref,
     keys_ref,
     values_ref,
     sems,
 ):
-    copies = [
-        pltpu.make_async_copy(keys_hbm, keys_ref, sems.at[0]),
-        pltpu.make_async_copy(values_hbm, values_ref, sems.at[1]),
-    ]
-    for copy in copies:
+    key_step = keys_ref.shape[0] // FETCHES
+    value_step = values_ref.shape[1] // FETCHES
+    key_copies, value_copies = [], []
+    for fetch in range(FETCHES):
+        rows = pl.ds(fetch * key_step, key_step)
+        key_copies.append(
+            pltpu.make_async_copy(keys_hbm.at[rows], keys_ref.at[rows], sems.at[0, fetch])
+        )
+        rows = pl.ds(fetch * value_step, value_step)
+        for head in range(values_ref.shape[0]):
+            value_copies.append(
+                pltpu.make_async_copy(
+                    values_hbm.at[head, rows], values_ref.at[head, rows], sems.at[1 + head, fetch]
+                )
+            )
+    for copy in key_copies + value_copies:
         copy.start()
     sources, capacity, part_width = arrived_ref.shape
     local_heads = part_width // HD
@@ -118,7 +132,7 @@
             query_ref[head, pl.ds(offset, capacity), :] = rows
         return offset + counts_ref[source]
 
-    total = lax.fori_loop(0, sources, take, jnp.int32(0))
+    total = lax.fori_loop(0, sources, take, jnp.int32(0), unroll=UNROLL)
     blocks = (total + ROW_BLOCK - 1) // ROW_BLOCK
     lane = lax.broadcasted_iota(jnp.int32, (ROW_BLOCK, LANES), 1)
 
@@ -161,22 +175,30 @@
         answer_ref[head, rows, :] = mixed[:, :HD] / row_sum
         top = top_ref[slot]
         if head == 0:
-            stat_ref[rows, :] = jnp.where(lane == 0, top, row_sum)
+            stats = jnp.where(lane == 0, top, row_sum)
         else:
-            before = stat_ref[rows, :]
-            with_top = jnp.where(lane == head, top, before)
-            stat_ref[rows, :] = jnp.where(lane == local_heads + head, row_sum, with_top)
+            stats = jnp.where(lane == head, top, stat_ref[...])
+            stats = jnp.where(lane == local_heads + head, row_sum, stats)
+        if head + 1 < local_heads:
+            stat_ref[...] = stats
+        else:
+            for half in range(ROW_BLOCK // LANES):
+                turned_ref[block * (ROW_BLOCK // LANES) + half] = jnp.transpose(
+                    stats[half * LANES : (half + 1) * LANES]
+                )[:STAT_ROWS, :]
 
     def slot_of(block, head):
         return (block * local_heads + head) % 2 if local_heads % 2 else head % 2
 
-    for copy in copies:
+    for copy in key_copies:
         copy.wait()
     first_rows = load_queries(0, 0)
     part_top = None
     for chunk in range(chunks):
         part_top = score_chunk(first_rows, 0, 0, chunk, part_top)
     finish_top(part_top, 0)
+    for copy in value_copies:
+        copy.wait()
 
     def one_block(block, carry):
         for head in range(local_heads):
@@ -202,7 +224,9 @@
 
     def give(source, offset):
         rows = [answer_ref[head, pl.ds(offset, capacity), :] for head in range(local_heads)]
-        turned = jnp.transpose(stat_ref[pl.ds(offset, LANES), :])[:STAT_ROWS, :]
+        tile = offset // LANES
+        window = jnp.concatenate([turned_ref[tile], turned_ref[tile + 1]], axis=1)
+        turned = pltpu.roll(window, (2 * LANES - offset % LANES) % (2 * LANES), 1)[:, :LANES]
         if part_width > LANES:
             turned = jnp.concatenate(
                 [turned, jnp.zeros((STAT_ROWS, part_width - LANES), jnp.float32)], axis=1
@@ -211,7 +235,7 @@
         out_ref[source] = jnp.concatenate([rows, turned], axis=0).astype(jnp.bfloat16)
         return offset + counts_ref[source]
 
-    lax.fori_loop(0, sources, give, jnp.int32(0))
+    lax.fori_loop(0, sources, give, jnp.int32(0), unroll=UNROLL)
 
 
 def attend_prefix(counts, arrived, turned_keys, wide_values):
@@ -227,12 +251,13 @@
         scratch_shapes=[
             pltpu.VMEM((local_heads, row_total, HD), jnp.float32),
             pltpu.VMEM((local_heads, row_total, HD), jnp.float32),
-            pltpu.VMEM((row_total, LANES), jnp.float32),
+            pltpu.VMEM((ROW_BLOCK, LANES), jnp.float32),
+            pltpu.VMEM((row_total // LANES + 1, STAT_ROWS, LANES), jnp.float32),
             pltpu.VMEM((2, ROW_BLOCK, key_total), jnp.float32),
             pltpu.VMEM((2, ROW_BLOCK, LANES), jnp.float32),
             pltpu.VMEM(turned_keys.shape, jnp.bfloat16),
             pltpu.VMEM(wide_values.shape, jnp.bfloat16),
-            pltpu.SemaphoreType.DMA((2,)),
+            pltpu.SemaphoreType.DMA((1 + local_heads, FETCHES)),
         ],
         compiler_params=pltpu.CompilerParams(vmem_limit_bytes=58 * mebibyte),
         cost_estimate=pl.CostEstimate(

time: 204 us -> 204 us (level)
  no operation moved by 1% of the time
where the time goes in v11:
time: 204 us; the launch traced here: 203 us
  waiting for transfers between devices  79.8 us (39%)
  Pallas kernels  60.5 us (30%)
  starting transfers between devices  36.2 us (18%)
  local copies, waits for them, and re-layouts  24 us (12%)
  other arithmetic  2.29 us (1%)
    ppermute x26, waiting for transfers between devices, swap(): lax.ppermute(leaf, ('grp', 'dev'), pairs)  79.8 us
    pallas_call x3, Pallas kernels, feed_forward(): pl.pallas_call(functools.partial(mlp_kernel, pieces, up_plan, down_plan),...  31.1 us
    ppermute x26, starting transfers between devices, swap(): lax.ppermute(leaf, ('grp', 'dev'), pairs)  24.1 us
    pallas_call x1, Pallas kernels, attend_prefix(): pl.pallas_call(far_kernel, out_shape=jax.ShapeDtypeStruct((sources, capac...  19.2 us
    unnamed x74, local copies, waits for them, and re-layouts  12.6 us
    all_to_all x1, starting transfers between devices, on_device(): lax.all_to_all(outgoing.reshape(sources, capacity, part_width), ('grp', '...  7.3 us
    all_to_all x1, starting transfers between devices, on_device(): lax.all_to_all(answer_part, ('grp', 'dev'), split_axis=0, concat_axis=0,...  4.72 us
    pallas_call x1, Pallas kernels, attend_suffix(): pl.pallas_call(functools.partial(own_kernel, local_heads), out_shape=(jax...  4.48 us
  transfers between devices with their start and end apart: 28, of which 10 were waited for; matrix products, arithmetic and copies ran while one was open for 11% of the time, Pallas kernels for 27%

profile of v11, /device:TPU:0, one launch (start us, length us, event | category | flops | bytes accessed | tf_op | source)
XLA Modules:
  0.0 203.4 jit_solution(9522395632679685704)
XLA Ops:
  0.0 2.3 %pack_queries.1 = bf16[4,8,64,256]{3,2,1,0:T(8,128)(2,1)} custom-call(s32[1,4]{1,0:T(1,128)} %lengths_ref.5, s32[1,4]{1,0:T(1,128)} %groups_ref.3, bf16[128,2048]{1,0:T(8,128)(2,1)} %query_ref.3), custom_call_target="tpu_custom_call" | custom-call | tf_op jit(solution)/shard_map/pack_queries/pallas_call | solution.py:76
  2.3 7.3 %all-to-all-start = ((bf16[32,64,256]{2,1,0:T(8,128)(2,1)}), bf16[32,64,256]{2,1,0:T(8,128)(2,1)S(1)}, u32[]{:S(2)}, u32[]{:S(2)}) async-start(bf16[32,64,256]{2,1,0:T(8,128)(2,1)} %bitcast.20), calls=%async_computation | async-start | bytes 2097152 | tf_op jit(solution)/shard_map/all_to_all | solution.py:644
  15.0 4.1 %copy.18 = bf16[1,4096,256]{1,2,0:T(8,128)(2,1)} copy(bf16[1,4096,256]{2,1,0:T(8,128)(2,1)} %param.22) | data formatting | bytes 4194304 | tf_op args[6]
  19.1 4.1 %copy.19 = bf16[1,4096,256]{1,2,0:T(8,128)(2,1)} copy(bf16[1,4096,256]{2,1,0:T(8,128)(2,1)} %param.23) | data formatting | bytes 4194304 | tf_op args[7]
  23.2 4.1 %copy.20 = bf16[4096,2,128]{2,0,1:T(8,128)(2,1)} copy(bf16[4096,2,128]{0,2,1:T(8,128)(2,1)} %bitcast.19) | data formatting | bytes 4194304 | tf_op jit(solution)/shard_map/reshape;squeeze | solution.py:656
  27.3 4.1 %concatenate.13.values_hbm = bf16[2,4096,256]{2,1,0:T(8,128)(2,1)} pad(bf16[2,4096,128]{2,1,0:T(8,128)(2,1)} %bitcast.18, bf16[]{:T(256)} %constant.0.clone.1), padding=0_0x0_0x0_128 | pad | bytes 6291458 | tf_op jit(solution)/shard_map/concatenate | solution.py:657
  31.5 4.5 %attend_suffix.1 = (f32[128,2048]{1,0:T(8,128)S(1)}, f32[128,128]{1,0:T(8,128)S(1)}, f32[128,128]{1,0:T(8,128)S(1)}) custom-call(s32[1,4]{1,0:T(1,128)S(1)} %copy-done.10, bf16[128,2048]{1,0:T(8,128)(2,1)S(1)} %copy-done.3, bf16[128,2048]{1,0:T(8,128)(2,1)S(1)} %copy-done.12, bf16[128,2048]{1,0:T(8,128)(2,1)S(1)} %copy-done.13), custom_call_target="tpu_custom_call" | custom-call | flops 1342177280 | bytes 2097152 | tf_op jit(solution)/shard_map/attend_suffix/pallas_call | solution.py:320
  35.9 2.3 %fusion.1 = (bf16[128,2048]{1,0:T(8,128)(2,1)}, bf16[128,2048]{1,0:T(8,128)(2,1)}) fusion(bf16[256,2048]{1,0:T(8,128)(2,1)} %refs_10_.2), kind=kLoop, calls=%fused_computation.11 | loop fusion | bytes 2097152 | tf_op jit(solution)/shard_map/slice | solution.py:640
  38.2 5.3 %collective-permute-done.2 = bf16[1280,256]{1,0:T(8,128)(2,1)} collective-permute-done((bf16[1280,256]{1,0:T(8,128)(2,1)}, bf16[1280,256]{1,0:T(8,128)(2,1)}, u32[]{:S(2)}, u32[]{:S(2)}) %collective-permute-start.2) | collective-permute-done | bytes 655392 | tf_op jit(solution)/shard_map/ppermute | solution.py:441
  43.5 3.0 %collective-permute-done.refs_3_ = bf16[2064,256]{1,0:T(8,128)(2,1)} collective-permute-done((bf16[2064,256]{1,0:T(8,128)(2,1)S(1)}, bf16[2064,256]{1,0:T(8,128)(2,1)}, u32[]{:S(2)}, u32[]{:S(2)}) %collective-permute-start) | collective-permute-done | bytes 1056800 | tf_op jit(solution)/shard_map/ppermute | solution.py:441
  50.2 19.2 %attend_prefix.1 = bf16[32,72,256]{2,1,0:T(8,128)(2,1)} custom-call(s32[32]{0:T(128)} %convert_reduce_fusion.counts_ref, bf16[32,64,256]{2,1,0:T(8,128)(2,1)} %copy-done.26, bf16[256,4096]{1,0:T(8,128)(2,1)} %bitcast.21, bf16[2,4096,256]{2,1,0:T(8,128)(2,1)} %concatenate.13.values_hbm), custom_call_target="tpu_custom_call" | custom-call | flops 8589934592 | bytes 8388608 | tf_op jit(solution)/shard_map/attend_prefix/pallas_call | solution.py:246
  69.7 2.7 %collective-permute-done.6.refs_11_ = bf16[256,2048]{1,0:T(8,128)(2,1)} collective-permute-done((bf16[256,2048]{1,0:T(8,128)(2,1)}, bf16[256,2048]{1,0:T(8,128)(2,1)}, u32[]{:S(2)}, u32[]{:S(2)}) %collective-permute-start.6) | collective-permute-done | bytes 1048608 | tf_op jit(solution)/shard_map/ppermute | solution.py:441
  72.4 4.7 %all-to-all-start.1 = ((bf16[32,72,256]{2,1,0:T(8,128)(2,1)}), bf16[32,72,256]{2,1,0:T(8,128)(2,1)S(1)}, u32[]{:S(2)}, u32[]{:S(2)}) async-start(bf16[32,72,256]{2,1,0:T(8,128)(2,1)} %attend_prefix.1), calls=%async_computation.1 | async-start | bytes 2359296 | tf_op jit(solution)/shard_map/all_to_all | solution.py:679
  82.0 28.0 %collective-permute-done.10 = bf16[128,2048]{1,0:T(8,128)(2,1)S(1)} collective-permute-done((bf16[128,2048]{1,0:T(8,128)(2,1)}, bf16[128,2048]{1,0:T(8,128)(2,1)S(1)}, u32[]{:S(2)}, u32[]{:S(2)}) %collective-permute-start.10) | collective-permute-done | bytes 524320 | tf_op jit(solution)/shard_map/ppermute | solution.py:441
  110.2 4.9 %collective-permute-done.8.refs_5_ = bf16[2064,256]{1,0:T(8,128)(2,1)S(1)} collective-permute-done((bf16[2064,256]{1,0:T(8,128)(2,1)S(1)}, bf16[2064,256]{1,0:T(8,128)(2,1)S(1)}, u32[]{:S(2)}, u32[]{:S(2)}) %collective-permute-start.8) | collective-permute-done | bytes 1056800 | tf_op jit(solution)/shard_map/ppermute | solution.py:441
  116.3 1.9 merge_parts.1
  118.8 2.2 %collective-permute-start.13 = (bf16[64,2048]{1,0:T(8,128)(2,1)S(1)}, bf16[64,2048]{1,0:T(8,128)(2,1)S(1)}, u32[]{:S(2)}, u32[]{:S(2)}) collective-permute-start(bf16[64,2048]{1,0:T(8,128)(2,1)S(1)} %get-tuple-element.151), channel_id=1, source_target_pairs={{0,4},{1,5},{2,6},{3,7},{4,0},{5,1},{6,2},{7,3},{8,12},{9,13},{10,... | collective-permute-start | bytes 786440 | tf_op jit(solution)/shard_map/ppermute | solution.py:441
  122.7 11.0 %collective-permute-done.13.refs_0_ = bf16[64,2048]{1,0:T(8,128)(2,1)S(1)} collective-permute-done((bf16[64,2048]{1,0:T(8,128)(2,1)S(1)}, bf16[64,2048]{1,0:T(8,128)(2,1)S(1)}, u32[]{:S(2)}, u32[]{:S(2)}) %collective-permute-start.13) | collective-permute-done | bytes 262176 | tf_op jit(solution)/shard_map/ppermute | solution.py:441
  135.2 12.5 %collective-permute-done.14.refs_0_ = bf16[64,2048]{1,0:T(8,128)(2,1)S(1)} collective-permute-done((bf16[64,2048]{1,0:T(8,128)(2,1)S(1)}, bf16[64,2048]{1,0:T(8,128)(2,1)S(1)}, u32[]{:S(2)}, u32[]{:S(2)}) %collective-permute-start.14) | collective-permute-done | bytes 262176 | tf_op jit(solution)/shard_map/ppermute | solution.py:441
  151.5 9.4 %feed_forward.3 = (bf16[64,2048]{1,0:T(8,128)(2,1)}, bf16[64,2048]{1,0:T(8,128)(2,1)}) custom-call(bf16[64,2048]{1,0:T(8,128)(2,1)} %copy-done.29, bf16[64,2048]{1,0:T(8,128)(2,1)} %copy-done.30, bf16[2064,256]{1,0:T(8,128)(2,1)} %copy-done.14, bf16[2064,256]{1,0:T(8,128)(2,1)} %collective-permute-done.refs_3_, bf16[2064,256]{1,0:T(8,128)(2,1)} %copy-done.15, ...), custom_call_target="tpu_custom_call" | custom-call | flops 2147483648 | bytes 16777216 | tf_op jit(solution)/shard_map/feed_forward/pallas_call | solution.py:538
  162.6 9.4 %feed_forward.4 = (bf16[64,2048]{1,0:T(8,128)(2,1)}, bf16[64,2048]{1,0:T(8,128)(2,1)}) custom-call(bf16[64,2048]{1,0:T(8,128)(2,1)} %copy-done.28, bf16[64,2048]{1,0:T(8,128)(2,1)} %copy-done.31, bf16[2064,256]{1,0:T(8,128)(2,1)} %copy-done.14, bf16[2064,256]{1,0:T(8,128)(2,1)} %collective-permute-done.refs_3_, bf16[2064,256]{1,0:T(8,128)(2,1)} %copy-done.15, ...), custom_call_target="tpu_custom_call" | custom-call | flops 2147483648 | bytes 16777216 | tf_op jit(solution)/shard_map/feed_forward/pallas_call | solution.py:538
  172.9 12.3 %feed_forward.5 = (bf16[128,2048]{1,0:T(8,128)(2,1)}, bf16[128,2048]{1,0:T(8,128)(2,1)}) custom-call(bf16[128,2048]{1,0:T(8,128)(2,1)} %copy-done.27, bf16[128,2048]{1,0:T(8,128)(2,1)} %copy-done, bf16[2064,256]{1,0:T(8,128)(2,1)} %copy-done.14, bf16[2064,256]{1,0:T(8,128)(2,1)} %collective-permute-done.refs_3_, bf16[2064,256]{1,0:T(8,128)(2,1)} %copy-done.15, ...), custom_call_target="tpu_custom_call" | custom-call | flops 4294967296 | bytes 16777216 | tf_op jit(solution)/shard_map/feed_forward/pallas_call | solution.py:538
  186.8 2.9 %collective-permute-start.25 = (bf16[64,2048]{1,0:T(8,128)(2,1)S(1)}, bf16[64,2048]{1,0:T(8,128)(2,1)S(1)}, u32[]{:S(2)}, u32[]{:S(2)}) collective-permute-start(bf16[64,2048]{1,0:T(8,128)(2,1)S(1)} %add_convert_fusion), channel_id=1, source_target_pairs={{0,4},{1,5},{2,6},{3,7},{4,0},{5,1},{6,2},{7,3},{8,12},{9,13},{10,... | collective-permute-start | bytes 786440 | tf_op jit(solution)/shard_map/ppermute | solution.py:441
  189.7 11.2 %collective-permute-done.25.far_b_ref = bf16[64,2048]{1,0:T(8,128)(2,1)S(1)} collective-permute-done((bf16[64,2048]{1,0:T(8,128)(2,1)S(1)}, bf16[64,2048]{1,0:T(8,128)(2,1)S(1)}, u32[]{:S(2)}, u32[]{:S(2)}) %collective-permute-start.25) | collective-permute-done | bytes 262176 | tf_op jit(solution)/shard_map/ppermute | solution.py:441
  (126 shorter events, 29.4 us)
Async XLA Ops:
  2.3 44.2 %all-to-all-start = ((bf16[32,64,256]{2,1,0:T(8,128)(2,1)}), bf16[32,64,256]{2,1,0:T(8,128)(2,1)S(1)}, u32[]{:S(2)}, u32[]{:S(2)}) async-start(bf16[32,64,256]{2,1,0:T(8,128)(2,1)} %bitcast.20), calls=%async_computation | async-start | bytes 2097152 | tf_op jit(solution)/shard_map/all_to_all | solution.py:644
  9.8 33.8 %collective-permute-start.1 = (bf16[2064,256]{1,0:T(8,128)(2,1)S(1)}, bf16[2064,256]{1,0:T(8,128)(2,1)}, u32[]{:S(2)}, u32[]{:S(2)}) collective-permute-start(bf16[2064,256]{1,0:T(8,128)(2,1)S(1)} %pad_maximum_fusion.refs_2_), channel_id=1, source_target_pairs={{0,8},{1,9},{2,10},{3,11},{4,12},{5,13},{6,14},{7,15},{8,0},{9,1},... | collective-permute-start | bytes 3170312 | tf_op jit(solution)/shard_map/ppermute | solution.py:441
  10.1 36.4 %collective-permute-start = (bf16[2064,256]{1,0:T(8,128)(2,1)S(1)}, bf16[2064,256]{1,0:T(8,128)(2,1)}, u32[]{:S(2)}, u32[]{:S(2)}) collective-permute-start(bf16[2064,256]{1,0:T(8,128)(2,1)S(1)} %pad_maximum_fusion.refs_2_), channel_id=1, source_target_pairs={{0,1},{1,0},{2,3},{3,2},{4,5},{5,4},{6,7},{7,6},{8,9},{9,8},{10,11... | collective-permute-start | bytes 3170312 | tf_op jit(solution)/shard_map/ppermute | solution.py:441
  11.8 31.8 %collective-permute-start.3 = (bf16[256,2048]{1,0:T(8,128)(2,1)}, bf16[256,2048]{1,0:T(8,128)(2,1)}, u32[]{:S(2)}, u32[]{:S(2)}) collective-permute-start(bf16[256,2048]{1,0:T(8,128)(2,1)} %refs_10_.2), channel_id=1, source_target_pairs={{0,8},{1,9},{2,10},{3,11},{4,12},{5,13},{6,14},{7,15},{8,0},{9,1},... | collective-permute-start | bytes 3145736 | tf_op jit(solution)/shard_map/ppermute | solution.py:441
  12.7 30.8 %collective-permute-start.2 = (bf16[1280,256]{1,0:T(8,128)(2,1)}, bf16[1280,256]{1,0:T(8,128)(2,1)}, u32[]{:S(2)}, u32[]{:S(2)}) collective-permute-start(bf16[1280,256]{1,0:T(8,128)(2,1)} %slice.15), channel_id=1, source_target_pairs={{0,2},{1,3},{2,0},{3,1},{4,6},{5,7},{6,4},{7,5},{8,10},{9,11},{10,... | collective-permute-start | bytes 1966088 | tf_op jit(solution)/shard_map/ppermute | solution.py:441
  46.5 25.9 %collective-permute-start.4 = (bf16[2064,256]{1,0:T(8,128)(2,1)}, bf16[2064,256]{1,0:T(8,128)(2,1)}, u32[]{:S(2)}, u32[]{:S(2)}) collective-permute-start(bf16[2064,256]{1,0:T(8,128)(2,1)} %collective-permute-done.refs_3_), channel_id=1, source_target_pairs={{0,8},{1,9},{2,10},{3,11},{4,12},{5,13},{6,14},{7,15},{8,0},{9,1},... | collective-permute-start | bytes 3170312 | tf_op jit(solution)/shard_map/ppermute | solution.py:441
  46.5 25.9 %collective-permute-start.6 = (bf16[256,2048]{1,0:T(8,128)(2,1)}, bf16[256,2048]{1,0:T(8,128)(2,1)}, u32[]{:S(2)}, u32[]{:S(2)}) collective-permute-start(bf16[256,2048]{1,0:T(8,128)(2,1)} %refs_10_.2), channel_id=1, source_target_pairs={{0,1},{1,0},{2,3},{3,2},{4,5},{5,4},{6,7},{7,6},{8,9},{9,8},{10,11... | collective-permute-start | bytes 3145736 | tf_op jit(solution)/shard_map/ppermute | solution.py:441
  46.9 22.5 %collective-permute-start.5 = (bf16[784,256]{1,0:T(8,128)(2,1)}, bf16[784,256]{1,0:T(8,128)(2,1)S(1)}, u32[]{:S(2)}, u32[]{:S(2)}) collective-permute-start(bf16[784,256]{1,0:T(8,128)(2,1)} %fusion), channel_id=1, source_target_pairs={{0,2},{1,3},{2,0},{3,1},{4,6},{5,7},{6,4},{7,5},{8,10},{9,11},{10,... | collective-permute-start | bytes 1204232 | tf_op jit(solution)/shard_map/ppermute | solution.py:441
  48.6 21.1 %collective-permute-start.7 = (bf16[128,2048]{1,0:T(8,128)(2,1)}, bf16[128,2048]{1,0:T(8,128)(2,1)S(1)}, u32[]{:S(2)}, u32[]{:S(2)}) collective-permute-start(bf16[128,2048]{1,0:T(8,128)(2,1)} %get-tuple-element.116), channel_id=1, source_target_pairs={{0,2},{1,3},{2,0},{3,1},{4,6},{5,7},{6,4},{7,5},{8,10},{9,11},{10,... | collective-permute-start | bytes 1572872 | tf_op jit(solution)/shard_map/ppermute | solution.py:441
  72.4 43.8 %all-to-all-start.1 = ((bf16[32,72,256]{2,1,0:T(8,128)(2,1)}), bf16[32,72,256]{2,1,0:T(8,128)(2,1)S(1)}, u32[]{:S(2)}, u32[]{:S(2)}) async-start(bf16[32,72,256]{2,1,0:T(8,128)(2,1)} %attend_prefix.1), calls=%async_computation.1 | async-start | bytes 2359296 | tf_op jit(solution)/shard_map/all_to_all | solution.py:679
  77.1 32.9 %collective-permute-start.10 = (bf16[128,2048]{1,0:T(8,128)(2,1)}, bf16[128,2048]{1,0:T(8,128)(2,1)S(1)}, u32[]{:S(2)}, u32[]{:S(2)}) collective-permute-start(bf16[128,2048]{1,0:T(8,128)(2,1)} %get-tuple-element.128), channel_id=1, source_target_pairs={{0,2},{1,3},{2,0},{3,1},{4,6},{5,7},{6,4},{7,5},{8,10},{9,11},{10,... | collective-permute-start | bytes 1572872 | tf_op jit(solution)/shard_map/ppermute | solution.py:441
  80.2 30.0 %collective-permute-start.9 = (bf16[2064,256]{1,0:T(8,128)(2,1)S(1)}, bf16[2064,256]{1,0:T(8,128)(2,1)S(1)}, u32[]{:S(2)}, u32[]{:S(2)}) collective-permute-start(bf16[2064,256]{1,0:T(8,128)(2,1)S(1)} %constant_dynamic-update-slice_fusion.refs_4_), channel_id=1, source_target_pairs={{0,8},{1,9},{2,10},{3,11},{4,12},{5,13},{6,14},{7,15},{8,0},{9,1},... | collective-permute-start | bytes 3170312 | tf_op jit(solution)/shard_map/ppermute | solution.py:441
  80.3 34.8 %collective-permute-start.8 = (bf16[2064,256]{1,0:T(8,128)(2,1)S(1)}, bf16[2064,256]{1,0:T(8,128)(2,1)S(1)}, u32[]{:S(2)}, u32[]{:S(2)}) collective-permute-start(bf16[2064,256]{1,0:T(8,128)(2,1)S(1)} %constant_dynamic-update-slice_fusion.refs_4_), channel_id=1, source_target_pairs={{0,1},{1,0},{2,3},{3,2},{4,5},{5,4},{6,7},{7,6},{8,9},{9,8},{10,11... | collective-permute-start | bytes 3170312 | tf_op jit(solution)/shard_map/ppermute | solution.py:441
  81.8 28.3 %collective-permute-start.11 = (bf16[256,2048]{1,0:T(8,128)(2,1)}, bf16[256,2048]{1,0:T(8,128)(2,1)S(1)}, u32[]{:S(2)}, u32[]{:S(2)}) collective-permute-start(bf16[256,2048]{1,0:T(8,128)(2,1)} %collective-permute-done.6.refs_11_), channel_id=1, source_target_pairs={{0,8},{1,9},{2,10},{3,11},{4,12},{5,13},{6,14},{7,15},{8,0},{9,1},... | collective-permute-start | bytes 3145736 | tf_op jit(solution)/shard_map/ppermute | solution.py:441
  118.2 29.6 %collective-permute-start.17 = (bf16[2064,256]{1,0:T(8,128)(2,1)S(1)}, bf16[2064,256]{1,0:T(8,128)(2,1)S(1)}, u32[]{:S(2)}, u32[]{:S(2)}) collective-permute-start(bf16[2064,256]{1,0:T(8,128)(2,1)S(1)} %copy-done.20), channel_id=1, source_target_pairs={{0,8},{1,9},{2,10},{3,11},{4,12},{5,13},{6,14},{7,15},{8,0},{9,1},... | collective-permute-start | bytes 3170312 | tf_op jit(solution)/shard_map/ppermute | solution.py:441
  118.2 29.5 %collective-permute-start.18 = (bf16[256,2048]{1,0:T(8,128)(2,1)S(1)}, bf16[256,2048]{1,0:T(8,128)(2,1)S(1)}, u32[]{:S(2)}, u32[]{:S(2)}) collective-permute-start(bf16[256,2048]{1,0:T(8,128)(2,1)S(1)} %copy-done.17), channel_id=1, source_target_pairs={{0,1},{1,0},{2,3},{3,2},{4,5},{5,4},{6,7},{7,6},{8,9},{9,8},{10,11... | collective-permute-start | bytes 3145736 | tf_op jit(solution)/shard_map/ppermute | solution.py:441
  118.8 14.9 %collective-permute-start.13 = (bf16[64,2048]{1,0:T(8,128)(2,1)S(1)}, bf16[64,2048]{1,0:T(8,128)(2,1)S(1)}, u32[]{:S(2)}, u32[]{:S(2)}) collective-permute-start(bf16[64,2048]{1,0:T(8,128)(2,1)S(1)} %get-tuple-element.151), channel_id=1, source_target_pairs={{0,4},{1,5},{2,6},{3,7},{4,0},{5,1},{6,2},{7,3},{8,12},{9,13},{10,... | collective-permute-start | bytes 786440 | tf_op jit(solution)/shard_map/ppermute | solution.py:441
  121.0 14.2 %collective-permute-start.16 = (bf16[128,2048]{1,0:T(8,128)(2,1)S(1)}, bf16[128,2048]{1,0:T(8,128)(2,1)S(1)}, u32[]{:S(2)}, u32[]{:S(2)}) collective-permute-start(bf16[128,2048]{1,0:T(8,128)(2,1)S(1)} %get-tuple-element.193.refs_1_.hidden_ref), channel_id=1, source_target_pairs={{0,16},{1,17},{2,18},{3,19},{4,20},{5,21},{6,22},{7,23},{8,24},{9,... | collective-permute-start | bytes 1572872 | tf_op jit(solution)/shard_map/ppermute | solution.py:441
  133.7 14.1 %collective-permute-start.14 = (bf16[64,2048]{1,0:T(8,128)(2,1)S(1)}, bf16[64,2048]{1,0:T(8,128)(2,1)S(1)}, u32[]{:S(2)}, u32[]{:S(2)}) collective-permute-start(bf16[64,2048]{1,0:T(8,128)(2,1)S(1)} %get-tuple-element.152), channel_id=1, source_target_pairs={{0,4},{1,5},{2,6},{3,7},{4,0},{5,1},{6,2},{7,3},{8,12},{9,13},{10,... | collective-permute-start | bytes 786440 | tf_op jit(solution)/shard_map/ppermute | solution.py:441
  133.7 14.1 %collective-permute-start.15 = (bf16[64,2048]{1,0:T(8,128)(2,1)S(1)}, bf16[64,2048]{1,0:T(8,128)(2,1)S(1)}, u32[]{:S(2)}, u32[]{:S(2)}) collective-permute-start(bf16[64,2048]{1,0:T(8,128)(2,1)S(1)} %collective-permute-done.13.refs_0_), channel_id=1, source_target_pairs={{0,16},{1,17},{2,18},{3,19},{4,20},{5,21},{6,22},{7,23},{8,24},{9,... | collective-permute-start | bytes 786440 | tf_op jit(solution)/shard_map/ppermute | solution.py:441
  172.1 14.6 %collective-permute-start.24 = (bf16[64,2048]{1,0:T(8,128)(2,1)S(1)}, bf16[64,2048]{1,0:T(8,128)(2,1)S(1)}, u32[]{:S(2)}, u32[]{:S(2)}) collective-permute-start(bf16[64,2048]{1,0:T(8,128)(2,1)S(1)} %add_convert_fusion.1), channel_id=1, source_target_pairs={{0,4},{1,5},{2,6},{3,7},{4,0},{5,1},{6,2},{7,3},{8,12},{9,13},{10,... | collective-permute-start | bytes 786440 | tf_op jit(solution)/shard_map/ppermute | solution.py:441
  172.2 14.5 %collective-permute-start.23 = (bf16[64,2048]{1,0:T(8,128)(2,1)}, bf16[64,2048]{1,0:T(8,128)(2,1)S(1)}, u32[]{:S(2)}, u32[]{:S(2)}) collective-permute-start(bf16[64,2048]{1,0:T(8,128)(2,1)} %get-tuple-element.197), channel_id=1, source_target_pairs={{0,16},{1,17},{2,18},{3,19},{4,20},{5,21},{6,22},{7,23},{8,24},{9,... | collective-permute-start | bytes 786440 | tf_op jit(solution)/shard_map/ppermute | solution.py:441
  185.3 15.6 %collective-permute-start.22 = (bf16[128,2048]{1,0:T(8,128)(2,1)}, bf16[128,2048]{1,0:T(8,128)(2,1)S(1)}, u32[]{:S(2)}, u32[]{:S(2)}) collective-permute-start(bf16[128,2048]{1,0:T(8,128)(2,1)} %get-tuple-element.196), channel_id=1, source_target_pairs={{0,16},{1,17},{2,18},{3,19},{4,20},{5,21},{6,22},{7,23},{8,24},{9,... | collective-permute-start | bytes 1572872 | tf_op jit(solution)/shard_map/ppermute | solution.py:441
  186.8 14.1 %collective-permute-start.25 = (bf16[64,2048]{1,0:T(8,128)(2,1)S(1)}, bf16[64,2048]{1,0:T(8,128)(2,1)S(1)}, u32[]{:S(2)}, u32[]{:S(2)}) collective-permute-start(bf16[64,2048]{1,0:T(8,128)(2,1)S(1)} %add_convert_fusion), channel_id=1, source_target_pairs={{0,4},{1,5},{2,6},{3,7},{4,0},{5,1},{6,2},{7,3},{8,12},{9,13},{10,... | collective-permute-start | bytes 786440 | tf_op jit(solution)/shard_map/ppermute | solution.py:441
  (39 other events, 510.3 us)

commit v12 on v11

--- a/solution.py
+++ b/solution.py
@@ -441,12 +441,19 @@
     return jax.tree.map(lambda leaf: lax.ppermute(leaf, ("grp", "dev"), pairs), value)
 
 
+def swap_block(block, mask, sent):
+    for array, _, _ in block:
+        if (id(array), mask) not in sent:
+            sent[id(array), mask] = (array, swap(array, mask))
+    return [(sent[id(array), mask][1], begin, rows) for array, begin, rows in block]
+
+
 def complete(held, masks):
-    held = dict(held)
+    held, sent = dict(held), {}
     for mask in masks:
         for at in list(held):
             if mask ^ at not in held:
-                held[mask ^ at] = swap(held[at], mask)
+                held[mask ^ at] = swap_block(held[at], mask, sent)
     return held
 
 
@@ -462,23 +469,21 @@
     ]
 
 
-def mlp_kernel(pieces, up_plan, down_plan, *refs):
+def mlp_kernel(pieces, held_total, up_plan, down_plan, *refs):
     parts = len(up_plan)
     row_refs, refs = refs[:pieces], refs[pieces:]
-    up_total, down_total = sum(map(len, up_plan)), sum(map(len, down_plan))
-    ups, refs = list(refs[:up_total]), refs[up_total:]
-    downs, refs = list(refs[:down_total]), refs[down_total:]
+    held_refs, refs = refs[:held_total], refs[held_total:]
     out_refs, (up_ref, down_ref, sems) = refs[:pieces], refs[pieces:]
     model_width = row_refs[0].shape[1]
     copies = []
-    for part, heights in enumerate(up_plan):
+    for part, block in enumerate(up_plan):
         begin, held = 0, []
-        for piece, height in enumerate(heights):
-            source = ups.pop(0)
+        for piece, (at, skip, height) in enumerate(block):
+            source = held_refs[at]
             for stream, (first, rows) in enumerate(cut(height)):
                 held.append(
                     pltpu.make_async_copy(
-                        source.at[pl.ds(first, rows)],
+                        source.at[pl.ds(skip + first, rows)],
                         up_ref.at[part, pl.ds(begin + first, rows)],
                         sems.at[part, 0, piece * STREAMS + stream],
                     )
@@ -486,14 +491,14 @@
             begin += height
         copies.append(held)
     begin = 0
-    for part, heights in enumerate(down_plan):
+    for part, block in enumerate(down_plan):
         held = []
-        for piece, height in enumerate(heights):
-            source = downs.pop(0)
+        for piece, (at, skip, height) in enumerate(block):
+            source = held_refs[at]
             for stream, (first, rows) in enumerate(cut(height)):
                 held.append(
                     pltpu.make_async_copy(
-                        source.at[pl.ds(first, rows)],
+                        source.at[pl.ds(skip + first, rows)],
                         down_ref.at[pl.ds(begin + first, rows)],
                         sems.at[part, 1, piece * STREAMS + stream],
                     )
@@ -529,14 +534,27 @@
 def feed_forward(rows, ups, downs):
     pieces, parts = len(rows), len(ups)
     row_total, model_width = sum(piece.shape[0] for piece in rows), rows[0].shape[1]
-    up_plan = [[piece.shape[0] for piece in block] for block in ups]
-    down_plan = [[piece.shape[0] for piece in block] for block in downs]
-    up_rows, down_rows = sum(up_plan[0]), sum(down_plan[0])
-    units = ups[0][0].shape[1]
-    flat = [piece for block in ups + downs for piece in block]
+    flat = []
+
+    def plan(blocks):
+        planned = []
+        for block in blocks:
+            entries = []
+            for array, begin, height in block:
+                places = [at for at, known in enumerate(flat) if known is array]
+                if not places:
+                    places = [len(flat)]
+                    flat.append(array)
+                entries.append((places[0], begin, height))
+            planned.append(entries)
+        return planned
+
+    up_plan, down_plan = plan(ups), plan(downs)
+    up_rows, down_rows = (sum(entry[2] for entry in held[0]) for held in (up_plan, down_plan))
+    units = ups[0][0][0].shape[1]
     most = max(map(len, up_plan + down_plan))
     return pl.pallas_call(
-        functools.partial(mlp_kernel, pieces, up_plan, down_plan),
+        functools.partial(mlp_kernel, pieces, len(flat), up_plan, down_plan),
         out_shape=tuple(jax.ShapeDtypeStruct(piece.shape, jnp.bfloat16) for piece in rows),
         in_specs=[vmem_spec()] * pieces + [hbm_spec()] * len(flat),
         out_specs=tuple(vmem_spec() for _ in rows),
@@ -635,10 +653,9 @@
     )
     bias_rows = jnp.broadcast_to(up_bias[None, :], (16, up_bias.shape[0]))
     up_block = jnp.concatenate([up_weight, bias_rows], axis=0)
-    up_cut, down_cut = up_weight.shape[0] * 5 // 8, down_weight.shape[0] // 2
-    up_pieces = (up_block[:up_cut], up_block[up_cut:])
-    down_pieces = (down_weight[:down_cut], down_weight[down_cut:])
-    ups, downs = {0: (up_block,)}, {0: (down_weight,)}
+    up_cut, down_cut = up_weight.shape[0] // 2, down_weight.shape[0] // 2
+    up_first, up_second = up_block[:up_cut], up_block[up_cut:]
+    down_first, down_second = down_weight[:down_cut], down_weight[down_cut:]
     high_mask = high_masks[0]
 
     arrived = lax.all_to_all(
@@ -648,63 +665,150 @@
         concat_axis=0,
         tiled=True,
     )
-    ups[low_mask] = swap(ups[0], low_mask)
-    up_first = swap(up_pieces[0], high_mask)
-    ups[core_mask] = swap(ups[0], core_mask)
-    downs[core_mask] = swap(downs[0], core_mask)
+    up_low_first = swap(up_first, low_mask)
+    up_high_first = swap(up_first, high_mask)
+    up_core = swap(up_block, core_mask)
+    down_core = swap(down_weight, core_mask)
     turned_keys = prefix_keys[0].T
     value_heads = prefix_values[0].reshape(-1, local_heads, HD).transpose(1, 0, 2)
     wide_values = jnp.concatenate([value_heads, jnp.ones_like(value_heads)], axis=2)
     own = attend_suffix(
         suffix_lengths, suffix_queries, suffix_keys, suffix_values, local_heads
     )
-    arrived, ups, up_first, up_pieces, downs, down_pieces, turned_keys, wide_values, own = (
-        lax.optimization_barrier(
-            (arrived, ups, up_first, up_pieces, downs, down_pieces, turned_keys, wide_values, own)
+    (
+        arrived,
+        up_low_first,
+        up_high_first,
+        up_core,
+        down_core,
+        up_second,
+        down_first,
+        down_second,
+        turned_keys,
+        wide_values,
+        own,
+    ) = lax.optimization_barrier(
+        (
+            arrived,
+            up_low_first,
+            up_high_first,
+            up_core,
+            down_core,
+            up_second,
+            down_first,
+            down_second,
+            turned_keys,
+            wide_values,
+            own,
         )
     )
 
     counts = jnp.sum((arrived[:, :, 0] < EMPTY / 2).astype(jnp.int32), axis=1)
     answer_part = attend_prefix(counts, arrived, turned_keys, wide_values)
-    downs[low_mask] = swap(downs[0], low_mask)
-    up_second = swap(up_pieces[1], high_mask)
-    down_first = swap(down_pieces[0], high_mask)
-    ups[core_mask ^ low_mask] = swap(ups[low_mask], core_mask)
-    answer_part, ups, up_first, up_second, downs, down_first, down_pieces = (
-        lax.optimization_barrier(
-            (answer_part, ups, up_first, up_second, downs, down_first, down_pieces)
+    up_low_second = swap(up_second, low_mask)
+    up_high_second = swap(up_second, high_mask)
+    down_low_first = swap(down_first, low_mask)
+    down_high_first = swap(down_first, high_mask)
+    (
+        answer_part,
+        up_low_second,
+        up_high_second,
+        down_low_first,
+        down_high_first,
+        down_second,
+    ) = lax.optimization_barrier(
+        (
+            answer_part,
+            up_low_second,
+            up_high_second,
+            down_low_first,
+            down_high_first,
+            down_second,
         )
     )
 
     answer = lax.all_to_all(
         answer_part, ("grp", "dev"), split_axis=0, concat_axis=0, tiled=True
     ).reshape(group_count, column_count, capacity + STAT_ROWS, part_width)
-    ups[high_mask] = (jnp.concatenate([up_first, up_second], axis=0),)
-    ups[core_mask ^ high_mask] = swap(ups[high_mask], core_mask)
-    downs[core_mask ^ low_mask] = swap(downs[low_mask], core_mask)
-    down_second = swap(down_pieces[1], high_mask)
-    downs[high_mask] = (jnp.concatenate([down_first, down_second], axis=0),)
-    downs[core_mask ^ high_mask] = swap(downs[high_mask], core_mask)
-    ups[low_mask ^ high_mask] = swap(ups[high_mask], low_mask)
-    answer, ups, downs = lax.optimization_barrier((answer, ups, downs))
+    up_high = jnp.concatenate([up_high_first, up_high_second], axis=0)
+    up_low = jnp.concatenate([up_low_first, up_low_second], axis=0)
+    down_high_second = swap(down_second, high_mask)
+    up_cross = swap(up_high, low_mask)
+    up_high_core = swap(up_high, core_mask)
+    up_low_core = swap(up_low, core_mask)
+    down_low_first_core = swap(down_low_first, core_mask)
+    down_high = jnp.concatenate([down_high_first, down_high_second], axis=0)
+    down_high_core = swap(down_high, core_mask)
+    down_late = jnp.concatenate([down_second, down_high_second], axis=0)
+    (
+        answer,
+        up_cross,
+        up_high_core,
+        up_low_core,
+        down_low_first_core,
+        down_high,
+        down_high_core,
+        down_late,
+        down_low_first,
+    ) = lax.optimization_barrier(
+        (
+            answer,
+            up_cross,
+            up_high_core,
+            up_low_core,
+            down_low_first_core,
+            down_high,
+            down_high_core,
+            down_late,
+            down_low_first,
+        )
+    )
 
     hidden_a, hidden_b, hidden = merge_parts(
         suffix_lengths, request_group, answer, *own, layer_input, attn_gain, attn_shift
     )
 
-    (hidden_a, hidden_b, hidden), ups, downs = lax.optimization_barrier(
-        ((hidden_a, hidden_b, hidden), ups, downs)
+    (hidden_a, hidden_b, hidden), up_cross, down_late, down_low_first = lax.optimization_barrier(
+        ((hidden_a, hidden_b, hidden), up_cross, down_late, down_low_first)
     )
     far_a = swap(hidden_a, far_mask)
+    down_late = swap(down_late, low_mask)
+    down_cross_first = swap(down_low_first, high_mask)
+    far_a, hidden_b, hidden, up_cross = lax.optimization_barrier(
+        (far_a, hidden_b, hidden, up_cross)
+    )
+    far_b = swap(hidden_b, far_mask)
+    cross_a = swap(far_a, near_mask)
     near = swap(hidden, near_mask)
-    downs[low_mask ^ high_mask] = swap(downs[high_mask], low_mask)
+    up_cross_core = swap(up_cross, core_mask)
+    far_b, cross_a, near, up_cross_core, down_late, down_cross_first = lax.optimization_barrier(
+        (far_b, cross_a, near, up_cross_core, down_late, down_cross_first)
+    )
+    cross_b = swap(far_b, near_mask)
+    down_late_core = swap(down_late, core_mask)
+    down_cross_first_core = swap(down_cross_first, core_mask)
+
+    up_rows, down_rows = up_block.shape[0], down_weight.shape[0]
+    rest = down_rows - down_cut
+
+    def whole(array):
+        return [(array, 0, array.shape[0])]
+
+    ups = {0: up_block, low_mask: up_low, high_mask: up_high, low_mask ^ high_mask: up_cross}
+    up_cores = (up_core, up_low_core, up_high_core, up_cross_core)
+    ups.update({core_mask ^ at: array for at, array in zip(list(ups), up_cores)})
+    ups = {at: whole(array) for at, array in ups.items()}
+    downs = {0: whole(down_weight), high_mask: whole(down_high)}
+    downs[low_mask] = [(down_low_first, 0, down_cut), (down_late, 0, rest)]
+    downs[low_mask ^ high_mask] = [(down_cross_first, 0, down_cut), (down_late, rest, rest)]
+    downs[core_mask] = whole(down_core)
+    downs[core_mask ^ high_mask] = whole(down_high_core)
+    downs[core_mask ^ low_mask] = [(down_low_first_core, 0, down_cut), (down_late_core, 0, rest)]
+    downs[core_mask ^ low_mask ^ high_mask] = [
+        (down_cross_first_core, 0, down_cut),
+        (down_late_core, rest, rest),
+    ]
     ups = complete(ups, group_masks + column_masks)
-    far_b = swap(tie(hidden_b, far_a), far_mask)
-    cross_a = swap(far_a, near_mask)
-    far_b, cross_a, near, ups, downs = lax.optimization_barrier(
-        (far_b, cross_a, near, ups, downs)
-    )
-    cross_b = swap(far_b, near_mask)
     downs = complete(downs, group_masks + column_masks)
     order = sorted(ups)
     ups = [ups[mask] for mask in order]

time: 204 us -> 217 us (1.064)
  starting transfers between devices: 36.2 us -> 42.9 us
  local copies, waits for them, and re-layouts: 24 us -> 28.4 us
    ppermute x26 -> x29, starting transfers between devices: 24.1 us -> 29.8 us  [swap(): lax.ppermute(leaf, ('grp', 'dev'), pairs)]
    unnamed x74 -> x93, local copies, waits for them, and re-layouts: 12.6 us -> 16.1 us
    pallas_call x1, Pallas kernels: 19.2 us -> 16.7 us  [attend_prefix(): pl.pallas_call(far_kernel, out_shape=jax.ShapeDtypeStruct((sources, capac...]
    ppermute x26 -> x29, waiting for transfers between devices: 79.8 us -> 81.2 us  [swap(): lax.ppermute(leaf, ('grp', 'dev'), pairs)]
  transfers between devices with their start and end apart: 28 -> 31, of which waited for: 10 -> 11; matrix products, arithmetic and copies ran while one was open for 11% -> 12% of each run, Pallas kernels for 27% -> 25%
where the time goes in v12:
time: 217 us; the launch traced here: 216 us
  waiting for transfers between devices  81.2 us (37%)
  Pallas kernels  59.6 us (27%)
  starting transfers between devices  42.9 us (20%)
  local copies, waits for them, and re-layouts  28.4 us (13%)
  other arithmetic  3.34 us (2%)
    ppermute x29, waiting for transfers between devices, swap(): lax.ppermute(leaf, ('grp', 'dev'), pairs)  81.2 us
    pallas_call x3, Pallas kernels, feed_forward(): pl.pallas_call(functools.partial(mlp_kernel, pieces, len(flat), up_plan,...  32.8 us
    ppermute x29, starting transfers between devices, swap(): lax.ppermute(leaf, ('grp', 'dev'), pairs)  29.8 us
    pallas_call x1, Pallas kernels, attend_prefix(): pl.pallas_call(far_kernel, out_shape=jax.ShapeDtypeStruct((sources, capac...  16.7 us
    unnamed x93, local copies, waits for them, and re-layouts  16.1 us
    all_to_all x1, starting transfers between devices, on_device(): lax.all_to_all(outgoing.reshape(sources, capacity, part_width), ('grp', '...  7.3 us
    all_to_all x1, starting transfers between devices, on_device(): lax.all_to_all(answer_part, ('grp', 'dev'), split_axis=0, concat_axis=0,...  5.75 us
    pallas_call x1, Pallas kernels, attend_suffix(): pl.pallas_call(functools.partial(own_kernel, local_heads), out_shape=(jax...  4.48 us
  transfers between devices with their start and end apart: 31, of which 11 were waited for; matrix products, arithmetic and copies ran while one was open for 12% of the time, Pallas kernels for 25%

profile of v12, /device:TPU:0, one launch (start us, length us, event | category | flops | bytes accessed | tf_op | source)
XLA Modules:
  0.0 216.1 jit_solution(12480865763952037625)
XLA Ops:
  0.0 2.3 %pack_queries.1 = bf16[4,8,64,256]{3,2,1,0:T(8,128)(2,1)} custom-call(s32[1,4]{1,0:T(1,128)} %lengths_ref.5, s32[1,4]{1,0:T(1,128)} %groups_ref.3, bf16[128,2048]{1,0:T(8,128)(2,1)} %query_ref.3), custom_call_target="tpu_custom_call" | custom-call | tf_op jit(solution)/shard_map/pack_queries/pallas_call | solution.py:76
  2.3 7.3 %all-to-all-start = ((bf16[32,64,256]{2,1,0:T(8,128)(2,1)}), bf16[32,64,256]{2,1,0:T(8,128)(2,1)S(1)}, u32[]{:S(2)}, u32[]{:S(2)}) async-start(bf16[32,64,256]{2,1,0:T(8,128)(2,1)} %bitcast.20), calls=%async_computation | async-start | bytes 2097152 | tf_op jit(solution)/shard_map/all_to_all | solution.py:661
  15.3 4.5 %attend_suffix.1 = (f32[128,2048]{1,0:T(8,128)S(1)}, f32[128,128]{1,0:T(8,128)S(1)}, f32[128,128]{1,0:T(8,128)S(1)}) custom-call(s32[1,4]{1,0:T(1,128)S(1)} %copy-done.10, bf16[128,2048]{1,0:T(8,128)(2,1)S(1)} %copy-done.3, bf16[128,2048]{1,0:T(8,128)(2,1)S(1)} %copy-done.12, bf16[128,2048]{1,0:T(8,128)(2,1)S(1)} %copy-done.13), custom_call_target="tpu_custom_call" | custom-call | flops 1342177280 | bytes 2097152 | tf_op jit(solution)/shard_map/attend_suffix/pallas_call | solution.py:320
  19.8 4.1 %copy.18 = bf16[1,4096,256]{1,2,0:T(8,128)(2,1)} copy(bf16[1,4096,256]{2,1,0:T(8,128)(2,1)} %param.22) | data formatting | bytes 4194304 | tf_op args[6]
  23.9 4.1 %copy.19 = bf16[1,4096,256]{1,2,0:T(8,128)(2,1)} copy(bf16[1,4096,256]{2,1,0:T(8,128)(2,1)} %param.23) | data formatting | bytes 4194304 | tf_op args[7]
  28.0 4.1 %copy.20 = bf16[4096,2,128]{2,0,1:T(8,128)(2,1)} copy(bf16[4096,2,128]{0,2,1:T(8,128)(2,1)} %bitcast.19) | data formatting | bytes 4194304 | tf_op jit(solution)/shard_map/reshape;squeeze | solution.py:673
  32.1 3.9 %concatenate.19.values_hbm = bf16[2,4096,256]{2,1,0:T(8,128)(2,1)} pad(bf16[2,4096,128]{2,1,0:T(8,128)(2,1)} %bitcast.18, bf16[]{:T(256)} %constant.0.clone.1), padding=0_0x0_0x0_128 | pad | bytes 6291458 | tf_op jit(solution)/shard_map/concatenate | solution.py:674
  36.0 2.3 %fusion.1 = (bf16[128,2048]{1,0:T(8,128)(2,1)}, bf16[128,2048]{1,0:T(8,128)(2,1)}) fusion(bf16[256,2048]{1,0:T(8,128)(2,1)} %refs_10_.5), kind=kLoop, calls=%fused_computation.14 | loop fusion | bytes 2097152 | tf_op jit(solution)/shard_map/slice | solution.py:658
  38.3 2.3 %collective-permute-done.1 = bf16[1024,256]{1,0:T(8,128)(2,1)} collective-permute-done((bf16[1024,256]{1,0:T(8,128)(2,1)}, bf16[1024,256]{1,0:T(8,128)(2,1)}, u32[]{:S(2)}, u32[]{:S(2)}) %collective-permute-start.1) | collective-permute-done | bytes 524320 | tf_op jit(solution)/shard_map/ppermute | solution.py:441
  46.0 16.7 %attend_prefix.1 = bf16[32,72,256]{2,1,0:T(8,128)(2,1)} custom-call(s32[32]{0:T(128)} %convert_reduce_fusion.counts_ref, bf16[32,64,256]{2,1,0:T(8,128)(2,1)} %copy-done.30, bf16[256,4096]{1,0:T(8,128)(2,1)} %bitcast.21, bf16[2,4096,256]{2,1,0:T(8,128)(2,1)} %concatenate.19.values_hbm), custom_call_target="tpu_custom_call" | custom-call | flops 8589934592 | bytes 8388608 | tf_op jit(solution)/shard_map/attend_prefix/pallas_call | solution.py:246
  63.5 2.5 %collective-permute-done.5 = bf16[1040,256]{1,0:T(8,128)(2,1)} collective-permute-done((bf16[1040,256]{1,0:T(8,128)(2,1)}, bf16[1040,256]{1,0:T(8,128)(2,1)}, u32[]{:S(2)}, u32[]{:S(2)}) %collective-permute-start.5) | collective-permute-done | bytes 532512 | tf_op jit(solution)/shard_map/ppermute | solution.py:441
  66.9 5.7 %all-to-all-start.1 = ((bf16[32,72,256]{2,1,0:T(8,128)(2,1)}), bf16[32,72,256]{2,1,0:T(8,128)(2,1)S(1)}, u32[]{:S(2)}, u32[]{:S(2)}) async-start(bf16[32,72,256]{2,1,0:T(8,128)(2,1)} %attend_prefix.1), calls=%async_computation.1 | async-start | bytes 2359296 | tf_op jit(solution)/shard_map/all_to_all | solution.py:730
  79.9 25.7 %collective-permute-done.12 = bf16[128,2048]{1,0:T(8,128)(2,1)S(1)} collective-permute-done((bf16[128,2048]{1,0:T(8,128)(2,1)S(1)}, bf16[128,2048]{1,0:T(8,128)(2,1)S(1)}, u32[]{:S(2)}, u32[]{:S(2)}) %collective-permute-start.12) | collective-permute-done | bytes 524320 | tf_op jit(solution)/shard_map/ppermute | solution.py:441
  109.2 2.0 collective-permute-done.8.refs_5_
  114.1 2.0 collective-permute-start.14
  116.1 12.8 %collective-permute-done.14.refs_0_ = bf16[64,2048]{1,0:T(8,128)(2,1)S(1)} collective-permute-done((bf16[64,2048]{1,0:T(8,128)(2,1)S(1)}, bf16[64,2048]{1,0:T(8,128)(2,1)S(1)}, u32[]{:S(2)}, u32[]{:S(2)}) %collective-permute-start.14) | collective-permute-done | bytes 262176 | tf_op jit(solution)/shard_map/ppermute | solution.py:441
  131.5 2.9 %collective-permute-start.15 = (bf16[64,2048]{1,0:T(8,128)(2,1)S(1)}, bf16[64,2048]{1,0:T(8,128)(2,1)S(1)}, u32[]{:S(2)}, u32[]{:S(2)}) collective-permute-start(bf16[64,2048]{1,0:T(8,128)(2,1)S(1)} %get-tuple-element.102), channel_id=1, source_target_pairs={{0,4},{1,5},{2,6},{3,7},{4,0},{5,1},{6,2},{7,3},{8,12},{9,13},{10,... | collective-permute-start | bytes 786440 | tf_op jit(solution)/shard_map/ppermute | solution.py:441
  134.4 15.2 %collective-permute-done.20.refs_14_ = bf16[128,2048]{1,0:T(8,128)(2,1)S(1)} collective-permute-done((bf16[128,2048]{1,0:T(8,128)(2,1)S(1)}, bf16[128,2048]{1,0:T(8,128)(2,1)S(1)}, u32[]{:S(2)}, u32[]{:S(2)}) %collective-permute-start.20) | collective-permute-done | bytes 524320 | tf_op jit(solution)/shard_map/ppermute | solution.py:441
  151.1 6.1 %collective-permute-done.16.refs_1_ = bf16[64,2048]{1,0:T(8,128)(2,1)S(1)} collective-permute-done((bf16[64,2048]{1,0:T(8,128)(2,1)S(1)}, bf16[64,2048]{1,0:T(8,128)(2,1)S(1)}, u32[]{:S(2)}, u32[]{:S(2)}) %collective-permute-start.16) | collective-permute-done | bytes 262176 | tf_op jit(solution)/shard_map/ppermute | solution.py:441
  162.5 10.0 %feed_forward.3 = (bf16[64,2048]{1,0:T(8,128)(2,1)}, bf16[64,2048]{1,0:T(8,128)(2,1)}) custom-call(bf16[64,2048]{1,0:T(8,128)(2,1)} %copy-done.38, bf16[64,2048]{1,0:T(8,128)(2,1)} %copy-done.40, bf16[2064,256]{1,0:T(8,128)(2,1)} %copy-done.14, bf16[2064,256]{1,0:T(8,128)(2,1)} %copy-done.15, bf16[2064,256]{1,0:T(8,128)(2,1)} %copy-done.16, ...), custom_call_target="tpu_custom_call" | custom-call | flops 2147483648 | bytes 16777216 | tf_op jit(solution)/shard_map/feed_forward/pallas_call | solution.py:556
  174.0 10.0 %feed_forward.4 = (bf16[64,2048]{1,0:T(8,128)(2,1)}, bf16[64,2048]{1,0:T(8,128)(2,1)}) custom-call(bf16[64,2048]{1,0:T(8,128)(2,1)} %copy-done.39, bf16[64,2048]{1,0:T(8,128)(2,1)} %collective-permute-done.21.refs_1_, bf16[2064,256]{1,0:T(8,128)(2,1)} %copy-done.14, bf16[2064,256]{1,0:T(8,128)(2,1)} %copy-done.15, bf16[2064,256]{1,0:T(8,128)(2,1)} %copy-done.16, ...), custom_call_target="tpu_custom_call" | custom-call | flops 2147483648 | bytes 16777216 | tf_op jit(solution)/shard_map/feed_forward/pallas_call | solution.py:556
  185.2 12.9 %feed_forward.5 = (bf16[128,2048]{1,0:T(8,128)(2,1)}, bf16[128,2048]{1,0:T(8,128)(2,1)}) custom-call(bf16[128,2048]{1,0:T(8,128)(2,1)} %copy-done.35, bf16[128,2048]{1,0:T(8,128)(2,1)} %copy-done, bf16[2064,256]{1,0:T(8,128)(2,1)} %copy-done.14, bf16[2064,256]{1,0:T(8,128)(2,1)} %copy-done.15, bf16[2064,256]{1,0:T(8,128)(2,1)} %copy-done.16, ...), custom_call_target="tpu_custom_call" | custom-call | flops 4294967296 | bytes 16777216 | tf_op jit(solution)/shard_map/feed_forward/pallas_call | solution.py:556
  199.8 2.5 %collective-permute-start.28 = (bf16[64,2048]{1,0:T(8,128)(2,1)S(1)}, bf16[64,2048]{1,0:T(8,128)(2,1)S(1)}, u32[]{:S(2)}, u32[]{:S(2)}) collective-permute-start(bf16[64,2048]{1,0:T(8,128)(2,1)S(1)} %add_convert_fusion), channel_id=1, source_target_pairs={{0,4},{1,5},{2,6},{3,7},{4,0},{5,1},{6,2},{7,3},{8,12},{9,13},{10,... | collective-permute-start | bytes 786440 | tf_op jit(solution)/shard_map/ppermute | solution.py:441
  202.3 11.3 %collective-permute-done.28.far_b_ref = bf16[64,2048]{1,0:T(8,128)(2,1)S(1)} collective-permute-done((bf16[64,2048]{1,0:T(8,128)(2,1)S(1)}, bf16[64,2048]{1,0:T(8,128)(2,1)S(1)}, u32[]{:S(2)}, u32[]{:S(2)}) %collective-permute-start.28) | collective-permute-done | bytes 262176 | tf_op jit(solution)/shard_map/ppermute | solution.py:441
  (153 shorter events, 42.3 us)
Async XLA Ops:
  2.3 38.4 %all-to-all-start = ((bf16[32,64,256]{2,1,0:T(8,128)(2,1)}), bf16[32,64,256]{2,1,0:T(8,128)(2,1)S(1)}, u32[]{:S(2)}, u32[]{:S(2)}) async-start(bf16[32,64,256]{2,1,0:T(8,128)(2,1)} %bitcast.20), calls=%async_computation | async-start | bytes 2097152 | tf_op jit(solution)/shard_map/all_to_all | solution.py:661
  9.8 30.9 %collective-permute-start.2 = (bf16[2064,256]{1,0:T(8,128)(2,1)S(1)}, bf16[2064,256]{1,0:T(8,128)(2,1)}, u32[]{:S(2)}, u32[]{:S(2)}) collective-permute-start(bf16[2064,256]{1,0:T(8,128)(2,1)S(1)} %pad_maximum_fusion.refs_2_), channel_id=1, source_target_pairs={{0,8},{1,9},{2,10},{3,11},{4,12},{5,13},{6,14},{7,15},{8,0},{9,1},... | collective-permute-start | bytes 3170312 | tf_op jit(solution)/shard_map/ppermute | solution.py:441
  10.1 30.6 %collective-permute-start.3 = (bf16[256,2048]{1,0:T(8,128)(2,1)}, bf16[256,2048]{1,0:T(8,128)(2,1)}, u32[]{:S(2)}, u32[]{:S(2)}) collective-permute-start(bf16[256,2048]{1,0:T(8,128)(2,1)} %refs_10_.5), channel_id=1, source_target_pairs={{0,8},{1,9},{2,10},{3,11},{4,12},{5,13},{6,14},{7,15},{8,0},{9,1},... | collective-permute-start | bytes 3145736 | tf_op jit(solution)/shard_map/ppermute | solution.py:441
  11.2 29.5 %collective-permute-start.1 = (bf16[1024,256]{1,0:T(8,128)(2,1)}, bf16[1024,256]{1,0:T(8,128)(2,1)}, u32[]{:S(2)}, u32[]{:S(2)}) collective-permute-start(bf16[1024,256]{1,0:T(8,128)(2,1)} %slice.15), channel_id=1, source_target_pairs={{0,2},{1,3},{2,0},{3,1},{4,6},{5,7},{6,4},{7,5},{8,10},{9,11},{10,... | collective-permute-start | bytes 1572872 | tf_op jit(solution)/shard_map/ppermute | solution.py:441
  13.0 27.7 %collective-permute-start = (bf16[1024,256]{1,0:T(8,128)(2,1)}, bf16[1024,256]{1,0:T(8,128)(2,1)}, u32[]{:S(2)}, u32[]{:S(2)}) collective-permute-start(bf16[1024,256]{1,0:T(8,128)(2,1)} %slice.15), channel_id=1, source_target_pairs={{0,1},{1,0},{2,3},{3,2},{4,5},{5,4},{6,7},{7,6},{8,9},{9,8},{10,11... | collective-permute-start | bytes 1572872 | tf_op jit(solution)/shard_map/ppermute | solution.py:441
  40.7 22.0 %collective-permute-start.7 = (bf16[128,2048]{1,0:T(8,128)(2,1)}, bf16[128,2048]{1,0:T(8,128)(2,1)S(1)}, u32[]{:S(2)}, u32[]{:S(2)}) collective-permute-start(bf16[128,2048]{1,0:T(8,128)(2,1)} %get-tuple-element.78), channel_id=1, source_target_pairs={{0,2},{1,3},{2,0},{3,1},{4,6},{5,7},{6,4},{7,5},{8,10},{9,11},{10,... | collective-permute-start | bytes 1572872 | tf_op jit(solution)/shard_map/ppermute | solution.py:441
  41.1 21.6 %collective-permute-start.6 = (bf16[128,2048]{1,0:T(8,128)(2,1)}, bf16[128,2048]{1,0:T(8,128)(2,1)S(1)}, u32[]{:S(2)}, u32[]{:S(2)}) collective-permute-start(bf16[128,2048]{1,0:T(8,128)(2,1)} %get-tuple-element.78), channel_id=1, source_target_pairs={{0,1},{1,0},{2,3},{3,2},{4,5},{5,4},{6,7},{7,6},{8,9},{9,8},{10,11... | collective-permute-start | bytes 1572872 | tf_op jit(solution)/shard_map/ppermute | solution.py:441
  42.8 23.1 %collective-permute-start.5 = (bf16[1040,256]{1,0:T(8,128)(2,1)}, bf16[1040,256]{1,0:T(8,128)(2,1)}, u32[]{:S(2)}, u32[]{:S(2)}) collective-permute-start(bf16[1040,256]{1,0:T(8,128)(2,1)} %fusion), channel_id=1, source_target_pairs={{0,2},{1,3},{2,0},{3,1},{4,6},{5,7},{6,4},{7,5},{8,10},{9,11},{10,... | collective-permute-start | bytes 1597448 | tf_op jit(solution)/shard_map/ppermute | solution.py:441
  44.3 21.8 %collective-permute-start.4 = (bf16[1040,256]{1,0:T(8,128)(2,1)}, bf16[1040,256]{1,0:T(8,128)(2,1)S(1)}, u32[]{:S(2)}, u32[]{:S(2)}) collective-permute-start(bf16[1040,256]{1,0:T(8,128)(2,1)} %fusion), channel_id=1, source_target_pairs={{0,1},{1,0},{2,3},{3,2},{4,5},{5,4},{6,7},{7,6},{8,9},{9,8},{10,11... | collective-permute-start | bytes 1597448 | tf_op jit(solution)/shard_map/ppermute | solution.py:441
  66.9 45.2 %all-to-all-start.1 = ((bf16[32,72,256]{2,1,0:T(8,128)(2,1)}), bf16[32,72,256]{2,1,0:T(8,128)(2,1)S(1)}, u32[]{:S(2)}, u32[]{:S(2)}) async-start(bf16[32,72,256]{2,1,0:T(8,128)(2,1)} %attend_prefix.1), calls=%async_computation.1 | async-start | bytes 2359296 | tf_op jit(solution)/shard_map/all_to_all | solution.py:730
  75.0 30.6 %collective-permute-start.12 = (bf16[128,2048]{1,0:T(8,128)(2,1)S(1)}, bf16[128,2048]{1,0:T(8,128)(2,1)S(1)}, u32[]{:S(2)}, u32[]{:S(2)}) collective-permute-start(bf16[128,2048]{1,0:T(8,128)(2,1)S(1)} %copy-done.31), channel_id=1, source_target_pairs={{0,2},{1,3},{2,0},{3,1},{4,6},{5,7},{6,4},{7,5},{8,10},{9,11},{10,... | collective-permute-start | bytes 1572872 | tf_op jit(solution)/shard_map/ppermute | solution.py:441
  77.9 31.2 %collective-permute-start.9 = (bf16[2064,256]{1,0:T(8,128)(2,1)S(1)}, bf16[2064,256]{1,0:T(8,128)(2,1)S(1)}, u32[]{:S(2)}, u32[]{:S(2)}) collective-permute-start(bf16[2064,256]{1,0:T(8,128)(2,1)S(1)} %constant_dynamic-update-slice_fusion.refs_4_), channel_id=1, source_target_pairs={{0,8},{1,9},{2,10},{3,11},{4,12},{5,13},{6,14},{7,15},{8,0},{9,1},... | collective-permute-start | bytes 3170312 | tf_op jit(solution)/shard_map/ppermute | solution.py:441
  78.0 33.1 %collective-permute-start.8 = (bf16[2064,256]{1,0:T(8,128)(2,1)S(1)}, bf16[2064,256]{1,0:T(8,128)(2,1)S(1)}, u32[]{:S(2)}, u32[]{:S(2)}) collective-permute-start(bf16[2064,256]{1,0:T(8,128)(2,1)S(1)} %constant_dynamic-update-slice_fusion.refs_4_), channel_id=1, source_target_pairs={{0,1},{1,0},{2,3},{3,2},{4,5},{5,4},{6,7},{7,6},{8,9},{9,8},{10,11... | collective-permute-start | bytes 3170312 | tf_op jit(solution)/shard_map/ppermute | solution.py:441
  79.6 29.6 %collective-permute-start.10 = (bf16[2064,256]{1,0:T(8,128)(2,1)S(1)}, bf16[2064,256]{1,0:T(8,128)(2,1)S(1)}, u32[]{:S(2)}, u32[]{:S(2)}) collective-permute-start(bf16[2064,256]{1,0:T(8,128)(2,1)S(1)} %constant_dynamic-update-slice_fusion.2.refs_3_), channel_id=1, source_target_pairs={{0,8},{1,9},{2,10},{3,11},{4,12},{5,13},{6,14},{7,15},{8,0},{9,1},... | collective-permute-start | bytes 3170312 | tf_op jit(solution)/shard_map/ppermute | solution.py:441
  114.1 14.8 %collective-permute-start.14 = (bf16[64,2048]{1,0:T(8,128)(2,1)S(1)}, bf16[64,2048]{1,0:T(8,128)(2,1)S(1)}, u32[]{:S(2)}, u32[]{:S(2)}) collective-permute-start(bf16[64,2048]{1,0:T(8,128)(2,1)S(1)} %get-tuple-element.98), channel_id=1, source_target_pairs={{0,4},{1,5},{2,6},{3,7},{4,0},{5,1},{6,2},{7,3},{8,12},{9,13},{10,... | collective-permute-start | bytes 786440 | tf_op jit(solution)/shard_map/ppermute | solution.py:441
  128.9 28.3 %collective-permute-start.18 = (bf16[2064,256]{1,0:T(8,128)(2,1)S(1)}, bf16[2064,256]{1,0:T(8,128)(2,1)S(1)}, u32[]{:S(2)}, u32[]{:S(2)}) collective-permute-start(bf16[2064,256]{1,0:T(8,128)(2,1)S(1)} %copy-done.20), channel_id=1, source_target_pairs={{0,8},{1,9},{2,10},{3,11},{4,12},{5,13},{6,14},{7,15},{8,0},{9,1},... | collective-permute-start | bytes 3170312 | tf_op jit(solution)/shard_map/ppermute | solution.py:441
  128.9 28.3 %collective-permute-start.19 = (bf16[256,2048]{1,0:T(8,128)(2,1)S(1)}, bf16[256,2048]{1,0:T(8,128)(2,1)S(1)}, u32[]{:S(2)}, u32[]{:S(2)}) collective-permute-start(bf16[256,2048]{1,0:T(8,128)(2,1)S(1)} %copy-done.32), channel_id=1, source_target_pairs={{0,1},{1,0},{2,3},{3,2},{4,5},{5,4},{6,7},{7,6},{8,9},{9,8},{10,11... | collective-permute-start | bytes 3145736 | tf_op jit(solution)/shard_map/ppermute | solution.py:441
  130.0 19.6 %collective-permute-start.20 = (bf16[128,2048]{1,0:T(8,128)(2,1)S(1)}, bf16[128,2048]{1,0:T(8,128)(2,1)S(1)}, u32[]{:S(2)}, u32[]{:S(2)}) collective-permute-start(bf16[128,2048]{1,0:T(8,128)(2,1)S(1)} %collective-permute-done.6.refs_11_), channel_id=1, source_target_pairs={{0,2},{1,3},{2,0},{3,1},{4,6},{5,7},{6,4},{7,5},{8,10},{9,11},{10,... | collective-permute-start | bytes 1572872 | tf_op jit(solution)/shard_map/ppermute | solution.py:441
  130.0 27.2 %collective-permute-start.17 = (bf16[128,2048]{1,0:T(8,128)(2,1)S(1)}, bf16[128,2048]{1,0:T(8,128)(2,1)S(1)}, u32[]{:S(2)}, u32[]{:S(2)}) collective-permute-start(bf16[128,2048]{1,0:T(8,128)(2,1)S(1)} %get-tuple-element.129.refs_1_.hidden_ref), channel_id=1, source_target_pairs={{0,16},{1,17},{2,18},{3,19},{4,20},{5,21},{6,22},{7,23},{8,24},{9,... | collective-permute-start | bytes 1572872 | tf_op jit(solution)/shard_map/ppermute | solution.py:441
  131.5 19.6 %collective-permute-start.15 = (bf16[64,2048]{1,0:T(8,128)(2,1)S(1)}, bf16[64,2048]{1,0:T(8,128)(2,1)S(1)}, u32[]{:S(2)}, u32[]{:S(2)}) collective-permute-start(bf16[64,2048]{1,0:T(8,128)(2,1)S(1)} %get-tuple-element.102), channel_id=1, source_target_pairs={{0,4},{1,5},{2,6},{3,7},{4,0},{5,1},{6,2},{7,3},{8,12},{9,13},{10,... | collective-permute-start | bytes 786440 | tf_op jit(solution)/shard_map/ppermute | solution.py:441
  157.8 14.7 %collective-permute-start.21 = (bf16[64,2048]{1,0:T(8,128)(2,1)S(1)}, bf16[64,2048]{1,0:T(8,128)(2,1)}, u32[]{:S(2)}, u32[]{:S(2)}) collective-permute-start(bf16[64,2048]{1,0:T(8,128)(2,1)S(1)} %collective-permute-done.15.refs_0_), channel_id=1, source_target_pairs={{0,16},{1,17},{2,18},{3,19},{4,20},{5,21},{6,22},{7,23},{8,24},{9,... | collective-permute-start | bytes 786440 | tf_op jit(solution)/shard_map/ppermute | solution.py:441
  184.2 15.5 %collective-permute-start.27 = (bf16[64,2048]{1,0:T(8,128)(2,1)S(1)}, bf16[64,2048]{1,0:T(8,128)(2,1)S(1)}, u32[]{:S(2)}, u32[]{:S(2)}) collective-permute-start(bf16[64,2048]{1,0:T(8,128)(2,1)S(1)} %add_convert_fusion.1), channel_id=1, source_target_pairs={{0,4},{1,5},{2,6},{3,7},{4,0},{5,1},{6,2},{7,3},{8,12},{9,13},{10,... | collective-permute-start | bytes 786440 | tf_op jit(solution)/shard_map/ppermute | solution.py:441
  184.7 15.0 %collective-permute-start.26 = (bf16[64,2048]{1,0:T(8,128)(2,1)}, bf16[64,2048]{1,0:T(8,128)(2,1)S(1)}, u32[]{:S(2)}, u32[]{:S(2)}) collective-permute-start(bf16[64,2048]{1,0:T(8,128)(2,1)} %get-tuple-element.133), channel_id=1, source_target_pairs={{0,16},{1,17},{2,18},{3,19},{4,20},{5,21},{6,22},{7,23},{8,24},{9,... | collective-permute-start | bytes 786440 | tf_op jit(solution)/shard_map/ppermute | solution.py:441
  198.2 15.4 %collective-permute-start.25 = (bf16[128,2048]{1,0:T(8,128)(2,1)}, bf16[128,2048]{1,0:T(8,128)(2,1)S(1)}, u32[]{:S(2)}, u32[]{:S(2)}) collective-permute-start(bf16[128,2048]{1,0:T(8,128)(2,1)} %get-tuple-element.132), channel_id=1, source_target_pairs={{0,16},{1,17},{2,18},{3,19},{4,20},{5,21},{6,22},{7,23},{8,24},{9,... | collective-permute-start | bytes 1572872 | tf_op jit(solution)/shard_map/ppermute | solution.py:441
  (51 other events, 562.2 us)

commit v13 on v12

--- a/solution.py
+++ b/solution.py
@@ -774,10 +774,7 @@
     far_a = swap(hidden_a, far_mask)
     down_late = swap(down_late, low_mask)
     down_cross_first = swap(down_low_first, high_mask)
-    far_a, hidden_b, hidden, up_cross = lax.optimization_barrier(
-        (far_a, hidden_b, hidden, up_cross)
-    )
-    far_b = swap(hidden_b, far_mask)
+    far_b = swap(tie(hidden_b, far_a), far_mask)
     cross_a = swap(far_a, near_mask)
     near = swap(hidden, near_mask)
     up_cross_core = swap(up_cross, core_mask)

time: 217 us -> 205 us (0.945)
  waiting for transfers between devices: 81.2 us -> 71.3 us
  starting transfers between devices: 42.9 us -> 38.1 us
  Pallas kernels: 59.6 us -> 62.2 us
    ppermute x29, waiting for transfers between devices: 81.2 us -> 71.3 us  [swap(): lax.ppermute(leaf, ('grp', 'dev'), pairs)]
    ppermute x29, starting transfers between devices: 29.8 us -> 25.1 us  [swap(): lax.ppermute(leaf, ('grp', 'dev'), pairs)]
    pallas_call x1, Pallas kernels: 16.7 us -> 19.3 us  [attend_prefix(): pl.pallas_call(far_kernel, out_shape=jax.ShapeDtypeStruct((sources, capac...]
  transfers between devices with their start and end apart: 31 -> 31, of which waited for: 11 -> 9; matrix products, arithmetic and copies ran while one was open for 12% -> 13% of each run, Pallas kernels for 25% -> 28%
where the time goes in v13:
time: 205 us; the launch traced here: 204 us
  waiting for transfers between devices  71.3 us (35%)
  Pallas kernels  62.2 us (30%)
  starting transfers between devices  38.1 us (19%)
  local copies, waits for them, and re-layouts  28.4 us (14%)
  other arithmetic  3.34 us (2%)
    ppermute x29, waiting for transfers between devices, swap(): lax.ppermute(leaf, ('grp', 'dev'), pairs)  71.3 us
    pallas_call x3, Pallas kernels, feed_forward(): pl.pallas_call(functools.partial(mlp_kernel, pieces, len(flat), up_plan,...  32.8 us
    ppermute x29, starting transfers between devices, swap(): lax.ppermute(leaf, ('grp', 'dev'), pairs)  25.1 us
    pallas_call x1, Pallas kernels, attend_prefix(): pl.pallas_call(far_kernel, out_shape=jax.ShapeDtypeStruct((sources, capac...  19.3 us
    unnamed x93, local copies, waits for them, and re-layouts  16.1 us
    all_to_all x1, starting transfers between devices, on_device(): lax.all_to_all(outgoing.reshape(sources, capacity, part_width), ('grp', '...  7.3 us
    all_to_all x1, starting transfers between devices, on_device(): lax.all_to_all(answer_part, ('grp', 'dev'), split_axis=0, concat_axis=0,...  5.65 us
    pallas_call x1, Pallas kernels, attend_suffix(): pl.pallas_call(functools.partial(own_kernel, local_heads), out_shape=(jax...  4.48 us
  transfers between devices with their start and end apart: 31, of which 9 were waited for; matrix products, arithmetic and copies ran while one was open for 13% of the time, Pallas kernels for 28%

profile of v13, /device:TPU:0, one launch (start us, length us, event | category | flops | bytes accessed | tf_op | source)
XLA Modules:
  0.0 204.0 jit_solution(16372087471485243810)
XLA Ops:
  0.0 2.3 %pack_queries.1 = bf16[4,8,64,256]{3,2,1,0:T(8,128)(2,1)} custom-call(s32[1,4]{1,0:T(1,128)} %lengths_ref.5, s32[1,4]{1,0:T(1,128)} %groups_ref.3, bf16[128,2048]{1,0:T(8,128)(2,1)} %query_ref.3), custom_call_target="tpu_custom_call" | custom-call | tf_op jit(solution)/shard_map/pack_queries/pallas_call | solution.py:76
  2.3 7.3 %all-to-all-start = ((bf16[32,64,256]{2,1,0:T(8,128)(2,1)}), bf16[32,64,256]{2,1,0:T(8,128)(2,1)S(1)}, u32[]{:S(2)}, u32[]{:S(2)}) async-start(bf16[32,64,256]{2,1,0:T(8,128)(2,1)} %bitcast.20), calls=%async_computation | async-start | bytes 2097152 | tf_op jit(solution)/shard_map/all_to_all | solution.py:661
  15.3 4.5 %attend_suffix.1 = (f32[128,2048]{1,0:T(8,128)S(1)}, f32[128,128]{1,0:T(8,128)S(1)}, f32[128,128]{1,0:T(8,128)S(1)}) custom-call(s32[1,4]{1,0:T(1,128)S(1)} %copy-done.10, bf16[128,2048]{1,0:T(8,128)(2,1)S(1)} %copy-done.3, bf16[128,2048]{1,0:T(8,128)(2,1)S(1)} %copy-done.12, bf16[128,2048]{1,0:T(8,128)(2,1)S(1)} %copy-done.13), custom_call_target="tpu_custom_call" | custom-call | flops 1342177280 | bytes 2097152 | tf_op jit(solution)/shard_map/attend_suffix/pallas_call | solution.py:320
  19.8 4.1 %copy.18 = bf16[1,4096,256]{1,2,0:T(8,128)(2,1)} copy(bf16[1,4096,256]{2,1,0:T(8,128)(2,1)} %param.22) | data formatting | bytes 4194304 | tf_op args[6]
  23.9 4.1 %copy.19 = bf16[1,4096,256]{1,2,0:T(8,128)(2,1)} copy(bf16[1,4096,256]{2,1,0:T(8,128)(2,1)} %param.23) | data formatting | bytes 4194304 | tf_op args[7]
  28.0 4.1 %copy.20 = bf16[4096,2,128]{2,0,1:T(8,128)(2,1)} copy(bf16[4096,2,128]{0,2,1:T(8,128)(2,1)} %bitcast.19) | data formatting | bytes 4194304 | tf_op jit(solution)/shard_map/reshape;squeeze | solution.py:673
  32.1 3.9 %concatenate.19.values_hbm = bf16[2,4096,256]{2,1,0:T(8,128)(2,1)} pad(bf16[2,4096,128]{2,1,0:T(8,128)(2,1)} %bitcast.18, bf16[]{:T(256)} %constant.0.clone.1), padding=0_0x0_0x0_128 | pad | bytes 6291458 | tf_op jit(solution)/shard_map/concatenate | solution.py:674
  36.0 2.3 %fusion.1 = (bf16[128,2048]{1,0:T(8,128)(2,1)}, bf16[128,2048]{1,0:T(8,128)(2,1)}) fusion(bf16[256,2048]{1,0:T(8,128)(2,1)} %refs_10_.5), kind=kLoop, calls=%fused_computation.14 | loop fusion | bytes 2097152 | tf_op jit(solution)/shard_map/slice | solution.py:658
  38.3 2.3 %collective-permute-done.1 = bf16[1024,256]{1,0:T(8,128)(2,1)} collective-permute-done((bf16[1024,256]{1,0:T(8,128)(2,1)}, bf16[1024,256]{1,0:T(8,128)(2,1)}, u32[]{:S(2)}, u32[]{:S(2)}) %collective-permute-start.1) | collective-permute-done | bytes 524320 | tf_op jit(solution)/shard_map/ppermute | solution.py:441
  46.0 19.3 %attend_prefix.1 = bf16[32,72,256]{2,1,0:T(8,128)(2,1)} custom-call(s32[32]{0:T(128)} %convert_reduce_fusion.counts_ref, bf16[32,64,256]{2,1,0:T(8,128)(2,1)} %copy-done.30, bf16[256,4096]{1,0:T(8,128)(2,1)} %bitcast.21, bf16[2,4096,256]{2,1,0:T(8,128)(2,1)} %concatenate.19.values_hbm), custom_call_target="tpu_custom_call" | custom-call | flops 8589934592 | bytes 8388608 | tf_op jit(solution)/shard_map/attend_prefix/pallas_call | solution.py:246
  67.0 5.6 %all-to-all-start.1 = ((bf16[32,72,256]{2,1,0:T(8,128)(2,1)}), bf16[32,72,256]{2,1,0:T(8,128)(2,1)S(1)}, u32[]{:S(2)}, u32[]{:S(2)}) async-start(bf16[32,72,256]{2,1,0:T(8,128)(2,1)} %attend_prefix.1), calls=%async_computation.1 | async-start | bytes 2359296 | tf_op jit(solution)/shard_map/all_to_all | solution.py:730
  79.9 25.7 %collective-permute-done.12 = bf16[128,2048]{1,0:T(8,128)(2,1)S(1)} collective-permute-done((bf16[128,2048]{1,0:T(8,128)(2,1)S(1)}, bf16[128,2048]{1,0:T(8,128)(2,1)S(1)}, u32[]{:S(2)}, u32[]{:S(2)}) %collective-permute-start.12) | collective-permute-done | bytes 524320 | tf_op jit(solution)/shard_map/ppermute | solution.py:441
  109.2 2.0 collective-permute-done.8.refs_5_
  112.2 1.9 merge_parts.1
  116.7 2.7 %collective-permute-start.14 = (bf16[64,2048]{1,0:T(8,128)(2,1)S(1)}, bf16[64,2048]{1,0:T(8,128)(2,1)S(1)}, u32[]{:S(2)}, u32[]{:S(2)}) collective-permute-start(bf16[64,2048]{1,0:T(8,128)(2,1)S(1)} %get-tuple-element.96), channel_id=1, source_target_pairs={{0,4},{1,5},{2,6},{3,7},{4,0},{5,1},{6,2},{7,3},{8,12},{9,13},{10,... | collective-permute-start | bytes 786440 | tf_op jit(solution)/shard_map/ppermute | solution.py:441
  119.6 11.8 %collective-permute-done.14.refs_0_ = bf16[64,2048]{1,0:T(8,128)(2,1)S(1)} collective-permute-done((bf16[64,2048]{1,0:T(8,128)(2,1)S(1)}, bf16[64,2048]{1,0:T(8,128)(2,1)S(1)}, u32[]{:S(2)}, u32[]{:S(2)}) %collective-permute-start.14) | collective-permute-done | bytes 262176 | tf_op jit(solution)/shard_map/ppermute | solution.py:441
  132.1 8.3 %collective-permute-done.20.refs_14_ = bf16[128,2048]{1,0:T(8,128)(2,1)S(1)} collective-permute-done((bf16[128,2048]{1,0:T(8,128)(2,1)S(1)}, bf16[128,2048]{1,0:T(8,128)(2,1)S(1)}, u32[]{:S(2)}, u32[]{:S(2)}) %collective-permute-start.20) | collective-permute-done | bytes 524320 | tf_op jit(solution)/shard_map/ppermute | solution.py:441
  140.4 5.8 %collective-permute-done.15.refs_0_ = bf16[64,2048]{1,0:T(8,128)(2,1)S(1)} collective-permute-done((bf16[64,2048]{1,0:T(8,128)(2,1)S(1)}, bf16[64,2048]{1,0:T(8,128)(2,1)S(1)}, u32[]{:S(2)}, u32[]{:S(2)}) %collective-permute-start.15) | collective-permute-done | bytes 262176 | tf_op jit(solution)/shard_map/ppermute | solution.py:441
  147.3 2.4 %collective-permute-done.23.refs_19_ = bf16[128,2048]{1,0:T(8,128)(2,1)S(1)} collective-permute-done((bf16[128,2048]{1,0:T(8,128)(2,1)S(1)}, bf16[128,2048]{1,0:T(8,128)(2,1)S(1)}, u32[]{:S(2)}, u32[]{:S(2)}) %collective-permute-start.23) | collective-permute-done | bytes 524320 | tf_op jit(solution)/shard_map/ppermute | solution.py:441
  151.5 9.9 %feed_forward.3 = (bf16[64,2048]{1,0:T(8,128)(2,1)}, bf16[64,2048]{1,0:T(8,128)(2,1)}) custom-call(bf16[64,2048]{1,0:T(8,128)(2,1)} %copy-done.39, bf16[64,2048]{1,0:T(8,128)(2,1)} %copy-done.40, bf16[2064,256]{1,0:T(8,128)(2,1)} %copy-done.14, bf16[2064,256]{1,0:T(8,128)(2,1)} %copy-done.15, bf16[2064,256]{1,0:T(8,128)(2,1)} %copy-done.16, ...), custom_call_target="tpu_custom_call" | custom-call | flops 2147483648 | bytes 16777216 | tf_op jit(solution)/shard_map/feed_forward/pallas_call | solution.py:556
  162.1 10.0 %feed_forward.4 = (bf16[64,2048]{1,0:T(8,128)(2,1)}, bf16[64,2048]{1,0:T(8,128)(2,1)}) custom-call(bf16[64,2048]{1,0:T(8,128)(2,1)} %copy-done.38, bf16[64,2048]{1,0:T(8,128)(2,1)} %collective-permute-done.21.refs_1_, bf16[2064,256]{1,0:T(8,128)(2,1)} %copy-done.14, bf16[2064,256]{1,0:T(8,128)(2,1)} %copy-done.15, bf16[2064,256]{1,0:T(8,128)(2,1)} %copy-done.16, ...), custom_call_target="tpu_custom_call" | custom-call | flops 2147483648 | bytes 16777216 | tf_op jit(solution)/shard_map/feed_forward/pallas_call | solution.py:556
  173.8 12.9 %feed_forward.5 = (bf16[128,2048]{1,0:T(8,128)(2,1)}, bf16[128,2048]{1,0:T(8,128)(2,1)}) custom-call(bf16[128,2048]{1,0:T(8,128)(2,1)} %copy-done.35, bf16[128,2048]{1,0:T(8,128)(2,1)} %copy-done, bf16[2064,256]{1,0:T(8,128)(2,1)} %copy-done.14, bf16[2064,256]{1,0:T(8,128)(2,1)} %copy-done.15, bf16[2064,256]{1,0:T(8,128)(2,1)} %copy-done.16, ...), custom_call_target="tpu_custom_call" | custom-call | flops 4294967296 | bytes 16777216 | tf_op jit(solution)/shard_map/feed_forward/pallas_call | solution.py:556
  187.4 2.9 %collective-permute-start.28 = (bf16[64,2048]{1,0:T(8,128)(2,1)S(1)}, bf16[64,2048]{1,0:T(8,128)(2,1)S(1)}, u32[]{:S(2)}, u32[]{:S(2)}) collective-permute-start(bf16[64,2048]{1,0:T(8,128)(2,1)S(1)} %add_convert_fusion), channel_id=1, source_target_pairs={{0,4},{1,5},{2,6},{3,7},{4,0},{5,1},{6,2},{7,3},{8,12},{9,13},{10,... | collective-permute-start | bytes 786440 | tf_op jit(solution)/shard_map/ppermute | solution.py:441
  190.3 11.2 %collective-permute-done.28.far_b_ref = bf16[64,2048]{1,0:T(8,128)(2,1)S(1)} collective-permute-done((bf16[64,2048]{1,0:T(8,128)(2,1)S(1)}, bf16[64,2048]{1,0:T(8,128)(2,1)S(1)}, u32[]{:S(2)}, u32[]{:S(2)}) %collective-permute-start.28) | collective-permute-done | bytes 262176 | tf_op jit(solution)/shard_map/ppermute | solution.py:441
  (153 shorter events, 36.1 us)
Async XLA Ops:
  2.3 38.4 %all-to-all-start = ((bf16[32,64,256]{2,1,0:T(8,128)(2,1)}), bf16[32,64,256]{2,1,0:T(8,128)(2,1)S(1)}, u32[]{:S(2)}, u32[]{:S(2)}) async-start(bf16[32,64,256]{2,1,0:T(8,128)(2,1)} %bitcast.20), calls=%async_computation | async-start | bytes 2097152 | tf_op jit(solution)/shard_map/all_to_all | solution.py:661
  9.8 30.9 %collective-permute-start.2 = (bf16[2064,256]{1,0:T(8,128)(2,1)S(1)}, bf16[2064,256]{1,0:T(8,128)(2,1)}, u32[]{:S(2)}, u32[]{:S(2)}) collective-permute-start(bf16[2064,256]{1,0:T(8,128)(2,1)S(1)} %pad_maximum_fusion.refs_2_), channel_id=1, source_target_pairs={{0,8},{1,9},{2,10},{3,11},{4,12},{5,13},{6,14},{7,15},{8,0},{9,1},... | collective-permute-start | bytes 3170312 | tf_op jit(solution)/shard_map/ppermute | solution.py:441
  10.1 30.6 %collective-permute-start.3 = (bf16[256,2048]{1,0:T(8,128)(2,1)}, bf16[256,2048]{1,0:T(8,128)(2,1)}, u32[]{:S(2)}, u32[]{:S(2)}) collective-permute-start(bf16[256,2048]{1,0:T(8,128)(2,1)} %refs_10_.5), channel_id=1, source_target_pairs={{0,8},{1,9},{2,10},{3,11},{4,12},{5,13},{6,14},{7,15},{8,0},{9,1},... | collective-permute-start | bytes 3145736 | tf_op jit(solution)/shard_map/ppermute | solution.py:441
  11.2 29.5 %collective-permute-start.1 = (bf16[1024,256]{1,0:T(8,128)(2,1)}, bf16[1024,256]{1,0:T(8,128)(2,1)}, u32[]{:S(2)}, u32[]{:S(2)}) collective-permute-start(bf16[1024,256]{1,0:T(8,128)(2,1)} %slice.15), channel_id=1, source_target_pairs={{0,2},{1,3},{2,0},{3,1},{4,6},{5,7},{6,4},{7,5},{8,10},{9,11},{10,... | collective-permute-start | bytes 1572872 | tf_op jit(solution)/shard_map/ppermute | solution.py:441
  13.0 27.7 %collective-permute-start = (bf16[1024,256]{1,0:T(8,128)(2,1)}, bf16[1024,256]{1,0:T(8,128)(2,1)}, u32[]{:S(2)}, u32[]{:S(2)}) collective-permute-start(bf16[1024,256]{1,0:T(8,128)(2,1)} %slice.15), channel_id=1, source_target_pairs={{0,1},{1,0},{2,3},{3,2},{4,5},{5,4},{6,7},{7,6},{8,9},{9,8},{10,11... | collective-permute-start | bytes 1572872 | tf_op jit(solution)/shard_map/ppermute | solution.py:441
  40.7 24.6 %collective-permute-start.7 = (bf16[128,2048]{1,0:T(8,128)(2,1)}, bf16[128,2048]{1,0:T(8,128)(2,1)S(1)}, u32[]{:S(2)}, u32[]{:S(2)}) collective-permute-start(bf16[128,2048]{1,0:T(8,128)(2,1)} %get-tuple-element.75), channel_id=1, source_target_pairs={{0,2},{1,3},{2,0},{3,1},{4,6},{5,7},{6,4},{7,5},{8,10},{9,11},{10,... | collective-permute-start | bytes 1572872 | tf_op jit(solution)/shard_map/ppermute | solution.py:441
  41.1 24.2 %collective-permute-start.6 = (bf16[128,2048]{1,0:T(8,128)(2,1)}, bf16[128,2048]{1,0:T(8,128)(2,1)S(1)}, u32[]{:S(2)}, u32[]{:S(2)}) collective-permute-start(bf16[128,2048]{1,0:T(8,128)(2,1)} %get-tuple-element.75), channel_id=1, source_target_pairs={{0,1},{1,0},{2,3},{3,2},{4,5},{5,4},{6,7},{7,6},{8,9},{9,8},{10,11... | collective-permute-start | bytes 1572872 | tf_op jit(solution)/shard_map/ppermute | solution.py:441
  42.8 23.3 %collective-permute-start.5 = (bf16[1040,256]{1,0:T(8,128)(2,1)}, bf16[1040,256]{1,0:T(8,128)(2,1)}, u32[]{:S(2)}, u32[]{:S(2)}) collective-permute-start(bf16[1040,256]{1,0:T(8,128)(2,1)} %fusion), channel_id=1, source_target_pairs={{0,2},{1,3},{2,0},{3,1},{4,6},{5,7},{6,4},{7,5},{8,10},{9,11},{10,... | collective-permute-start | bytes 1597448 | tf_op jit(solution)/shard_map/ppermute | solution.py:441
  44.3 21.9 %collective-permute-start.4 = (bf16[1040,256]{1,0:T(8,128)(2,1)}, bf16[1040,256]{1,0:T(8,128)(2,1)S(1)}, u32[]{:S(2)}, u32[]{:S(2)}) collective-permute-start(bf16[1040,256]{1,0:T(8,128)(2,1)} %fusion), channel_id=1, source_target_pairs={{0,1},{1,0},{2,3},{3,2},{4,5},{5,4},{6,7},{7,6},{8,9},{9,8},{10,11... | collective-permute-start | bytes 1597448 | tf_op jit(solution)/shard_map/ppermute | solution.py:441
  67.0 45.1 %all-to-all-start.1 = ((bf16[32,72,256]{2,1,0:T(8,128)(2,1)}), bf16[32,72,256]{2,1,0:T(8,128)(2,1)S(1)}, u32[]{:S(2)}, u32[]{:S(2)}) async-start(bf16[32,72,256]{2,1,0:T(8,128)(2,1)} %attend_prefix.1), calls=%async_computation.1 | async-start | bytes 2359296 | tf_op jit(solution)/shard_map/all_to_all | solution.py:730
  75.0 30.6 %collective-permute-start.12 = (bf16[128,2048]{1,0:T(8,128)(2,1)S(1)}, bf16[128,2048]{1,0:T(8,128)(2,1)S(1)}, u32[]{:S(2)}, u32[]{:S(2)}) collective-permute-start(bf16[128,2048]{1,0:T(8,128)(2,1)S(1)} %copy-done.31), channel_id=1, source_target_pairs={{0,2},{1,3},{2,0},{3,1},{4,6},{5,7},{6,4},{7,5},{8,10},{9,11},{10,... | collective-permute-start | bytes 1572872 | tf_op jit(solution)/shard_map/ppermute | solution.py:441
  77.9 31.2 %collective-permute-start.9 = (bf16[2064,256]{1,0:T(8,128)(2,1)S(1)}, bf16[2064,256]{1,0:T(8,128)(2,1)S(1)}, u32[]{:S(2)}, u32[]{:S(2)}) collective-permute-start(bf16[2064,256]{1,0:T(8,128)(2,1)S(1)} %constant_dynamic-update-slice_fusion.refs_4_), channel_id=1, source_target_pairs={{0,8},{1,9},{2,10},{3,11},{4,12},{5,13},{6,14},{7,15},{8,0},{9,1},... | collective-permute-start | bytes 3170312 | tf_op jit(solution)/shard_map/ppermute | solution.py:441
  78.0 33.1 %collective-permute-start.8 = (bf16[2064,256]{1,0:T(8,128)(2,1)S(1)}, bf16[2064,256]{1,0:T(8,128)(2,1)S(1)}, u32[]{:S(2)}, u32[]{:S(2)}) collective-permute-start(bf16[2064,256]{1,0:T(8,128)(2,1)S(1)} %constant_dynamic-update-slice_fusion.refs_4_), channel_id=1, source_target_pairs={{0,1},{1,0},{2,3},{3,2},{4,5},{5,4},{6,7},{7,6},{8,9},{9,8},{10,11... | collective-permute-start | bytes 3170312 | tf_op jit(solution)/shard_map/ppermute | solution.py:441
  79.6 29.6 %collective-permute-start.10 = (bf16[2064,256]{1,0:T(8,128)(2,1)S(1)}, bf16[2064,256]{1,0:T(8,128)(2,1)S(1)}, u32[]{:S(2)}, u32[]{:S(2)}) collective-permute-start(bf16[2064,256]{1,0:T(8,128)(2,1)S(1)} %constant_dynamic-update-slice_fusion.2.refs_3_), channel_id=1, source_target_pairs={{0,8},{1,9},{2,10},{3,11},{4,12},{5,13},{6,14},{7,15},{8,0},{9,1},... | collective-permute-start | bytes 3170312 | tf_op jit(solution)/shard_map/ppermute | solution.py:441
  114.1 32.1 %collective-permute-start.18 = (bf16[2064,256]{1,0:T(8,128)(2,1)S(1)}, bf16[2064,256]{1,0:T(8,128)(2,1)S(1)}, u32[]{:S(2)}, u32[]{:S(2)}) collective-permute-start(bf16[2064,256]{1,0:T(8,128)(2,1)S(1)} %copy-done.20), channel_id=1, source_target_pairs={{0,8},{1,9},{2,10},{3,11},{4,12},{5,13},{6,14},{7,15},{8,0},{9,1},... | collective-permute-start | bytes 3170312 | tf_op jit(solution)/shard_map/ppermute | solution.py:441
  114.2 32.0 %collective-permute-start.19 = (bf16[256,2048]{1,0:T(8,128)(2,1)S(1)}, bf16[256,2048]{1,0:T(8,128)(2,1)S(1)}, u32[]{:S(2)}, u32[]{:S(2)}) collective-permute-start(bf16[256,2048]{1,0:T(8,128)(2,1)S(1)} %copy-done.32), channel_id=1, source_target_pairs={{0,1},{1,0},{2,3},{3,2},{4,5},{5,4},{6,7},{7,6},{8,9},{9,8},{10,11... | collective-permute-start | bytes 3145736 | tf_op jit(solution)/shard_map/ppermute | solution.py:441
  115.2 16.2 %collective-permute-start.17 = (bf16[128,2048]{1,0:T(8,128)(2,1)S(1)}, bf16[128,2048]{1,0:T(8,128)(2,1)S(1)}, u32[]{:S(2)}, u32[]{:S(2)}) collective-permute-start(bf16[128,2048]{1,0:T(8,128)(2,1)S(1)} %get-tuple-element.123.refs_1_.hidden_ref), channel_id=1, source_target_pairs={{0,16},{1,17},{2,18},{3,19},{4,20},{5,21},{6,22},{7,23},{8,24},{9,... | collective-permute-start | bytes 1572872 | tf_op jit(solution)/shard_map/ppermute | solution.py:441
  116.7 14.7 %collective-permute-start.14 = (bf16[64,2048]{1,0:T(8,128)(2,1)S(1)}, bf16[64,2048]{1,0:T(8,128)(2,1)S(1)}, u32[]{:S(2)}, u32[]{:S(2)}) collective-permute-start(bf16[64,2048]{1,0:T(8,128)(2,1)S(1)} %get-tuple-element.96), channel_id=1, source_target_pairs={{0,4},{1,5},{2,6},{3,7},{4,0},{5,1},{6,2},{7,3},{8,12},{9,13},{10,... | collective-permute-start | bytes 786440 | tf_op jit(solution)/shard_map/ppermute | solution.py:441
  119.4 21.0 %collective-permute-start.20 = (bf16[128,2048]{1,0:T(8,128)(2,1)S(1)}, bf16[128,2048]{1,0:T(8,128)(2,1)S(1)}, u32[]{:S(2)}, u32[]{:S(2)}) collective-permute-start(bf16[128,2048]{1,0:T(8,128)(2,1)S(1)} %collective-permute-done.6.refs_11_), channel_id=1, source_target_pairs={{0,2},{1,3},{2,0},{3,1},{4,6},{5,7},{6,4},{7,5},{8,10},{9,11},{10,... | collective-permute-start | bytes 1572872 | tf_op jit(solution)/shard_map/ppermute | solution.py:441
  131.4 14.7 %collective-permute-start.15 = (bf16[64,2048]{1,0:T(8,128)(2,1)S(1)}, bf16[64,2048]{1,0:T(8,128)(2,1)S(1)}, u32[]{:S(2)}, u32[]{:S(2)}) collective-permute-start(bf16[64,2048]{1,0:T(8,128)(2,1)S(1)} %get-tuple-element.97), channel_id=1, source_target_pairs={{0,4},{1,5},{2,6},{3,7},{4,0},{5,1},{6,2},{7,3},{8,12},{9,13},{10,... | collective-permute-start | bytes 786440 | tf_op jit(solution)/shard_map/ppermute | solution.py:441
  131.4 14.7 %collective-permute-start.16 = (bf16[64,2048]{1,0:T(8,128)(2,1)S(1)}, bf16[64,2048]{1,0:T(8,128)(2,1)S(1)}, u32[]{:S(2)}, u32[]{:S(2)}) collective-permute-start(bf16[64,2048]{1,0:T(8,128)(2,1)S(1)} %collective-permute-done.14.refs_0_), channel_id=1, source_target_pairs={{0,16},{1,17},{2,18},{3,19},{4,20},{5,21},{6,22},{7,23},{8,24},{9,... | collective-permute-start | bytes 786440 | tf_op jit(solution)/shard_map/ppermute | solution.py:441
  172.2 15.2 %collective-permute-start.27 = (bf16[64,2048]{1,0:T(8,128)(2,1)S(1)}, bf16[64,2048]{1,0:T(8,128)(2,1)S(1)}, u32[]{:S(2)}, u32[]{:S(2)}) collective-permute-start(bf16[64,2048]{1,0:T(8,128)(2,1)S(1)} %add_convert_fusion.1), channel_id=1, source_target_pairs={{0,4},{1,5},{2,6},{3,7},{4,0},{5,1},{6,2},{7,3},{8,12},{9,13},{10,... | collective-permute-start | bytes 786440 | tf_op jit(solution)/shard_map/ppermute | solution.py:441
  172.3 15.1 %collective-permute-start.26 = (bf16[64,2048]{1,0:T(8,128)(2,1)}, bf16[64,2048]{1,0:T(8,128)(2,1)S(1)}, u32[]{:S(2)}, u32[]{:S(2)}) collective-permute-start(bf16[64,2048]{1,0:T(8,128)(2,1)} %get-tuple-element.127), channel_id=1, source_target_pairs={{0,16},{1,17},{2,18},{3,19},{4,20},{5,21},{6,22},{7,23},{8,24},{9,... | collective-permute-start | bytes 786440 | tf_op jit(solution)/shard_map/ppermute | solution.py:441
  186.8 14.8 %collective-permute-start.25 = (bf16[128,2048]{1,0:T(8,128)(2,1)}, bf16[128,2048]{1,0:T(8,128)(2,1)S(1)}, u32[]{:S(2)}, u32[]{:S(2)}) collective-permute-start(bf16[128,2048]{1,0:T(8,128)(2,1)} %get-tuple-element.126), channel_id=1, source_target_pairs={{0,16},{1,17},{2,18},{3,19},{4,20},{5,21},{6,22},{7,23},{8,24},{9,... | collective-permute-start | bytes 1572872 | tf_op jit(solution)/shard_map/ppermute | solution.py:441
  (51 other events, 505.9 us)

commit v14 on v13

--- a/solution.py
+++ b/solution.py
@@ -11,7 +11,7 @@
 HD = 128
 LANES = 128
 STAT_ROWS = 8
-STREAMS = 4
+STREAMS = 1
 FETCHES = 8
 UNROLL = 4
 EMPTY = 64.0
@@ -505,7 +505,7 @@
                 )
             begin += height
         copies.append(held)
-    for held in copies:
+    for held in copies[:parts]:
         for copy in held:
             copy.start()
     rows = jnp.concatenate([ref[...] for ref in row_refs], axis=0)
@@ -513,6 +513,10 @@
     for part in range(parts):
         for copy in copies[part]:
             copy.wait()
+        if part == 0:
+            for held in copies[parts:]:
+                for copy in held:
+                    copy.start()
         product = jnp.dot(
             rows, up_ref[part, :model_width, :], preferred_element_type=jnp.float32
         )
@@ -731,8 +735,8 @@
         answer_part, ("grp", "dev"), split_axis=0, concat_axis=0, tiled=True
     ).reshape(group_count, column_count, capacity + STAT_ROWS, part_width)
     up_high = jnp.concatenate([up_high_first, up_high_second], axis=0)
-    up_low = jnp.concatenate([up_low_first, up_low_second], axis=0)
     down_high_second = swap(down_second, high_mask)
+    up_low = jnp.concatenate(tie([up_low_first, up_low_second], down_high_second), axis=0)
     up_cross = swap(up_high, low_mask)
     up_high_core = swap(up_high, core_mask)
     up_low_core = swap(up_low, core_mask)

time: 205 us -> 205 us (level)
  Pallas kernels: 62.2 us -> 57.4 us
  waiting for transfers between devices: 71.3 us -> 74.1 us
    ppermute x29, waiting for transfers between devices: 71.3 us -> 74.1 us  [swap(): lax.ppermute(leaf, ('grp', 'dev'), pairs)]
    pallas_call x1, Pallas kernels: 19.3 us -> 16.7 us  [attend_prefix(): pl.pallas_call(far_kernel, out_shape=jax.ShapeDtypeStruct((sources, capac...]
    pallas_call x3, Pallas kernels: 32.8 us -> 30.7 us  [feed_forward(): pl.pallas_call(functools.partial(mlp_kernel, pieces, len(flat), up_plan,...]
    unnamed x93 -> x95, local copies, waits for them, and re-layouts: 16.1 us -> 17.7 us
  transfers between devices with their start and end apart: 31 -> 31, of which waited for: 9 -> 10; matrix products, arithmetic and copies ran while one was open for 13% -> 13% of each run, Pallas kernels for 28% -> 25%
where the time goes in v14:
time: 205 us; the launch traced here: 204 us
  waiting for transfers between devices  74.1 us (36%)
  Pallas kernels  57.4 us (28%)
  starting transfers between devices  38.7 us (19%)
  local copies, waits for them, and re-layouts  30 us (15%)
  other arithmetic  3.37 us (2%)
    ppermute x29, waiting for transfers between devices, swap(): lax.ppermute(leaf, ('grp', 'dev'), pairs)  74.1 us
    pallas_call x3, Pallas kernels, feed_forward(): pl.pallas_call(functools.partial(mlp_kernel, pieces, len(flat), up_plan,...  30.7 us
    ppermute x29, starting transfers between devices, swap(): lax.ppermute(leaf, ('grp', 'dev'), pairs)  25.7 us
    unnamed x95, local copies, waits for them, and re-layouts  17.7 us
    pallas_call x1, Pallas kernels, attend_prefix(): pl.pallas_call(far_kernel, out_shape=jax.ShapeDtypeStruct((sources, capac...  16.7 us
    all_to_all x1, starting transfers between devices, on_device(): lax.all_to_all(outgoing.reshape(sources, capacity, part_width), ('grp', '...  7.3 us
    all_to_all x1, starting transfers between devices, on_device(): lax.all_to_all(answer_part, ('grp', 'dev'), split_axis=0, concat_axis=0,...  5.75 us
    pallas_call x1, Pallas kernels, attend_suffix(): pl.pallas_call(functools.partial(own_kernel, local_heads), out_shape=(jax...  4.48 us
  transfers between devices with their start and end apart: 31, of which 10 were waited for; matrix products, arithmetic and copies ran while one was open for 13% of the time, Pallas kernels for 25%

profile of v14, /device:TPU:0, one launch (start us, length us, event | category | flops | bytes accessed | tf_op | source)
XLA Modules:
  0.0 204.3 jit_solution(16639002252472954825)
XLA Ops:
  0.0 2.3 %pack_queries.1 = bf16[4,8,64,256]{3,2,1,0:T(8,128)(2,1)} custom-call(s32[1,4]{1,0:T(1,128)} %lengths_ref.5, s32[1,4]{1,0:T(1,128)} %groups_ref.3, bf16[128,2048]{1,0:T(8,128)(2,1)} %query_ref.3), custom_call_target="tpu_custom_call" | custom-call | tf_op jit(solution)/shard_map/pack_queries/pallas_call | solution.py:76
  2.3 7.3 %all-to-all-start = ((bf16[32,64,256]{2,1,0:T(8,128)(2,1)}), bf16[32,64,256]{2,1,0:T(8,128)(2,1)S(1)}, u32[]{:S(2)}, u32[]{:S(2)}) async-start(bf16[32,64,256]{2,1,0:T(8,128)(2,1)} %bitcast.20), calls=%async_computation | async-start | bytes 2097152 | tf_op jit(solution)/shard_map/all_to_all | solution.py:665
  15.3 4.5 %attend_suffix.1 = (f32[128,2048]{1,0:T(8,128)S(1)}, f32[128,128]{1,0:T(8,128)S(1)}, f32[128,128]{1,0:T(8,128)S(1)}) custom-call(s32[1,4]{1,0:T(1,128)S(1)} %copy-done.10, bf16[128,2048]{1,0:T(8,128)(2,1)S(1)} %copy-done.3, bf16[128,2048]{1,0:T(8,128)(2,1)S(1)} %copy-done.12, bf16[128,2048]{1,0:T(8,128)(2,1)S(1)} %copy-done.13), custom_call_target="tpu_custom_call" | custom-call | flops 1342177280 | bytes 2097152 | tf_op jit(solution)/shard_map/attend_suffix/pallas_call | solution.py:320
  19.8 4.1 %copy.18 = bf16[1,4096,256]{1,2,0:T(8,128)(2,1)} copy(bf16[1,4096,256]{2,1,0:T(8,128)(2,1)} %param.22) | data formatting | bytes 4194304 | tf_op args[6]
  23.9 4.1 %copy.19 = bf16[1,4096,256]{1,2,0:T(8,128)(2,1)} copy(bf16[1,4096,256]{2,1,0:T(8,128)(2,1)} %param.23) | data formatting | bytes 4194304 | tf_op args[7]
  28.0 4.1 %copy.20 = bf16[4096,2,128]{2,0,1:T(8,128)(2,1)} copy(bf16[4096,2,128]{0,2,1:T(8,128)(2,1)} %bitcast.19) | data formatting | bytes 4194304 | tf_op jit(solution)/shard_map/reshape;squeeze | solution.py:677
  32.1 3.9 %concatenate.19.values_hbm = bf16[2,4096,256]{2,1,0:T(8,128)(2,1)} pad(bf16[2,4096,128]{2,1,0:T(8,128)(2,1)} %bitcast.18, bf16[]{:T(256)} %constant.0.clone.1), padding=0_0x0_0x0_128 | pad | bytes 6291458 | tf_op jit(solution)/shard_map/concatenate | solution.py:678
  36.1 2.3 %fusion.1 = (bf16[128,2048]{1,0:T(8,128)(2,1)}, bf16[128,2048]{1,0:T(8,128)(2,1)}) fusion(bf16[256,2048]{1,0:T(8,128)(2,1)} %refs_10_.5), kind=kLoop, calls=%fused_computation.14 | loop fusion | bytes 2097152 | tf_op jit(solution)/shard_map/slice | solution.py:662
  38.3 2.3 %collective-permute-done.1 = bf16[1024,256]{1,0:T(8,128)(2,1)} collective-permute-done((bf16[1024,256]{1,0:T(8,128)(2,1)}, bf16[1024,256]{1,0:T(8,128)(2,1)}, u32[]{:S(2)}, u32[]{:S(2)}) %collective-permute-start.1) | collective-permute-done | bytes 524320 | tf_op jit(solution)/shard_map/ppermute | solution.py:441
  46.0 16.7 %attend_prefix.1 = bf16[32,72,256]{2,1,0:T(8,128)(2,1)} custom-call(s32[32]{0:T(128)} %convert_reduce_fusion.counts_ref, bf16[32,64,256]{2,1,0:T(8,128)(2,1)} %copy-done.30, bf16[256,4096]{1,0:T(8,128)(2,1)} %bitcast.21, bf16[2,4096,256]{2,1,0:T(8,128)(2,1)} %concatenate.19.values_hbm), custom_call_target="tpu_custom_call" | custom-call | flops 8589934592 | bytes 8388608 | tf_op jit(solution)/shard_map/attend_prefix/pallas_call | solution.py:246
  63.5 2.4 %collective-permute-done.5 = bf16[1040,256]{1,0:T(8,128)(2,1)} collective-permute-done((bf16[1040,256]{1,0:T(8,128)(2,1)}, bf16[1040,256]{1,0:T(8,128)(2,1)}, u32[]{:S(2)}, u32[]{:S(2)}) %collective-permute-start.5) | collective-permute-done | bytes 532512 | tf_op jit(solution)/shard_map/ppermute | solution.py:441
  66.9 5.7 %all-to-all-start.1 = ((bf16[32,72,256]{2,1,0:T(8,128)(2,1)}), bf16[32,72,256]{2,1,0:T(8,128)(2,1)S(1)}, u32[]{:S(2)}, u32[]{:S(2)}) async-start(bf16[32,72,256]{2,1,0:T(8,128)(2,1)} %attend_prefix.1), calls=%async_computation.1 | async-start | bytes 2359296 | tf_op jit(solution)/shard_map/all_to_all | solution.py:734
  78.4 27.2 %collective-permute-done.10 = bf16[128,2048]{1,0:T(8,128)(2,1)S(1)} collective-permute-done((bf16[128,2048]{1,0:T(8,128)(2,1)S(1)}, bf16[128,2048]{1,0:T(8,128)(2,1)S(1)}, u32[]{:S(2)}, u32[]{:S(2)}) %collective-permute-start.10) | collective-permute-done | bytes 524320 | tf_op jit(solution)/shard_map/ppermute | solution.py:441
  109.0 2.7 %collective-permute-done.12.refs_16_ = bf16[128,2048]{1,0:T(8,128)(2,1)S(1)} collective-permute-done((bf16[128,2048]{1,0:T(8,128)(2,1)S(1)}, bf16[128,2048]{1,0:T(8,128)(2,1)S(1)}, u32[]{:S(2)}, u32[]{:S(2)}) %collective-permute-start.12) | collective-permute-done | bytes 524320 | tf_op jit(solution)/shard_map/ppermute | solution.py:441
  119.2 2.5 %collective-permute-start.14 = (bf16[64,2048]{1,0:T(8,128)(2,1)S(1)}, bf16[64,2048]{1,0:T(8,128)(2,1)S(1)}, u32[]{:S(2)}, u32[]{:S(2)}) collective-permute-start(bf16[64,2048]{1,0:T(8,128)(2,1)S(1)} %get-tuple-element.100), channel_id=1, source_target_pairs={{0,4},{1,5},{2,6},{3,7},{4,0},{5,1},{6,2},{7,3},{8,12},{9,13},{10,... | collective-permute-start | bytes 786440 | tf_op jit(solution)/shard_map/ppermute | solution.py:441
  122.2 11.7 %collective-permute-done.14.refs_0_ = bf16[64,2048]{1,0:T(8,128)(2,1)S(1)} collective-permute-done((bf16[64,2048]{1,0:T(8,128)(2,1)S(1)}, bf16[64,2048]{1,0:T(8,128)(2,1)S(1)}, u32[]{:S(2)}, u32[]{:S(2)}) %collective-permute-start.14) | collective-permute-done | bytes 262176 | tf_op jit(solution)/shard_map/ppermute | solution.py:441
  134.5 8.3 %collective-permute-done.20.refs_14_ = bf16[128,2048]{1,0:T(8,128)(2,1)S(1)} collective-permute-done((bf16[128,2048]{1,0:T(8,128)(2,1)S(1)}, bf16[128,2048]{1,0:T(8,128)(2,1)S(1)}, u32[]{:S(2)}, u32[]{:S(2)}) %collective-permute-start.20) | collective-permute-done | bytes 524320 | tf_op jit(solution)/shard_map/ppermute | solution.py:441
  142.8 5.8 %collective-permute-done.15.refs_0_ = bf16[64,2048]{1,0:T(8,128)(2,1)S(1)} collective-permute-done((bf16[64,2048]{1,0:T(8,128)(2,1)S(1)}, bf16[64,2048]{1,0:T(8,128)(2,1)S(1)}, u32[]{:S(2)}, u32[]{:S(2)}) %collective-permute-start.15) | collective-permute-done | bytes 262176 | tf_op jit(solution)/shard_map/ppermute | solution.py:441
  149.7 2.3 %collective-permute-done.23.refs_19_ = bf16[128,2048]{1,0:T(8,128)(2,1)S(1)} collective-permute-done((bf16[128,2048]{1,0:T(8,128)(2,1)S(1)}, bf16[128,2048]{1,0:T(8,128)(2,1)S(1)}, u32[]{:S(2)}, u32[]{:S(2)}) %collective-permute-start.23) | collective-permute-done | bytes 524320 | tf_op jit(solution)/shard_map/ppermute | solution.py:441
  153.9 9.3 %feed_forward.3 = (bf16[64,2048]{1,0:T(8,128)(2,1)}, bf16[64,2048]{1,0:T(8,128)(2,1)}) custom-call(bf16[64,2048]{1,0:T(8,128)(2,1)} %copy-done.40, bf16[64,2048]{1,0:T(8,128)(2,1)} %copy-done.41, bf16[2064,256]{1,0:T(8,128)(2,1)} %copy-done.14, bf16[2064,256]{1,0:T(8,128)(2,1)} %copy-done.16, bf16[2064,256]{1,0:T(8,128)(2,1)} %copy-done.15, ...), custom_call_target="tpu_custom_call" | custom-call | flops 2147483648 | bytes 16777216 | tf_op jit(solution)/shard_map/feed_forward/pallas_call | solution.py:560
  163.9 9.3 %feed_forward.4 = (bf16[64,2048]{1,0:T(8,128)(2,1)}, bf16[64,2048]{1,0:T(8,128)(2,1)}) custom-call(bf16[64,2048]{1,0:T(8,128)(2,1)} %copy-done.39, bf16[64,2048]{1,0:T(8,128)(2,1)} %collective-permute-done.21.refs_1_, bf16[2064,256]{1,0:T(8,128)(2,1)} %copy-done.14, bf16[2064,256]{1,0:T(8,128)(2,1)} %copy-done.16, bf16[2064,256]{1,0:T(8,128)(2,1)} %copy-done.15, ...), custom_call_target="tpu_custom_call" | custom-call | flops 2147483648 | bytes 16777216 | tf_op jit(solution)/shard_map/feed_forward/pallas_call | solution.py:560
  175.0 12.0 %feed_forward.5 = (bf16[128,2048]{1,0:T(8,128)(2,1)}, bf16[128,2048]{1,0:T(8,128)(2,1)}) custom-call(bf16[128,2048]{1,0:T(8,128)(2,1)} %copy-done.36, bf16[128,2048]{1,0:T(8,128)(2,1)} %copy-done, bf16[2064,256]{1,0:T(8,128)(2,1)} %copy-done.14, bf16[2064,256]{1,0:T(8,128)(2,1)} %copy-done.16, bf16[2064,256]{1,0:T(8,128)(2,1)} %copy-done.15, ...), custom_call_target="tpu_custom_call" | custom-call | flops 4294967296 | bytes 16777216 | tf_op jit(solution)/shard_map/feed_forward/pallas_call | solution.py:560
  187.7 2.9 %collective-permute-start.28 = (bf16[64,2048]{1,0:T(8,128)(2,1)S(1)}, bf16[64,2048]{1,0:T(8,128)(2,1)S(1)}, u32[]{:S(2)}, u32[]{:S(2)}) collective-permute-start(bf16[64,2048]{1,0:T(8,128)(2,1)S(1)} %add_convert_fusion), channel_id=1, source_target_pairs={{0,4},{1,5},{2,6},{3,7},{4,0},{5,1},{6,2},{7,3},{8,12},{9,13},{10,... | collective-permute-start | bytes 786440 | tf_op jit(solution)/shard_map/ppermute | solution.py:441
  190.6 11.2 %collective-permute-done.28.far_b_ref = bf16[64,2048]{1,0:T(8,128)(2,1)S(1)} collective-permute-done((bf16[64,2048]{1,0:T(8,128)(2,1)S(1)}, bf16[64,2048]{1,0:T(8,128)(2,1)S(1)}, u32[]{:S(2)}, u32[]{:S(2)}) %collective-permute-start.28) | collective-permute-done | bytes 262176 | tf_op jit(solution)/shard_map/ppermute | solution.py:441
  (155 shorter events, 38.6 us)
Async XLA Ops:
  2.3 38.4 %all-to-all-start = ((bf16[32,64,256]{2,1,0:T(8,128)(2,1)}), bf16[32,64,256]{2,1,0:T(8,128)(2,1)S(1)}, u32[]{:S(2)}, u32[]{:S(2)}) async-start(bf16[32,64,256]{2,1,0:T(8,128)(2,1)} %bitcast.20), calls=%async_computation | async-start | bytes 2097152 | tf_op jit(solution)/shard_map/all_to_all | solution.py:665
  9.8 30.9 %collective-permute-start.2 = (bf16[2064,256]{1,0:T(8,128)(2,1)S(1)}, bf16[2064,256]{1,0:T(8,128)(2,1)}, u32[]{:S(2)}, u32[]{:S(2)}) collective-permute-start(bf16[2064,256]{1,0:T(8,128)(2,1)S(1)} %pad_maximum_fusion.refs_2_), channel_id=1, source_target_pairs={{0,8},{1,9},{2,10},{3,11},{4,12},{5,13},{6,14},{7,15},{8,0},{9,1},... | collective-permute-start | bytes 3170312 | tf_op jit(solution)/shard_map/ppermute | solution.py:441
  10.1 30.6 %collective-permute-start.3 = (bf16[256,2048]{1,0:T(8,128)(2,1)}, bf16[256,2048]{1,0:T(8,128)(2,1)}, u32[]{:S(2)}, u32[]{:S(2)}) collective-permute-start(bf16[256,2048]{1,0:T(8,128)(2,1)} %refs_10_.5), channel_id=1, source_target_pairs={{0,8},{1,9},{2,10},{3,11},{4,12},{5,13},{6,14},{7,15},{8,0},{9,1},... | collective-permute-start | bytes 3145736 | tf_op jit(solution)/shard_map/ppermute | solution.py:441
  11.2 29.5 %collective-permute-start.1 = (bf16[1024,256]{1,0:T(8,128)(2,1)}, bf16[1024,256]{1,0:T(8,128)(2,1)}, u32[]{:S(2)}, u32[]{:S(2)}) collective-permute-start(bf16[1024,256]{1,0:T(8,128)(2,1)} %slice.15), channel_id=1, source_target_pairs={{0,2},{1,3},{2,0},{3,1},{4,6},{5,7},{6,4},{7,5},{8,10},{9,11},{10,... | collective-permute-start | bytes 1572872 | tf_op jit(solution)/shard_map/ppermute | solution.py:441
  13.0 27.7 %collective-permute-start = (bf16[1024,256]{1,0:T(8,128)(2,1)}, bf16[1024,256]{1,0:T(8,128)(2,1)}, u32[]{:S(2)}, u32[]{:S(2)}) collective-permute-start(bf16[1024,256]{1,0:T(8,128)(2,1)} %slice.15), channel_id=1, source_target_pairs={{0,1},{1,0},{2,3},{3,2},{4,5},{5,4},{6,7},{7,6},{8,9},{9,8},{10,11... | collective-permute-start | bytes 1572872 | tf_op jit(solution)/shard_map/ppermute | solution.py:441
  40.7 22.0 %collective-permute-start.7 = (bf16[128,2048]{1,0:T(8,128)(2,1)}, bf16[128,2048]{1,0:T(8,128)(2,1)S(1)}, u32[]{:S(2)}, u32[]{:S(2)}) collective-permute-start(bf16[128,2048]{1,0:T(8,128)(2,1)} %get-tuple-element.77), channel_id=1, source_target_pairs={{0,2},{1,3},{2,0},{3,1},{4,6},{5,7},{6,4},{7,5},{8,10},{9,11},{10,... | collective-permute-start | bytes 1572872 | tf_op jit(solution)/shard_map/ppermute | solution.py:441
  41.1 21.6 %collective-permute-start.6 = (bf16[128,2048]{1,0:T(8,128)(2,1)}, bf16[128,2048]{1,0:T(8,128)(2,1)S(1)}, u32[]{:S(2)}, u32[]{:S(2)}) collective-permute-start(bf16[128,2048]{1,0:T(8,128)(2,1)} %get-tuple-element.77), channel_id=1, source_target_pairs={{0,1},{1,0},{2,3},{3,2},{4,5},{5,4},{6,7},{7,6},{8,9},{9,8},{10,11... | collective-permute-start | bytes 1572872 | tf_op jit(solution)/shard_map/ppermute | solution.py:441
  42.8 23.1 %collective-permute-start.5 = (bf16[1040,256]{1,0:T(8,128)(2,1)}, bf16[1040,256]{1,0:T(8,128)(2,1)}, u32[]{:S(2)}, u32[]{:S(2)}) collective-permute-start(bf16[1040,256]{1,0:T(8,128)(2,1)} %fusion), channel_id=1, source_target_pairs={{0,2},{1,3},{2,0},{3,1},{4,6},{5,7},{6,4},{7,5},{8,10},{9,11},{10,... | collective-permute-start | bytes 1597448 | tf_op jit(solution)/shard_map/ppermute | solution.py:441
  44.3 21.8 %collective-permute-start.4 = (bf16[1040,256]{1,0:T(8,128)(2,1)}, bf16[1040,256]{1,0:T(8,128)(2,1)S(1)}, u32[]{:S(2)}, u32[]{:S(2)}) collective-permute-start(bf16[1040,256]{1,0:T(8,128)(2,1)} %fusion), channel_id=1, source_target_pairs={{0,1},{1,0},{2,3},{3,2},{4,5},{5,4},{6,7},{7,6},{8,9},{9,8},{10,11... | collective-permute-start | bytes 1597448 | tf_op jit(solution)/shard_map/ppermute | solution.py:441
  66.9 47.2 %all-to-all-start.1 = ((bf16[32,72,256]{2,1,0:T(8,128)(2,1)}), bf16[32,72,256]{2,1,0:T(8,128)(2,1)S(1)}, u32[]{:S(2)}, u32[]{:S(2)}) async-start(bf16[32,72,256]{2,1,0:T(8,128)(2,1)} %attend_prefix.1), calls=%async_computation.1 | async-start | bytes 2359296 | tf_op jit(solution)/shard_map/all_to_all | solution.py:734
  72.7 32.9 %collective-permute-start.10 = (bf16[128,2048]{1,0:T(8,128)(2,1)S(1)}, bf16[128,2048]{1,0:T(8,128)(2,1)S(1)}, u32[]{:S(2)}, u32[]{:S(2)}) collective-permute-start(bf16[128,2048]{1,0:T(8,128)(2,1)S(1)} %copy-done.31), channel_id=1, source_target_pairs={{0,2},{1,3},{2,0},{3,1},{4,6},{5,7},{6,4},{7,5},{8,10},{9,11},{10,... | collective-permute-start | bytes 1572872 | tf_op jit(solution)/shard_map/ppermute | solution.py:441
  76.7 35.0 %collective-permute-start.9 = (bf16[2064,256]{1,0:T(8,128)(2,1)S(1)}, bf16[2064,256]{1,0:T(8,128)(2,1)S(1)}, u32[]{:S(2)}, u32[]{:S(2)}) collective-permute-start(bf16[2064,256]{1,0:T(8,128)(2,1)S(1)} %constant_dynamic-update-slice_fusion.refs_4_), channel_id=1, source_target_pairs={{0,8},{1,9},{2,10},{3,11},{4,12},{5,13},{6,14},{7,15},{8,0},{9,1},... | collective-permute-start | bytes 3170312 | tf_op jit(solution)/shard_map/ppermute | solution.py:441
  76.8 34.9 %collective-permute-start.8 = (bf16[2064,256]{1,0:T(8,128)(2,1)S(1)}, bf16[2064,256]{1,0:T(8,128)(2,1)S(1)}, u32[]{:S(2)}, u32[]{:S(2)}) collective-permute-start(bf16[2064,256]{1,0:T(8,128)(2,1)S(1)} %constant_dynamic-update-slice_fusion.refs_4_), channel_id=1, source_target_pairs={{0,1},{1,0},{2,3},{3,2},{4,5},{5,4},{6,7},{7,6},{8,9},{9,8},{10,11... | collective-permute-start | bytes 3170312 | tf_op jit(solution)/shard_map/ppermute | solution.py:441
  116.1 32.5 %collective-permute-start.18 = (bf16[2064,256]{1,0:T(8,128)(2,1)S(1)}, bf16[2064,256]{1,0:T(8,128)(2,1)S(1)}, u32[]{:S(2)}, u32[]{:S(2)}) collective-permute-start(bf16[2064,256]{1,0:T(8,128)(2,1)S(1)} %copy-done.20), channel_id=1, source_target_pairs={{0,8},{1,9},{2,10},{3,11},{4,12},{5,13},{6,14},{7,15},{8,0},{9,1},... | collective-permute-start | bytes 3170312 | tf_op jit(solution)/shard_map/ppermute | solution.py:441
  116.3 32.3 %collective-permute-start.19 = (bf16[256,2048]{1,0:T(8,128)(2,1)S(1)}, bf16[256,2048]{1,0:T(8,128)(2,1)S(1)}, u32[]{:S(2)}, u32[]{:S(2)}) collective-permute-start(bf16[256,2048]{1,0:T(8,128)(2,1)S(1)} %copy-done.33), channel_id=1, source_target_pairs={{0,1},{1,0},{2,3},{3,2},{4,5},{5,4},{6,7},{7,6},{8,9},{9,8},{10,11... | collective-permute-start | bytes 3145736 | tf_op jit(solution)/shard_map/ppermute | solution.py:441
  117.8 16.1 %collective-permute-start.17 = (bf16[128,2048]{1,0:T(8,128)(2,1)S(1)}, bf16[128,2048]{1,0:T(8,128)(2,1)S(1)}, u32[]{:S(2)}, u32[]{:S(2)}) collective-permute-start(bf16[128,2048]{1,0:T(8,128)(2,1)S(1)} %get-tuple-element.127.refs_1_.hidden_ref), channel_id=1, source_target_pairs={{0,16},{1,17},{2,18},{3,19},{4,20},{5,21},{6,22},{7,23},{8,24},{9,... | collective-permute-start | bytes 1572872 | tf_op jit(solution)/shard_map/ppermute | solution.py:441
  119.2 14.6 %collective-permute-start.14 = (bf16[64,2048]{1,0:T(8,128)(2,1)S(1)}, bf16[64,2048]{1,0:T(8,128)(2,1)S(1)}, u32[]{:S(2)}, u32[]{:S(2)}) collective-permute-start(bf16[64,2048]{1,0:T(8,128)(2,1)S(1)} %get-tuple-element.100), channel_id=1, source_target_pairs={{0,4},{1,5},{2,6},{3,7},{4,0},{5,1},{6,2},{7,3},{8,12},{9,13},{10,... | collective-permute-start | bytes 786440 | tf_op jit(solution)/shard_map/ppermute | solution.py:441
  121.7 21.1 %collective-permute-start.20 = (bf16[128,2048]{1,0:T(8,128)(2,1)S(1)}, bf16[128,2048]{1,0:T(8,128)(2,1)S(1)}, u32[]{:S(2)}, u32[]{:S(2)}) collective-permute-start(bf16[128,2048]{1,0:T(8,128)(2,1)S(1)} %collective-permute-done.6.refs_11_), channel_id=1, source_target_pairs={{0,2},{1,3},{2,0},{3,1},{4,6},{5,7},{6,4},{7,5},{8,10},{9,11},{10,... | collective-permute-start | bytes 1572872 | tf_op jit(solution)/shard_map/ppermute | solution.py:441
  133.9 14.7 %collective-permute-start.15 = (bf16[64,2048]{1,0:T(8,128)(2,1)S(1)}, bf16[64,2048]{1,0:T(8,128)(2,1)S(1)}, u32[]{:S(2)}, u32[]{:S(2)}) collective-permute-start(bf16[64,2048]{1,0:T(8,128)(2,1)S(1)} %get-tuple-element.101), channel_id=1, source_target_pairs={{0,4},{1,5},{2,6},{3,7},{4,0},{5,1},{6,2},{7,3},{8,12},{9,13},{10,... | collective-permute-start | bytes 786440 | tf_op jit(solution)/shard_map/ppermute | solution.py:441
  133.9 14.7 %collective-permute-start.16 = (bf16[64,2048]{1,0:T(8,128)(2,1)S(1)}, bf16[64,2048]{1,0:T(8,128)(2,1)S(1)}, u32[]{:S(2)}, u32[]{:S(2)}) collective-permute-start(bf16[64,2048]{1,0:T(8,128)(2,1)S(1)} %collective-permute-done.14.refs_0_), channel_id=1, source_target_pairs={{0,16},{1,17},{2,18},{3,19},{4,20},{5,21},{6,22},{7,23},{8,24},{9,... | collective-permute-start | bytes 786440 | tf_op jit(solution)/shard_map/ppermute | solution.py:441
  173.4 14.3 %collective-permute-start.27 = (bf16[64,2048]{1,0:T(8,128)(2,1)S(1)}, bf16[64,2048]{1,0:T(8,128)(2,1)S(1)}, u32[]{:S(2)}, u32[]{:S(2)}) collective-permute-start(bf16[64,2048]{1,0:T(8,128)(2,1)S(1)} %add_convert_fusion.1), channel_id=1, source_target_pairs={{0,4},{1,5},{2,6},{3,7},{4,0},{5,1},{6,2},{7,3},{8,12},{9,13},{10,... | collective-permute-start | bytes 786440 | tf_op jit(solution)/shard_map/ppermute | solution.py:441
  173.4 14.2 %collective-permute-start.26 = (bf16[64,2048]{1,0:T(8,128)(2,1)}, bf16[64,2048]{1,0:T(8,128)(2,1)S(1)}, u32[]{:S(2)}, u32[]{:S(2)}) collective-permute-start(bf16[64,2048]{1,0:T(8,128)(2,1)} %get-tuple-element.131), channel_id=1, source_target_pairs={{0,16},{1,17},{2,18},{3,19},{4,20},{5,21},{6,22},{7,23},{8,24},{9,... | collective-permute-start | bytes 786440 | tf_op jit(solution)/shard_map/ppermute | solution.py:441
  187.0 14.8 %collective-permute-start.25 = (bf16[128,2048]{1,0:T(8,128)(2,1)}, bf16[128,2048]{1,0:T(8,128)(2,1)S(1)}, u32[]{:S(2)}, u32[]{:S(2)}) collective-permute-start(bf16[128,2048]{1,0:T(8,128)(2,1)} %get-tuple-element.130), channel_id=1, source_target_pairs={{0,16},{1,17},{2,18},{3,19},{4,20},{5,21},{6,22},{7,23},{8,24},{9,... | collective-permute-start | bytes 1572872 | tf_op jit(solution)/shard_map/ppermute | solution.py:441
  187.7 14.1 %collective-permute-start.28 = (bf16[64,2048]{1,0:T(8,128)(2,1)S(1)}, bf16[64,2048]{1,0:T(8,128)(2,1)S(1)}, u32[]{:S(2)}, u32[]{:S(2)}) collective-permute-start(bf16[64,2048]{1,0:T(8,128)(2,1)S(1)} %add_convert_fusion), channel_id=1, source_target_pairs={{0,4},{1,5},{2,6},{3,7},{4,0},{5,1},{6,2},{7,3},{8,12},{9,13},{10,... | collective-permute-start | bytes 786440 | tf_op jit(solution)/shard_map/ppermute | solution.py:441
  (52 other events, 533.1 us)

commit v15 on v14

--- a/solution.py
+++ b/solution.py
@@ -741,6 +741,7 @@
     up_high_core = swap(up_high, core_mask)
     up_low_core = swap(up_low, core_mask)
     down_low_first_core = swap(down_low_first, core_mask)
+    down_cross_first = swap(tie(down_low_first, down_high_second), high_mask)
     down_high = jnp.concatenate([down_high_first, down_high_second], axis=0)
     down_high_core = swap(down_high, core_mask)
     down_late = jnp.concatenate([down_second, down_high_second], axis=0)
@@ -753,7 +754,7 @@
         down_high,
         down_high_core,
         down_late,
-        down_low_first,
+        down_cross_first,
     ) = lax.optimization_barrier(
         (
             answer,
@@ -764,7 +765,7 @@
             down_high,
             down_high_core,
             down_late,
-            down_low_first,
+            down_cross_first,
         )
     )
 
@@ -772,12 +773,11 @@
         suffix_lengths, request_group, answer, *own, layer_input, attn_gain, attn_shift
     )
 
-    (hidden_a, hidden_b, hidden), up_cross, down_late, down_low_first = lax.optimization_barrier(
-        ((hidden_a, hidden_b, hidden), up_cross, down_late, down_low_first)
+    (hidden_a, hidden_b, hidden), up_cross, down_late = lax.optimization_barrier(
+        ((hidden_a, hidden_b, hidden), up_cross, down_late)
     )
     far_a = swap(hidden_a, far_mask)
     down_late = swap(down_late, low_mask)
-    down_cross_first = swap(down_low_first, high_mask)
     far_b = swap(tie(hidden_b, far_a), far_mask)
     cross_a = swap(far_a, near_mask)
     near = swap(hidden, near_mask)

time: 205 us -> 216 us (1.054)
  waiting for transfers between devices: 74.1 us -> 80.9 us
  starting transfers between devices: 38.7 us -> 43 us
    ppermute x29, waiting for transfers between devices: 74.1 us -> 80.9 us  [swap(): lax.ppermute(leaf, ('grp', 'dev'), pairs)]
    ppermute x29, starting transfers between devices: 25.7 us -> 28.2 us  [swap(): lax.ppermute(leaf, ('grp', 'dev'), pairs)]
    unnamed x95 -> x99, local copies, waits for them, and re-layouts: 17.7 us -> 18.2 us
  transfers between devices with their start and end apart: 31 -> 31, of which waited for: 10 -> 9; matrix products, arithmetic and copies ran while one was open for 13% -> 12% of each run, Pallas kernels for 25% -> 24%
where the time goes in v15:
time: 216 us
  waiting for transfers between devices  80.9 us (37%)
  Pallas kernels  57.4 us (27%)
  starting transfers between devices  43 us (20%)
  local copies, waits for them, and re-layouts  30.5 us (14%)
  other arithmetic  3.36 us (2%)
    ppermute x29, waiting for transfers between devices, swap(): lax.ppermute(leaf, ('grp', 'dev'), pairs)  80.9 us
    pallas_call x3, Pallas kernels, feed_forward(): pl.pallas_call(functools.partial(mlp_kernel, pieces, len(flat), up_plan,...  30.7 us
    ppermute x29, starting transfers between devices, swap(): lax.ppermute(leaf, ('grp', 'dev'), pairs)  28.2 us
    unnamed x99, local copies, waits for them, and re-layouts  18.2 us
    pallas_call x1, Pallas kernels, attend_prefix(): pl.pallas_call(far_kernel, out_shape=jax.ShapeDtypeStruct((sources, capac...  16.6 us
    all_to_all x1, starting transfers between devices, on_device(): lax.all_to_all(answer_part, ('grp', 'dev'), split_axis=0, concat_axis=0,...  7.51 us
    all_to_all x1, starting transfers between devices, on_device(): lax.all_to_all(outgoing.reshape(sources, capacity, part_width), ('grp', '...  7.3 us
    pallas_call x1, Pallas kernels, attend_suffix(): pl.pallas_call(functools.partial(own_kernel, local_heads), out_shape=(jax...  4.49 us
  transfers between devices with their start and end apart: 31, of which 9 were waited for; matrix products, arithmetic and copies ran while one was open for 12% of the time, Pallas kernels for 24%

profile of v15, /device:TPU:0, one launch (start us, length us, event | category | flops | bytes accessed | tf_op | source)
XLA Modules:
  0.0 215.9 jit_solution(13047449270805055046)
XLA Ops:
  0.0 2.3 %pack_queries.1 = bf16[4,8,64,256]{3,2,1,0:T(8,128)(2,1)} custom-call(s32[1,4]{1,0:T(1,128)} %lengths_ref.5, s32[1,4]{1,0:T(1,128)} %groups_ref.3, bf16[128,2048]{1,0:T(8,128)(2,1)} %query_ref.3), custom_call_target="tpu_custom_call" | custom-call | tf_op jit(solution)/shard_map/pack_queries/pallas_call | solution.py:76
  2.3 7.3 %all-to-all-start = ((bf16[32,64,256]{2,1,0:T(8,128)(2,1)}), bf16[32,64,256]{2,1,0:T(8,128)(2,1)S(1)}, u32[]{:S(2)}, u32[]{:S(2)}) async-start(bf16[32,64,256]{2,1,0:T(8,128)(2,1)} %bitcast.20), calls=%async_computation | async-start | bytes 2097152 | tf_op jit(solution)/shard_map/all_to_all | solution.py:665
  15.3 4.5 %attend_suffix.1 = (f32[128,2048]{1,0:T(8,128)S(1)}, f32[128,128]{1,0:T(8,128)S(1)}, f32[128,128]{1,0:T(8,128)S(1)}) custom-call(s32[1,4]{1,0:T(1,128)S(1)} %copy-done.10, bf16[128,2048]{1,0:T(8,128)(2,1)S(1)} %copy-done.3, bf16[128,2048]{1,0:T(8,128)(2,1)S(1)} %copy-done.12, bf16[128,2048]{1,0:T(8,128)(2,1)S(1)} %copy-done.13), custom_call_target="tpu_custom_call" | custom-call | flops 1342177280 | bytes 2097152 | tf_op jit(solution)/shard_map/attend_suffix/pallas_call | solution.py:320
  19.8 4.1 %copy.18 = bf16[1,4096,256]{1,2,0:T(8,128)(2,1)} copy(bf16[1,4096,256]{2,1,0:T(8,128)(2,1)} %param.22) | data formatting | bytes 4194304 | tf_op args[6]
  23.9 4.1 %copy.19 = bf16[1,4096,256]{1,2,0:T(8,128)(2,1)} copy(bf16[1,4096,256]{2,1,0:T(8,128)(2,1)} %param.23) | data formatting | bytes 4194304 | tf_op args[7]
  28.0 4.1 %copy.20 = bf16[4096,2,128]{2,0,1:T(8,128)(2,1)} copy(bf16[4096,2,128]{0,2,1:T(8,128)(2,1)} %bitcast.19) | data formatting | bytes 4194304 | tf_op jit(solution)/shard_map/reshape;squeeze | solution.py:677
  32.1 4.0 %concatenate.19.values_hbm = bf16[2,4096,256]{2,1,0:T(8,128)(2,1)} pad(bf16[2,4096,128]{2,1,0:T(8,128)(2,1)} %bitcast.18, bf16[]{:T(256)} %constant.0.clone.1), padding=0_0x0_0x0_128 | pad | bytes 6291458 | tf_op jit(solution)/shard_map/concatenate | solution.py:678
  36.1 2.3 %fusion.1 = (bf16[128,2048]{1,0:T(8,128)(2,1)}, bf16[128,2048]{1,0:T(8,128)(2,1)}) fusion(bf16[256,2048]{1,0:T(8,128)(2,1)} %refs_10_.5), kind=kLoop, calls=%fused_computation.14 | loop fusion | bytes 2097152 | tf_op jit(solution)/shard_map/slice | solution.py:662
  38.3 2.3 %collective-permute-done.1 = bf16[1024,256]{1,0:T(8,128)(2,1)} collective-permute-done((bf16[1024,256]{1,0:T(8,128)(2,1)}, bf16[1024,256]{1,0:T(8,128)(2,1)}, u32[]{:S(2)}, u32[]{:S(2)}) %collective-permute-start.1) | collective-permute-done | bytes 524320 | tf_op jit(solution)/shard_map/ppermute | solution.py:441
  46.0 16.6 %attend_prefix.1 = bf16[32,72,256]{2,1,0:T(8,128)(2,1)} custom-call(s32[32]{0:T(128)} %convert_reduce_fusion.counts_ref, bf16[32,64,256]{2,1,0:T(8,128)(2,1)} %copy-done.31, bf16[256,4096]{1,0:T(8,128)(2,1)} %bitcast.21, bf16[2,4096,256]{2,1,0:T(8,128)(2,1)} %concatenate.19.values_hbm), custom_call_target="tpu_custom_call" | custom-call | flops 8589934592 | bytes 8388608 | tf_op jit(solution)/shard_map/attend_prefix/pallas_call | solution.py:246
  63.5 2.5 %collective-permute-done.5 = bf16[1040,256]{1,0:T(8,128)(2,1)} collective-permute-done((bf16[1040,256]{1,0:T(8,128)(2,1)}, bf16[1040,256]{1,0:T(8,128)(2,1)}, u32[]{:S(2)}, u32[]{:S(2)}) %collective-permute-start.5) | collective-permute-done | bytes 532512 | tf_op jit(solution)/shard_map/ppermute | solution.py:441
  66.9 7.5 %all-to-all-start.1 = ((bf16[32,72,256]{2,1,0:T(8,128)(2,1)}), bf16[32,72,256]{2,1,0:T(8,128)(2,1)S(1)}, u32[]{:S(2)}, u32[]{:S(2)}) async-start(bf16[32,72,256]{2,1,0:T(8,128)(2,1)} %attend_prefix.1), calls=%async_computation.1 | async-start | bytes 2359296 | tf_op jit(solution)/shard_map/all_to_all | solution.py:734
  74.4 1.8 collective-permute-start.10
  80.3 27.0 %collective-permute-done.10 = bf16[128,2048]{1,0:T(8,128)(2,1)S(1)} collective-permute-done((bf16[128,2048]{1,0:T(8,128)(2,1)S(1)}, bf16[128,2048]{1,0:T(8,128)(2,1)S(1)}, u32[]{:S(2)}, u32[]{:S(2)}) %collective-permute-start.10) | collective-permute-done | bytes 524320 | tf_op jit(solution)/shard_map/ppermute | solution.py:441
  111.5 12.4 %collective-permute-done.14.refs_14_ = bf16[128,2048]{1,0:T(8,128)(2,1)S(1)} collective-permute-done((bf16[128,2048]{1,0:T(8,128)(2,1)S(1)}, bf16[128,2048]{1,0:T(8,128)(2,1)S(1)}, u32[]{:S(2)}, u32[]{:S(2)}) %collective-permute-start.14) | collective-permute-done | bytes 524320 | tf_op jit(solution)/shard_map/ppermute | solution.py:441
  126.4 1.9 merge_parts.1
  129.9 2.4 %collective-permute-start.15 = (bf16[64,2048]{1,0:T(8,128)(2,1)S(1)}, bf16[64,2048]{1,0:T(8,128)(2,1)S(1)}, u32[]{:S(2)}, u32[]{:S(2)}) collective-permute-start(bf16[64,2048]{1,0:T(8,128)(2,1)S(1)} %get-tuple-element.100), channel_id=1, source_target_pairs={{0,4},{1,5},{2,6},{3,7},{4,0},{5,1},{6,2},{7,3},{8,12},{9,13},{10,... | collective-permute-start | bytes 786440 | tf_op jit(solution)/shard_map/ppermute | solution.py:441
  133.9 11.0 %collective-permute-done.15.refs_0_ = bf16[64,2048]{1,0:T(8,128)(2,1)S(1)} collective-permute-done((bf16[64,2048]{1,0:T(8,128)(2,1)S(1)}, bf16[64,2048]{1,0:T(8,128)(2,1)S(1)}, u32[]{:S(2)}, u32[]{:S(2)}) %collective-permute-start.15) | collective-permute-done | bytes 262176 | tf_op jit(solution)/shard_map/ppermute | solution.py:441
  146.3 12.3 %collective-permute-done.16.refs_0_ = bf16[64,2048]{1,0:T(8,128)(2,1)S(1)} collective-permute-done((bf16[64,2048]{1,0:T(8,128)(2,1)S(1)}, bf16[64,2048]{1,0:T(8,128)(2,1)S(1)}, u32[]{:S(2)}, u32[]{:S(2)}) %collective-permute-start.16) | collective-permute-done | bytes 262176 | tf_op jit(solution)/shard_map/ppermute | solution.py:441
  163.9 9.3 %feed_forward.3 = (bf16[64,2048]{1,0:T(8,128)(2,1)}, bf16[64,2048]{1,0:T(8,128)(2,1)}) custom-call(bf16[64,2048]{1,0:T(8,128)(2,1)} %copy-done.41, bf16[64,2048]{1,0:T(8,128)(2,1)} %copy-done.42, bf16[2064,256]{1,0:T(8,128)(2,1)} %copy-done.14, bf16[2064,256]{1,0:T(8,128)(2,1)} %copy-done.16, bf16[2064,256]{1,0:T(8,128)(2,1)} %copy-done.15, ...), custom_call_target="tpu_custom_call" | custom-call | flops 2147483648 | bytes 16777216 | tf_op jit(solution)/shard_map/feed_forward/pallas_call | solution.py:560
  174.8 9.4 %feed_forward.4 = (bf16[64,2048]{1,0:T(8,128)(2,1)}, bf16[64,2048]{1,0:T(8,128)(2,1)}) custom-call(bf16[64,2048]{1,0:T(8,128)(2,1)} %copy-done.40, bf16[64,2048]{1,0:T(8,128)(2,1)} %copy-done.43, bf16[2064,256]{1,0:T(8,128)(2,1)} %copy-done.14, bf16[2064,256]{1,0:T(8,128)(2,1)} %copy-done.16, bf16[2064,256]{1,0:T(8,128)(2,1)} %copy-done.15, ...), custom_call_target="tpu_custom_call" | custom-call | flops 2147483648 | bytes 16777216 | tf_op jit(solution)/shard_map/feed_forward/pallas_call | solution.py:560
  185.1 12.0 %feed_forward.5 = (bf16[128,2048]{1,0:T(8,128)(2,1)}, bf16[128,2048]{1,0:T(8,128)(2,1)}) custom-call(bf16[128,2048]{1,0:T(8,128)(2,1)} %copy-done.37, bf16[128,2048]{1,0:T(8,128)(2,1)} %copy-done, bf16[2064,256]{1,0:T(8,128)(2,1)} %copy-done.14, bf16[2064,256]{1,0:T(8,128)(2,1)} %copy-done.16, bf16[2064,256]{1,0:T(8,128)(2,1)} %copy-done.15, ...), custom_call_target="tpu_custom_call" | custom-call | flops 4294967296 | bytes 16777216 | tf_op jit(solution)/shard_map/feed_forward/pallas_call | solution.py:560
  198.6 2.9 %collective-permute-start.28 = (bf16[64,2048]{1,0:T(8,128)(2,1)S(1)}, bf16[64,2048]{1,0:T(8,128)(2,1)S(1)}, u32[]{:S(2)}, u32[]{:S(2)}) collective-permute-start(bf16[64,2048]{1,0:T(8,128)(2,1)S(1)} %add_convert_fusion), channel_id=1, source_target_pairs={{0,4},{1,5},{2,6},{3,7},{4,0},{5,1},{6,2},{7,3},{8,12},{9,13},{10,... | collective-permute-start | bytes 786440 | tf_op jit(solution)/shard_map/ppermute | solution.py:441
  201.6 11.8 %collective-permute-done.28.far_b_ref = bf16[64,2048]{1,0:T(8,128)(2,1)S(1)} collective-permute-done((bf16[64,2048]{1,0:T(8,128)(2,1)S(1)}, bf16[64,2048]{1,0:T(8,128)(2,1)S(1)}, u32[]{:S(2)}, u32[]{:S(2)}) %collective-permute-start.28) | collective-permute-done | bytes 262176 | tf_op jit(solution)/shard_map/ppermute | solution.py:441
  (159 shorter events, 39.4 us)
Async XLA Ops:
  2.3 38.4 %all-to-all-start = ((bf16[32,64,256]{2,1,0:T(8,128)(2,1)}), bf16[32,64,256]{2,1,0:T(8,128)(2,1)S(1)}, u32[]{:S(2)}, u32[]{:S(2)}) async-start(bf16[32,64,256]{2,1,0:T(8,128)(2,1)} %bitcast.20), calls=%async_computation | async-start | bytes 2097152 | tf_op jit(solution)/shard_map/all_to_all | solution.py:665
  9.8 30.9 %collective-permute-start.2 = (bf16[2064,256]{1,0:T(8,128)(2,1)S(1)}, bf16[2064,256]{1,0:T(8,128)(2,1)}, u32[]{:S(2)}, u32[]{:S(2)}) collective-permute-start(bf16[2064,256]{1,0:T(8,128)(2,1)S(1)} %pad_maximum_fusion.refs_2_), channel_id=1, source_target_pairs={{0,8},{1,9},{2,10},{3,11},{4,12},{5,13},{6,14},{7,15},{8,0},{9,1},... | collective-permute-start | bytes 3170312 | tf_op jit(solution)/shard_map/ppermute | solution.py:441
  10.1 30.6 %collective-permute-start.3 = (bf16[256,2048]{1,0:T(8,128)(2,1)}, bf16[256,2048]{1,0:T(8,128)(2,1)}, u32[]{:S(2)}, u32[]{:S(2)}) collective-permute-start(bf16[256,2048]{1,0:T(8,128)(2,1)} %refs_10_.5), channel_id=1, source_target_pairs={{0,8},{1,9},{2,10},{3,11},{4,12},{5,13},{6,14},{7,15},{8,0},{9,1},... | collective-permute-start | bytes 3145736 | tf_op jit(solution)/shard_map/ppermute | solution.py:441
  11.2 29.5 %collective-permute-start.1 = (bf16[1024,256]{1,0:T(8,128)(2,1)}, bf16[1024,256]{1,0:T(8,128)(2,1)}, u32[]{:S(2)}, u32[]{:S(2)}) collective-permute-start(bf16[1024,256]{1,0:T(8,128)(2,1)} %slice.15), channel_id=1, source_target_pairs={{0,2},{1,3},{2,0},{3,1},{4,6},{5,7},{6,4},{7,5},{8,10},{9,11},{10,... | collective-permute-start | bytes 1572872 | tf_op jit(solution)/shard_map/ppermute | solution.py:441
  13.0 27.7 %collective-permute-start = (bf16[1024,256]{1,0:T(8,128)(2,1)}, bf16[1024,256]{1,0:T(8,128)(2,1)}, u32[]{:S(2)}, u32[]{:S(2)}) collective-permute-start(bf16[1024,256]{1,0:T(8,128)(2,1)} %slice.15), channel_id=1, source_target_pairs={{0,1},{1,0},{2,3},{3,2},{4,5},{5,4},{6,7},{7,6},{8,9},{9,8},{10,11... | collective-permute-start | bytes 1572872 | tf_op jit(solution)/shard_map/ppermute | solution.py:441
  40.7 22.0 %collective-permute-start.7 = (bf16[128,2048]{1,0:T(8,128)(2,1)}, bf16[128,2048]{1,0:T(8,128)(2,1)S(1)}, u32[]{:S(2)}, u32[]{:S(2)}) collective-permute-start(bf16[128,2048]{1,0:T(8,128)(2,1)} %get-tuple-element.77), channel_id=1, source_target_pairs={{0,2},{1,3},{2,0},{3,1},{4,6},{5,7},{6,4},{7,5},{8,10},{9,11},{10,... | collective-permute-start | bytes 1572872 | tf_op jit(solution)/shard_map/ppermute | solution.py:441
  41.1 21.6 %collective-permute-start.6 = (bf16[128,2048]{1,0:T(8,128)(2,1)}, bf16[128,2048]{1,0:T(8,128)(2,1)S(1)}, u32[]{:S(2)}, u32[]{:S(2)}) collective-permute-start(bf16[128,2048]{1,0:T(8,128)(2,1)} %get-tuple-element.77), channel_id=1, source_target_pairs={{0,1},{1,0},{2,3},{3,2},{4,5},{5,4},{6,7},{7,6},{8,9},{9,8},{10,11... | collective-permute-start | bytes 1572872 | tf_op jit(solution)/shard_map/ppermute | solution.py:441
  42.8 23.1 %collective-permute-start.5 = (bf16[1040,256]{1,0:T(8,128)(2,1)}, bf16[1040,256]{1,0:T(8,128)(2,1)}, u32[]{:S(2)}, u32[]{:S(2)}) collective-permute-start(bf16[1040,256]{1,0:T(8,128)(2,1)} %fusion), channel_id=1, source_target_pairs={{0,2},{1,3},{2,0},{3,1},{4,6},{5,7},{6,4},{7,5},{8,10},{9,11},{10,... | collective-permute-start | bytes 1597448 | tf_op jit(solution)/shard_map/ppermute | solution.py:441
  44.3 21.8 %collective-permute-start.4 = (bf16[1040,256]{1,0:T(8,128)(2,1)}, bf16[1040,256]{1,0:T(8,128)(2,1)S(1)}, u32[]{:S(2)}, u32[]{:S(2)}) collective-permute-start(bf16[1040,256]{1,0:T(8,128)(2,1)} %fusion), channel_id=1, source_target_pairs={{0,1},{1,0},{2,3},{3,2},{4,5},{5,4},{6,7},{7,6},{8,9},{9,8},{10,11... | collective-permute-start | bytes 1597448 | tf_op jit(solution)/shard_map/ppermute | solution.py:441
  66.9 59.5 %all-to-all-start.1 = ((bf16[32,72,256]{2,1,0:T(8,128)(2,1)}), bf16[32,72,256]{2,1,0:T(8,128)(2,1)S(1)}, u32[]{:S(2)}, u32[]{:S(2)}) async-start(bf16[32,72,256]{2,1,0:T(8,128)(2,1)} %attend_prefix.1), calls=%async_computation.1 | async-start | bytes 2359296 | tf_op jit(solution)/shard_map/all_to_all | solution.py:734
  74.4 32.9 %collective-permute-start.10 = (bf16[128,2048]{1,0:T(8,128)(2,1)S(1)}, bf16[128,2048]{1,0:T(8,128)(2,1)S(1)}, u32[]{:S(2)}, u32[]{:S(2)}) collective-permute-start(bf16[128,2048]{1,0:T(8,128)(2,1)S(1)} %copy-done.32), channel_id=1, source_target_pairs={{0,2},{1,3},{2,0},{3,1},{4,6},{5,7},{6,4},{7,5},{8,10},{9,11},{10,... | collective-permute-start | bytes 1572872 | tf_op jit(solution)/shard_map/ppermute | solution.py:441
  78.4 45.4 %collective-permute-start.9 = (bf16[2064,256]{1,0:T(8,128)(2,1)S(1)}, bf16[2064,256]{1,0:T(8,128)(2,1)S(1)}, u32[]{:S(2)}, u32[]{:S(2)}) collective-permute-start(bf16[2064,256]{1,0:T(8,128)(2,1)S(1)} %constant_dynamic-update-slice_fusion.refs_4_), channel_id=1, source_target_pairs={{0,8},{1,9},{2,10},{3,11},{4,12},{5,13},{6,14},{7,15},{8,0},{9,1},... | collective-permute-start | bytes 3170312 | tf_op jit(solution)/shard_map/ppermute | solution.py:441
  78.5 45.3 %collective-permute-start.8 = (bf16[2064,256]{1,0:T(8,128)(2,1)S(1)}, bf16[2064,256]{1,0:T(8,128)(2,1)S(1)}, u32[]{:S(2)}, u32[]{:S(2)}) collective-permute-start(bf16[2064,256]{1,0:T(8,128)(2,1)S(1)} %constant_dynamic-update-slice_fusion.refs_4_), channel_id=1, source_target_pairs={{0,1},{1,0},{2,3},{3,2},{4,5},{5,4},{6,7},{7,6},{8,9},{9,8},{10,11... | collective-permute-start | bytes 3170312 | tf_op jit(solution)/shard_map/ppermute | solution.py:441
  80.1 29.1 %collective-permute-start.12 = (bf16[128,2048]{1,0:T(8,128)(2,1)S(1)}, bf16[128,2048]{1,0:T(8,128)(2,1)S(1)}, u32[]{:S(2)}, u32[]{:S(2)}) collective-permute-start(bf16[128,2048]{1,0:T(8,128)(2,1)S(1)} %collective-permute-done.6.refs_11_), channel_id=1, source_target_pairs={{0,8},{1,9},{2,10},{3,11},{4,12},{5,13},{6,14},{7,15},{8,0},{9,1},... | collective-permute-start | bytes 1572872 | tf_op jit(solution)/shard_map/ppermute | solution.py:441
  108.4 17.9 %collective-permute-start.11 = (bf16[2064,256]{1,0:T(8,128)(2,1)S(1)}, bf16[2064,256]{1,0:T(8,128)(2,1)}, u32[]{:S(2)}, u32[]{:S(2)}) collective-permute-start(bf16[2064,256]{1,0:T(8,128)(2,1)S(1)} %constant_dynamic-update-slice_fusion.2.refs_3_), channel_id=1, source_target_pairs={{0,8},{1,9},{2,10},{3,11},{4,12},{5,13},{6,14},{7,15},{8,0},{9,1},... | collective-permute-start | bytes 3170312 | tf_op jit(solution)/shard_map/ppermute | solution.py:441
  108.6 15.2 %collective-permute-start.13 = (bf16[256,2048]{1,0:T(8,128)(2,1)S(1)}, bf16[256,2048]{1,0:T(8,128)(2,1)S(1)}, u32[]{:S(2)}, u32[]{:S(2)}) collective-permute-start(bf16[256,2048]{1,0:T(8,128)(2,1)S(1)} %constant_dynamic-update-slice_fusion.4.refs_13_), channel_id=1, source_target_pairs={{0,8},{1,9},{2,10},{3,11},{4,12},{5,13},{6,14},{7,15},{8,0},{9,1},... | collective-permute-start | bytes 3145736 | tf_op jit(solution)/shard_map/ppermute | solution.py:441
  128.3 30.3 %collective-permute-start.19 = (bf16[2064,256]{1,0:T(8,128)(2,1)S(1)}, bf16[2064,256]{1,0:T(8,128)(2,1)S(1)}, u32[]{:S(2)}, u32[]{:S(2)}) collective-permute-start(bf16[2064,256]{1,0:T(8,128)(2,1)S(1)} %copy-done.20), channel_id=1, source_target_pairs={{0,8},{1,9},{2,10},{3,11},{4,12},{5,13},{6,14},{7,15},{8,0},{9,1},... | collective-permute-start | bytes 3170312 | tf_op jit(solution)/shard_map/ppermute | solution.py:441
  128.4 30.2 %collective-permute-start.20 = (bf16[256,2048]{1,0:T(8,128)(2,1)S(1)}, bf16[256,2048]{1,0:T(8,128)(2,1)S(1)}, u32[]{:S(2)}, u32[]{:S(2)}) collective-permute-start(bf16[256,2048]{1,0:T(8,128)(2,1)S(1)} %copy-done.34), channel_id=1, source_target_pairs={{0,1},{1,0},{2,3},{3,2},{4,5},{5,4},{6,7},{7,6},{8,9},{9,8},{10,11... | collective-permute-start | bytes 3145736 | tf_op jit(solution)/shard_map/ppermute | solution.py:441
  129.9 14.9 %collective-permute-start.15 = (bf16[64,2048]{1,0:T(8,128)(2,1)S(1)}, bf16[64,2048]{1,0:T(8,128)(2,1)S(1)}, u32[]{:S(2)}, u32[]{:S(2)}) collective-permute-start(bf16[64,2048]{1,0:T(8,128)(2,1)S(1)} %get-tuple-element.100), channel_id=1, source_target_pairs={{0,4},{1,5},{2,6},{3,7},{4,0},{5,1},{6,2},{7,3},{8,12},{9,13},{10,... | collective-permute-start | bytes 786440 | tf_op jit(solution)/shard_map/ppermute | solution.py:441
  159.2 14.1 %collective-permute-start.21 = (bf16[64,2048]{1,0:T(8,128)(2,1)S(1)}, bf16[64,2048]{1,0:T(8,128)(2,1)S(1)}, u32[]{:S(2)}, u32[]{:S(2)}) collective-permute-start(bf16[64,2048]{1,0:T(8,128)(2,1)S(1)} %collective-permute-done.16.refs_0_), channel_id=1, source_target_pairs={{0,16},{1,17},{2,18},{3,19},{4,20},{5,21},{6,22},{7,23},{8,24},{9,... | collective-permute-start | bytes 786440 | tf_op jit(solution)/shard_map/ppermute | solution.py:441
  184.3 14.2 %collective-permute-start.27 = (bf16[64,2048]{1,0:T(8,128)(2,1)S(1)}, bf16[64,2048]{1,0:T(8,128)(2,1)S(1)}, u32[]{:S(2)}, u32[]{:S(2)}) collective-permute-start(bf16[64,2048]{1,0:T(8,128)(2,1)S(1)} %add_convert_fusion.1), channel_id=1, source_target_pairs={{0,4},{1,5},{2,6},{3,7},{4,0},{5,1},{6,2},{7,3},{8,12},{9,13},{10,... | collective-permute-start | bytes 786440 | tf_op jit(solution)/shard_map/ppermute | solution.py:441
  184.4 14.2 %collective-permute-start.26 = (bf16[64,2048]{1,0:T(8,128)(2,1)}, bf16[64,2048]{1,0:T(8,128)(2,1)S(1)}, u32[]{:S(2)}, u32[]{:S(2)}) collective-permute-start(bf16[64,2048]{1,0:T(8,128)(2,1)} %get-tuple-element.131), channel_id=1, source_target_pairs={{0,16},{1,17},{2,18},{3,19},{4,20},{5,21},{6,22},{7,23},{8,24},{9,... | collective-permute-start | bytes 786440 | tf_op jit(solution)/shard_map/ppermute | solution.py:441
  197.1 16.3 %collective-permute-start.25 = (bf16[128,2048]{1,0:T(8,128)(2,1)}, bf16[128,2048]{1,0:T(8,128)(2,1)S(1)}, u32[]{:S(2)}, u32[]{:S(2)}) collective-permute-start(bf16[128,2048]{1,0:T(8,128)(2,1)} %get-tuple-element.130), channel_id=1, source_target_pairs={{0,16},{1,17},{2,18},{3,19},{4,20},{5,21},{6,22},{7,23},{8,24},{9,... | collective-permute-start | bytes 1572872 | tf_op jit(solution)/shard_map/ppermute | solution.py:441
  198.6 14.7 %collective-permute-start.28 = (bf16[64,2048]{1,0:T(8,128)(2,1)S(1)}, bf16[64,2048]{1,0:T(8,128)(2,1)S(1)}, u32[]{:S(2)}, u32[]{:S(2)}) collective-permute-start(bf16[64,2048]{1,0:T(8,128)(2,1)S(1)} %add_convert_fusion), channel_id=1, source_target_pairs={{0,4},{1,5},{2,6},{3,7},{4,0},{5,1},{6,2},{7,3},{8,12},{9,13},{10,... | collective-permute-start | bytes 786440 | tf_op jit(solution)/shard_map/ppermute | solution.py:441
  (54 other events, 625.9 us)

commit v16 on v11

--- a/solution.py
+++ b/solution.py
@@ -11,7 +11,7 @@
 HD = 128
 LANES = 128
 STAT_ROWS = 8
-STREAMS = 4
+STREAMS = 1
 FETCHES = 8
 UNROLL = 4
 EMPTY = 64.0
@@ -500,7 +500,7 @@
                 )
             begin += height
         copies.append(held)
-    for held in copies:
+    for held in copies[:parts]:
         for copy in held:
             copy.start()
     rows = jnp.concatenate([ref[...] for ref in row_refs], axis=0)
@@ -508,6 +508,10 @@
     for part in range(parts):
         for copy in copies[part]:
             copy.wait()
+        if part == 0:
+            for held in copies[parts:]:
+                for copy in held:
+                    copy.start()
         product = jnp.dot(
             rows, up_ref[part, :model_width, :], preferred_element_type=jnp.float32
         )

time: 204 us -> 203 us (level)
  Pallas kernels: 60.5 us -> 57.1 us
  waiting for transfers between devices: 79.8 us -> 82.5 us
    pallas_call x1, Pallas kernels: 19.2 us -> 16.6 us  [attend_prefix(): pl.pallas_call(far_kernel, out_shape=jax.ShapeDtypeStruct((sources, capac...]
    ppermute x26, waiting for transfers between devices: 79.8 us -> 82.5 us  [swap(): lax.ppermute(leaf, ('grp', 'dev'), pairs)]
  transfers between devices with their start and end apart: 28 -> 28, of which waited for: 10 -> 10; matrix products, arithmetic and copies ran while one was open for 11% -> 11% of each run, Pallas kernels for 27% -> 25%
where the time goes in v16:
time: 203 us
  waiting for transfers between devices  82.5 us (41%)
  Pallas kernels  57.1 us (28%)
  starting transfers between devices  36.2 us (18%)
  local copies, waits for them, and re-layouts  24 us (12%)
  other arithmetic  2.29 us (1%)
    ppermute x26, waiting for transfers between devices, swap(): lax.ppermute(leaf, ('grp', 'dev'), pairs)  82.5 us
    pallas_call x3, Pallas kernels, feed_forward(): pl.pallas_call(functools.partial(mlp_kernel, pieces, up_plan, down_plan),...  30.4 us
    ppermute x26, starting transfers between devices, swap(): lax.ppermute(leaf, ('grp', 'dev'), pairs)  24.1 us
    pallas_call x1, Pallas kernels, attend_prefix(): pl.pallas_call(far_kernel, out_shape=jax.ShapeDtypeStruct((sources, capac...  16.6 us
    unnamed x74, local copies, waits for them, and re-layouts  12.6 us
    all_to_all x1, starting transfers between devices, on_device(): lax.all_to_all(outgoing.reshape(sources, capacity, part_width), ('grp', '...  7.3 us
    all_to_all x1, starting transfers between devices, on_device(): lax.all_to_all(answer_part, ('grp', 'dev'), split_axis=0, concat_axis=0,...  4.72 us
    pallas_call x1, Pallas kernels, attend_suffix(): pl.pallas_call(functools.partial(own_kernel, local_heads), out_shape=(jax...  4.48 us
  transfers between devices with their start and end apart: 28, of which 10 were waited for; matrix products, arithmetic and copies ran while one was open for 11% of the time, Pallas kernels for 25%

profile of v16, /device:TPU:0, one launch (start us, length us, event | category | flops | bytes accessed | tf_op | source)
XLA Modules:
  0.0 202.7 jit_solution(2078943119189599263)
XLA Ops:
  0.0 2.3 %pack_queries.1 = bf16[4,8,64,256]{3,2,1,0:T(8,128)(2,1)} custom-call(s32[1,4]{1,0:T(1,128)} %lengths_ref.5, s32[1,4]{1,0:T(1,128)} %groups_ref.3, bf16[128,2048]{1,0:T(8,128)(2,1)} %query_ref.3), custom_call_target="tpu_custom_call" | custom-call | tf_op jit(solution)/shard_map/pack_queries/pallas_call | solution.py:76
  2.3 7.3 %all-to-all-start = ((bf16[32,64,256]{2,1,0:T(8,128)(2,1)}), bf16[32,64,256]{2,1,0:T(8,128)(2,1)S(1)}, u32[]{:S(2)}, u32[]{:S(2)}) async-start(bf16[32,64,256]{2,1,0:T(8,128)(2,1)} %bitcast.20), calls=%async_computation | async-start | bytes 2097152 | tf_op jit(solution)/shard_map/all_to_all | solution.py:648
  15.0 4.1 %copy.18 = bf16[1,4096,256]{1,2,0:T(8,128)(2,1)} copy(bf16[1,4096,256]{2,1,0:T(8,128)(2,1)} %param.22) | data formatting | bytes 4194304 | tf_op args[6]
  19.1 4.1 %copy.19 = bf16[1,4096,256]{1,2,0:T(8,128)(2,1)} copy(bf16[1,4096,256]{2,1,0:T(8,128)(2,1)} %param.23) | data formatting | bytes 4194304 | tf_op args[7]
  23.2 4.1 %copy.20 = bf16[4096,2,128]{2,0,1:T(8,128)(2,1)} copy(bf16[4096,2,128]{0,2,1:T(8,128)(2,1)} %bitcast.19) | data formatting | bytes 4194304 | tf_op jit(solution)/shard_map/reshape;squeeze | solution.py:660
  27.3 4.1 %concatenate.13.values_hbm = bf16[2,4096,256]{2,1,0:T(8,128)(2,1)} pad(bf16[2,4096,128]{2,1,0:T(8,128)(2,1)} %bitcast.18, bf16[]{:T(256)} %constant.0.clone.1), padding=0_0x0_0x0_128 | pad | bytes 6291458 | tf_op jit(solution)/shard_map/concatenate | solution.py:661
  31.5 4.5 %attend_suffix.1 = (f32[128,2048]{1,0:T(8,128)S(1)}, f32[128,128]{1,0:T(8,128)S(1)}, f32[128,128]{1,0:T(8,128)S(1)}) custom-call(s32[1,4]{1,0:T(1,128)S(1)} %copy-done.10, bf16[128,2048]{1,0:T(8,128)(2,1)S(1)} %copy-done.3, bf16[128,2048]{1,0:T(8,128)(2,1)S(1)} %copy-done.12, bf16[128,2048]{1,0:T(8,128)(2,1)S(1)} %copy-done.13), custom_call_target="tpu_custom_call" | custom-call | flops 1342177280 | bytes 2097152 | tf_op jit(solution)/shard_map/attend_suffix/pallas_call | solution.py:320
  35.9 2.3 %fusion.1 = (bf16[128,2048]{1,0:T(8,128)(2,1)}, bf16[128,2048]{1,0:T(8,128)(2,1)}) fusion(bf16[256,2048]{1,0:T(8,128)(2,1)} %refs_10_.2), kind=kLoop, calls=%fused_computation.11 | loop fusion | bytes 2097152 | tf_op jit(solution)/shard_map/slice | solution.py:644
  38.2 5.3 %collective-permute-done.2 = bf16[1280,256]{1,0:T(8,128)(2,1)} collective-permute-done((bf16[1280,256]{1,0:T(8,128)(2,1)}, bf16[1280,256]{1,0:T(8,128)(2,1)}, u32[]{:S(2)}, u32[]{:S(2)}) %collective-permute-start.2) | collective-permute-done | bytes 655392 | tf_op jit(solution)/shard_map/ppermute | solution.py:441
  43.5 3.0 %collective-permute-done.refs_3_ = bf16[2064,256]{1,0:T(8,128)(2,1)} collective-permute-done((bf16[2064,256]{1,0:T(8,128)(2,1)S(1)}, bf16[2064,256]{1,0:T(8,128)(2,1)}, u32[]{:S(2)}, u32[]{:S(2)}) %collective-permute-start) | collective-permute-done | bytes 1056800 | tf_op jit(solution)/shard_map/ppermute | solution.py:441
  50.2 16.6 %attend_prefix.1 = bf16[32,72,256]{2,1,0:T(8,128)(2,1)} custom-call(s32[32]{0:T(128)} %convert_reduce_fusion.counts_ref, bf16[32,64,256]{2,1,0:T(8,128)(2,1)} %copy-done.26, bf16[256,4096]{1,0:T(8,128)(2,1)} %bitcast.21, bf16[2,4096,256]{2,1,0:T(8,128)(2,1)} %concatenate.13.values_hbm), custom_call_target="tpu_custom_call" | custom-call | flops 8589934592 | bytes 8388608 | tf_op jit(solution)/shard_map/attend_prefix/pallas_call | solution.py:246
  66.9 2.9 %collective-permute-done.7 = bf16[128,2048]{1,0:T(8,128)(2,1)S(1)} collective-permute-done((bf16[128,2048]{1,0:T(8,128)(2,1)}, bf16[128,2048]{1,0:T(8,128)(2,1)S(1)}, u32[]{:S(2)}, u32[]{:S(2)}) %collective-permute-start.7) | collective-permute-done | bytes 524320 | tf_op jit(solution)/shard_map/ppermute | solution.py:441
  69.7 2.7 %collective-permute-done.6.refs_11_ = bf16[256,2048]{1,0:T(8,128)(2,1)} collective-permute-done((bf16[256,2048]{1,0:T(8,128)(2,1)}, bf16[256,2048]{1,0:T(8,128)(2,1)}, u32[]{:S(2)}, u32[]{:S(2)}) %collective-permute-start.6) | collective-permute-done | bytes 1048608 | tf_op jit(solution)/shard_map/ppermute | solution.py:441
  72.4 4.7 %all-to-all-start.1 = ((bf16[32,72,256]{2,1,0:T(8,128)(2,1)}), bf16[32,72,256]{2,1,0:T(8,128)(2,1)S(1)}, u32[]{:S(2)}, u32[]{:S(2)}) async-start(bf16[32,72,256]{2,1,0:T(8,128)(2,1)} %attend_prefix.1), calls=%async_computation.1 | async-start | bytes 2359296 | tf_op jit(solution)/shard_map/all_to_all | solution.py:683
  82.0 28.0 %collective-permute-done.10 = bf16[128,2048]{1,0:T(8,128)(2,1)S(1)} collective-permute-done((bf16[128,2048]{1,0:T(8,128)(2,1)}, bf16[128,2048]{1,0:T(8,128)(2,1)S(1)}, u32[]{:S(2)}, u32[]{:S(2)}) %collective-permute-start.10) | collective-permute-done | bytes 524320 | tf_op jit(solution)/shard_map/ppermute | solution.py:441
  110.2 4.9 %collective-permute-done.8.refs_5_ = bf16[2064,256]{1,0:T(8,128)(2,1)S(1)} collective-permute-done((bf16[2064,256]{1,0:T(8,128)(2,1)S(1)}, bf16[2064,256]{1,0:T(8,128)(2,1)S(1)}, u32[]{:S(2)}, u32[]{:S(2)}) %collective-permute-start.8) | collective-permute-done | bytes 1056800 | tf_op jit(solution)/shard_map/ppermute | solution.py:441
  118.8 2.2 %collective-permute-start.13 = (bf16[64,2048]{1,0:T(8,128)(2,1)S(1)}, bf16[64,2048]{1,0:T(8,128)(2,1)S(1)}, u32[]{:S(2)}, u32[]{:S(2)}) collective-permute-start(bf16[64,2048]{1,0:T(8,128)(2,1)S(1)} %get-tuple-element.151), channel_id=1, source_target_pairs={{0,4},{1,5},{2,6},{3,7},{4,0},{5,1},{6,2},{7,3},{8,12},{9,13},{10,... | collective-permute-start | bytes 786440 | tf_op jit(solution)/shard_map/ppermute | solution.py:441
  122.7 11.0 %collective-permute-done.13.refs_0_ = bf16[64,2048]{1,0:T(8,128)(2,1)S(1)} collective-permute-done((bf16[64,2048]{1,0:T(8,128)(2,1)S(1)}, bf16[64,2048]{1,0:T(8,128)(2,1)S(1)}, u32[]{:S(2)}, u32[]{:S(2)}) %collective-permute-start.13) | collective-permute-done | bytes 262176 | tf_op jit(solution)/shard_map/ppermute | solution.py:441
  135.2 12.5 %collective-permute-done.14.refs_0_ = bf16[64,2048]{1,0:T(8,128)(2,1)S(1)} collective-permute-done((bf16[64,2048]{1,0:T(8,128)(2,1)S(1)}, bf16[64,2048]{1,0:T(8,128)(2,1)S(1)}, u32[]{:S(2)}, u32[]{:S(2)}) %collective-permute-start.14) | collective-permute-done | bytes 262176 | tf_op jit(solution)/shard_map/ppermute | solution.py:441
  151.5 9.2 %feed_forward.3 = (bf16[64,2048]{1,0:T(8,128)(2,1)}, bf16[64,2048]{1,0:T(8,128)(2,1)}) custom-call(bf16[64,2048]{1,0:T(8,128)(2,1)} %copy-done.29, bf16[64,2048]{1,0:T(8,128)(2,1)} %copy-done.30, bf16[2064,256]{1,0:T(8,128)(2,1)} %copy-done.14, bf16[2064,256]{1,0:T(8,128)(2,1)} %collective-permute-done.refs_3_, bf16[2064,256]{1,0:T(8,128)(2,1)} %copy-done.15, ...), custom_call_target="tpu_custom_call" | custom-call | flops 2147483648 | bytes 16777216 | tf_op jit(solution)/shard_map/feed_forward/pallas_call | solution.py:542
  162.4 9.2 %feed_forward.4 = (bf16[64,2048]{1,0:T(8,128)(2,1)}, bf16[64,2048]{1,0:T(8,128)(2,1)}) custom-call(bf16[64,2048]{1,0:T(8,128)(2,1)} %copy-done.28, bf16[64,2048]{1,0:T(8,128)(2,1)} %copy-done.31, bf16[2064,256]{1,0:T(8,128)(2,1)} %copy-done.14, bf16[2064,256]{1,0:T(8,128)(2,1)} %collective-permute-done.refs_3_, bf16[2064,256]{1,0:T(8,128)(2,1)} %copy-done.15, ...), custom_call_target="tpu_custom_call" | custom-call | flops 2147483648 | bytes 16777216 | tf_op jit(solution)/shard_map/feed_forward/pallas_call | solution.py:542
  172.6 11.9 %feed_forward.5 = (bf16[128,2048]{1,0:T(8,128)(2,1)}, bf16[128,2048]{1,0:T(8,128)(2,1)}) custom-call(bf16[128,2048]{1,0:T(8,128)(2,1)} %copy-done.27, bf16[128,2048]{1,0:T(8,128)(2,1)} %copy-done, bf16[2064,256]{1,0:T(8,128)(2,1)} %copy-done.14, bf16[2064,256]{1,0:T(8,128)(2,1)} %collective-permute-done.refs_3_, bf16[2064,256]{1,0:T(8,128)(2,1)} %copy-done.15, ...), custom_call_target="tpu_custom_call" | custom-call | flops 4294967296 | bytes 16777216 | tf_op jit(solution)/shard_map/feed_forward/pallas_call | solution.py:542
  186.0 2.9 %collective-permute-start.25 = (bf16[64,2048]{1,0:T(8,128)(2,1)S(1)}, bf16[64,2048]{1,0:T(8,128)(2,1)S(1)}, u32[]{:S(2)}, u32[]{:S(2)}) collective-permute-start(bf16[64,2048]{1,0:T(8,128)(2,1)S(1)} %add_convert_fusion), channel_id=1, source_target_pairs={{0,4},{1,5},{2,6},{3,7},{4,0},{5,1},{6,2},{7,3},{8,12},{9,13},{10,... | collective-permute-start | bytes 786440 | tf_op jit(solution)/shard_map/ppermute | solution.py:441
  189.0 11.2 %collective-permute-done.25.far_b_ref = bf16[64,2048]{1,0:T(8,128)(2,1)S(1)} collective-permute-done((bf16[64,2048]{1,0:T(8,128)(2,1)S(1)}, bf16[64,2048]{1,0:T(8,128)(2,1)S(1)}, u32[]{:S(2)}, u32[]{:S(2)}) %collective-permute-start.25) | collective-permute-done | bytes 262176 | tf_op jit(solution)/shard_map/ppermute | solution.py:441
  (126 shorter events, 31.0 us)
Async XLA Ops:
  2.3 44.2 %all-to-all-start = ((bf16[32,64,256]{2,1,0:T(8,128)(2,1)}), bf16[32,64,256]{2,1,0:T(8,128)(2,1)S(1)}, u32[]{:S(2)}, u32[]{:S(2)}) async-start(bf16[32,64,256]{2,1,0:T(8,128)(2,1)} %bitcast.20), calls=%async_computation | async-start | bytes 2097152 | tf_op jit(solution)/shard_map/all_to_all | solution.py:648
  9.8 33.8 %collective-permute-start.1 = (bf16[2064,256]{1,0:T(8,128)(2,1)S(1)}, bf16[2064,256]{1,0:T(8,128)(2,1)}, u32[]{:S(2)}, u32[]{:S(2)}) collective-permute-start(bf16[2064,256]{1,0:T(8,128)(2,1)S(1)} %pad_maximum_fusion.refs_2_), channel_id=1, source_target_pairs={{0,8},{1,9},{2,10},{3,11},{4,12},{5,13},{6,14},{7,15},{8,0},{9,1},... | collective-permute-start | bytes 3170312 | tf_op jit(solution)/shard_map/ppermute | solution.py:441
  10.1 36.4 %collective-permute-start = (bf16[2064,256]{1,0:T(8,128)(2,1)S(1)}, bf16[2064,256]{1,0:T(8,128)(2,1)}, u32[]{:S(2)}, u32[]{:S(2)}) collective-permute-start(bf16[2064,256]{1,0:T(8,128)(2,1)S(1)} %pad_maximum_fusion.refs_2_), channel_id=1, source_target_pairs={{0,1},{1,0},{2,3},{3,2},{4,5},{5,4},{6,7},{7,6},{8,9},{9,8},{10,11... | collective-permute-start | bytes 3170312 | tf_op jit(solution)/shard_map/ppermute | solution.py:441
  11.8 31.8 %collective-permute-start.3 = (bf16[256,2048]{1,0:T(8,128)(2,1)}, bf16[256,2048]{1,0:T(8,128)(2,1)}, u32[]{:S(2)}, u32[]{:S(2)}) collective-permute-start(bf16[256,2048]{1,0:T(8,128)(2,1)} %refs_10_.2), channel_id=1, source_target_pairs={{0,8},{1,9},{2,10},{3,11},{4,12},{5,13},{6,14},{7,15},{8,0},{9,1},... | collective-permute-start | bytes 3145736 | tf_op jit(solution)/shard_map/ppermute | solution.py:441
  12.7 30.8 %collective-permute-start.2 = (bf16[1280,256]{1,0:T(8,128)(2,1)}, bf16[1280,256]{1,0:T(8,128)(2,1)}, u32[]{:S(2)}, u32[]{:S(2)}) collective-permute-start(bf16[1280,256]{1,0:T(8,128)(2,1)} %slice.15), channel_id=1, source_target_pairs={{0,2},{1,3},{2,0},{3,1},{4,6},{5,7},{6,4},{7,5},{8,10},{9,11},{10,... | collective-permute-start | bytes 1966088 | tf_op jit(solution)/shard_map/ppermute | solution.py:441
  46.5 25.9 %collective-permute-start.4 = (bf16[2064,256]{1,0:T(8,128)(2,1)}, bf16[2064,256]{1,0:T(8,128)(2,1)}, u32[]{:S(2)}, u32[]{:S(2)}) collective-permute-start(bf16[2064,256]{1,0:T(8,128)(2,1)} %collective-permute-done.refs_3_), channel_id=1, source_target_pairs={{0,8},{1,9},{2,10},{3,11},{4,12},{5,13},{6,14},{7,15},{8,0},{9,1},... | collective-permute-start | bytes 3170312 | tf_op jit(solution)/shard_map/ppermute | solution.py:441
  46.5 25.9 %collective-permute-start.6 = (bf16[256,2048]{1,0:T(8,128)(2,1)}, bf16[256,2048]{1,0:T(8,128)(2,1)}, u32[]{:S(2)}, u32[]{:S(2)}) collective-permute-start(bf16[256,2048]{1,0:T(8,128)(2,1)} %refs_10_.2), channel_id=1, source_target_pairs={{0,1},{1,0},{2,3},{3,2},{4,5},{5,4},{6,7},{7,6},{8,9},{9,8},{10,11... | collective-permute-start | bytes 3145736 | tf_op jit(solution)/shard_map/ppermute | solution.py:441
  46.9 19.9 %collective-permute-start.5 = (bf16[784,256]{1,0:T(8,128)(2,1)}, bf16[784,256]{1,0:T(8,128)(2,1)S(1)}, u32[]{:S(2)}, u32[]{:S(2)}) collective-permute-start(bf16[784,256]{1,0:T(8,128)(2,1)} %fusion), channel_id=1, source_target_pairs={{0,2},{1,3},{2,0},{3,1},{4,6},{5,7},{6,4},{7,5},{8,10},{9,11},{10,... | collective-permute-start | bytes 1204232 | tf_op jit(solution)/shard_map/ppermute | solution.py:441
  48.6 21.1 %collective-permute-start.7 = (bf16[128,2048]{1,0:T(8,128)(2,1)}, bf16[128,2048]{1,0:T(8,128)(2,1)S(1)}, u32[]{:S(2)}, u32[]{:S(2)}) collective-permute-start(bf16[128,2048]{1,0:T(8,128)(2,1)} %get-tuple-element.116), channel_id=1, source_target_pairs={{0,2},{1,3},{2,0},{3,1},{4,6},{5,7},{6,4},{7,5},{8,10},{9,11},{10,... | collective-permute-start | bytes 1572872 | tf_op jit(solution)/shard_map/ppermute | solution.py:441
  72.4 43.8 %all-to-all-start.1 = ((bf16[32,72,256]{2,1,0:T(8,128)(2,1)}), bf16[32,72,256]{2,1,0:T(8,128)(2,1)S(1)}, u32[]{:S(2)}, u32[]{:S(2)}) async-start(bf16[32,72,256]{2,1,0:T(8,128)(2,1)} %attend_prefix.1), calls=%async_computation.1 | async-start | bytes 2359296 | tf_op jit(solution)/shard_map/all_to_all | solution.py:683
  77.1 32.9 %collective-permute-start.10 = (bf16[128,2048]{1,0:T(8,128)(2,1)}, bf16[128,2048]{1,0:T(8,128)(2,1)S(1)}, u32[]{:S(2)}, u32[]{:S(2)}) collective-permute-start(bf16[128,2048]{1,0:T(8,128)(2,1)} %get-tuple-element.128), channel_id=1, source_target_pairs={{0,2},{1,3},{2,0},{3,1},{4,6},{5,7},{6,4},{7,5},{8,10},{9,11},{10,... | collective-permute-start | bytes 1572872 | tf_op jit(solution)/shard_map/ppermute | solution.py:441
  80.2 30.0 %collective-permute-start.9 = (bf16[2064,256]{1,0:T(8,128)(2,1)S(1)}, bf16[2064,256]{1,0:T(8,128)(2,1)S(1)}, u32[]{:S(2)}, u32[]{:S(2)}) collective-permute-start(bf16[2064,256]{1,0:T(8,128)(2,1)S(1)} %constant_dynamic-update-slice_fusion.refs_4_), channel_id=1, source_target_pairs={{0,8},{1,9},{2,10},{3,11},{4,12},{5,13},{6,14},{7,15},{8,0},{9,1},... | collective-permute-start | bytes 3170312 | tf_op jit(solution)/shard_map/ppermute | solution.py:441
  80.3 34.8 %collective-permute-start.8 = (bf16[2064,256]{1,0:T(8,128)(2,1)S(1)}, bf16[2064,256]{1,0:T(8,128)(2,1)S(1)}, u32[]{:S(2)}, u32[]{:S(2)}) collective-permute-start(bf16[2064,256]{1,0:T(8,128)(2,1)S(1)} %constant_dynamic-update-slice_fusion.refs_4_), channel_id=1, source_target_pairs={{0,1},{1,0},{2,3},{3,2},{4,5},{5,4},{6,7},{7,6},{8,9},{9,8},{10,11... | collective-permute-start | bytes 3170312 | tf_op jit(solution)/shard_map/ppermute | solution.py:441
  81.8 28.3 %collective-permute-start.11 = (bf16[256,2048]{1,0:T(8,128)(2,1)}, bf16[256,2048]{1,0:T(8,128)(2,1)S(1)}, u32[]{:S(2)}, u32[]{:S(2)}) collective-permute-start(bf16[256,2048]{1,0:T(8,128)(2,1)} %collective-permute-done.6.refs_11_), channel_id=1, source_target_pairs={{0,8},{1,9},{2,10},{3,11},{4,12},{5,13},{6,14},{7,15},{8,0},{9,1},... | collective-permute-start | bytes 3145736 | tf_op jit(solution)/shard_map/ppermute | solution.py:441
  118.2 29.6 %collective-permute-start.17 = (bf16[2064,256]{1,0:T(8,128)(2,1)S(1)}, bf16[2064,256]{1,0:T(8,128)(2,1)S(1)}, u32[]{:S(2)}, u32[]{:S(2)}) collective-permute-start(bf16[2064,256]{1,0:T(8,128)(2,1)S(1)} %copy-done.20), channel_id=1, source_target_pairs={{0,8},{1,9},{2,10},{3,11},{4,12},{5,13},{6,14},{7,15},{8,0},{9,1},... | collective-permute-start | bytes 3170312 | tf_op jit(solution)/shard_map/ppermute | solution.py:441
  118.2 29.5 %collective-permute-start.18 = (bf16[256,2048]{1,0:T(8,128)(2,1)S(1)}, bf16[256,2048]{1,0:T(8,128)(2,1)S(1)}, u32[]{:S(2)}, u32[]{:S(2)}) collective-permute-start(bf16[256,2048]{1,0:T(8,128)(2,1)S(1)} %copy-done.17), channel_id=1, source_target_pairs={{0,1},{1,0},{2,3},{3,2},{4,5},{5,4},{6,7},{7,6},{8,9},{9,8},{10,11... | collective-permute-start | bytes 3145736 | tf_op jit(solution)/shard_map/ppermute | solution.py:441
  118.8 14.9 %collective-permute-start.13 = (bf16[64,2048]{1,0:T(8,128)(2,1)S(1)}, bf16[64,2048]{1,0:T(8,128)(2,1)S(1)}, u32[]{:S(2)}, u32[]{:S(2)}) collective-permute-start(bf16[64,2048]{1,0:T(8,128)(2,1)S(1)} %get-tuple-element.151), channel_id=1, source_target_pairs={{0,4},{1,5},{2,6},{3,7},{4,0},{5,1},{6,2},{7,3},{8,12},{9,13},{10,... | collective-permute-start | bytes 786440 | tf_op jit(solution)/shard_map/ppermute | solution.py:441
  121.0 14.2 %collective-permute-start.16 = (bf16[128,2048]{1,0:T(8,128)(2,1)S(1)}, bf16[128,2048]{1,0:T(8,128)(2,1)S(1)}, u32[]{:S(2)}, u32[]{:S(2)}) collective-permute-start(bf16[128,2048]{1,0:T(8,128)(2,1)S(1)} %get-tuple-element.193.refs_1_.hidden_ref), channel_id=1, source_target_pairs={{0,16},{1,17},{2,18},{3,19},{4,20},{5,21},{6,22},{7,23},{8,24},{9,... | collective-permute-start | bytes 1572872 | tf_op jit(solution)/shard_map/ppermute | solution.py:441
  133.7 14.1 %collective-permute-start.14 = (bf16[64,2048]{1,0:T(8,128)(2,1)S(1)}, bf16[64,2048]{1,0:T(8,128)(2,1)S(1)}, u32[]{:S(2)}, u32[]{:S(2)}) collective-permute-start(bf16[64,2048]{1,0:T(8,128)(2,1)S(1)} %get-tuple-element.152), channel_id=1, source_target_pairs={{0,4},{1,5},{2,6},{3,7},{4,0},{5,1},{6,2},{7,3},{8,12},{9,13},{10,... | collective-permute-start | bytes 786440 | tf_op jit(solution)/shard_map/ppermute | solution.py:441
  133.7 14.1 %collective-permute-start.15 = (bf16[64,2048]{1,0:T(8,128)(2,1)S(1)}, bf16[64,2048]{1,0:T(8,128)(2,1)S(1)}, u32[]{:S(2)}, u32[]{:S(2)}) collective-permute-start(bf16[64,2048]{1,0:T(8,128)(2,1)S(1)} %collective-permute-done.13.refs_0_), channel_id=1, source_target_pairs={{0,16},{1,17},{2,18},{3,19},{4,20},{5,21},{6,22},{7,23},{8,24},{9,... | collective-permute-start | bytes 786440 | tf_op jit(solution)/shard_map/ppermute | solution.py:441
  171.8 14.1 %collective-permute-start.24 = (bf16[64,2048]{1,0:T(8,128)(2,1)S(1)}, bf16[64,2048]{1,0:T(8,128)(2,1)S(1)}, u32[]{:S(2)}, u32[]{:S(2)}) collective-permute-start(bf16[64,2048]{1,0:T(8,128)(2,1)S(1)} %add_convert_fusion.1), channel_id=1, source_target_pairs={{0,4},{1,5},{2,6},{3,7},{4,0},{5,1},{6,2},{7,3},{8,12},{9,13},{10,... | collective-permute-start | bytes 786440 | tf_op jit(solution)/shard_map/ppermute | solution.py:441
  171.9 14.1 %collective-permute-start.23 = (bf16[64,2048]{1,0:T(8,128)(2,1)}, bf16[64,2048]{1,0:T(8,128)(2,1)S(1)}, u32[]{:S(2)}, u32[]{:S(2)}) collective-permute-start(bf16[64,2048]{1,0:T(8,128)(2,1)} %get-tuple-element.197), channel_id=1, source_target_pairs={{0,16},{1,17},{2,18},{3,19},{4,20},{5,21},{6,22},{7,23},{8,24},{9,... | collective-permute-start | bytes 786440 | tf_op jit(solution)/shard_map/ppermute | solution.py:441
  184.5 15.6 %collective-permute-start.22 = (bf16[128,2048]{1,0:T(8,128)(2,1)}, bf16[128,2048]{1,0:T(8,128)(2,1)S(1)}, u32[]{:S(2)}, u32[]{:S(2)}) collective-permute-start(bf16[128,2048]{1,0:T(8,128)(2,1)} %get-tuple-element.196), channel_id=1, source_target_pairs={{0,16},{1,17},{2,18},{3,19},{4,20},{5,21},{6,22},{7,23},{8,24},{9,... | collective-permute-start | bytes 1572872 | tf_op jit(solution)/shard_map/ppermute | solution.py:441
  186.0 14.1 %collective-permute-start.25 = (bf16[64,2048]{1,0:T(8,128)(2,1)S(1)}, bf16[64,2048]{1,0:T(8,128)(2,1)S(1)}, u32[]{:S(2)}, u32[]{:S(2)}) collective-permute-start(bf16[64,2048]{1,0:T(8,128)(2,1)S(1)} %add_convert_fusion), channel_id=1, source_target_pairs={{0,4},{1,5},{2,6},{3,7},{4,0},{5,1},{6,2},{7,3},{8,12},{9,13},{10,... | collective-permute-start | bytes 786440 | tf_op jit(solution)/shard_map/ppermute | solution.py:441
  (39 other events, 507.6 us)

commit v17 on v16

--- a/solution.py
+++ b/solution.py
@@ -16,7 +16,7 @@
 UNROLL = 4
 EMPTY = 64.0
 ROW_BLOCK = 256
-KEY_CHUNK = 1024
+KEY_CHUNK = 512
 
 norm_eps = 1e-12
 score_scale = HD ** (-0.5)

time: 203 us -> 203 us (level)
  Pallas kernels: 57.1 us -> 54.5 us
  waiting for transfers between devices: 82.5 us -> 85 us
    pallas_call x1, Pallas kernels: 16.6 us -> 14 us  [attend_prefix(): pl.pallas_call(far_kernel, out_shape=jax.ShapeDtypeStruct((sources, capac...]
    ppermute x26, waiting for transfers between devices: 82.5 us -> 85 us  [swap(): lax.ppermute(leaf, ('grp', 'dev'), pairs)]
  transfers between devices with their start and end apart: 28 -> 28, of which waited for: 10 -> 10; matrix products, arithmetic and copies ran while one was open for 11% -> 11% of each run, Pallas kernels for 25% -> 24%
where the time goes in v17:
time: 203 us
  waiting for transfers between devices  85 us (42%)
  Pallas kernels  54.5 us (27%)
  starting transfers between devices  36.2 us (18%)
  local copies, waits for them, and re-layouts  24 us (12%)
  other arithmetic  2.29 us (1%)
    ppermute x26, waiting for transfers between devices, swap(): lax.ppermute(leaf, ('grp', 'dev'), pairs)  85 us
    pallas_call x3, Pallas kernels, feed_forward(): pl.pallas_call(functools.partial(mlp_kernel, pieces, up_plan, down_plan),...  30.4 us
    ppermute x26, starting transfers between devices, swap(): lax.ppermute(leaf, ('grp', 'dev'), pairs)  24.2 us
    pallas_call x1, Pallas kernels, attend_prefix(): pl.pallas_call(far_kernel, out_shape=jax.ShapeDtypeStruct((sources, capac...  14 us
    unnamed x74, local copies, waits for them, and re-layouts  12.6 us
    all_to_all x1, starting transfers between devices, on_device(): lax.all_to_all(outgoing.reshape(sources, capacity, part_width), ('grp', '...  7.3 us
    all_to_all x1, starting transfers between devices, on_device(): lax.all_to_all(answer_part, ('grp', 'dev'), split_axis=0, concat_axis=0,...  4.72 us
    pallas_call x1, Pallas kernels, attend_suffix(): pl.pallas_call(functools.partial(own_kernel, local_heads), out_shape=(jax...  4.48 us
  transfers between devices with their start and end apart: 28, of which 10 were waited for; matrix products, arithmetic and copies ran while one was open for 11% of the time, Pallas kernels for 24%

profile of v17, /device:TPU:0, one launch (start us, length us, event | category | flops | bytes accessed | tf_op | source)
XLA Modules:
  0.0 202.7 jit_solution(13078003799601268848)
XLA Ops:
  0.0 2.3 %pack_queries.1 = bf16[4,8,64,256]{3,2,1,0:T(8,128)(2,1)} custom-call(s32[1,4]{1,0:T(1,128)} %lengths_ref.5, s32[1,4]{1,0:T(1,128)} %groups_ref.3, bf16[128,2048]{1,0:T(8,128)(2,1)} %query_ref.3), custom_call_target="tpu_custom_call" | custom-call | tf_op jit(solution)/shard_map/pack_queries/pallas_call | solution.py:76
  2.3 7.3 %all-to-all-start = ((bf16[32,64,256]{2,1,0:T(8,128)(2,1)}), bf16[32,64,256]{2,1,0:T(8,128)(2,1)S(1)}, u32[]{:S(2)}, u32[]{:S(2)}) async-start(bf16[32,64,256]{2,1,0:T(8,128)(2,1)} %bitcast.20), calls=%async_computation | async-start | bytes 2097152 | tf_op jit(solution)/shard_map/all_to_all | solution.py:648
  15.0 4.1 %copy.18 = bf16[1,4096,256]{1,2,0:T(8,128)(2,1)} copy(bf16[1,4096,256]{2,1,0:T(8,128)(2,1)} %param.22) | data formatting | bytes 4194304 | tf_op args[6]
  19.1 4.1 %copy.19 = bf16[1,4096,256]{1,2,0:T(8,128)(2,1)} copy(bf16[1,4096,256]{2,1,0:T(8,128)(2,1)} %param.23) | data formatting | bytes 4194304 | tf_op args[7]
  23.2 4.1 %copy.20 = bf16[4096,2,128]{2,0,1:T(8,128)(2,1)} copy(bf16[4096,2,128]{0,2,1:T(8,128)(2,1)} %bitcast.19) | data formatting | bytes 4194304 | tf_op jit(solution)/shard_map/reshape;squeeze | solution.py:660
  27.3 4.1 %concatenate.13.values_hbm = bf16[2,4096,256]{2,1,0:T(8,128)(2,1)} pad(bf16[2,4096,128]{2,1,0:T(8,128)(2,1)} %bitcast.18, bf16[]{:T(256)} %constant.0.clone.1), padding=0_0x0_0x0_128 | pad | bytes 6291458 | tf_op jit(solution)/shard_map/concatenate | solution.py:661
  31.5 4.5 %attend_suffix.1 = (f32[128,2048]{1,0:T(8,128)S(1)}, f32[128,128]{1,0:T(8,128)S(1)}, f32[128,128]{1,0:T(8,128)S(1)}) custom-call(s32[1,4]{1,0:T(1,128)S(1)} %copy-done.10, bf16[128,2048]{1,0:T(8,128)(2,1)S(1)} %copy-done.3, bf16[128,2048]{1,0:T(8,128)(2,1)S(1)} %copy-done.12, bf16[128,2048]{1,0:T(8,128)(2,1)S(1)} %copy-done.13), custom_call_target="tpu_custom_call" | custom-call | flops 1342177280 | bytes 2097152 | tf_op jit(solution)/shard_map/attend_suffix/pallas_call | solution.py:320
  35.9 2.3 %fusion.1 = (bf16[128,2048]{1,0:T(8,128)(2,1)}, bf16[128,2048]{1,0:T(8,128)(2,1)}) fusion(bf16[256,2048]{1,0:T(8,128)(2,1)} %refs_10_.2), kind=kLoop, calls=%fused_computation.11 | loop fusion | bytes 2097152 | tf_op jit(solution)/shard_map/slice | solution.py:644
  38.2 5.3 %collective-permute-done.2 = bf16[1280,256]{1,0:T(8,128)(2,1)} collective-permute-done((bf16[1280,256]{1,0:T(8,128)(2,1)}, bf16[1280,256]{1,0:T(8,128)(2,1)}, u32[]{:S(2)}, u32[]{:S(2)}) %collective-permute-start.2) | collective-permute-done | bytes 655392 | tf_op jit(solution)/shard_map/ppermute | solution.py:441
  43.5 3.0 %collective-permute-done.refs_3_ = bf16[2064,256]{1,0:T(8,128)(2,1)} collective-permute-done((bf16[2064,256]{1,0:T(8,128)(2,1)S(1)}, bf16[2064,256]{1,0:T(8,128)(2,1)}, u32[]{:S(2)}, u32[]{:S(2)}) %collective-permute-start) | collective-permute-done | bytes 1056800 | tf_op jit(solution)/shard_map/ppermute | solution.py:441
  50.2 14.0 %attend_prefix.1 = bf16[32,72,256]{2,1,0:T(8,128)(2,1)} custom-call(s32[32]{0:T(128)} %convert_reduce_fusion.counts_ref, bf16[32,64,256]{2,1,0:T(8,128)(2,1)} %copy-done.26, bf16[256,4096]{1,0:T(8,128)(2,1)} %bitcast.21, bf16[2,4096,256]{2,1,0:T(8,128)(2,1)} %concatenate.13.values_hbm), custom_call_target="tpu_custom_call" | custom-call | flops 8589934592 | bytes 8388608 | tf_op jit(solution)/shard_map/attend_prefix/pallas_call | solution.py:246
  64.3 5.5 %collective-permute-done.7 = bf16[128,2048]{1,0:T(8,128)(2,1)S(1)} collective-permute-done((bf16[128,2048]{1,0:T(8,128)(2,1)}, bf16[128,2048]{1,0:T(8,128)(2,1)S(1)}, u32[]{:S(2)}, u32[]{:S(2)}) %collective-permute-start.7) | collective-permute-done | bytes 524320 | tf_op jit(solution)/shard_map/ppermute | solution.py:441
  69.7 2.7 %collective-permute-done.6.refs_11_ = bf16[256,2048]{1,0:T(8,128)(2,1)} collective-permute-done((bf16[256,2048]{1,0:T(8,128)(2,1)}, bf16[256,2048]{1,0:T(8,128)(2,1)}, u32[]{:S(2)}, u32[]{:S(2)}) %collective-permute-start.6) | collective-permute-done | bytes 1048608 | tf_op jit(solution)/shard_map/ppermute | solution.py:441
  72.4 4.7 %all-to-all-start.1 = ((bf16[32,72,256]{2,1,0:T(8,128)(2,1)}), bf16[32,72,256]{2,1,0:T(8,128)(2,1)S(1)}, u32[]{:S(2)}, u32[]{:S(2)}) async-start(bf16[32,72,256]{2,1,0:T(8,128)(2,1)} %attend_prefix.1), calls=%async_computation.1 | async-start | bytes 2359296 | tf_op jit(solution)/shard_map/all_to_all | solution.py:683
  82.0 28.0 %collective-permute-done.10 = bf16[128,2048]{1,0:T(8,128)(2,1)S(1)} collective-permute-done((bf16[128,2048]{1,0:T(8,128)(2,1)}, bf16[128,2048]{1,0:T(8,128)(2,1)S(1)}, u32[]{:S(2)}, u32[]{:S(2)}) %collective-permute-start.10) | collective-permute-done | bytes 524320 | tf_op jit(solution)/shard_map/ppermute | solution.py:441
  110.2 4.9 %collective-permute-done.8.refs_5_ = bf16[2064,256]{1,0:T(8,128)(2,1)S(1)} collective-permute-done((bf16[2064,256]{1,0:T(8,128)(2,1)S(1)}, bf16[2064,256]{1,0:T(8,128)(2,1)S(1)}, u32[]{:S(2)}, u32[]{:S(2)}) %collective-permute-start.8) | collective-permute-done | bytes 1056800 | tf_op jit(solution)/shard_map/ppermute | solution.py:441
  118.8 2.2 %collective-permute-start.13 = (bf16[64,2048]{1,0:T(8,128)(2,1)S(1)}, bf16[64,2048]{1,0:T(8,128)(2,1)S(1)}, u32[]{:S(2)}, u32[]{:S(2)}) collective-permute-start(bf16[64,2048]{1,0:T(8,128)(2,1)S(1)} %get-tuple-element.151), channel_id=1, source_target_pairs={{0,4},{1,5},{2,6},{3,7},{4,0},{5,1},{6,2},{7,3},{8,12},{9,13},{10,... | collective-permute-start | bytes 786440 | tf_op jit(solution)/shard_map/ppermute | solution.py:441
  122.7 11.0 %collective-permute-done.13.refs_0_ = bf16[64,2048]{1,0:T(8,128)(2,1)S(1)} collective-permute-done((bf16[64,2048]{1,0:T(8,128)(2,1)S(1)}, bf16[64,2048]{1,0:T(8,128)(2,1)S(1)}, u32[]{:S(2)}, u32[]{:S(2)}) %collective-permute-start.13) | collective-permute-done | bytes 262176 | tf_op jit(solution)/shard_map/ppermute | solution.py:441
  135.2 12.5 %collective-permute-done.14.refs_0_ = bf16[64,2048]{1,0:T(8,128)(2,1)S(1)} collective-permute-done((bf16[64,2048]{1,0:T(8,128)(2,1)S(1)}, bf16[64,2048]{1,0:T(8,128)(2,1)S(1)}, u32[]{:S(2)}, u32[]{:S(2)}) %collective-permute-start.14) | collective-permute-done | bytes 262176 | tf_op jit(solution)/shard_map/ppermute | solution.py:441
  151.5 9.2 %feed_forward.3 = (bf16[64,2048]{1,0:T(8,128)(2,1)}, bf16[64,2048]{1,0:T(8,128)(2,1)}) custom-call(bf16[64,2048]{1,0:T(8,128)(2,1)} %copy-done.29, bf16[64,2048]{1,0:T(8,128)(2,1)} %copy-done.30, bf16[2064,256]{1,0:T(8,128)(2,1)} %copy-done.14, bf16[2064,256]{1,0:T(8,128)(2,1)} %collective-permute-done.refs_3_, bf16[2064,256]{1,0:T(8,128)(2,1)} %copy-done.15, ...), custom_call_target="tpu_custom_call" | custom-call | flops 2147483648 | bytes 16777216 | tf_op jit(solution)/shard_map/feed_forward/pallas_call | solution.py:542
  162.4 9.2 %feed_forward.4 = (bf16[64,2048]{1,0:T(8,128)(2,1)}, bf16[64,2048]{1,0:T(8,128)(2,1)}) custom-call(bf16[64,2048]{1,0:T(8,128)(2,1)} %copy-done.28, bf16[64,2048]{1,0:T(8,128)(2,1)} %copy-done.31, bf16[2064,256]{1,0:T(8,128)(2,1)} %copy-done.14, bf16[2064,256]{1,0:T(8,128)(2,1)} %collective-permute-done.refs_3_, bf16[2064,256]{1,0:T(8,128)(2,1)} %copy-done.15, ...), custom_call_target="tpu_custom_call" | custom-call | flops 2147483648 | bytes 16777216 | tf_op jit(solution)/shard_map/feed_forward/pallas_call | solution.py:542
  172.6 11.9 %feed_forward.5 = (bf16[128,2048]{1,0:T(8,128)(2,1)}, bf16[128,2048]{1,0:T(8,128)(2,1)}) custom-call(bf16[128,2048]{1,0:T(8,128)(2,1)} %copy-done.27, bf16[128,2048]{1,0:T(8,128)(2,1)} %copy-done, bf16[2064,256]{1,0:T(8,128)(2,1)} %copy-done.14, bf16[2064,256]{1,0:T(8,128)(2,1)} %collective-permute-done.refs_3_, bf16[2064,256]{1,0:T(8,128)(2,1)} %copy-done.15, ...), custom_call_target="tpu_custom_call" | custom-call | flops 4294967296 | bytes 16777216 | tf_op jit(solution)/shard_map/feed_forward/pallas_call | solution.py:542
  186.1 2.9 %collective-permute-start.25 = (bf16[64,2048]{1,0:T(8,128)(2,1)S(1)}, bf16[64,2048]{1,0:T(8,128)(2,1)S(1)}, u32[]{:S(2)}, u32[]{:S(2)}) collective-permute-start(bf16[64,2048]{1,0:T(8,128)(2,1)S(1)} %add_convert_fusion), channel_id=1, source_target_pairs={{0,4},{1,5},{2,6},{3,7},{4,0},{5,1},{6,2},{7,3},{8,12},{9,13},{10,... | collective-permute-start | bytes 786440 | tf_op jit(solution)/shard_map/ppermute | solution.py:441
  189.0 11.2 %collective-permute-done.25.far_b_ref = bf16[64,2048]{1,0:T(8,128)(2,1)S(1)} collective-permute-done((bf16[64,2048]{1,0:T(8,128)(2,1)S(1)}, bf16[64,2048]{1,0:T(8,128)(2,1)S(1)}, u32[]{:S(2)}, u32[]{:S(2)}) %collective-permute-start.25) | collective-permute-done | bytes 262176 | tf_op jit(solution)/shard_map/ppermute | solution.py:441
  (126 shorter events, 31.0 us)
Async XLA Ops:
  2.3 44.2 %all-to-all-start = ((bf16[32,64,256]{2,1,0:T(8,128)(2,1)}), bf16[32,64,256]{2,1,0:T(8,128)(2,1)S(1)}, u32[]{:S(2)}, u32[]{:S(2)}) async-start(bf16[32,64,256]{2,1,0:T(8,128)(2,1)} %bitcast.20), calls=%async_computation | async-start | bytes 2097152 | tf_op jit(solution)/shard_map/all_to_all | solution.py:648
  9.8 33.8 %collective-permute-start.1 = (bf16[2064,256]{1,0:T(8,128)(2,1)S(1)}, bf16[2064,256]{1,0:T(8,128)(2,1)}, u32[]{:S(2)}, u32[]{:S(2)}) collective-permute-start(bf16[2064,256]{1,0:T(8,128)(2,1)S(1)} %pad_maximum_fusion.refs_2_), channel_id=1, source_target_pairs={{0,8},{1,9},{2,10},{3,11},{4,12},{5,13},{6,14},{7,15},{8,0},{9,1},... | collective-permute-start | bytes 3170312 | tf_op jit(solution)/shard_map/ppermute | solution.py:441
  10.1 36.4 %collective-permute-start = (bf16[2064,256]{1,0:T(8,128)(2,1)S(1)}, bf16[2064,256]{1,0:T(8,128)(2,1)}, u32[]{:S(2)}, u32[]{:S(2)}) collective-permute-start(bf16[2064,256]{1,0:T(8,128)(2,1)S(1)} %pad_maximum_fusion.refs_2_), channel_id=1, source_target_pairs={{0,1},{1,0},{2,3},{3,2},{4,5},{5,4},{6,7},{7,6},{8,9},{9,8},{10,11... | collective-permute-start | bytes 3170312 | tf_op jit(solution)/shard_map/ppermute | solution.py:441
  11.8 31.8 %collective-permute-start.3 = (bf16[256,2048]{1,0:T(8,128)(2,1)}, bf16[256,2048]{1,0:T(8,128)(2,1)}, u32[]{:S(2)}, u32[]{:S(2)}) collective-permute-start(bf16[256,2048]{1,0:T(8,128)(2,1)} %refs_10_.2), channel_id=1, source_target_pairs={{0,8},{1,9},{2,10},{3,11},{4,12},{5,13},{6,14},{7,15},{8,0},{9,1},... | collective-permute-start | bytes 3145736 | tf_op jit(solution)/shard_map/ppermute | solution.py:441
  12.7 30.8 %collective-permute-start.2 = (bf16[1280,256]{1,0:T(8,128)(2,1)}, bf16[1280,256]{1,0:T(8,128)(2,1)}, u32[]{:S(2)}, u32[]{:S(2)}) collective-permute-start(bf16[1280,256]{1,0:T(8,128)(2,1)} %slice.15), channel_id=1, source_target_pairs={{0,2},{1,3},{2,0},{3,1},{4,6},{5,7},{6,4},{7,5},{8,10},{9,11},{10,... | collective-permute-start | bytes 1966088 | tf_op jit(solution)/shard_map/ppermute | solution.py:441
  46.5 25.9 %collective-permute-start.4 = (bf16[2064,256]{1,0:T(8,128)(2,1)}, bf16[2064,256]{1,0:T(8,128)(2,1)}, u32[]{:S(2)}, u32[]{:S(2)}) collective-permute-start(bf16[2064,256]{1,0:T(8,128)(2,1)} %collective-permute-done.refs_3_), channel_id=1, source_target_pairs={{0,8},{1,9},{2,10},{3,11},{4,12},{5,13},{6,14},{7,15},{8,0},{9,1},... | collective-permute-start | bytes 3170312 | tf_op jit(solution)/shard_map/ppermute | solution.py:441
  46.5 25.9 %collective-permute-start.6 = (bf16[256,2048]{1,0:T(8,128)(2,1)}, bf16[256,2048]{1,0:T(8,128)(2,1)}, u32[]{:S(2)}, u32[]{:S(2)}) collective-permute-start(bf16[256,2048]{1,0:T(8,128)(2,1)} %refs_10_.2), channel_id=1, source_target_pairs={{0,1},{1,0},{2,3},{3,2},{4,5},{5,4},{6,7},{7,6},{8,9},{9,8},{10,11... | collective-permute-start | bytes 3145736 | tf_op jit(solution)/shard_map/ppermute | solution.py:441
  46.9 17.3 %collective-permute-start.5 = (bf16[784,256]{1,0:T(8,128)(2,1)}, bf16[784,256]{1,0:T(8,128)(2,1)S(1)}, u32[]{:S(2)}, u32[]{:S(2)}) collective-permute-start(bf16[784,256]{1,0:T(8,128)(2,1)} %fusion), channel_id=1, source_target_pairs={{0,2},{1,3},{2,0},{3,1},{4,6},{5,7},{6,4},{7,5},{8,10},{9,11},{10,... | collective-permute-start | bytes 1204232 | tf_op jit(solution)/shard_map/ppermute | solution.py:441
  48.6 21.1 %collective-permute-start.7 = (bf16[128,2048]{1,0:T(8,128)(2,1)}, bf16[128,2048]{1,0:T(8,128)(2,1)S(1)}, u32[]{:S(2)}, u32[]{:S(2)}) collective-permute-start(bf16[128,2048]{1,0:T(8,128)(2,1)} %get-tuple-element.116), channel_id=1, source_target_pairs={{0,2},{1,3},{2,0},{3,1},{4,6},{5,7},{6,4},{7,5},{8,10},{9,11},{10,... | collective-permute-start | bytes 1572872 | tf_op jit(solution)/shard_map/ppermute | solution.py:441
  72.4 43.8 %all-to-all-start.1 = ((bf16[32,72,256]{2,1,0:T(8,128)(2,1)}), bf16[32,72,256]{2,1,0:T(8,128)(2,1)S(1)}, u32[]{:S(2)}, u32[]{:S(2)}) async-start(bf16[32,72,256]{2,1,0:T(8,128)(2,1)} %attend_prefix.1), calls=%async_computation.1 | async-start | bytes 2359296 | tf_op jit(solution)/shard_map/all_to_all | solution.py:683
  77.1 32.9 %collective-permute-start.10 = (bf16[128,2048]{1,0:T(8,128)(2,1)}, bf16[128,2048]{1,0:T(8,128)(2,1)S(1)}, u32[]{:S(2)}, u32[]{:S(2)}) collective-permute-start(bf16[128,2048]{1,0:T(8,128)(2,1)} %get-tuple-element.128), channel_id=1, source_target_pairs={{0,2},{1,3},{2,0},{3,1},{4,6},{5,7},{6,4},{7,5},{8,10},{9,11},{10,... | collective-permute-start | bytes 1572872 | tf_op jit(solution)/shard_map/ppermute | solution.py:441
  80.2 30.0 %collective-permute-start.9 = (bf16[2064,256]{1,0:T(8,128)(2,1)S(1)}, bf16[2064,256]{1,0:T(8,128)(2,1)S(1)}, u32[]{:S(2)}, u32[]{:S(2)}) collective-permute-start(bf16[2064,256]{1,0:T(8,128)(2,1)S(1)} %constant_dynamic-update-slice_fusion.refs_4_), channel_id=1, source_target_pairs={{0,8},{1,9},{2,10},{3,11},{4,12},{5,13},{6,14},{7,15},{8,0},{9,1},... | collective-permute-start | bytes 3170312 | tf_op jit(solution)/shard_map/ppermute | solution.py:441
  80.3 34.8 %collective-permute-start.8 = (bf16[2064,256]{1,0:T(8,128)(2,1)S(1)}, bf16[2064,256]{1,0:T(8,128)(2,1)S(1)}, u32[]{:S(2)}, u32[]{:S(2)}) collective-permute-start(bf16[2064,256]{1,0:T(8,128)(2,1)S(1)} %constant_dynamic-update-slice_fusion.refs_4_), channel_id=1, source_target_pairs={{0,1},{1,0},{2,3},{3,2},{4,5},{5,4},{6,7},{7,6},{8,9},{9,8},{10,11... | collective-permute-start | bytes 3170312 | tf_op jit(solution)/shard_map/ppermute | solution.py:441
  81.8 28.3 %collective-permute-start.11 = (bf16[256,2048]{1,0:T(8,128)(2,1)}, bf16[256,2048]{1,0:T(8,128)(2,1)S(1)}, u32[]{:S(2)}, u32[]{:S(2)}) collective-permute-start(bf16[256,2048]{1,0:T(8,128)(2,1)} %collective-permute-done.6.refs_11_), channel_id=1, source_target_pairs={{0,8},{1,9},{2,10},{3,11},{4,12},{5,13},{6,14},{7,15},{8,0},{9,1},... | collective-permute-start | bytes 3145736 | tf_op jit(solution)/shard_map/ppermute | solution.py:441
  118.2 29.6 %collective-permute-start.17 = (bf16[2064,256]{1,0:T(8,128)(2,1)S(1)}, bf16[2064,256]{1,0:T(8,128)(2,1)S(1)}, u32[]{:S(2)}, u32[]{:S(2)}) collective-permute-start(bf16[2064,256]{1,0:T(8,128)(2,1)S(1)} %copy-done.20), channel_id=1, source_target_pairs={{0,8},{1,9},{2,10},{3,11},{4,12},{5,13},{6,14},{7,15},{8,0},{9,1},... | collective-permute-start | bytes 3170312 | tf_op jit(solution)/shard_map/ppermute | solution.py:441
  118.2 29.5 %collective-permute-start.18 = (bf16[256,2048]{1,0:T(8,128)(2,1)S(1)}, bf16[256,2048]{1,0:T(8,128)(2,1)S(1)}, u32[]{:S(2)}, u32[]{:S(2)}) collective-permute-start(bf16[256,2048]{1,0:T(8,128)(2,1)S(1)} %copy-done.17), channel_id=1, source_target_pairs={{0,1},{1,0},{2,3},{3,2},{4,5},{5,4},{6,7},{7,6},{8,9},{9,8},{10,11... | collective-permute-start | bytes 3145736 | tf_op jit(solution)/shard_map/ppermute | solution.py:441
  118.8 14.9 %collective-permute-start.13 = (bf16[64,2048]{1,0:T(8,128)(2,1)S(1)}, bf16[64,2048]{1,0:T(8,128)(2,1)S(1)}, u32[]{:S(2)}, u32[]{:S(2)}) collective-permute-start(bf16[64,2048]{1,0:T(8,128)(2,1)S(1)} %get-tuple-element.151), channel_id=1, source_target_pairs={{0,4},{1,5},{2,6},{3,7},{4,0},{5,1},{6,2},{7,3},{8,12},{9,13},{10,... | collective-permute-start | bytes 786440 | tf_op jit(solution)/shard_map/ppermute | solution.py:441
  121.0 14.2 %collective-permute-start.16 = (bf16[128,2048]{1,0:T(8,128)(2,1)S(1)}, bf16[128,2048]{1,0:T(8,128)(2,1)S(1)}, u32[]{:S(2)}, u32[]{:S(2)}) collective-permute-start(bf16[128,2048]{1,0:T(8,128)(2,1)S(1)} %get-tuple-element.193.refs_1_.hidden_ref), channel_id=1, source_target_pairs={{0,16},{1,17},{2,18},{3,19},{4,20},{5,21},{6,22},{7,23},{8,24},{9,... | collective-permute-start | bytes 1572872 | tf_op jit(solution)/shard_map/ppermute | solution.py:441
  133.7 14.1 %collective-permute-start.14 = (bf16[64,2048]{1,0:T(8,128)(2,1)S(1)}, bf16[64,2048]{1,0:T(8,128)(2,1)S(1)}, u32[]{:S(2)}, u32[]{:S(2)}) collective-permute-start(bf16[64,2048]{1,0:T(8,128)(2,1)S(1)} %get-tuple-element.152), channel_id=1, source_target_pairs={{0,4},{1,5},{2,6},{3,7},{4,0},{5,1},{6,2},{7,3},{8,12},{9,13},{10,... | collective-permute-start | bytes 786440 | tf_op jit(solution)/shard_map/ppermute | solution.py:441
  133.7 14.1 %collective-permute-start.15 = (bf16[64,2048]{1,0:T(8,128)(2,1)S(1)}, bf16[64,2048]{1,0:T(8,128)(2,1)S(1)}, u32[]{:S(2)}, u32[]{:S(2)}) collective-permute-start(bf16[64,2048]{1,0:T(8,128)(2,1)S(1)} %collective-permute-done.13.refs_0_), channel_id=1, source_target_pairs={{0,16},{1,17},{2,18},{3,19},{4,20},{5,21},{6,22},{7,23},{8,24},{9,... | collective-permute-start | bytes 786440 | tf_op jit(solution)/shard_map/ppermute | solution.py:441
  171.8 14.1 %collective-permute-start.24 = (bf16[64,2048]{1,0:T(8,128)(2,1)S(1)}, bf16[64,2048]{1,0:T(8,128)(2,1)S(1)}, u32[]{:S(2)}, u32[]{:S(2)}) collective-permute-start(bf16[64,2048]{1,0:T(8,128)(2,1)S(1)} %add_convert_fusion.1), channel_id=1, source_target_pairs={{0,4},{1,5},{2,6},{3,7},{4,0},{5,1},{6,2},{7,3},{8,12},{9,13},{10,... | collective-permute-start | bytes 786440 | tf_op jit(solution)/shard_map/ppermute | solution.py:441
  171.9 14.1 %collective-permute-start.23 = (bf16[64,2048]{1,0:T(8,128)(2,1)}, bf16[64,2048]{1,0:T(8,128)(2,1)S(1)}, u32[]{:S(2)}, u32[]{:S(2)}) collective-permute-start(bf16[64,2048]{1,0:T(8,128)(2,1)} %get-tuple-element.197), channel_id=1, source_target_pairs={{0,16},{1,17},{2,18},{3,19},{4,20},{5,21},{6,22},{7,23},{8,24},{9,... | collective-permute-start | bytes 786440 | tf_op jit(solution)/shard_map/ppermute | solution.py:441
  184.5 15.6 %collective-permute-start.22 = (bf16[128,2048]{1,0:T(8,128)(2,1)}, bf16[128,2048]{1,0:T(8,128)(2,1)S(1)}, u32[]{:S(2)}, u32[]{:S(2)}) collective-permute-start(bf16[128,2048]{1,0:T(8,128)(2,1)} %get-tuple-element.196), channel_id=1, source_target_pairs={{0,16},{1,17},{2,18},{3,19},{4,20},{5,21},{6,22},{7,23},{8,24},{9,... | collective-permute-start | bytes 1572872 | tf_op jit(solution)/shard_map/ppermute | solution.py:441
  186.1 14.1 %collective-permute-start.25 = (bf16[64,2048]{1,0:T(8,128)(2,1)S(1)}, bf16[64,2048]{1,0:T(8,128)(2,1)S(1)}, u32[]{:S(2)}, u32[]{:S(2)}) collective-permute-start(bf16[64,2048]{1,0:T(8,128)(2,1)S(1)} %add_convert_fusion), channel_id=1, source_target_pairs={{0,4},{1,5},{2,6},{3,7},{4,0},{5,1},{6,2},{7,3},{8,12},{9,13},{10,... | collective-permute-start | bytes 786440 | tf_op jit(solution)/shard_map/ppermute | solution.py:441
  (39 other events, 507.6 us)
